TPU v7x, 512 devices: a whole 4x4x16 slice. The times are simulated.
512 devices in a mesh: pp: 16 (over z), ep: 32 (over y, x, core).
Axes of the slice: x: 4, y: 4, z: 16, core: 2. Of those that a mesh axis runs over, the one named last changes fastest.
Arguments:
- state_fwd: bfloat16 [16, 768, 3584], P('pp', 'ep'), may hold values from -6 to 6
- state_bwd: bfloat16 [16, 768, 3584], P('pp', 'ep'), may hold values from -6 to 6
- enter_fwd: bfloat16 [1, 768, 3584], P(None, 'ep', 'pp'), may hold values from -6 to 6
- enter_bwd: bfloat16 [1, 768, 3584], P(None, 'ep', 'pp'), may hold values from -6 to 6
- norm_gain: float32 [16, 3584], P('pp'), may hold values from 0.1 to 1.9
- w_gate: bfloat16 [16, 3584, 4096], P('pp', None, 'ep'), may hold values from -0.09375 to 0.09375
- w_up: bfloat16 [16, 3584, 4096], P('pp', None, 'ep'), may hold values from -0.09375 to 0.09375
- w_down: bfloat16 [16, 4096, 3584], P('pp', 'ep'), may hold values from -0.1875 to 0.1875
- route_ids: int32 [16, 1, 2, 768, 2], P('pp', None, None, 'ep'), may hold values from 0 to 3, all different within a row; in each aligned block of 24 rows (0 to 23, 24 to 47, ..., all dimensions but the last counted through in order) at most 15 rows name the same one
- route_gates: float32 [16, 1, 2, 768, 2], P('pp', None, None, 'ep'), may hold values from 0.2 to 1
Outputs:
- out_fwd: bfloat16 [16, 768, 3584], P('pp', 'ep')
- out_bwd: bfloat16 [16, 768, 3584], P('pp', 'ep')
- leave_fwd: bfloat16 [1, 768, 3584], P(None, 'ep', 'pp')
- leave_bwd: bfloat16 [1, 768, 3584], P(None, 'ep', 'pp')
Inputs may be any that keep to these rules, and one draw needn't show every extreme that they name: `route_ids`: each row names 2 different experts. In the rows of one device at each section, step and direction (aligned blocks of 24 rows), no expert is named by more than 15 rows, and in some blocks one expert is named by exactly 15.
All inputs are finite; a program needn't handle non-finite values.
Results may differ from a plain program's by a relative error of at most 0.009.
Values may be sent and summed in bfloat16 or wider, within the bound.
No kernel may reach another device: no remote copies, remote signals or barrier semaphores. Data moves between devices by JAX's collectives and lax.ppermute only.
A program may use at most 128 MiB of HBM per device.

v0:
```python
import jax
import jax.numpy as jnp
from jax import lax
from jax.sharding import PartitionSpec as P

eps = 1e-06


def from_behind(block, axis, distance):
    devices = range(lax.axis_size(axis))
    route = [(i - distance, i) for i in devices if i - distance in devices]
    return lax.ppermute(block, axis, route)


def spread(value, axis, source):
    kept = jnp.where(lax.axis_index(axis) == source, value, 0).astype(value.dtype)
    return lax.psum(kept, axis)


def rms_normed(values, norm_scale):
    widened = values.astype(jnp.float32)
    inverse = lax.rsqrt(jnp.mean(widened * widened, axis=-1, keepdims=True) + eps)
    return (widened * inverse * norm_scale[None, :]).astype(jnp.bfloat16)


def slot_tables(expert_ids, weights, experts, capacity):
    row_count, pick_count = expert_ids.shape
    flat_ids = expert_ids.reshape(row_count * pick_count)
    columns = lax.broadcasted_iota(jnp.int32, (row_count * pick_count, experts), 1)
    onehot = (flat_ids[:, None] == columns).astype(jnp.int32)
    before = jnp.cumsum(onehot, axis=0) - onehot
    slot_index = jnp.sum(before * onehot, axis=1)
    target = (flat_ids * capacity + slot_index).reshape(row_count, pick_count)
    places = lax.broadcasted_iota(jnp.int32, (experts * capacity, row_count, pick_count), 0)
    matched = target[None, :, :] == places
    dispatch = jnp.sum(matched.astype(jnp.float32), axis=2).astype(jnp.bfloat16)
    combine = jnp.sum(
        jnp.where(matched, weights[None, :, :], jnp.zeros_like(weights)[None, :, :]), axis=2
    ).T
    return (dispatch, combine)


def expert_rows(incoming, gate_matrix, up_matrix, down_matrix):
    feature_count = incoming.shape[-1]
    flat_rows = incoming.reshape(-1, feature_count)
    gate_act = jnp.dot(flat_rows, gate_matrix, preferred_element_type=jnp.float32)
    up_act = jnp.dot(flat_rows, up_matrix, preferred_element_type=jnp.float32)
    hidden = (jax.nn.silu(gate_act) * up_act).astype(jnp.bfloat16)
    result = jnp.dot(hidden, down_matrix, preferred_element_type=jnp.float32).astype(jnp.bfloat16)
    return result.reshape(incoming.shape)


def prepare(values, norm_scale, expert_ids, weights, experts, capacity, share):
    normed = rms_normed(values, norm_scale)
    dispatch, combine = slot_tables(expert_ids, weights, experts, capacity)
    outgoing = jnp.dot(dispatch, normed, preferred_element_type=jnp.float32).astype(jnp.bfloat16)
    grouped = outgoing.reshape(experts, capacity, normed.shape[-1])
    return (jnp.repeat(grouped, share, axis=0), combine)


def finish(values, returned, combine, experts, share):
    feature_count = returned.shape[-1]
    capacity = returned.shape[1]
    summed = jnp.sum(
        returned.reshape(experts, share, capacity, feature_count).astype(jnp.float32), axis=1
    )
    mixture = jnp.dot(
        combine, summed.reshape(experts * capacity, feature_count), precision=lax.Precision.HIGHEST
    )
    return (values.astype(jnp.float32) + mixture).astype(jnp.bfloat16)


def body(
    state_fwd,
    state_bwd,
    enter_fwd,
    enter_bwd,
    norm_gain,
    w_gate,
    w_up,
    w_down,
    route_ids,
    route_gates,
):
    ep_count = lax.axis_size("ep")
    experts = max(2, ep_count // 8)
    share = ep_count // experts
    sections = lax.axis_size("pp")
    section_index = lax.axis_index("pp")
    tok_rows = state_fwd.shape[1]
    pick_count = route_ids.shape[-1]
    capacity = min(tok_rows, max(2, 5 * tok_rows * pick_count // (4 * experts)))
    gain_row = norm_gain[0]
    gate_matrix = w_gate[0]
    up_matrix = w_up[0]
    down_matrix = w_down[0]

    def run_expert(incoming):
        return expert_rows(incoming, gate_matrix, up_matrix, down_matrix)

    def one_direction(outgoing):
        finished = run_expert(
            lax.all_to_all(outgoing, "ep", split_axis=0, concat_axis=0, tiled=True)
        )
        return lax.all_to_all(finished, "ep", split_axis=0, concat_axis=0, tiled=True)

    arrivals_fwd, arrivals_bwd = (
        lax.all_gather(enter_fwd, "pp", axis=2, tiled=True),
        lax.all_gather(enter_bwd, "pp", axis=2, tiled=True),
    )
    fwd_in = state_fwd[0]
    bwd_in = state_bwd[0]
    send_fwd, table_fwd = prepare(
        fwd_in, gain_row, route_ids[0, 0, 0], route_gates[0, 0, 0], experts, capacity, share
    )
    send_bwd, table_bwd = prepare(
        bwd_in, gain_row, route_ids[0, 0, 1], route_gates[0, 0, 1], experts, capacity, share
    )
    back_fwd = one_direction(send_fwd)
    back_bwd = one_direction(send_bwd)
    fwd_out = finish(fwd_in, back_fwd, table_fwd, experts, share)
    bwd_out = finish(bwd_in, back_bwd, table_bwd, experts, share)
    exits_fwd = [fwd_out]
    exits_bwd = [bwd_out]
    fwd_shifted = from_behind(fwd_out, "pp", 1)
    bwd_shifted = from_behind(bwd_out, "pp", -1)
    fwd_in = jnp.where(section_index == 0, arrivals_fwd[0], fwd_shifted)
    bwd_in = jnp.where(section_index == sections - 1, arrivals_bwd[0], bwd_shifted)
    leaving_fwd = jnp.stack(exits_fwd)
    leaving_bwd = jnp.stack(exits_bwd)
    column_count = leaving_fwd.shape[2] // sections
    whole_fwd = spread(leaving_fwd, "pp", sections - 1)
    whole_bwd = spread(leaving_bwd, "pp", 0)
    leave_fwd = lax.dynamic_slice_in_dim(whole_fwd, section_index * column_count, column_count, 2)
    leave_bwd = lax.dynamic_slice_in_dim(whole_bwd, section_index * column_count, column_count, 2)
    return (fwd_in[None], bwd_in[None], leave_fwd, leave_bwd)


def solution(mesh):
    placed = (
        P("pp", "ep", None),
        P("pp", "ep", None),
        P(None, "ep", "pp"),
        P(None, "ep", "pp"),
        P("pp", None),
        P("pp", None, "ep"),
        P("pp", None, "ep"),
        P("pp", "ep", None),
        P("pp", None, None, "ep", None),
        P("pp", None, None, "ep", None),
    )
    return jax.shard_map(
        body,
        mesh=mesh,
        in_specs=placed,
        out_specs=(
            P("pp", "ep", None),
            P("pp", "ep", None),
            P(None, "ep", "pp"),
            P(None, "ep", "pp"),
        ),
        check_vma=False,
    )
```

profile of v0, /device:TPU:2, one launch (start us, length us, event | category | flops | bytes accessed | tf_op | source)
XLA Modules:
  0.0 434.2 jit_solution(9590195404590270709)
XLA Ops:
  7.2 0.8 fusion.48
  10.1 1.1 fusion.14
  12.7 1.3 convolution_convert_fusion.3
  14.1 2.2 broadcast_in_dim.50
  16.3 10.5 %all-to-all-start = ((bf16[32,15,3584]{2,1,0:T(8,128)(2,1)}), bf16[32,15,3584]{2,1,0:T(8,128)(2,1)}, u32[]{:S(2)}, u32[]{:S(2)}) async-start(bf16[32,15,3584]{2,1,0:T(8,128)(2,1)} %bitcast.79), calls=%async_computation | async-start | bytes 7340032 | tf_op jit(solution)/shard_map/all_to_all | solution.py:103
  27.5 45.0 %all-to-all-done = bf16[32,15,3584]{2,1,0:T(8,128)(2,1)} async-done(((bf16[32,15,3584]{2,1,0:T(8,128)(2,1)}), bf16[32,15,3584]{2,1,0:T(8,128)(2,1)}, u32[]{:S(2)}, u32[]{:S(2)}) %all-to-all-start) | async-done | bytes 3440672 | tf_op jit(solution)/shard_map/all_to_all | solution.py:103
  72.5 2.3 broadcast_in_dim.54
  74.8 6.8 %all-to-all-start.2 = ((bf16[32,15,3584]{2,1,0:T(8,128)(2,1)}), bf16[32,15,3584]{2,1,0:T(8,128)(2,1)}, u32[]{:S(2)}, u32[]{:S(2)}) async-start(bf16[32,15,3584]{2,1,0:T(8,128)(2,1)} %bitcast.80), calls=%async_computation.2 | async-start | bytes 7340032 | tf_op jit(solution)/shard_map/all_to_all | solution.py:103
  81.6 4.9 %reshape.96 = bf16[480,3584]{1,0:T(8,128)(2,1)} reshape(bf16[32,15,3584]{2,1,0:T(8,128)(2,1)} %all-to-all-done) | data formatting | bytes 6881280 | tf_op jit(solution)/shard_map/reshape | solution.py:45
  86.5 3.1 fusion.12
  89.7 7.4 %convolution_convert_fusion.1 = bf16[480,3584]{1,0:T(8,128)(2,1)} fusion(bf16[480,3584]{1,0:T(8,128)(2,1)} %reshape.96, bf16[1,128,3584]{2,1,0:T(8,128)(2,1)S(1)} %copy-done, bf16[1,3584,128]{2,1,0:T(8,128)(2,1)S(1)} %copy-done.1, f32[480,128]{1,0:T(8,128)S(1)} %fusion.12), kind=kOutput, calls=%fused_computation.3 | convolution fusion | flops 882892800 | bytes 8962048 | tf_op jit(solution)/shard_map/dot_general | solution.py:49
  97.1 4.8 %reshape.97 = bf16[32,15,3584]{2,1,0:T(8,128)(2,1)} reshape(bf16[480,3584]{1,0:T(8,128)(2,1)} %convolution_convert_fusion.1) | data formatting | bytes 6881280 | tf_op jit(solution)/shard_map/reshape | solution.py:50
  101.9 25.4 %all-to-all-done.2 = bf16[32,15,3584]{2,1,0:T(8,128)(2,1)} async-done(((bf16[32,15,3584]{2,1,0:T(8,128)(2,1)}), bf16[32,15,3584]{2,1,0:T(8,128)(2,1)}, u32[]{:S(2)}, u32[]{:S(2)}) %all-to-all-start.2) | async-done | bytes 3440672 | tf_op jit(solution)/shard_map/all_to_all | solution.py:103
  127.3 6.9 %all-to-all-start.1 = ((bf16[32,15,3584]{2,1,0:T(8,128)(2,1)}), bf16[32,15,3584]{2,1,0:T(8,128)(2,1)}, u32[]{:S(2)}, u32[]{:S(2)}) async-start(bf16[32,15,3584]{2,1,0:T(8,128)(2,1)} %reshape.97), calls=%async_computation.1 | async-start | bytes 7340032 | tf_op jit(solution)/shard_map/all_to_all | solution.py:105
  134.2 4.8 %reshape.101 = bf16[480,3584]{1,0:T(8,128)(2,1)} reshape(bf16[32,15,3584]{2,1,0:T(8,128)(2,1)} %all-to-all-done.2) | data formatting | bytes 6881280 | tf_op jit(solution)/shard_map/reshape | solution.py:45
  139.0 3.0 fusion.10
  142.0 7.4 %convolution_convert_fusion = bf16[480,3584]{1,0:T(8,128)(2,1)} fusion(bf16[480,3584]{1,0:T(8,128)(2,1)} %reshape.101, bf16[1,128,3584]{2,1,0:T(8,128)(2,1)S(1)} %copy-done, bf16[1,3584,128]{2,1,0:T(8,128)(2,1)S(1)} %copy-done.1, f32[480,128]{1,0:T(8,128)S(1)} %fusion.10), kind=kOutput, calls=%fused_computation.2 | convolution fusion | flops 882892800 | bytes 8962048 | tf_op jit(solution)/shard_map/dot_general | solution.py:49
  149.4 4.8 %reshape.102 = bf16[32,15,3584]{2,1,0:T(8,128)(2,1)} reshape(bf16[480,3584]{1,0:T(8,128)(2,1)} %convolution_convert_fusion) | data formatting | bytes 6881280 | tf_op jit(solution)/shard_map/reshape | solution.py:50
  154.2 25.6 %all-to-all-done.1 = bf16[32,15,3584]{2,1,0:T(8,128)(2,1)} async-done(((bf16[32,15,3584]{2,1,0:T(8,128)(2,1)}), bf16[32,15,3584]{2,1,0:T(8,128)(2,1)}, u32[]{:S(2)}, u32[]{:S(2)}) %all-to-all-start.1) | async-done | bytes 3440672 | tf_op jit(solution)/shard_map/all_to_all | solution.py:105
  179.8 6.8 %all-to-all-start.3 = ((bf16[32,15,3584]{2,1,0:T(8,128)(2,1)}), bf16[32,15,3584]{2,1,0:T(8,128)(2,1)}, u32[]{:S(2)}, u32[]{:S(2)}) async-start(bf16[32,15,3584]{2,1,0:T(8,128)(2,1)} %reshape.102), calls=%async_computation.3 | async-start | bytes 7340032 | tf_op jit(solution)/shard_map/all_to_all | solution.py:105
  186.9 44.7 %all_gather.6 = bf16[1,24,3584]{1,0,2:T(2,128)(2,1)S(1)} all-gather(bf16[1,24,224]{1,0,2:T(2,128)(2,1)S(1)} %copy.42), channel_id=1, replica_groups=mesh['pp'=16,'ep'=32] {'pp'}, dimensions={2}, use_global_device_ids=true | all-gather | bytes 182784 | tf_op jit(solution)/shard_map/all_gather | solution.py:108
  231.6 1.9 copy.43
  233.6 38.8 %all_gather.7 = bf16[1,24,3584]{1,0,2:T(2,128)(2,1)S(1)} all-gather(bf16[1,24,224]{1,0,2:T(2,128)(2,1)S(1)} %copy.46), channel_id=1, replica_groups=mesh['pp'=16,'ep'=32] {'pp'}, dimensions={2}, use_global_device_ids=true | all-gather | bytes 182784 | tf_op jit(solution)/shard_map/all_gather | solution.py:109
  272.4 3.0 copy.47
  275.4 2.8 convert_reduce_fusion.1
  278.9 5.1 %collective-permute-start = (bf16[24,3584]{1,0:T(8,128)(2,1)S(1)}, bf16[24,3584]{1,0:T(8,128)(2,1)}, u32[]{:S(2)}, u32[]{:S(2)}) collective-permute-start(bf16[24,3584]{1,0:T(8,128)(2,1)S(1)} %fusion), channel_id=1, source_target_pairs={{0,32},{32,64},{64,96},{96,128},{128,160},{160,192},{192,224},{224... | collective-permute-start | bytes 516104 | tf_op jit(solution)/shard_map/ppermute | solution.py:12
  283.9 2.7 convert_reduce_fusion
  287.4 1.3 collective-permute-start.1
  290.8 3.9 collective-permute-done.1
  295.4 129.1 %all-reduce.3.cloned.1.call-done = (bf16[1,24,3584]{2,1,0:T(8,128)(2,1)}, bf16[1,24,3584]{2,1,0:T(8,128)(2,1)}) async-done(((bf16[1,24,3584]{2,1,0:T(8,128)(2,1)}, bf16[1,24,3584]{2,1,0:T(8,128)(2,1)}), (bf16[1,24,3584]{2,1,0:T(8,128)(2,1)}, bf16[1,24,3584]{2,1,0:T(8,128)(2,1)})) %all-reduce.3.cloned.1.call-update) | async-done | bytes 344080 | tf_op jit(solution)/shard_map/psum | solution.py:17
  424.5 1.4 constant_dynamic-slice_fusion
  425.9 1.4 constant_dynamic-slice_fusion.1
  (54 shorter events, 8.9 us)
Async XLA Ops:
  7.2 82.5 %copy-start = (bf16[1,128,3584]{2,1,0:T(8,128)(2,1)S(1)}, bf16[1,128,3584]{2,1,0:T(8,128)(2,1)}, u32[]{:S(2)}) copy-start(bf16[1,128,3584]{2,1,0:T(8,128)(2,1)} %param.17) | copy-start | bytes 2752516
  16.3 10.5 %copy-start.4 = (bf16[1,24,3584]{2,1,0:T(8,128)(2,1)S(1)}, bf16[1,24,3584]{2,1,0:T(8,128)(2,1)}, u32[]{:S(2)}) copy-start(bf16[1,24,3584]{2,1,0:T(8,128)(2,1)} %param.11) | copy-start | bytes 516100
  16.3 56.1 %all-to-all-start = ((bf16[32,15,3584]{2,1,0:T(8,128)(2,1)}), bf16[32,15,3584]{2,1,0:T(8,128)(2,1)}, u32[]{:S(2)}, u32[]{:S(2)}) async-start(bf16[32,15,3584]{2,1,0:T(8,128)(2,1)} %bitcast.79), calls=%async_computation | async-start | bytes 7340032 | tf_op jit(solution)/shard_map/all_to_all | solution.py:103
  74.8 52.5 %all-to-all-start.2 = ((bf16[32,15,3584]{2,1,0:T(8,128)(2,1)}), bf16[32,15,3584]{2,1,0:T(8,128)(2,1)}, u32[]{:S(2)}, u32[]{:S(2)}) async-start(bf16[32,15,3584]{2,1,0:T(8,128)(2,1)} %bitcast.80), calls=%async_computation.2 | async-start | bytes 7340032 | tf_op jit(solution)/shard_map/all_to_all | solution.py:103
  81.6 4.9 %copy-start.2 = (bf16[1,3584,128]{2,1,0:T(8,128)(2,1)S(1)}, bf16[1,3584,128]{2,1,0:T(8,128)(2,1)}, u32[]{:S(2)}) copy-start(bf16[1,3584,128]{2,1,0:T(8,128)(2,1)} %param.15) | copy-start | bytes 2752516
  86.5 3.1 copy-start.1
  127.3 52.5 %all-to-all-start.1 = ((bf16[32,15,3584]{2,1,0:T(8,128)(2,1)}), bf16[32,15,3584]{2,1,0:T(8,128)(2,1)}, u32[]{:S(2)}, u32[]{:S(2)}) async-start(bf16[32,15,3584]{2,1,0:T(8,128)(2,1)} %reshape.97), calls=%async_computation.1 | async-start | bytes 7340032 | tf_op jit(solution)/shard_map/all_to_all | solution.py:105
  154.2 32.5 %copy-start.6 = (bf16[1,24,224]{2,1,0:T(8,128)(2,1)S(1)}, bf16[1,24,224]{2,1,0:T(8,128)(2,1)}, u32[]{:S(2)}) copy-start(bf16[1,24,224]{2,1,0:T(8,128)(2,1)} %param.12) | copy-start | bytes 32260
  179.8 104.1 %all-to-all-start.3 = ((bf16[32,15,3584]{2,1,0:T(8,128)(2,1)}), bf16[32,15,3584]{2,1,0:T(8,128)(2,1)}, u32[]{:S(2)}, u32[]{:S(2)}) async-start(bf16[32,15,3584]{2,1,0:T(8,128)(2,1)} %reshape.102), calls=%async_computation.3 | async-start | bytes 7340032 | tf_op jit(solution)/shard_map/all_to_all | solution.py:105
  186.7 46.8 %copy-start.7 = (bf16[1,24,224]{2,1,0:T(8,128)(2,1)S(1)}, bf16[1,24,224]{2,1,0:T(8,128)(2,1)}, u32[]{:S(2)}) copy-start(bf16[1,24,224]{2,1,0:T(8,128)(2,1)} %param.13) | copy-start | bytes 32260
  186.7 237.8 %all-reduce.3.cloned.1.call-start = ((), (), s32[]{:S(2)}) async-start(), calls=%async_computation.4 | async-start | bytes 688128 | tf_op jit(solution)/shard_map/psum | solution.py:17
  275.4 2.9 copy-start.3
  278.9 11.2 %collective-permute-start = (bf16[24,3584]{1,0:T(8,128)(2,1)S(1)}, bf16[24,3584]{1,0:T(8,128)(2,1)}, u32[]{:S(2)}, u32[]{:S(2)}) collective-permute-start(bf16[24,3584]{1,0:T(8,128)(2,1)S(1)} %fusion), channel_id=1, source_target_pairs={{0,32},{32,64},{64,96},{96,128},{128,160},{160,192},{192,224},{224... | collective-permute-start | bytes 516104 | tf_op jit(solution)/shard_map/ppermute | solution.py:12
  286.7 8.0 %copy-start.5 = (bf16[1,24,3584]{2,1,0:T(8,128)(2,1)S(1)}, bf16[1,24,3584]{2,1,0:T(8,128)(2,1)}, u32[]{:S(2)}) copy-start(bf16[1,24,3584]{2,1,0:T(8,128)(2,1)} %copy.47) | copy-start | bytes 516100
  287.4 7.3 %collective-permute-start.1 = (bf16[24,3584]{1,0:T(8,128)(2,1)S(1)}, bf16[24,3584]{1,0:T(8,128)(2,1)S(1)}, u32[]{:S(2)}, u32[]{:S(2)}) collective-permute-start(bf16[24,3584]{1,0:T(8,128)(2,1)S(1)} %fusion.1), channel_id=1, source_target_pairs={{32,0},{64,32},{96,64},{128,96},{160,128},{192,160},{224,192},{256... | collective-permute-start | bytes 516104 | tf_op jit(solution)/shard_map/ppermute | solution.py:12
Sparse Core Ops, SparseCore 0:
  290.2 134.2 all-reduce.2
where the time goes:
time: 435 us; the launch traced here: 434 us
  waiting for transfers between devices  229 us (53%)
  blocking collectives  83.5 us (19%)
  starting transfers between devices  37.4 us (9%)
  local copies, waits for them, and re-layouts  34.5 us (8%)
  matrix products  23.6 us (5%)
  between operations  14.3 us (3%)
  other arithmetic  11.7 us (3%)
    psum x1, waiting for transfers between devices, spread(): return lax.psum(kept, axis)  129 us
    all_to_all x2, waiting for transfers between devices, one_direction(): lax.all_to_all(outgoing, 'ep', split_axis=0, concat_axis=0, tiled=True)  70.4 us
    all_gather x1, blocking collectives, body(): lax.all_gather(enter_fwd, 'pp', axis=2, tiled=True)  44.7 us
    all_gather x1, blocking collectives, body(): lax.all_gather(enter_bwd, 'pp', axis=2, tiled=True)  38.8 us
    all_to_all x2, waiting for transfers between devices, one_direction(): lax.all_to_all(finished, 'ep', split_axis=0, concat_axis=0, tiled=True)  25.6 us
    all_to_all x2, starting transfers between devices, one_direction(): lax.all_to_all(outgoing, 'ep', split_axis=0, concat_axis=0, tiled=True)  17.3 us
    dot_general x2, matrix products, expert_rows(): jnp.dot(hidden, down_matrix, preferred_element_type=jnp.float32)  14.8 us
    all_to_all x2, starting transfers between devices, one_direction(): lax.all_to_all(finished, 'ep', split_axis=0, concat_axis=0, tiled=True)  13.7 us
  transfers between devices with their start and end apart: 7, of which 5 were waited for; matrix products, arithmetic and copies ran while one was open for 13% of the time, Pallas kernels for 0%

commit v1 on v0

v1 whole, which is shorter than its diff:
```python
import jax
import jax.numpy as jnp
from jax import lax
from jax.experimental import pallas as pl
from jax.experimental.pallas import tpu as pltpu
from jax.sharding import PartitionSpec as P

EPS = 1e-06
BF = jnp.bfloat16
F32 = jnp.float32
EXPERTS = 4
COLS = 4
CAP = 15
ROWS = 24
BOTH = 2 * ROWS
SLOTS = 2 * CAP
EXTRA = 128
WIDE = 512


def device(y, x, core):
    return (y * COLS + x) * 2 + core


Y_FIRST = [[device(y, x, 0) for y in range(EXPERTS)] for x in range(COLS)] + [
    [device(y, x, 1) for x in range(COLS)] for y in range(EXPERTS)
]
X_FIRST = [[device(y, x, 0) for x in range(COLS)] for y in range(EXPERTS)] + [
    [device(y, x, 1) for y in range(EXPERTS)] for x in range(COLS)
]


def exchange(rows, groups):
    return lax.all_to_all(
        rows, "ep", split_axis=0, concat_axis=0, axis_index_groups=groups, tiled=True
    )


def iota(shape, dim):
    return lax.broadcasted_iota(jnp.int32, shape, dim)


def dot(a, b):
    return jnp.dot(a, b, preferred_element_type=F32)


def split_gate(gate):
    high = gate.astype(BF).astype(F32)
    return high, (gate - high).astype(BF).astype(F32)


def send_kernel(core_ref, fwd_ref, bwd_ref, gain_ref, ids_ref, gates_ref, out_ref, meta_ref):
    ids = ids_ref[...]
    gates = gates_ref[...]
    lanes = iota((BOTH, EXTRA), 1)
    row = iota((BOTH, EXTRA), 0)
    first, second = ids[:, 0:1], ids[:, 1:2]
    named = jnp.where((lanes == first) | (lanes == second), 1.0, 0.0)
    r0, r1 = iota((BOTH, BOTH), 0), iota((BOTH, BOTH), 1)
    earlier = jnp.where((r1 < r0) & ((r1 < ROWS) == (r0 < ROWS)), 1.0, 0.0)
    rank = dot(earlier.astype(BF), named.astype(BF))
    offset = jnp.where(row[:, 0:1] < ROWS, 0, CAP)
    slots = []
    for chosen in (first, second):
        taken = jnp.sum(jnp.where(lanes == chosen, rank, 0.0), axis=1, keepdims=True)
        slots.append(taken.astype(jnp.int32) + offset)
    fields = [first.astype(F32), slots[0].astype(F32), second.astype(F32), slots[1].astype(F32)]
    fields += split_gate(gates[:, 0:1])
    fields += split_gate(gates[:, 1:2])
    meta = jnp.zeros((BOTH, EXTRA), F32)
    for place, field in enumerate(fields):
        meta = jnp.where(lanes == place, field, meta)
    meta_ref[...] = meta

    def as_row(column):
        return jnp.sum(jnp.where(r0 == r1, column, 0), axis=0, keepdims=True)

    target = iota((EXPERTS * BOTH, BOTH), 0)
    source = iota((EXPERTS * BOTH, BOTH), 1)
    routed = (target == as_row(first * BOTH + slots[0])) | (
        target == as_row(second * BOTH + slots[1])
    )
    copied = target == source
    for part in range(1, COLS):
        copied = copied | (target == source + part * BOTH)
    routed_f = jnp.where(routed, 1.0, 0.0)
    copied_f = jnp.where(copied, 1.0, 0.0)
    pick = jnp.where(core_ref[0] == 0, routed_f, copied_f).astype(BF)
    values = jnp.concatenate([fwd_ref[...].astype(F32), bwd_ref[...].astype(F32)], axis=0)
    features = values.shape[1]
    inverse = lax.rsqrt(jnp.mean(values * values, axis=-1, keepdims=True) + EPS)
    normed = (values * inverse * gain_ref[...]).astype(BF)
    for start in range(0, features, WIDE):
        out_ref[:, start : start + WIDE] = dot(pick, normed[:, start : start + WIDE]).astype(BF)
    out_ref[:, features:] = dot(pick, meta.astype(BF)).astype(BF)


def spread_kernel(core_ref, rows_ref, extra_ref, out_ref, high_ref, low_ref, pick_ref):
    total = EXPERTS * BOTH
    slots = EXPERTS * COLS * SLOTS

    @pl.when(pl.program_id(0) == 0)
    def _():
        extra = extra_ref[...].astype(F32)
        row = iota((total, 1), 0)
        part = (
            (row >= BOTH).astype(jnp.int32)
            + (row >= 2 * BOTH).astype(jnp.int32)
            + (row >= 3 * BOTH).astype(jnp.int32)
        )
        place = row - part * BOTH
        on_first = core_ref[0] == 0
        none = jnp.full((total, 1), -1, jnp.int32)
        packed = jnp.where(place < SLOTS, part * SLOTS + place, -slots)
        block = COLS * SLOTS
        targets, highs, lows = [], [], []
        for k in range(COLS):
            if k < 2:
                expert = extra[:, 2 * k : 2 * k + 1].astype(jnp.int32)
                slot = extra[:, 2 * k + 1 : 2 * k + 2].astype(jnp.int32)
                there = expert * block + part * SLOTS + slot
                high = extra[:, 4 + 2 * k : 5 + 2 * k]
                low = extra[:, 5 + 2 * k : 6 + 2 * k]
            else:
                there, high, low = none, jnp.zeros((total, 1), F32), jnp.zeros((total, 1), F32)
            targets.append(jnp.where(on_first, packed + k * block, there))
            highs.append(jnp.where(on_first, 1.0, high))
            lows.append(jnp.where(on_first, 0.0, low))
        column = iota((total, slots), 1)
        pick = jnp.zeros((total, slots), F32)
        high_m = jnp.zeros((total, slots), F32)
        low_m = jnp.zeros((total, slots), F32)
        for target, high, low in zip(targets, highs, lows):
            here = column == target
            pick = jnp.where(here, 1.0, pick)
            high_m = jnp.where(here, high, high_m)
            low_m = jnp.where(here, low, low_m)
        high_ref[...] = high_m.astype(BF)
        low_ref[...] = low_m.astype(BF)
        pick_ref[...] = pick.T.astype(BF)

    out_ref[...] = dot(pick_ref[...], rows_ref[...]).astype(BF)


def expert_kernel(
    steps, rows_ref, g0_ref, g1_ref, u0_ref, u1_ref, d0_ref, d1_ref, out_ref, gate_acc, up_acc, hid_ref
):
    step = pl.program_id(0)
    half = g0_ref.shape[1]

    @pl.when(step == 0)
    def _():
        gate_acc[...] = jnp.zeros_like(gate_acc)
        up_acc[...] = jnp.zeros_like(up_acc)

    @pl.when(step < steps)
    def _():
        rows = rows_ref[...]
        gate_acc[...] += dot(rows, jnp.concatenate([g0_ref[...], g1_ref[...]], axis=1))
        up_acc[...] += dot(rows, jnp.concatenate([u0_ref[...], u1_ref[...]], axis=1))

    @pl.when(step == steps - 1)
    def _():
        gate = gate_acc[...]
        hid_ref[...] = (gate / (1.0 + jnp.exp(-gate)) * up_acc[...]).astype(BF)

    @pl.when(step >= steps)
    def _():
        hidden = hid_ref[...]
        down = jnp.concatenate([d0_ref[...], d1_ref[...]], axis=0)
        out_ref[...] = dot(hidden, down).astype(BF)


def gather_kernel(high_ref, low_ref, rows_ref, out_ref):
    rows = rows_ref[...]
    out_ref[...] = (dot(high_ref[...], rows) + dot(low_ref[...], rows)).astype(BF)


def finish_kernel(core_ref, meta_ref, rows_ref, fwd_ref, bwd_ref, of_ref, ob_ref, high_ref, low_ref):
    @pl.when(pl.program_id(0) == 0)
    def _():
        meta = meta_ref[...]
        total = EXPERTS * BOTH
        column = iota((BOTH, total), 1)
        row = iota((BOTH, total), 0)
        high = jnp.zeros((BOTH, total), F32)
        low = jnp.zeros((BOTH, total), F32)
        for k in range(2):
            there = (meta[:, 2 * k : 2 * k + 1] * BOTH + meta[:, 2 * k + 1 : 2 * k + 2]).astype(
                jnp.int32
            )
            high = jnp.where(column == there, meta[:, 4 + 2 * k : 5 + 2 * k], high)
            low = jnp.where(column == there, meta[:, 5 + 2 * k : 6 + 2 * k], low)
        same = column == row
        for part in range(1, COLS):
            same = same | (column == row + part * BOTH)
        ones = jnp.where(same, 1.0, 0.0)
        on_first = core_ref[0] == 0
        high_ref[...] = jnp.where(on_first, high, ones).astype(BF)
        low_ref[...] = jnp.where(on_first, low, 0.0).astype(BF)

    rows = rows_ref[...]
    mixture = dot(high_ref[...], rows) + dot(low_ref[...], rows)
    of_ref[...] = (fwd_ref[...].astype(F32) + mixture[:ROWS]).astype(BF)
    ob_ref[...] = (bwd_ref[...].astype(F32) + mixture[ROWS:]).astype(BF)


SMEM = pl.BlockSpec(memory_space=pltpu.SMEM)
PARAMS = pltpu.CompilerParams(vmem_limit_bytes=48 * 1024 * 1024)


def whole(shape):
    return pl.BlockSpec(shape, lambda i: (0,) * len(shape))


def tile(rows, width=WIDE):
    return pl.BlockSpec((rows, width), lambda i: (0, i))


def shape(rows, columns, dtype=BF):
    return jax.ShapeDtypeStruct((rows, columns), dtype)


def make_send(core, fwd, bwd, gain, ids, gates):
    features = fwd.shape[1]
    vmem = pl.BlockSpec(memory_space=pltpu.VMEM)
    return pl.pallas_call(
        send_kernel,
        out_shape=(shape(EXPERTS * BOTH, features + EXTRA), shape(BOTH, EXTRA, F32)),
        in_specs=[SMEM] + [vmem] * 5,
        out_specs=(vmem, vmem),
        compiler_params=PARAMS,
        name="normed",
    )(core, fwd, bwd, gain, ids, gates)


def make_spread(core, rows):
    total = rows.shape[0]
    features = rows.shape[1] - EXTRA
    slots = EXPERTS * COLS * SLOTS
    return pl.pallas_call(
        spread_kernel,
        grid=(features // WIDE,),
        out_shape=(shape(slots, features), shape(total, slots), shape(total, slots)),
        in_specs=[
            SMEM,
            tile(total),
            pl.BlockSpec((total, EXTRA), lambda i: (0, features // EXTRA)),
        ],
        out_specs=(tile(slots), whole((total, slots)), whole((total, slots))),
        scratch_shapes=[pltpu.VMEM((slots, total), BF)],
        compiler_params=PARAMS,
        name="spread",
    )(core, rows, rows)


def run_experts(rows, gates, ups, downs):
    count, features = rows.shape
    width = gates[0].shape[1]
    steps = features // WIDE
    first = lambda i: jnp.minimum(i, steps - 1)
    later = lambda i: jnp.maximum(i - steps, 0)
    tall = pl.BlockSpec((WIDE, width), lambda i: (first(i), 0))
    flat = pl.BlockSpec((width, WIDE), lambda i: (0, later(i)))

    def body(*refs):
        expert_kernel(steps, *refs)

    return pl.pallas_call(
        body,
        grid=(2 * steps,),
        out_shape=shape(count, features),
        in_specs=[pl.BlockSpec((count, WIDE), lambda i: (0, first(i)))] + [tall] * 4 + [flat] * 2,
        out_specs=pl.BlockSpec((count, WIDE), lambda i: (0, later(i))),
        scratch_shapes=[
            pltpu.VMEM((count, 2 * width), F32),
            pltpu.VMEM((count, 2 * width), F32),
            pltpu.VMEM((count, 2 * width), BF),
        ],
        compiler_params=PARAMS,
        name="experts",
    )(rows, gates[0], gates[1], ups[0], ups[1], downs[0], downs[1])


def make_gather(high, low, rows):
    slots, features = rows.shape
    total = high.shape[0]
    return pl.pallas_call(
        gather_kernel,
        grid=(features // WIDE,),
        out_shape=shape(total, features),
        in_specs=[whole((total, slots)), whole((total, slots)), tile(slots)],
        out_specs=tile(total),
        compiler_params=PARAMS,
        name="gather",
    )(high, low, rows)


def make_finish(core, meta, rows, fwd, bwd):
    total, features = rows.shape
    return pl.pallas_call(
        finish_kernel,
        grid=(features // WIDE,),
        out_shape=(shape(ROWS, features), shape(ROWS, features)),
        in_specs=[SMEM, whole((BOTH, EXTRA)), tile(total), tile(ROWS), tile(ROWS)],
        out_specs=(tile(ROWS), tile(ROWS)),
        scratch_shapes=[pltpu.VMEM((BOTH, total), BF), pltpu.VMEM((BOTH, total), BF)],
        compiler_params=PARAMS,
        name="finish",
    )(core, meta, rows, fwd, bwd)


def shifted(block, distance, count):
    route = [(i, i + distance) for i in range(count) if 0 <= i + distance < count]
    return lax.ppermute(block, "pp", route)


def from_other_core(block):
    return lax.ppermute(block, "ep", [(i, i ^ 1) for i in range(lax.axis_size("ep"))])


def across_sections(blocks):
    return lax.all_to_all(blocks, "pp", split_axis=0, concat_axis=0, tiled=True)


def body(
    state_fwd,
    state_bwd,
    enter_fwd,
    enter_bwd,
    norm_gain,
    w_gate,
    w_up,
    w_down,
    route_ids,
    route_gates,
):
    sections = lax.axis_size("pp")
    section = lax.axis_index("pp")
    core = (lax.axis_index("ep") % 2).astype(jnp.int32).reshape(1)
    fwd, bwd = state_fwd[0], state_bwd[0]
    features = fwd.shape[1]
    part = features // sections
    ids = route_ids[0, 0].reshape(BOTH, 2)
    gates = route_gates[0, 0].reshape(BOTH, 2)

    own = (w_gate[0], w_up[0], w_down[0])
    others = tuple(from_other_core(w) for w in own)

    target = lax.broadcasted_iota(jnp.int32, (sections, 1, 1), 0)
    entering = jnp.where(target == sections - 1, enter_bwd, enter_fwd)
    entered = across_sections(entering).transpose(1, 0, 2).reshape(ROWS, features)

    send, meta = make_send(core, fwd, bwd, norm_gain, ids, gates)
    spread, high, low = make_spread(core, exchange(send, Y_FIRST))
    done = run_experts(exchange(spread, X_FIRST), *zip(own, others))
    gathered = make_gather(high, low, exchange(done, X_FIRST))
    fwd_out, bwd_out = make_finish(core, meta, exchange(gathered, Y_FIRST), fwd, bwd)

    fwd_next = jnp.where(section == 0, entered, shifted(fwd_out, 1, sections))
    bwd_next = jnp.where(section == sections - 1, entered, shifted(bwd_out, -1, sections))
    leaving = jnp.where(section == 0, bwd_out, fwd_out)
    left = across_sections(leaving.reshape(ROWS, sections, part).transpose(1, 0, 2))
    return (fwd_next[None], bwd_next[None], left[sections - 1 :], left[:1])


def solution(mesh):
    placed = (
        P("pp", "ep", None),
        P("pp", "ep", None),
        P(None, "ep", "pp"),
        P(None, "ep", "pp"),
        P("pp", None),
        P("pp", None, "ep"),
        P("pp", None, "ep"),
        P("pp", "ep", None),
        P("pp", None, None, "ep", None),
        P("pp", None, None, "ep", None),
    )
    return jax.shard_map(
        body,
        mesh=mesh,
        in_specs=placed,
        out_specs=(
            P("pp", "ep", None),
            P("pp", "ep", None),
            P(None, "ep", "pp"),
            P(None, "ep", "pp"),
        ),
        check_vma=False,
    )
```

time: 435 us -> 175 us (0.40)
  the two profiles are of different devices: /device:TPU:2 before, /device:TPU:32 now
where the time goes in v1:
time: 175 us; the launch traced here: 174 us
  waiting for transfers between devices  68.7 us (39%)
  starting transfers between devices  46.1 us (26%)
  Pallas kernels  21.5 us (12%)
  local copies, waits for them, and re-layouts  17.7 us (10%)
  blocking collectives  17.2 us (10%)
    all_to_all x3, waiting for transfers between devices, exchange(): lax.all_to_all(rows, 'ep', split_axis=0, concat_axis=0, axis_index_groups...  48.3 us
    all_to_all x2, starting transfers between devices, across_sections(): return lax.all_to_all(blocks, 'pp', split_axis=0, concat_axis=0, tiled=True)  21.6 us
    all_to_all x2, waiting for transfers between devices, across_sections(): return lax.all_to_all(blocks, 'pp', split_axis=0, concat_axis=0, tiled=True)  19.9 us
    all_to_all x1, blocking collectives, exchange(): lax.all_to_all(rows, 'ep', split_axis=0, concat_axis=0, axis_index_groups...  17.2 us
    unnamed x42, local copies, waits for them, and re-layouts  13.3 us
    all_to_all x3, starting transfers between devices, exchange(): lax.all_to_all(rows, 'ep', split_axis=0, concat_axis=0, axis_index_groups...  12.4 us
    pallas_call x1, Pallas kernels, run_experts(): pl.pallas_call(body, grid=(2 * steps,), out_shape=shape(count, features),...  10.7 us
    ppermute x3, starting transfers between devices, from_other_core(): lax.ppermute(block, 'ep', [(i, i ^ 1) for i in range(lax.axis_size('ep'))])  6.25 us
  transfers between devices with their start and end apart: 10, of which 6 were waited for; matrix products, arithmetic and copies ran while one was open for 2% of the time, Pallas kernels for 2%

profile of v1, /device:TPU:32, one launch (start us, length us, event | category | flops | bytes accessed | tf_op | source)
XLA Modules:
  0.0 173.6 jit_solution(8722371362010945802)
XLA Ops:
  2.2 0.9 copy-done.10
  3.1 0.9 copy-done.12
  5.6 17.2 %all_to_all.54 = bf16[4,48,3712]{2,1,0:T(8,128)(2,1)S(1)} all-to-all(bf16[4,48,3712]{2,1,0:T(8,128)(2,1)S(1)} %bitcast.31), channel_id=1, replica_groups={{0,8,16,24},{2,10,18,26},{4,12,20,28},{6,14,22,30},{1,3,5,7},{9,11,13,1..., dimensions={0} | all-to-all | bytes 2850816 | tf_op jit(solution)/shard_map/all_to_all | solution.py:34
  22.8 5.1 %spread.1 = (bf16[480,3584]{1,0:T(8,128)(2,1)}, bf16[192,480]{1,0:T(8,128)(2,1)S(1)}, bf16[192,480]{1,0:T(8,128)(2,1)S(1)}) custom-call(s32[1]{0:T(128)} %bitcast.3.core_ref, bf16[192,3712]{1,0:T(8,128)(2,1)S(1)} %bitcast.27, bf16[192,3712]{1,0:T(8,128)(2,1)S(1)} %bitcast.28), custom_call_target="tpu_custom_call" | custom-call | tf_op jit(solution)/shard_map/spread/pallas_call | solution.py:241
  29.3 5.0 %all-to-all-start.2 = ((bf16[4,120,3584]{2,1,0:T(8,128)(2,1)}), bf16[4,120,3584]{2,1,0:T(8,128)(2,1)}, u32[]{:S(2)}, u32[]{:S(2)}) async-start(bf16[4,120,3584]{2,1,0:T(8,128)(2,1)} %bitcast.10), calls=%async_computation.2 | async-start | bytes 6881280 | tf_op jit(solution)/shard_map/all_to_all | solution.py:34
  34.3 1.9 %collective-permute-start = (bf16[3584,128]{1,0:T(8,128)(2,1)S(1)}, bf16[3584,128]{1,0:T(8,128)(2,1)S(1)}, u32[]{:S(2)}, u32[]{:S(2)}) collective-permute-start(bf16[3584,128]{1,0:T(8,128)(2,1)S(1)} %bitcast.32), channel_id=1, source_target_pairs={{0,1},{1,0},{2,3},{3,2},{4,5},{5,4},{6,7},{7,6},{8,9},{9,8},{10,11... | collective-permute-start | bytes 2752520 | tf_op jit(solution)/shard_map/ppermute | solution.py:319
  36.3 2.4 %collective-permute-start.1 = (bf16[3584,128]{1,0:T(8,128)(2,1)S(1)}, bf16[3584,128]{1,0:T(8,128)(2,1)S(1)}, u32[]{:S(2)}, u32[]{:S(2)}) collective-permute-start(bf16[3584,128]{1,0:T(8,128)(2,1)S(1)} %bitcast.34), channel_id=1, source_target_pairs={{0,1},{1,0},{2,3},{3,2},{4,5},{5,4},{6,7},{7,6},{8,9},{9,8},{10,11... | collective-permute-start | bytes 2752520 | tf_op jit(solution)/shard_map/ppermute | solution.py:319
  38.7 1.9 %collective-permute-start.2 = (bf16[128,3584]{1,0:T(8,128)(2,1)S(1)}, bf16[128,3584]{1,0:T(8,128)(2,1)S(1)}, u32[]{:S(2)}, u32[]{:S(2)}) collective-permute-start(bf16[128,3584]{1,0:T(8,128)(2,1)S(1)} %bitcast.36), channel_id=1, source_target_pairs={{0,1},{1,0},{2,3},{3,2},{4,5},{5,4},{6,7},{7,6},{8,9},{9,8},{10,11... | collective-permute-start | bytes 2752520 | tf_op jit(solution)/shard_map/ppermute | solution.py:319
  40.6 0.9 copy-done.4
  41.6 1.0 copy-done.6
  43.1 0.9 copy-done.8
  44.0 14.1 %all-to-all-done.2 = bf16[4,120,3584]{2,1,0:T(8,128)(2,1)} async-done(((bf16[4,120,3584]{2,1,0:T(8,128)(2,1)}), bf16[4,120,3584]{2,1,0:T(8,128)(2,1)}, u32[]{:S(2)}, u32[]{:S(2)}) %all-to-all-start.2) | async-done | bytes 3440672 | tf_op jit(solution)/shard_map/all_to_all | solution.py:34
  58.1 1.2 copy-done.5
  59.3 1.2 copy-done.7
  60.4 1.2 copy-done.9
  61.6 10.7 %experts.1 = bf16[480,3584]{1,0:T(8,128)(2,1)} custom-call(bf16[480,3584]{1,0:T(8,128)(2,1)} %bitcast.11.refs_0_, bf16[3584,128]{1,0:T(8,128)(2,1)S(1)} %bitcast.33, bf16[3584,128]{1,0:T(8,128)(2,1)S(1)} %copy-done.5, bf16[3584,128]{1,0:T(8,128)(2,1)S(1)} %bitcast.35, bf16[3584,128]{1,0:T(8,128)(2,1)S(1)} %copy-done.7, bf16[128,3584]{1,0:T(8,128)(2,1)S(1)} %bitcast.37, ...), custom_call_target="tpu_custom_call" | custom-call | tf_op jit(solution)/shard_map/experts/pallas_call | solution.py:269
  72.3 3.9 %all-to-all-start.3 = ((bf16[4,120,3584]{2,1,0:T(8,128)(2,1)}), bf16[4,120,3584]{2,1,0:T(8,128)(2,1)S(1)}, u32[]{:S(2)}, u32[]{:S(2)}) async-start(bf16[4,120,3584]{2,1,0:T(8,128)(2,1)} %bitcast.44), calls=%async_computation.3 | async-start | bytes 6881280 | tf_op jit(solution)/shard_map/all_to_all | solution.py:34
  77.0 22.9 %all-to-all-done.3 = bf16[4,120,3584]{2,1,0:T(8,128)(2,1)S(1)} async-done(((bf16[4,120,3584]{2,1,0:T(8,128)(2,1)}), bf16[4,120,3584]{2,1,0:T(8,128)(2,1)S(1)}, u32[]{:S(2)}, u32[]{:S(2)}) %all-to-all-start.3) | async-done | bytes 3440672 | tf_op jit(solution)/shard_map/all_to_all | solution.py:34
  99.9 15.2 %all-to-all-start = ((bf16[16,24,224]{2,1,0:T(8,128)(2,1)}), bf16[16,24,224]{2,1,0:T(8,128)(2,1)}, u32[]{:S(2)}, u32[]{:S(2)}) async-start(bf16[16,24,224]{2,1,0:T(8,128)(2,1)} %broadcast_select_fusion), calls=%async_computation | async-start | bytes 393216 | tf_op jit(solution)/shard_map/all_to_all | solution.py:323
  115.1 0.9 copy-done.15
  116.0 0.9 copy-done.17
  116.9 2.9 %gather.1 = bf16[192,3584]{1,0:T(8,128)(2,1)S(1)} custom-call(bf16[192,480]{1,0:T(8,128)(2,1)S(1)} %copy-done.15, bf16[192,480]{1,0:T(8,128)(2,1)S(1)} %copy-done.17, bf16[480,3584]{1,0:T(8,128)(2,1)S(1)} %bitcast.26), custom_call_target="tpu_custom_call" | custom-call | tf_op jit(solution)/shard_map/gather/pallas_call | solution.py:288
  119.9 1.1 copy-done
  121.0 7.6 %all-to-all-done = bf16[16,24,224]{2,1,0:T(8,128)(2,1)} async-done(((bf16[16,24,224]{2,1,0:T(8,128)(2,1)}), bf16[16,24,224]{2,1,0:T(8,128)(2,1)}, u32[]{:S(2)}, u32[]{:S(2)}) %all-to-all-start) | async-done | bytes 172064 | tf_op jit(solution)/shard_map/all_to_all | solution.py:323
  128.6 3.5 %all-to-all-start.4 = ((bf16[4,48,3584]{2,1,0:T(8,128)(2,1)}), bf16[4,48,3584]{2,1,0:T(8,128)(2,1)S(1)}, u32[]{:S(2)}, u32[]{:S(2)}) async-start(bf16[4,48,3584]{2,1,0:T(8,128)(2,1)} %bitcast.29), calls=%async_computation.4 | async-start | bytes 2752512 | tf_op jit(solution)/shard_map/all_to_all | solution.py:34
  132.1 1.0 copy.19
  133.3 11.4 %all-to-all-done.4 = bf16[4,48,3584]{2,1,0:T(8,128)(2,1)S(1)} async-done(((bf16[4,48,3584]{2,1,0:T(8,128)(2,1)}), bf16[4,48,3584]{2,1,0:T(8,128)(2,1)S(1)}, u32[]{:S(2)}, u32[]{:S(2)}) %all-to-all-start.4) | async-done | bytes 1376288 | tf_op jit(solution)/shard_map/all_to_all | solution.py:34
  144.7 1.8 %finish.1 = (bf16[24,3584]{1,0:T(8,128)(2,1)S(1)}, bf16[24,3584]{1,0:T(8,128)(2,1)S(1)}) custom-call(s32[1]{0:T(128)} %bitcast.3.core_ref, f32[48,128]{1,0:T(8,128)S(1)} %get-tuple-element.11.meta_ref, bf16[192,3584]{1,0:T(8,128)(2,1)S(1)} %bitcast.30, bf16[24,3584]{1,0:T(8,128)(2,1)S(1)} %bitcast.39, bf16[24,3584]{1,0:T(8,128)(2,1)S(1)} %bitcast.41), custom_call_target="tpu_custom_call" | custom-call | tf_op jit(solution)/shard_map/finish/pallas_call | solution.py:301
  146.6 2.8 %collective-permute-start.3 = (bf16[24,3584]{1,0:T(8,128)(2,1)S(1)}, bf16[24,3584]{1,0:T(8,128)(2,1)S(1)}, u32[]{:S(2)}, u32[]{:S(2)}) collective-permute-start(bf16[24,3584]{1,0:T(8,128)(2,1)S(1)} %get-tuple-element.16), channel_id=1, source_target_pairs={{0,32},{32,64},{64,96},{96,128},{128,160},{160,192},{192,224},{224... | collective-permute-start | bytes 516104 | tf_op jit(solution)/shard_map/ppermute | solution.py:315
  149.4 3.0 %collective-permute-start.4 = (bf16[24,3584]{1,0:T(8,128)(2,1)S(1)}, bf16[24,3584]{1,0:T(8,128)(2,1)S(1)}, u32[]{:S(2)}, u32[]{:S(2)}) collective-permute-start(bf16[24,3584]{1,0:T(8,128)(2,1)S(1)} %get-tuple-element.17), channel_id=1, source_target_pairs={{32,0},{64,32},{96,64},{128,96},{160,128},{192,160},{224,192},{256... | collective-permute-start | bytes 516104 | tf_op jit(solution)/shard_map/ppermute | solution.py:315
  153.5 6.4 %all-to-all-start.5 = ((bf16[16,24,224]{2,1,0:T(8,128)(2,1)}), bf16[16,24,224]{2,1,0:T(8,128)(2,1)S(1)}, u32[]{:S(2)}, u32[]{:S(2)}) async-start(bf16[16,24,224]{2,1,0:T(8,128)(2,1)} %bitcast.25), calls=%async_computation.5 | async-start | bytes 393216 | tf_op jit(solution)/shard_map/all_to_all | solution.py:323
  160.6 12.3 %all-to-all-done.5 = bf16[16,24,224]{2,1,0:T(8,128)(2,1)S(1)} async-done(((bf16[16,24,224]{2,1,0:T(8,128)(2,1)}), bf16[16,24,224]{2,1,0:T(8,128)(2,1)S(1)}, u32[]{:S(2)}, u32[]{:S(2)}) %all-to-all-start.5) | async-done | bytes 172064 | tf_op jit(solution)/shard_map/all_to_all | solution.py:323
  (47 shorter events, 8.5 us)
Async XLA Ops:
  2.2 0.9 copy-start.10
  3.1 0.9 copy-start.12
  4.0 0.7 copy-start.18
  27.9 0.7 copy-start.14
  28.6 0.7 copy-start.16
  29.3 5.0 %copy-start.1 = (bf16[1,3584,128]{2,1,0:T(8,128)(2,1)S(1)}, bf16[1,3584,128]{2,1,0:T(8,128)(2,1)}, u32[]{:S(2)}) copy-start(bf16[1,3584,128]{2,1,0:T(8,128)(2,1)} %param.15) | copy-start | bytes 2752516
  29.3 6.9 %copy-start.2 = (bf16[1,3584,128]{2,1,0:T(8,128)(2,1)S(1)}, bf16[1,3584,128]{2,1,0:T(8,128)(2,1)}, u32[]{:S(2)}) copy-start(bf16[1,3584,128]{2,1,0:T(8,128)(2,1)} %param.16) | copy-start | bytes 2752516
  29.3 9.3 %copy-start.3 = (bf16[1,128,3584]{2,1,0:T(8,128)(2,1)S(1)}, bf16[1,128,3584]{2,1,0:T(8,128)(2,1)}, u32[]{:S(2)}) copy-start(bf16[1,128,3584]{2,1,0:T(8,128)(2,1)} %param.17) | copy-start | bytes 2752516
  29.3 28.7 %all-to-all-start.2 = ((bf16[4,120,3584]{2,1,0:T(8,128)(2,1)}), bf16[4,120,3584]{2,1,0:T(8,128)(2,1)}, u32[]{:S(2)}, u32[]{:S(2)}) async-start(bf16[4,120,3584]{2,1,0:T(8,128)(2,1)} %bitcast.10), calls=%async_computation.2 | async-start | bytes 6881280 | tf_op jit(solution)/shard_map/all_to_all | solution.py:34
  34.3 6.3 %collective-permute-start = (bf16[3584,128]{1,0:T(8,128)(2,1)S(1)}, bf16[3584,128]{1,0:T(8,128)(2,1)S(1)}, u32[]{:S(2)}, u32[]{:S(2)}) collective-permute-start(bf16[3584,128]{1,0:T(8,128)(2,1)S(1)} %bitcast.32), channel_id=1, source_target_pairs={{0,1},{1,0},{2,3},{3,2},{4,5},{5,4},{6,7},{7,6},{8,9},{9,8},{10,11... | collective-permute-start | bytes 2752520 | tf_op jit(solution)/shard_map/ppermute | solution.py:319
  36.3 5.3 %collective-permute-start.1 = (bf16[3584,128]{1,0:T(8,128)(2,1)S(1)}, bf16[3584,128]{1,0:T(8,128)(2,1)S(1)}, u32[]{:S(2)}, u32[]{:S(2)}) collective-permute-start(bf16[3584,128]{1,0:T(8,128)(2,1)S(1)} %bitcast.34), channel_id=1, source_target_pairs={{0,1},{1,0},{2,3},{3,2},{4,5},{5,4},{6,7},{7,6},{8,9},{9,8},{10,11... | collective-permute-start | bytes 2752520 | tf_op jit(solution)/shard_map/ppermute | solution.py:319
  38.7 4.4 %collective-permute-start.2 = (bf16[128,3584]{1,0:T(8,128)(2,1)S(1)}, bf16[128,3584]{1,0:T(8,128)(2,1)S(1)}, u32[]{:S(2)}, u32[]{:S(2)}) collective-permute-start(bf16[128,3584]{1,0:T(8,128)(2,1)S(1)} %bitcast.36), channel_id=1, source_target_pairs={{0,1},{1,0},{2,3},{3,2},{4,5},{5,4},{6,7},{7,6},{8,9},{9,8},{10,11... | collective-permute-start | bytes 2752520 | tf_op jit(solution)/shard_map/ppermute | solution.py:319
  40.6 1.0 copy-start.4
  41.6 1.0 copy-start.6
  43.0 0.9 copy-start.8
  58.1 1.2 copy-start.5
  59.3 1.2 copy-start.7
  60.4 1.2 copy-start.9
  72.3 3.9 %copy-start.19 = (bf16[1,24,224]{2,1,0:T(8,128)(2,1)S(1)}, bf16[1,24,224]{2,1,0:T(8,128)(2,1)}, u32[]{:S(2)}) copy-start(bf16[1,24,224]{2,1,0:T(8,128)(2,1)} %param.12) | copy-start | bytes 32260
  72.3 3.9 %copy-start.20 = (bf16[1,24,224]{2,1,0:T(8,128)(2,1)S(1)}, bf16[1,24,224]{2,1,0:T(8,128)(2,1)}, u32[]{:S(2)}) copy-start(bf16[1,24,224]{2,1,0:T(8,128)(2,1)} %param.13) | copy-start | bytes 32260
  72.3 27.5 %all-to-all-start.3 = ((bf16[4,120,3584]{2,1,0:T(8,128)(2,1)}), bf16[4,120,3584]{2,1,0:T(8,128)(2,1)S(1)}, u32[]{:S(2)}, u32[]{:S(2)}) async-start(bf16[4,120,3584]{2,1,0:T(8,128)(2,1)} %bitcast.44), calls=%async_computation.3 | async-start | bytes 6881280 | tf_op jit(solution)/shard_map/all_to_all | solution.py:34
  99.9 28.7 %all-to-all-start = ((bf16[16,24,224]{2,1,0:T(8,128)(2,1)}), bf16[16,24,224]{2,1,0:T(8,128)(2,1)}, u32[]{:S(2)}, u32[]{:S(2)}) async-start(bf16[16,24,224]{2,1,0:T(8,128)(2,1)} %broadcast_select_fusion), calls=%async_computation | async-start | bytes 393216 | tf_op jit(solution)/shard_map/all_to_all | solution.py:323
  115.1 0.9 copy-start.15
  116.0 0.9 copy-start.17
  119.9 1.1 copy-start
  121.0 23.7 %copy-start.11 = (bf16[1,24,3584]{2,1,0:T(8,128)(2,1)S(1)}, bf16[1,24,3584]{2,1,0:T(8,128)(2,1)}, u32[]{:S(2)}) copy-start(bf16[1,24,3584]{2,1,0:T(8,128)(2,1)} %param.10) | copy-start | bytes 516100
  121.0 23.7 %copy-start.13 = (bf16[1,24,3584]{2,1,0:T(8,128)(2,1)S(1)}, bf16[1,24,3584]{2,1,0:T(8,128)(2,1)}, u32[]{:S(2)}) copy-start(bf16[1,24,3584]{2,1,0:T(8,128)(2,1)} %param.11) | copy-start | bytes 516100
  128.6 16.2 %all-to-all-start.4 = ((bf16[4,48,3584]{2,1,0:T(8,128)(2,1)}), bf16[4,48,3584]{2,1,0:T(8,128)(2,1)S(1)}, u32[]{:S(2)}, u32[]{:S(2)}) async-start(bf16[4,48,3584]{2,1,0:T(8,128)(2,1)} %bitcast.29), calls=%async_computation.4 | async-start | bytes 2752512 | tf_op jit(solution)/shard_map/all_to_all | solution.py:34
  146.6 13.3 %collective-permute-start.3 = (bf16[24,3584]{1,0:T(8,128)(2,1)S(1)}, bf16[24,3584]{1,0:T(8,128)(2,1)S(1)}, u32[]{:S(2)}, u32[]{:S(2)}) collective-permute-start(bf16[24,3584]{1,0:T(8,128)(2,1)S(1)} %get-tuple-element.16), channel_id=1, source_target_pairs={{0,32},{32,64},{64,96},{96,128},{128,160},{160,192},{192,224},{224... | collective-permute-start | bytes 516104 | tf_op jit(solution)/shard_map/ppermute | solution.py:315
  149.4 10.5 %collective-permute-start.4 = (bf16[24,3584]{1,0:T(8,128)(2,1)S(1)}, bf16[24,3584]{1,0:T(8,128)(2,1)S(1)}, u32[]{:S(2)}, u32[]{:S(2)}) collective-permute-start(bf16[24,3584]{1,0:T(8,128)(2,1)S(1)} %get-tuple-element.17), channel_id=1, source_target_pairs={{32,0},{64,32},{96,64},{128,96},{160,128},{192,160},{224,192},{256... | collective-permute-start | bytes 516104 | tf_op jit(solution)/shard_map/ppermute | solution.py:315
  153.5 19.5 %all-to-all-start.5 = ((bf16[16,24,224]{2,1,0:T(8,128)(2,1)}), bf16[16,24,224]{2,1,0:T(8,128)(2,1)S(1)}, u32[]{:S(2)}, u32[]{:S(2)}) async-start(bf16[16,24,224]{2,1,0:T(8,128)(2,1)} %bitcast.25), calls=%async_computation.5 | async-start | bytes 393216 | tf_op jit(solution)/shard_map/all_to_all | solution.py:323

commit v2 on v1

v2 whole, which is shorter than its diff:
```python
import jax
import jax.numpy as jnp
from jax import lax
from jax.experimental import pallas as pl
from jax.experimental.pallas import tpu as pltpu
from jax.sharding import PartitionSpec as P

EPS = 1e-06
BF = jnp.bfloat16
F32 = jnp.float32
EXPERTS = 4
COLS = 4
CAP = 15
ROWS = 24
BOTH = 2 * ROWS
SLOTS = 2 * CAP
EXTRA = 128
WIDE = 1792
CARRIED = 1536
CHUNK = 512
LANES = 128


def device(y, x, core):
    return (y * COLS + x) * 2 + core


def hop(block, distance, y_first):
    route = []
    for y in range(EXPERTS):
        for x in range(COLS):
            for core in range(2):
                along_y = (core == 0) == y_first
                there = ((y + distance) % EXPERTS, x) if along_y else (y, (x + distance) % COLS)
                route.append((device(y, x, core), device(*there, core)))
    return lax.ppermute(block, "ep", route)


def iota(shape, dim):
    return lax.broadcasted_iota(jnp.int32, shape, dim)


def dot(a, b):
    return jnp.dot(a, b, preferred_element_type=F32)


def split_gate(gate):
    high = gate.astype(BF).astype(F32)
    return high, (gate - high).astype(BF).astype(F32)


def send_kernel(place_ref, fwd_ref, bwd_ref, gain_ref, ids_ref, gates_ref, *outs):
    meta_ref = outs[-1]
    lanes = iota((BOTH, EXTRA), 1)
    row = iota((BOTH, EXTRA), 0)
    in_fwd = row < ROWS
    own = lanes[:, :ROWS] == row[:, :ROWS] - jnp.where(in_fwd[:, :ROWS], 0, ROWS)

    def column(ref, k):
        both = jnp.where(in_fwd[:, :ROWS], ref[0, k : k + 1, :], ref[1, k : k + 1, :])
        return jnp.sum(jnp.where(own, both, jnp.zeros_like(both)), axis=1, keepdims=True)

    first, second = [
        jnp.bitwise_and(column(ids_ref, k) - place_ref[1] + EXPERTS, EXPERTS - 1) for k in range(2)
    ]
    named = jnp.where((lanes == first) | (lanes == second), 1.0, 0.0)
    r0, r1 = iota((BOTH, BOTH), 0), iota((BOTH, BOTH), 1)
    earlier = jnp.where((r1 < r0) & ((r1 < ROWS) == (r0 < ROWS)), 1.0, 0.0)
    rank = dot(earlier.astype(BF), named.astype(BF))
    offset = jnp.where(in_fwd[:, 0:1], 0, CAP)
    slots = []
    for chosen in (first, second):
        taken = jnp.sum(jnp.where(lanes == chosen, rank, 0.0), axis=1, keepdims=True)
        slots.append(taken.astype(jnp.int32) + offset)
    fields = [first.astype(F32), slots[0].astype(F32), second.astype(F32), slots[1].astype(F32)]
    fields += split_gate(column(gates_ref, 0))
    fields += split_gate(column(gates_ref, 1))
    meta = jnp.zeros((BOTH, EXTRA), F32)
    for place, field in enumerate(fields):
        meta = jnp.where(lanes == place, field, meta)
    meta_ref[...] = meta

    def as_row(column):
        return jnp.sum(jnp.where(r0 == r1, column, 0), axis=0, keepdims=True)

    target = iota((EXPERTS * BOTH, BOTH), 0)
    source = iota((EXPERTS * BOTH, BOTH), 1)
    routed = (target == as_row(first * BOTH + slots[0])) | (
        target == as_row(second * BOTH + slots[1])
    )
    copied = target == source
    for part in range(1, COLS):
        copied = copied | (target == source + part * BOTH)
    routed_f = jnp.where(routed, 1.0, 0.0)
    copied_f = jnp.where(copied, 1.0, 0.0)
    pick = jnp.where(place_ref[0] == 0, routed_f, copied_f).astype(BF)
    values = jnp.concatenate([fwd_ref[...].astype(F32), bwd_ref[...].astype(F32)], axis=0)
    features = values.shape[1]
    inverse = lax.rsqrt(jnp.mean(values * values, axis=-1, keepdims=True) + EPS)
    normed = (values * inverse * gain_ref[...]).astype(BF)
    for start in range(0, features, CHUNK):
        picked = dot(pick, normed[:, start : start + CHUNK]).astype(BF)
        for part in range(EXPERTS):
            outs[part][:, start : start + CHUNK] = picked[part * BOTH : (part + 1) * BOTH]
    extra = dot(pick, meta.astype(BF)).astype(BF)
    for part in range(EXPERTS):
        outs[part][:, features:] = extra[part * BOTH : (part + 1) * BOTH]


def spread_kernel(place_ref, *refs):
    rows_refs, extra_refs, out_refs = refs[:4], refs[4:8], refs[8:12]
    high_ref, low_ref, pick_ref = refs[12:]
    total = EXPERTS * BOTH
    lanes = EXPERTS * LANES

    @pl.when(pl.program_id(0) == 0)
    def _():
        extra = jnp.concatenate([ref[...].astype(F32) for ref in extra_refs], axis=0)
        row = iota((total, 1), 0)
        part = (
            (row >= BOTH).astype(jnp.int32)
            + (row >= 2 * BOTH).astype(jnp.int32)
            + (row >= 3 * BOTH).astype(jnp.int32)
        )
        place = row - part * BOTH
        on_first = place_ref[0] == 0
        packed = jnp.where(place < SLOTS, part * SLOTS + place, -lanes)
        column = iota((total, lanes), 1)
        pick = jnp.zeros((total, lanes), F32)
        high_m = jnp.zeros((total, lanes), F32)
        low_m = jnp.zeros((total, lanes), F32)
        for k in range(COLS):
            there, high, low = -1, 0.0, 0.0
            if k < 2:
                expert = extra[:, 2 * k : 2 * k + 1].astype(jnp.int32)
                slot = extra[:, 2 * k + 1 : 2 * k + 2].astype(jnp.int32)
                there = expert * LANES + part * SLOTS + slot
                high = extra[:, 4 + 2 * k : 5 + 2 * k]
                low = extra[:, 5 + 2 * k : 6 + 2 * k]
            here = column == jnp.where(on_first, packed + k * LANES, there)
            pick = jnp.where(here, 1.0, pick)
            high_m = jnp.where(here, jnp.where(on_first, 1.0, high), high_m)
            low_m = jnp.where(here, jnp.where(on_first, 0.0, low), low_m)
        high_ref[...] = high_m.astype(BF)
        low_ref[...] = low_m.astype(BF)
        pick_ref[...] = pick.T.astype(BF)

    width = rows_refs[0].shape[1]
    for start in range(0, width, CHUNK):
        cut = slice(start, min(start + CHUNK, width))
        rows = jnp.concatenate([ref[:, cut] for ref in rows_refs], axis=0)
        for part, out_ref in enumerate(out_refs):
            moved = dot(pick_ref[part * LANES : (part + 1) * LANES, :], rows)
            out_ref[:, cut] = moved[: COLS * SLOTS].astype(BF)


def expert_kernel(steps, count, *refs):
    rows_refs = refs[:count]
    g0_ref, g1_ref, u0_ref, u1_ref, d0_ref, d1_ref = refs[count : count + 6]
    out_refs = refs[count + 6 : 2 * count + 6]
    gate_acc, up_acc, hid_ref = refs[2 * count + 6 :]
    step = pl.program_id(0)

    @pl.when(step < steps)
    def _():
        gate_w = jnp.concatenate([g0_ref[...], g1_ref[...]], axis=1)
        up_w = jnp.concatenate([u0_ref[...], u1_ref[...]], axis=1)
        for i, rows_ref in enumerate(rows_refs):
            gate = dot(rows_ref[...], gate_w)
            up = dot(rows_ref[...], up_w)

            @pl.when(step == 0)
            def _():
                gate_acc[i] = gate
                up_acc[i] = up

            @pl.when(step > 0)
            def _():
                gate_acc[i] += gate
                up_acc[i] += up

    @pl.when(step == steps - 1)
    def _():
        gate = gate_acc[...]
        hid_ref[...] = (gate / (1.0 + jnp.exp(-gate)) * up_acc[...]).astype(BF)

    @pl.when(step >= steps)
    def _():
        down = jnp.concatenate([d0_ref[...], d1_ref[...]], axis=0)
        for i, out_ref in enumerate(out_refs):
            out_ref[...] = dot(hid_ref[i], down).astype(BF)


def gather_kernel(high_ref, low_ref, *refs):
    rows_refs, out_refs = refs[:4], refs[4:]
    width = rows_refs[0].shape[1]
    used = COLS * SLOTS
    for start in range(0, width, CHUNK):
        cut = slice(start, min(start + CHUNK, width))
        total = 0.0
        for part, ref in enumerate(rows_refs):
            lanes = slice(part * LANES, part * LANES + used)
            rows = ref[:, cut]
            total += dot(high_ref[:, lanes], rows) + dot(low_ref[:, lanes], rows)
        total = total.astype(BF)
        for part, out_ref in enumerate(out_refs):
            out_ref[:, cut] = total[part * BOTH : (part + 1) * BOTH]


def finish_kernel(place_ref, meta_ref, *refs):
    rows_refs = refs[:4]
    fwd_ref, bwd_ref, of_ref, ob_ref, high_ref, low_ref = refs[4:]

    @pl.when(pl.program_id(0) == 0)
    def _():
        meta = meta_ref[...]
        total = EXPERTS * BOTH
        column = iota((BOTH, total), 1)
        row = iota((BOTH, total), 0)
        high = jnp.zeros((BOTH, total), F32)
        low = jnp.zeros((BOTH, total), F32)
        for k in range(2):
            there = (meta[:, 2 * k : 2 * k + 1] * BOTH + meta[:, 2 * k + 1 : 2 * k + 2]).astype(
                jnp.int32
            )
            high = jnp.where(column == there, meta[:, 4 + 2 * k : 5 + 2 * k], high)
            low = jnp.where(column == there, meta[:, 5 + 2 * k : 6 + 2 * k], low)
        same = column == row
        for part in range(1, COLS):
            same = same | (column == row + part * BOTH)
        ones = jnp.where(same, 1.0, 0.0)
        on_first = place_ref[0] == 0
        high_ref[...] = jnp.where(on_first, high, ones).astype(BF)
        low_ref[...] = jnp.where(on_first, low, 0.0).astype(BF)

    width = fwd_ref.shape[1]
    for start in range(0, width, CHUNK):
        cut = slice(start, min(start + CHUNK, width))
        rows = jnp.concatenate([ref[:, cut] for ref in rows_refs], axis=0)
        mixture = dot(high_ref[...], rows) + dot(low_ref[...], rows)
        of_ref[:, cut] = (fwd_ref[:, cut].astype(F32) + mixture[:ROWS]).astype(BF)
        ob_ref[:, cut] = (bwd_ref[:, cut].astype(F32) + mixture[ROWS:]).astype(BF)


SMEM = pl.BlockSpec(memory_space=pltpu.SMEM)
PARAMS = pltpu.CompilerParams(vmem_limit_bytes=24 * 1024 * 1024)


def whole(shape):
    return pl.BlockSpec(shape, lambda i: (0,) * len(shape))


def tile(rows, width=WIDE):
    return pl.BlockSpec((rows, width), lambda i: (0, i))


def shape(rows, columns, dtype=BF):
    return jax.ShapeDtypeStruct((rows, columns), dtype)


def make_send(place, fwd, bwd, gain, ids, gates):
    features = fwd.shape[1]
    vmem = pl.BlockSpec(memory_space=pltpu.VMEM)
    *blocks, meta = pl.pallas_call(
        send_kernel,
        out_shape=(shape(BOTH, features + EXTRA),) * 4 + (shape(BOTH, EXTRA, F32),),
        in_specs=[SMEM] + [vmem] * 5,
        out_specs=(vmem,) * 5,
        compiler_params=PARAMS,
        name="normed",
    )(place, fwd, bwd, gain, ids, gates)
    return blocks, meta


def make_spread(place, blocks):
    features = blocks[0].shape[1] - EXTRA
    total = EXPERTS * BOTH
    lanes = EXPERTS * LANES
    extra = pl.BlockSpec((BOTH, EXTRA), lambda i: (0, features // EXTRA))
    *blocks, high, low = pl.pallas_call(
        spread_kernel,
        grid=(features // WIDE,),
        out_shape=(shape(COLS * SLOTS, features),) * 4 + (shape(total, lanes),) * 2,
        in_specs=[SMEM] + [tile(BOTH)] * 4 + [extra] * 4,
        out_specs=(tile(COLS * SLOTS),) * 4 + (whole((total, lanes)),) * 2,
        scratch_shapes=[pltpu.VMEM((lanes, total), BF)],
        compiler_params=PARAMS,
        name="spread",
    )(place, *blocks, *blocks)
    return blocks, high, low


def run_experts(blocks, gates, ups, downs):
    count = len(blocks)
    rows, features = blocks[0].shape
    width = gates[0].shape[1]
    steps = features // WIDE
    first = lambda i: jnp.minimum(i, steps - 1)
    later = lambda i: jnp.maximum(i - steps, 0)
    tall = pl.BlockSpec((WIDE, width), lambda i: (first(i), 0))
    flat = pl.BlockSpec((width, WIDE), lambda i: (0, later(i)))

    def body(*refs):
        expert_kernel(steps, count, *refs)

    return pl.pallas_call(
        body,
        grid=(2 * steps,),
        out_shape=(shape(rows, features),) * count,
        in_specs=[pl.BlockSpec((rows, WIDE), lambda i: (0, first(i)))] * count
        + [tall] * 4
        + [flat] * 2,
        out_specs=(pl.BlockSpec((rows, WIDE), lambda i: (0, later(i))),) * count,
        scratch_shapes=[
            pltpu.VMEM((count, rows, 2 * width), F32),
            pltpu.VMEM((count, rows, 2 * width), F32),
            pltpu.VMEM((count, rows, 2 * width), BF),
        ],
        compiler_params=PARAMS,
        name="experts",
    )(*blocks, gates[0], gates[1], ups[0], ups[1], downs[0], downs[1])


def make_gather(high, low, blocks):
    rows, features = blocks[0].shape
    return pl.pallas_call(
        gather_kernel,
        grid=(features // WIDE,),
        out_shape=(shape(BOTH, features),) * 4,
        in_specs=[whole(high.shape), whole(low.shape)] + [tile(rows)] * 4,
        out_specs=(tile(BOTH),) * 4,
        compiler_params=PARAMS,
        name="gather",
    )(high, low, *blocks)


def make_finish(place, meta, blocks, fwd, bwd):
    features = fwd.shape[1]
    total = EXPERTS * BOTH
    return pl.pallas_call(
        finish_kernel,
        grid=(features // WIDE,),
        out_shape=(shape(ROWS, features), shape(ROWS, features)),
        in_specs=[SMEM, whole((BOTH, EXTRA))] + [tile(BOTH)] * 4 + [tile(ROWS), tile(ROWS)],
        out_specs=(tile(ROWS), tile(ROWS)),
        scratch_shapes=[pltpu.VMEM((BOTH, total), BF), pltpu.VMEM((BOTH, total), BF)],
        compiler_params=PARAMS,
        name="finish",
    )(place, meta, *blocks, fwd, bwd)


def shifted(block, distance, count):
    route = [(i, i + distance) for i in range(count) if 0 <= i + distance < count]
    return lax.ppermute(block, "pp", route)


def from_other_core(block):
    return lax.ppermute(block, "ep", [(i, i ^ 1) for i in range(lax.axis_size("ep"))])


def across_sections(blocks):
    return lax.all_to_all(blocks, "pp", split_axis=0, concat_axis=0, tiled=True)


def body(
    state_fwd,
    state_bwd,
    enter_fwd,
    enter_bwd,
    norm_gain,
    w_gate,
    w_up,
    w_down,
    route_ids,
    route_gates,
):
    sections = lax.axis_size("pp")
    section = lax.axis_index("pp")
    position = lax.axis_index("ep")
    place = jnp.stack([position % 2, position // (2 * COLS)]).astype(jnp.int32)
    fwd, bwd = state_fwd[0], state_bwd[0]
    features = fwd.shape[1]
    part = features // sections
    ids = route_ids[0, 0].transpose(0, 2, 1)
    gates = route_gates[0, 0].transpose(0, 2, 1)

    sent, meta = make_send(place, fwd, bwd, norm_gain, ids, gates)
    around = [hop(sent[d], d, True) for d in (1, 3, 2)]

    own = (w_gate[0], w_up[0], w_down[0])
    passed, entering, _ = lax.optimization_barrier((own, (enter_fwd[0], enter_bwd[0]), meta))
    weights = tuple(zip(own, (from_other_core(w) for w in passed)))
    both = jnp.concatenate(entering, axis=1)
    entered = lax.all_gather(
        jnp.pad(both, ((0, 0), (0, CARRIED - both.shape[1]))), "pp", axis=0, tiled=True
    )

    def joined(start):
        blocks = entered[:, start : start + part].reshape(sections, ROWS, part)
        return blocks.transpose(1, 0, 2).reshape(ROWS, features)

    spread, high, low = make_spread(place, [sent[0], around[0], around[2], around[1]])
    near, far, last = [hop(spread[d], d, False) for d in (1, 3, 2)]
    (done0,) = run_experts([spread[0]], *weights)
    near, far, done0 = lax.optimization_barrier((near, far, done0))
    done1, done3 = run_experts([near, far], *weights)
    last, done1, done3 = lax.optimization_barrier((last, done1, done3))
    back1, back3 = hop(done1, -1, False), hop(done3, -3, False)
    (done2,) = run_experts([last], *weights)
    back2 = hop(done2, -2, False)
    gathered = make_gather(high, low, [done0, back1, back2, back3])
    home = [gathered[0]] + [hop(gathered[d], -d, True) for d in (1, 2, 3)]
    fwd_out, bwd_out = make_finish(place, meta, home, fwd, bwd)

    arrived = jnp.where(section == 0, joined(0), joined(part))
    leaving = jnp.where(section == 0, bwd_out, fwd_out)
    left = across_sections(leaving.reshape(ROWS, sections, part).transpose(1, 0, 2))
    fwd_next = jnp.where(section == 0, arrived, shifted(fwd_out, 1, sections))
    bwd_next = jnp.where(section == sections - 1, arrived, shifted(bwd_out, -1, sections))
    return (fwd_next[None], bwd_next[None], left[sections - 1 :], left[:1])


def solution(mesh):
    placed = (
        P("pp", "ep", None),
        P("pp", "ep", None),
        P(None, "ep", "pp"),
        P(None, "ep", "pp"),
        P("pp", None),
        P("pp", None, "ep"),
        P("pp", None, "ep"),
        P("pp", "ep", None),
        P("pp", None, None, "ep", None),
        P("pp", None, None, "ep", None),
    )
    return jax.shard_map(
        body,
        mesh=mesh,
        in_specs=placed,
        out_specs=(
            P("pp", "ep", None),
            P("pp", "ep", None),
            P(None, "ep", "pp"),
            P(None, "ep", "pp"),
        ),
        check_vma=False,
    )
```

time: 175 us -> 164 us (0.937)
  the two profiles are of different devices: /device:TPU:32 before, /device:TPU:6 now
where the time goes in v2:
time: 164 us; the launch traced here: 163 us
  starting transfers between devices  65.1 us (40%)
  waiting for transfers between devices  57.7 us (35%)
  Pallas kernels  16.6 us (10%)
  between operations  14.4 us (9%)
  local copies, waits for them, and re-layouts  5.83 us (4%)
  other arithmetic  3.5 us (2%)
    ppermute x12, waiting for transfers between devices, hop(): return lax.ppermute(block, 'ep', route)  44.8 us
    ppermute x12, starting transfers between devices, hop(): return lax.ppermute(block, 'ep', route)  41.3 us
    all_to_all x1, starting transfers between devices, across_sections(): return lax.all_to_all(blocks, 'pp', split_axis=0, concat_axis=0, tiled=True)  14.7 us
    all_to_all x1, waiting for transfers between devices, across_sections(): return lax.all_to_all(blocks, 'pp', split_axis=0, concat_axis=0, tiled=True)  12.8 us
    pallas_call x3, Pallas kernels, run_experts(): pl.pallas_call(body, grid=(2 * steps,), out_shape=(shape(rows, features),...  7.14 us
    ppermute x3, starting transfers between devices, from_other_core(): lax.ppermute(block, 'ep', [(i, i ^ 1) for i in range(lax.axis_size('ep'))])  6.59 us
    unnamed x20, local copies, waits for them, and re-layouts  3.93 us
    pallas_call x1, Pallas kernels, make_gather(): pl.pallas_call(gather_kernel, grid=(features // WIDE,), out_shape=(shape(...  3.52 us
  transfers between devices with their start and end apart: 19, of which 10 were waited for; matrix products, arithmetic and copies ran while one was open for 3% of the time, Pallas kernels for 8%

profile of v2, /device:TPU:6, one launch (start us, length us, event | category | flops | bytes accessed | tf_op | source)
XLA Modules:
  0.0 163.2 jit_solution(6203987814725124444)
XLA Ops:
  12.6 1.9 %collective-permute-start.5 = (bf16[3584,128]{1,0:T(8,128)(2,1)}, bf16[3584,128]{1,0:T(8,128)(2,1)S(1)}, u32[]{:S(2)}, u32[]{:S(2)}) collective-permute-start(bf16[3584,128]{1,0:T(8,128)(2,1)} %bitcast.26), channel_id=1, source_target_pairs={{0,1},{1,0},{2,3},{3,2},{4,5},{5,4},{6,7},{7,6},{8,9},{9,8},{10,11... | collective-permute-start | bytes 2752520 | tf_op jit(solution)/shard_map/ppermute | solution.py:358
  14.6 3.5 %collective-permute-start = (bf16[48,3712]{1,0:T(8,128)(2,1)S(1)}, bf16[48,3712]{1,0:T(8,128)(2,1)S(1)}, u32[]{:S(2)}, u32[]{:S(2)}) collective-permute-start(bf16[48,3712]{1,0:T(8,128)(2,1)S(1)} %get-tuple-element.38), channel_id=1, source_target_pairs={{0,8},{1,3},{2,10},{3,5},{4,12},{5,7},{6,14},{7,1},{8,16},{9,11},{... | collective-permute-start | bytes 1069064 | tf_op jit(solution)/shard_map/ppermute | solution.py:36
  18.1 1.4 fusion.2
  19.5 4.8 %collective-permute-start.1 = (bf16[48,3712]{1,0:T(8,128)(2,1)S(1)}, bf16[48,3712]{1,0:T(8,128)(2,1)S(1)}, u32[]{:S(2)}, u32[]{:S(2)}) collective-permute-start(bf16[48,3712]{1,0:T(8,128)(2,1)S(1)} %get-tuple-element.39), channel_id=1, source_target_pairs={{0,16},{1,5},{2,18},{3,7},{4,20},{5,1},{6,22},{7,3},{8,24},{9,13},... | collective-permute-start | bytes 1069064 | tf_op jit(solution)/shard_map/ppermute | solution.py:36
  24.3 3.3 %collective-permute-start.2 = (bf16[48,3712]{1,0:T(8,128)(2,1)S(1)}, bf16[48,3712]{1,0:T(8,128)(2,1)S(1)}, u32[]{:S(2)}, u32[]{:S(2)}) collective-permute-start(bf16[48,3712]{1,0:T(8,128)(2,1)S(1)} %get-tuple-element.40), channel_id=1, source_target_pairs={{0,24},{1,7},{2,26},{3,1},{4,28},{5,3},{6,30},{7,5},{8,0},{9,15},{... | collective-permute-start | bytes 1069064 | tf_op jit(solution)/shard_map/ppermute | solution.py:36
  27.6 2.7 %collective-permute-start.6 = (bf16[3584,128]{1,0:T(8,128)(2,1)}, bf16[3584,128]{1,0:T(8,128)(2,1)S(1)}, u32[]{:S(2)}, u32[]{:S(2)}) collective-permute-start(bf16[3584,128]{1,0:T(8,128)(2,1)} %bitcast.30), channel_id=1, source_target_pairs={{0,1},{1,0},{2,3},{3,2},{4,5},{5,4},{6,7},{7,6},{8,9},{9,8},{10,11... | collective-permute-start | bytes 2752520 | tf_op jit(solution)/shard_map/ppermute | solution.py:358
  30.4 1.9 %collective-permute-start.7 = (bf16[128,3584]{1,0:T(8,128)(2,1)}, bf16[128,3584]{1,0:T(8,128)(2,1)S(1)}, u32[]{:S(2)}, u32[]{:S(2)}) collective-permute-start(bf16[128,3584]{1,0:T(8,128)(2,1)} %bitcast.34), channel_id=1, source_target_pairs={{0,1},{1,0},{2,3},{3,2},{4,5},{5,4},{6,7},{7,6},{8,9},{9,8},{10,11... | collective-permute-start | bytes 2752520 | tf_op jit(solution)/shard_map/ppermute | solution.py:358
  33.6 3.0 %spread.1 = (bf16[120,3584]{1,0:T(8,128)(2,1)S(1)}, bf16[120,3584]{1,0:T(8,128)(2,1)S(1)}, bf16[120,3584]{1,0:T(8,128)(2,1)S(1)}, bf16[120,3584]{1,0:T(8,128)(2,...) custom-call(s32[2]{0:T(128)S(1)} %pad_add_fusion.place_ref, ...), custom_call_target="tpu_custom_call" | custom-call | tf_op jit(solution)/shard_map/spread/pallas_call | solution.py:280
  36.6 7.3 %collective-permute-start.3 = (bf16[120,3584]{1,0:T(8,128)(2,1)S(1)}, bf16[120,3584]{1,0:T(8,128)(2,1)S(1)}, u32[]{:S(2)}, u32[]{:S(2)}) collective-permute-start(bf16[120,3584]{1,0:T(8,128)(2,1)S(1)} %get-tuple-element.43), channel_id=1, source_target_pairs={{0,2},{1,9},{2,4},{3,11},{4,6},{5,13},{6,0},{7,15},{8,10},{9,17},{... | collective-permute-start | bytes 2580488 | tf_op jit(solution)/shard_map/ppermute | solution.py:36
  43.9 1.9 %collective-permute-start.4 = (bf16[120,3584]{1,0:T(8,128)(2,1)S(1)}, bf16[120,3584]{1,0:T(8,128)(2,1)S(1)}, u32[]{:S(2)}, u32[]{:S(2)}) collective-permute-start(bf16[120,3584]{1,0:T(8,128)(2,1)S(1)} %get-tuple-element.44), channel_id=1, source_target_pairs={{0,6},{1,25},{2,0},{3,27},{4,2},{5,29},{6,4},{7,31},{8,14},{9,1},{... | collective-permute-start | bytes 2580488 | tf_op jit(solution)/shard_map/ppermute | solution.py:36
  45.9 3.4 %collective-permute-start.8 = (bf16[120,3584]{1,0:T(8,128)(2,1)S(1)}, bf16[120,3584]{1,0:T(8,128)(2,1)S(1)}, u32[]{:S(2)}, u32[]{:S(2)}) collective-permute-start(bf16[120,3584]{1,0:T(8,128)(2,1)S(1)} %get-tuple-element.50), channel_id=1, source_target_pairs={{0,4},{1,17},{2,6},{3,19},{4,0},{5,21},{6,2},{7,23},{8,12},{9,25},... | collective-permute-start | bytes 2580488 | tf_op jit(solution)/shard_map/ppermute | solution.py:36
  49.3 2.0 %experts.3.refs_0_ = bf16[120,3584]{1,0:T(8,128)(2,1)S(1)} custom-call(bf16[120,3584]{1,0:T(8,128)(2,1)S(1)} %get-tuple-element.45.refs_0_, bf16[3584,128]{1,0:T(8,128)(2,1)S(1)} %bitcast.27, bf16[3584,128]{1,0:T(8,128)(2,1)S(1)} %collective-permute-done.5.refs_2_.refs_3_, bf16[3584,128]{1,0:T(8,128)(2,1)S(1)} %bitcast.31, ...), custom_call_target="tpu_custom_call" | custom-call | tf_op jit(solution)/shard_map/experts/pallas_call | solution.py:306
  51.3 12.2 %collective-permute-done.3.refs_0_ = bf16[120,3584]{1,0:T(8,128)(2,1)S(1)} collective-permute-done((bf16[120,3584]{1,0:T(8,128)(2,1)S(1)}, bf16[120,3584]{1,0:T(8,128)(2,1)S(1)}, u32[]{:S(2)}, u32[]{:S(2)}) %collective-permute-start.3) | collective-permute-done | bytes 860192 | tf_op jit(solution)/shard_map/ppermute | solution.py:36
  63.4 5.6 %collective-permute-done.4.refs_1_ = bf16[120,3584]{1,0:T(8,128)(2,1)S(1)} collective-permute-done((bf16[120,3584]{1,0:T(8,128)(2,1)S(1)}, bf16[120,3584]{1,0:T(8,128)(2,1)S(1)}, u32[]{:S(2)}, u32[]{:S(2)}) %collective-permute-start.4) | collective-permute-done | bytes 860192 | tf_op jit(solution)/shard_map/ppermute | solution.py:36
  69.0 3.2 %experts.4 = (bf16[120,3584]{1,0:T(8,128)(2,1)S(1)}, bf16[120,3584]{1,0:T(8,128)(2,1)S(1)}) custom-call(bf16[120,3584]{1,0:T(8,128)(2,1)S(1)} %collective-permute-done.3.refs_0_, bf16[120,3584]{1,0:T(8,128)(2,1)S(1)} %collective-permute-done.4.refs_1_, bf16[3584,128]{1,0:T(8,128)(2,1)S(1)} %bitcast.28, ...), custom_call_target="tpu_custom_call" | custom-call | tf_op jit(solution)/shard_map/experts/pallas_call | solution.py:306
  72.3 2.0 %experts.5 = bf16[120,3584]{1,0:T(8,128)(2,1)S(1)} custom-call(bf16[120,3584]{1,0:T(8,128)(2,1)S(1)} %collective-permute-done.8.refs_0_, bf16[3584,128]{1,0:T(8,128)(2,1)S(1)} %bitcast.29, bf16[3584,128]{1,0:T(8,128)(2,1)S(1)} %collective-permute-done.5.refs_2_.refs_3_, bf16[3584,128]{1,0:T(8,128)(2,1)S(1)} %bitcast.33, ...), custom_call_target="tpu_custom_call" | custom-call | tf_op jit(solution)/shard_map/experts/pallas_call | solution.py:306
  74.2 1.9 %collective-permute-start.10 = (bf16[120,3584]{1,0:T(8,128)(2,1)S(1)}, bf16[120,3584]{1,0:T(8,128)(2,1)S(1)}, u32[]{:S(2)}, u32[]{:S(2)}) collective-permute-start(bf16[120,3584]{1,0:T(8,128)(2,1)S(1)} %experts.5), channel_id=1, source_target_pairs={{0,4},{1,17},{2,6},{3,19},{4,0},{5,21},{6,2},{7,23},{8,12},{9,25},... | collective-permute-start | bytes 2580488 | tf_op jit(solution)/shard_map/ppermute | solution.py:36
  76.2 1.9 %collective-permute-start.11 = (bf16[120,3584]{1,0:T(8,128)(2,1)S(1)}, bf16[120,3584]{1,0:T(8,128)(2,1)S(1)}, u32[]{:S(2)}, u32[]{:S(2)}) collective-permute-start(bf16[120,3584]{1,0:T(8,128)(2,1)S(1)} %get-tuple-element.57), channel_id=1, source_target_pairs={{0,2},{1,9},{2,4},{3,11},{4,6},{5,13},{6,0},{7,15},{8,10},{9,17},{... | collective-permute-start | bytes 2580488 | tf_op jit(solution)/shard_map/ppermute | solution.py:36
  78.1 3.9 %collective-permute-start.9 = (bf16[120,3584]{1,0:T(8,128)(2,1)S(1)}, bf16[120,3584]{1,0:T(8,128)(2,1)S(1)}, u32[]{:S(2)}, u32[]{:S(2)}) collective-permute-start(bf16[120,3584]{1,0:T(8,128)(2,1)S(1)} %get-tuple-element.55), channel_id=1, source_target_pairs={{0,6},{1,25},{2,0},{3,27},{4,2},{5,29},{6,4},{7,31},{8,14},{9,1},{... | collective-permute-start | bytes 2580488 | tf_op jit(solution)/shard_map/ppermute | solution.py:36
  82.0 8.5 %collective-permute-done.10.refs_2_ = bf16[120,3584]{1,0:T(8,128)(2,1)S(1)} collective-permute-done((bf16[120,3584]{1,0:T(8,128)(2,1)S(1)}, bf16[120,3584]{1,0:T(8,128)(2,1)S(1)}, u32[]{:S(2)}, u32[]{:S(2)}) %collective-permute-start.10) | collective-permute-done | bytes 860192 | tf_op jit(solution)/shard_map/ppermute | solution.py:36
  90.5 6.0 %collective-permute-done.11.refs_3_ = bf16[120,3584]{1,0:T(8,128)(2,1)S(1)} collective-permute-done((bf16[120,3584]{1,0:T(8,128)(2,1)S(1)}, bf16[120,3584]{1,0:T(8,128)(2,1)S(1)}, u32[]{:S(2)}, u32[]{:S(2)}) %collective-permute-start.11) | collective-permute-done | bytes 860192 | tf_op jit(solution)/shard_map/ppermute | solution.py:36
  96.5 3.1 %collective-permute-done.9.refs_1_ = bf16[120,3584]{1,0:T(8,128)(2,1)S(1)} collective-permute-done((bf16[120,3584]{1,0:T(8,128)(2,1)S(1)}, bf16[120,3584]{1,0:T(8,128)(2,1)S(1)}, u32[]{:S(2)}, u32[]{:S(2)}) %collective-permute-start.9) | collective-permute-done | bytes 860192 | tf_op jit(solution)/shard_map/ppermute | solution.py:36
  99.6 3.5 %gather.1 = (bf16[48,3584]{1,0:T(8,128)(2,1)S(1)}, bf16[48,3584]{1,0:T(8,128)(2,1)S(1)}, bf16[48,3584]{1,0:T(8,128)(2,1)S(1)}, bf16[48,3584]{1,0:T(8,128)(2,1)S(1)}) custom-call(bf16[192,512]{1,0:T(8,128)(2,1)S(1)} %get-tuple-element.41.high_ref, bf16[192,512]{1,0:T(8,128)(2,1)S(1)} %get-tuple-element.42.low_ref, bf16[120,3584]{1,0:T(8,128)(2,1)S(1)} %experts.3.refs_0_, ...), custom_call_target="tpu_custom_call" | custom-call | tf_op jit(solution)/shard_map/gather/pallas_call | solution.py:326
  103.2 4.7 %collective-permute-start.12 = (bf16[48,3584]{1,0:T(8,128)(2,1)S(1)}, bf16[48,3584]{1,0:T(8,128)(2,1)S(1)}, u32[]{:S(2)}, u32[]{:S(2)}) collective-permute-start(bf16[48,3584]{1,0:T(8,128)(2,1)S(1)} %get-tuple-element.59), channel_id=1, source_target_pairs={{0,24},{1,7},{2,26},{3,1},{4,28},{5,3},{6,30},{7,5},{8,0},{9,15},{... | collective-permute-start | bytes 1032200 | tf_op jit(solution)/shard_map/ppermute | solution.py:36
  107.9 1.9 %collective-permute-start.13 = (bf16[48,3584]{1,0:T(8,128)(2,1)S(1)}, bf16[48,3584]{1,0:T(8,128)(2,1)S(1)}, u32[]{:S(2)}, u32[]{:S(2)}) collective-permute-start(bf16[48,3584]{1,0:T(8,128)(2,1)S(1)} %get-tuple-element.60), channel_id=1, source_target_pairs={{0,16},{1,5},{2,18},{3,7},{4,20},{5,1},{6,22},{7,3},{8,24},{9,13},... | collective-permute-start | bytes 1032200 | tf_op jit(solution)/shard_map/ppermute | solution.py:36
  109.8 2.8 %collective-permute-start.14 = (bf16[48,3584]{1,0:T(8,128)(2,1)S(1)}, bf16[48,3584]{1,0:T(8,128)(2,1)S(1)}, u32[]{:S(2)}, u32[]{:S(2)}) collective-permute-start(bf16[48,3584]{1,0:T(8,128)(2,1)S(1)} %get-tuple-element.61), channel_id=1, source_target_pairs={{0,8},{1,3},{2,10},{3,5},{4,12},{5,7},{6,14},{7,1},{8,16},{9,11},{... | collective-permute-start | bytes 1032200 | tf_op jit(solution)/shard_map/ppermute | solution.py:36
  114.1 2.2 %collective-permute-done.12.refs_1_ = bf16[48,3584]{1,0:T(8,128)(2,1)S(1)} collective-permute-done((bf16[48,3584]{1,0:T(8,128)(2,1)S(1)}, bf16[48,3584]{1,0:T(8,128)(2,1)S(1)}, u32[]{:S(2)}, u32[]{:S(2)}) %collective-permute-start.12) | collective-permute-done | bytes 344096 | tf_op jit(solution)/shard_map/ppermute | solution.py:36
  116.3 2.3 %collective-permute-done.13.refs_2_ = bf16[48,3584]{1,0:T(8,128)(2,1)S(1)} collective-permute-done((bf16[48,3584]{1,0:T(8,128)(2,1)S(1)}, bf16[48,3584]{1,0:T(8,128)(2,1)S(1)}, u32[]{:S(2)}, u32[]{:S(2)}) %collective-permute-start.13) | collective-permute-done | bytes 344096 | tf_op jit(solution)/shard_map/ppermute | solution.py:36
  118.6 3.6 %collective-permute-done.14.refs_3_ = bf16[48,3584]{1,0:T(8,128)(2,1)S(1)} collective-permute-done((bf16[48,3584]{1,0:T(8,128)(2,1)S(1)}, bf16[48,3584]{1,0:T(8,128)(2,1)S(1)}, u32[]{:S(2)}, u32[]{:S(2)}) %collective-permute-start.14) | collective-permute-done | bytes 344096 | tf_op jit(solution)/shard_map/ppermute | solution.py:36
  122.2 1.6 finish.1
  127.4 14.7 %all-to-all-start = ((bf16[16,24,224]{2,1,0:T(8,128)(2,1)}), bf16[16,24,224]{2,1,0:T(8,128)(2,1)S(1)}, u32[]{:S(2)}, u32[]{:S(2)}) async-start(bf16[16,24,224]{2,1,0:T(8,128)(2,1)} %bitcast.24), calls=%async_computation | async-start | bytes 393216 | tf_op jit(solution)/shard_map/all_to_all | solution.py:362
  142.9 12.8 %all-to-all-done = bf16[16,24,224]{2,1,0:T(8,128)(2,1)S(1)} async-done(((bf16[16,24,224]{2,1,0:T(8,128)(2,1)}), bf16[16,24,224]{2,1,0:T(8,128)(2,1)S(1)}, u32[]{:S(2)}, u32[]{:S(2)}) %all-to-all-start) | async-done | bytes 172064 | tf_op jit(solution)/shard_map/all_to_all | solution.py:362
  (44 shorter events, 13.3 us)
Async XLA Ops:
  7.2 105.4 %all-gather.2.cloned.1.call-start = ((), (), s32[]{:S(2)}) async-start(), calls=%async_computation.1 | async-start | bytes 1253376 | tf_op jit(solution)/shard_map/all_gather | solution.py:394
  7.3 0.9 copy-start.3
  8.2 0.9 copy-start.5
  9.1 0.7 copy-start.7
  9.9 0.7 copy-start.8
  10.5 0.7 copy-start.9
  12.6 33.2 %collective-permute-start.5 = (bf16[3584,128]{1,0:T(8,128)(2,1)}, bf16[3584,128]{1,0:T(8,128)(2,1)S(1)}, u32[]{:S(2)}, u32[]{:S(2)}) collective-permute-start(bf16[3584,128]{1,0:T(8,128)(2,1)} %bitcast.26), channel_id=1, source_target_pairs={{0,1},{1,0},{2,3},{3,2},{4,5},{5,4},{6,7},{7,6},{8,9},{9,8},{10,11... | collective-permute-start | bytes 2752520 | tf_op jit(solution)/shard_map/ppermute | solution.py:358
  14.6 15.8 %collective-permute-start = (bf16[48,3712]{1,0:T(8,128)(2,1)S(1)}, bf16[48,3712]{1,0:T(8,128)(2,1)S(1)}, u32[]{:S(2)}, u32[]{:S(2)}) collective-permute-start(bf16[48,3712]{1,0:T(8,128)(2,1)S(1)} %get-tuple-element.38), channel_id=1, source_target_pairs={{0,8},{1,3},{2,10},{3,5},{4,12},{5,7},{6,14},{7,1},{8,16},{9,11},{... | collective-permute-start | bytes 1069064 | tf_op jit(solution)/shard_map/ppermute | solution.py:36
  19.5 12.8 %collective-permute-start.1 = (bf16[48,3712]{1,0:T(8,128)(2,1)S(1)}, bf16[48,3712]{1,0:T(8,128)(2,1)S(1)}, u32[]{:S(2)}, u32[]{:S(2)}) collective-permute-start(bf16[48,3712]{1,0:T(8,128)(2,1)S(1)} %get-tuple-element.39), channel_id=1, source_target_pairs={{0,16},{1,5},{2,18},{3,7},{4,20},{5,1},{6,22},{7,3},{8,24},{9,13},... | collective-permute-start | bytes 1069064 | tf_op jit(solution)/shard_map/ppermute | solution.py:36
  24.3 9.3 %collective-permute-start.2 = (bf16[48,3712]{1,0:T(8,128)(2,1)S(1)}, bf16[48,3712]{1,0:T(8,128)(2,1)S(1)}, u32[]{:S(2)}, u32[]{:S(2)}) collective-permute-start(bf16[48,3712]{1,0:T(8,128)(2,1)S(1)} %get-tuple-element.40), channel_id=1, source_target_pairs={{0,24},{1,7},{2,26},{3,1},{4,28},{5,3},{6,30},{7,5},{8,0},{9,15},{... | collective-permute-start | bytes 1069064 | tf_op jit(solution)/shard_map/ppermute | solution.py:36
  27.6 21.7 %collective-permute-start.6 = (bf16[3584,128]{1,0:T(8,128)(2,1)}, bf16[3584,128]{1,0:T(8,128)(2,1)S(1)}, u32[]{:S(2)}, u32[]{:S(2)}) collective-permute-start(bf16[3584,128]{1,0:T(8,128)(2,1)} %bitcast.30), channel_id=1, source_target_pairs={{0,1},{1,0},{2,3},{3,2},{4,5},{5,4},{6,7},{7,6},{8,9},{9,8},{10,11... | collective-permute-start | bytes 2752520 | tf_op jit(solution)/shard_map/ppermute | solution.py:358
  30.4 18.9 %collective-permute-start.7 = (bf16[128,3584]{1,0:T(8,128)(2,1)}, bf16[128,3584]{1,0:T(8,128)(2,1)S(1)}, u32[]{:S(2)}, u32[]{:S(2)}) collective-permute-start(bf16[128,3584]{1,0:T(8,128)(2,1)} %bitcast.34), channel_id=1, source_target_pairs={{0,1},{1,0},{2,3},{3,2},{4,5},{5,4},{6,7},{7,6},{8,9},{9,8},{10,11... | collective-permute-start | bytes 2752520 | tf_op jit(solution)/shard_map/ppermute | solution.py:358
  33.6 15.7 %copy-start = (bf16[1,3584,128]{2,1,0:T(8,128)(2,1)S(1)}, bf16[1,3584,128]{2,1,0:T(8,128)(2,1)}, u32[]{:S(2)}) copy-start(bf16[1,3584,128]{2,1,0:T(8,128)(2,1)} %param.15) | copy-start | bytes 2752516
  33.6 15.7 %copy-start.1 = (bf16[1,3584,128]{2,1,0:T(8,128)(2,1)S(1)}, bf16[1,3584,128]{2,1,0:T(8,128)(2,1)}, u32[]{:S(2)}) copy-start(bf16[1,3584,128]{2,1,0:T(8,128)(2,1)} %param.16) | copy-start | bytes 2752516
  33.6 15.7 %copy-start.2 = (bf16[1,128,3584]{2,1,0:T(8,128)(2,1)S(1)}, bf16[1,128,3584]{2,1,0:T(8,128)(2,1)}, u32[]{:S(2)}) copy-start(bf16[1,128,3584]{2,1,0:T(8,128)(2,1)} %param.17) | copy-start | bytes 2752516
  36.6 26.8 %collective-permute-start.3 = (bf16[120,3584]{1,0:T(8,128)(2,1)S(1)}, bf16[120,3584]{1,0:T(8,128)(2,1)S(1)}, u32[]{:S(2)}, u32[]{:S(2)}) collective-permute-start(bf16[120,3584]{1,0:T(8,128)(2,1)S(1)} %get-tuple-element.43), channel_id=1, source_target_pairs={{0,2},{1,9},{2,4},{3,11},{4,6},{5,13},{6,0},{7,15},{8,10},{9,17},{... | collective-permute-start | bytes 2580488 | tf_op jit(solution)/shard_map/ppermute | solution.py:36
  43.9 25.1 %collective-permute-start.4 = (bf16[120,3584]{1,0:T(8,128)(2,1)S(1)}, bf16[120,3584]{1,0:T(8,128)(2,1)S(1)}, u32[]{:S(2)}, u32[]{:S(2)}) collective-permute-start(bf16[120,3584]{1,0:T(8,128)(2,1)S(1)} %get-tuple-element.44), channel_id=1, source_target_pairs={{0,6},{1,25},{2,0},{3,27},{4,2},{5,29},{6,4},{7,31},{8,14},{9,1},{... | collective-permute-start | bytes 2580488 | tf_op jit(solution)/shard_map/ppermute | solution.py:36
  45.9 26.4 %collective-permute-start.8 = (bf16[120,3584]{1,0:T(8,128)(2,1)S(1)}, bf16[120,3584]{1,0:T(8,128)(2,1)S(1)}, u32[]{:S(2)}, u32[]{:S(2)}) collective-permute-start(bf16[120,3584]{1,0:T(8,128)(2,1)S(1)} %get-tuple-element.50), channel_id=1, source_target_pairs={{0,4},{1,17},{2,6},{3,19},{4,0},{5,21},{6,2},{7,23},{8,12},{9,25},... | collective-permute-start | bytes 2580488 | tf_op jit(solution)/shard_map/ppermute | solution.py:36
  74.2 16.3 %collective-permute-start.10 = (bf16[120,3584]{1,0:T(8,128)(2,1)S(1)}, bf16[120,3584]{1,0:T(8,128)(2,1)S(1)}, u32[]{:S(2)}, u32[]{:S(2)}) collective-permute-start(bf16[120,3584]{1,0:T(8,128)(2,1)S(1)} %experts.5), channel_id=1, source_target_pairs={{0,4},{1,17},{2,6},{3,19},{4,0},{5,21},{6,2},{7,23},{8,12},{9,25},... | collective-permute-start | bytes 2580488 | tf_op jit(solution)/shard_map/ppermute | solution.py:36
  76.2 20.4 %collective-permute-start.11 = (bf16[120,3584]{1,0:T(8,128)(2,1)S(1)}, bf16[120,3584]{1,0:T(8,128)(2,1)S(1)}, u32[]{:S(2)}, u32[]{:S(2)}) collective-permute-start(bf16[120,3584]{1,0:T(8,128)(2,1)S(1)} %get-tuple-element.57), channel_id=1, source_target_pairs={{0,2},{1,9},{2,4},{3,11},{4,6},{5,13},{6,0},{7,15},{8,10},{9,17},{... | collective-permute-start | bytes 2580488 | tf_op jit(solution)/shard_map/ppermute | solution.py:36
  78.1 21.5 %collective-permute-start.9 = (bf16[120,3584]{1,0:T(8,128)(2,1)S(1)}, bf16[120,3584]{1,0:T(8,128)(2,1)S(1)}, u32[]{:S(2)}, u32[]{:S(2)}) collective-permute-start(bf16[120,3584]{1,0:T(8,128)(2,1)S(1)} %get-tuple-element.55), channel_id=1, source_target_pairs={{0,6},{1,25},{2,0},{3,27},{4,2},{5,29},{6,4},{7,31},{8,14},{9,1},{... | collective-permute-start | bytes 2580488 | tf_op jit(solution)/shard_map/ppermute | solution.py:36
  103.2 19.0 %copy-start.4 = (bf16[1,24,3584]{2,1,0:T(8,128)(2,1)S(1)}, bf16[1,24,3584]{2,1,0:T(8,128)(2,1)}, u32[]{:S(2)}) copy-start(bf16[1,24,3584]{2,1,0:T(8,128)(2,1)} %param.10) | copy-start | bytes 516100
  103.2 19.0 %copy-start.6 = (bf16[1,24,3584]{2,1,0:T(8,128)(2,1)S(1)}, bf16[1,24,3584]{2,1,0:T(8,128)(2,1)}, u32[]{:S(2)}) copy-start(bf16[1,24,3584]{2,1,0:T(8,128)(2,1)} %param.11) | copy-start | bytes 516100
  103.2 13.1 %collective-permute-start.12 = (bf16[48,3584]{1,0:T(8,128)(2,1)S(1)}, bf16[48,3584]{1,0:T(8,128)(2,1)S(1)}, u32[]{:S(2)}, u32[]{:S(2)}) collective-permute-start(bf16[48,3584]{1,0:T(8,128)(2,1)S(1)} %get-tuple-element.59), channel_id=1, source_target_pairs={{0,24},{1,7},{2,26},{3,1},{4,28},{5,3},{6,30},{7,5},{8,0},{9,15},{... | collective-permute-start | bytes 1032200 | tf_op jit(solution)/shard_map/ppermute | solution.py:36
  107.9 10.8 %collective-permute-start.13 = (bf16[48,3584]{1,0:T(8,128)(2,1)S(1)}, bf16[48,3584]{1,0:T(8,128)(2,1)S(1)}, u32[]{:S(2)}, u32[]{:S(2)}) collective-permute-start(bf16[48,3584]{1,0:T(8,128)(2,1)S(1)} %get-tuple-element.60), channel_id=1, source_target_pairs={{0,16},{1,5},{2,18},{3,7},{4,20},{5,1},{6,22},{7,3},{8,24},{9,13},... | collective-permute-start | bytes 1032200 | tf_op jit(solution)/shard_map/ppermute | solution.py:36
  109.8 12.4 %collective-permute-start.14 = (bf16[48,3584]{1,0:T(8,128)(2,1)S(1)}, bf16[48,3584]{1,0:T(8,128)(2,1)S(1)}, u32[]{:S(2)}, u32[]{:S(2)}) collective-permute-start(bf16[48,3584]{1,0:T(8,128)(2,1)S(1)} %get-tuple-element.61), channel_id=1, source_target_pairs={{0,8},{1,3},{2,10},{3,5},{4,12},{5,7},{6,14},{7,1},{8,16},{9,11},{... | collective-permute-start | bytes 1032200 | tf_op jit(solution)/shard_map/ppermute | solution.py:36
  123.8 18.3 %collective-permute-start.15 = (bf16[24,3584]{1,0:T(8,128)(2,1)S(1)}, bf16[24,3584]{1,0:T(8,128)(2,1)S(1)}, u32[]{:S(2)}, u32[]{:S(2)}) collective-permute-start(bf16[24,3584]{1,0:T(8,128)(2,1)S(1)} %get-tuple-element.62), channel_id=1, source_target_pairs={{0,32},{32,64},{64,96},{96,128},{128,160},{160,192},{192,224},{224... | collective-permute-start | bytes 516104 | tf_op jit(solution)/shard_map/ppermute | solution.py:354
  125.1 17.0 %collective-permute-start.16 = (bf16[24,3584]{1,0:T(8,128)(2,1)S(1)}, bf16[24,3584]{1,0:T(8,128)(2,1)S(1)}, u32[]{:S(2)}, u32[]{:S(2)}) collective-permute-start(bf16[24,3584]{1,0:T(8,128)(2,1)S(1)} %get-tuple-element.63), channel_id=1, source_target_pairs={{32,0},{64,32},{96,64},{128,96},{160,128},{192,160},{224,192},{256... | collective-permute-start | bytes 516104 | tf_op jit(solution)/shard_map/ppermute | solution.py:354
  127.4 28.3 %all-to-all-start = ((bf16[16,24,224]{2,1,0:T(8,128)(2,1)}), bf16[16,24,224]{2,1,0:T(8,128)(2,1)S(1)}, u32[]{:S(2)}, u32[]{:S(2)}) async-start(bf16[16,24,224]{2,1,0:T(8,128)(2,1)} %bitcast.24), calls=%async_computation | async-start | bytes 393216 | tf_op jit(solution)/shard_map/all_to_all | solution.py:362
Sparse Core Ops, SparseCore 0:
  19.6 75.5 all-gather.1

commit v3 on v2

v3 whole, which is shorter than its diff:
```python
import jax
import jax.numpy as jnp
from jax import lax
from jax.experimental import pallas as pl
from jax.experimental.pallas import tpu as pltpu
from jax.sharding import PartitionSpec as P

EPS = 1e-06
BF = jnp.bfloat16
F32 = jnp.float32
EXPERTS = 4
COLS = 4
CAP = 15
ROWS = 24
BOTH = 2 * ROWS
SLOTS = 2 * CAP
EXTRA = 128
WIDE = 1792
CHUNK = 512
RADIX = 4
LANES = 128


def device(y, x, core):
    return (y * COLS + x) * 2 + core


def hop(block, distance):
    route = []
    for y in range(EXPERTS):
        for x in range(COLS):
            for core in range(2):
                along_y = core == 1
                there = ((y + distance) % EXPERTS, x) if along_y else (y, (x + distance) % COLS)
                route.append((device(y, x, core), device(*there, core)))
    return lax.ppermute(block, "ep", route)


def rings(along_y):
    groups = []
    for core in range(2):
        if (core == 0) == along_y:
            groups += [[device(y, x, core) for y in range(EXPERTS)] for x in range(COLS)]
        else:
            groups += [[device(y, x, core) for x in range(COLS)] for y in range(EXPERTS)]
    return groups


def exchange(rows):
    return lax.all_to_all(
        rows, "ep", split_axis=0, concat_axis=0, axis_index_groups=rings(True), tiled=True
    )


def iota(shape, dim):
    return lax.broadcasted_iota(jnp.int32, shape, dim)


def dot(a, b):
    return jnp.dot(a, b, preferred_element_type=F32)


def split_gate(gate):
    high = gate.astype(BF).astype(F32)
    return high, (gate - high).astype(BF).astype(F32)


def send_kernel(place_ref, fwd_ref, bwd_ref, gain_ref, ids_ref, gates_ref, out_ref, meta_ref):
    lanes = iota((BOTH, EXTRA), 1)
    row = iota((BOTH, EXTRA), 0)
    in_fwd = row < ROWS
    own = lanes[:, :ROWS] == row[:, :ROWS] - jnp.where(in_fwd[:, :ROWS], 0, ROWS)

    def column(ref, k):
        both = jnp.where(in_fwd[:, :ROWS], ref[0, k : k + 1, :], ref[1, k : k + 1, :])
        return jnp.sum(jnp.where(own, both, jnp.zeros_like(both)), axis=1, keepdims=True)

    first, second = column(ids_ref, 0), column(ids_ref, 1)
    named = jnp.where((lanes == first) | (lanes == second), 1.0, 0.0)
    r0, r1 = iota((BOTH, BOTH), 0), iota((BOTH, BOTH), 1)
    earlier = jnp.where((r1 < r0) & ((r1 < ROWS) == (r0 < ROWS)), 1.0, 0.0)
    rank = dot(earlier.astype(BF), named.astype(BF))
    offset = jnp.where(in_fwd[:, 0:1], 0, CAP)
    slots = []
    for chosen in (first, second):
        taken = jnp.sum(jnp.where(lanes == chosen, rank, 0.0), axis=1, keepdims=True)
        slots.append(taken.astype(jnp.int32) + offset)
    ahead = [
        jnp.bitwise_and(chosen - place_ref[1] + EXPERTS, EXPERTS - 1) for chosen in (first, second)
    ]
    fields = [ahead[0].astype(F32), slots[0].astype(F32), ahead[1].astype(F32), slots[1].astype(F32)]
    fields += split_gate(column(gates_ref, 0))
    fields += split_gate(column(gates_ref, 1))
    fields += [first.astype(F32), second.astype(F32)]
    meta = jnp.zeros((BOTH, EXTRA), F32)
    for place, field in enumerate(fields):
        meta = jnp.where(lanes == place, field, meta)
    meta_ref[...] = meta

    def as_row(column):
        return jnp.sum(jnp.where(r0 == r1, column, 0), axis=0, keepdims=True)

    target = iota((EXPERTS * BOTH, BOTH), 0)
    source = iota((EXPERTS * BOTH, BOTH), 1)
    routed = (target == as_row(first * BOTH + slots[0])) | (
        target == as_row(second * BOTH + slots[1])
    )
    copied = target == source
    for part in range(1, COLS):
        copied = copied | (target == source + part * BOTH)
    routed_f = jnp.where(routed, 1.0, 0.0)
    copied_f = jnp.where(copied, 1.0, 0.0)
    pick = jnp.where(place_ref[0] == 0, routed_f, copied_f).astype(BF)
    values = jnp.concatenate([fwd_ref[...].astype(F32), bwd_ref[...].astype(F32)], axis=0)
    features = values.shape[1]
    inverse = lax.rsqrt(jnp.mean(values * values, axis=-1, keepdims=True) + EPS)
    normed = (values * inverse * gain_ref[...]).astype(BF)
    for start in range(0, features, CHUNK):
        out_ref[:, start : start + CHUNK] = dot(pick, normed[:, start : start + CHUNK]).astype(BF)
    out_ref[:, features:] = dot(pick, meta.astype(BF)).astype(BF)


def slot_targets(place_ref, extra):
    total = EXPERTS * BOTH
    row = iota((total, 1), 0)
    part = (
        (row >= BOTH).astype(jnp.int32)
        + (row >= 2 * BOTH).astype(jnp.int32)
        + (row >= 3 * BOTH).astype(jnp.int32)
    )
    place = row - part * BOTH
    on_first = place_ref[0] == 0
    packed = jnp.where(place < SLOTS, part * SLOTS + place, -EXPERTS * LANES)
    found = []
    for k in range(COLS):
        there, high, low = -1, 0.0, 0.0
        if k < 2:
            expert = extra[:, 2 * k : 2 * k + 1].astype(jnp.int32)
            slot = extra[:, 2 * k + 1 : 2 * k + 2].astype(jnp.int32)
            there = expert * LANES + part * SLOTS + slot
            high = extra[:, 4 + 2 * k : 5 + 2 * k]
            low = extra[:, 5 + 2 * k : 6 + 2 * k]
        target = jnp.where(on_first, packed + k * LANES, there)
        found.append((target, jnp.where(on_first, 1.0, high), jnp.where(on_first, 0.0, low)))
    return found


def move(pick_ref, rows_ref, parts, out_refs):
    width = rows_ref.shape[1]
    for start in range(0, width, CHUNK):
        cut = slice(start, min(start + CHUNK, width))
        rows = rows_ref[:, cut]
        for part, out_ref in zip(parts, out_refs):
            moved = dot(pick_ref[part * LANES : (part + 1) * LANES, :], rows)
            out_ref[:, cut] = moved[: COLS * SLOTS].astype(BF)


def near_kernel(place_ref, rows_ref, extra_ref, first_ref, third_ref, pick_ref):
    @pl.when(pl.program_id(0) == 0)
    def _():
        column = iota((EXPERTS * BOTH, EXPERTS * LANES), 1)
        pick = jnp.zeros(column.shape, F32)
        for target, _, _ in slot_targets(place_ref, extra_ref[...].astype(F32)):
            pick = jnp.where(column == target, 1.0, pick)
        pick_ref[...] = pick.T.astype(BF)

    move(pick_ref, rows_ref, (1, 3), (first_ref, third_ref))


def rest_kernel(
    place_ref, rows_ref, extra_ref, pick_ref, own_ref, second_ref, high_ref, low_ref
):
    @pl.when(pl.program_id(0) == 0)
    def _():
        column = iota((EXPERTS * BOTH, EXPERTS * LANES), 1)
        high_m = jnp.zeros(column.shape, F32)
        low_m = jnp.zeros(column.shape, F32)
        for target, high, low in slot_targets(place_ref, extra_ref[...].astype(F32)):
            here = column == target
            high_m = jnp.where(here, high, high_m)
            low_m = jnp.where(here, low, low_m)
        high_ref[...] = high_m.astype(BF)
        low_ref[...] = low_m.astype(BF)

    move(pick_ref, rows_ref, (0, 2), (own_ref, second_ref))


def expert_kernel(steps, count, *refs):
    rows_refs = refs[:count]
    g0_ref, g1_ref, u0_ref, u1_ref, d0_ref, d1_ref = refs[count : count + 6]
    token_ref, gate_acc, up_acc, hid_ref = refs[-4:]
    out_refs = refs[-4 - count : -4]
    step = pl.program_id(0)
    token_ref[...] = jnp.zeros_like(token_ref)

    @pl.when(step < steps)
    def _():
        gate_w = jnp.concatenate([g0_ref[...], g1_ref[...]], axis=1)
        up_w = jnp.concatenate([u0_ref[...], u1_ref[...]], axis=1)
        for i, rows_ref in enumerate(rows_refs):
            gate = dot(rows_ref[...], gate_w)
            up = dot(rows_ref[...], up_w)

            @pl.when(step == 0)
            def _():
                gate_acc[i] = gate
                up_acc[i] = up

            @pl.when(step > 0)
            def _():
                gate_acc[i] += gate
                up_acc[i] += up

    @pl.when(step == steps - 1)
    def _():
        gate = gate_acc[...]
        hid_ref[...] = (gate / (1.0 + jnp.exp(-gate)) * up_acc[...]).astype(BF)

    @pl.when(step >= steps)
    def _():
        down = jnp.concatenate([d0_ref[...], d1_ref[...]], axis=0)
        for i, out_ref in enumerate(out_refs):
            out_ref[...] = dot(hid_ref[i], down).astype(BF)


def gather_kernel(parts, last, high_ref, low_ref, *refs):
    rows_refs, so_far_ref, out_ref = refs[: len(parts)], refs[len(parts)], refs[-1]
    width = rows_refs[0].shape[1]
    used = COLS * SLOTS
    for start in range(0, width, CHUNK):
        cut = slice(start, min(start + CHUNK, width))
        total = so_far_ref[:, cut] if last else 0.0
        for part, ref in zip(parts, rows_refs):
            lanes = slice(part * LANES, part * LANES + used)
            rows = ref[:, cut]
            total += dot(high_ref[:, lanes], rows) + dot(low_ref[:, lanes], rows)
        out_ref[:, cut] = total.astype(out_ref.dtype)


def finish_kernel(place_ref, meta_ref, rows_ref, fwd_ref, bwd_ref, of_ref, ob_ref, *leave_refs):
    meta = meta_ref[...]
    total = EXPERTS * BOTH
    column = iota((BOTH, total), 1)
    row = iota((BOTH, total), 0)
    high = jnp.zeros((BOTH, total), F32)
    low = jnp.zeros((BOTH, total), F32)
    for k in range(2):
        there = (meta[:, 8 + k : 9 + k] * BOTH + meta[:, 2 * k + 1 : 2 * k + 2]).astype(jnp.int32)
        high = jnp.where(column == there, meta[:, 4 + 2 * k : 5 + 2 * k], high)
        low = jnp.where(column == there, meta[:, 5 + 2 * k : 6 + 2 * k], low)
    same = column == row
    for part in range(1, COLS):
        same = same | (column == row + part * BOTH)
    ones = jnp.where(same, 1.0, 0.0)
    on_first = place_ref[0] == 0
    high = jnp.where(on_first, high, ones).astype(BF)
    low = jnp.where(on_first, low, 0.0).astype(BF)
    width = fwd_ref.shape[1] // RADIX
    for part in range(RADIX):
        cut = slice(part * width, (part + 1) * width)
        rows = rows_ref[:, cut]
        mixture = dot(high, rows) + dot(low, rows)
        of_ref[:, cut] = (fwd_ref[:, cut].astype(F32) + mixture[:ROWS]).astype(BF)
        ob_ref[:, cut] = (bwd_ref[:, cut].astype(F32) + mixture[ROWS:]).astype(BF)
    for part in range(RADIX):
        up = slice(part * width, (part + 1) * width)
        down = slice((RADIX - 1 - part) * width, (RADIX - part) * width)

        @pl.when(place_ref[2] == 0)
        def _():
            leave_refs[part][...] = ob_ref[:, up]

        @pl.when(place_ref[2] != 0)
        def _():
            leave_refs[part][...] = of_ref[:, down]


SMEM = pl.BlockSpec(memory_space=pltpu.SMEM)


def params(mib=20):
    return pltpu.CompilerParams(vmem_limit_bytes=mib * 1024 * 1024)


def whole(shape):
    return pl.BlockSpec(shape, lambda i: (0,) * len(shape))


def tile(rows, width=WIDE):
    return pl.BlockSpec((rows, width), lambda i: (0, i))


def shape(rows, columns, dtype=BF):
    return jax.ShapeDtypeStruct((rows, columns), dtype)


def make_send(place, fwd, bwd, gain, ids, gates):
    features = fwd.shape[1]
    vmem = pl.BlockSpec(memory_space=pltpu.VMEM)
    return pl.pallas_call(
        send_kernel,
        out_shape=(shape(EXPERTS * BOTH, features + EXTRA), shape(BOTH, EXTRA, F32)),
        in_specs=[SMEM] + [vmem] * 5,
        out_specs=(vmem, vmem),
        compiler_params=params(),
        name="normed",
    )(place, fwd, bwd, gain, ids, gates)


def make_near(place, rows):
    features = rows.shape[1] - EXTRA
    total = EXPERTS * BOTH
    lanes = EXPERTS * LANES
    return pl.pallas_call(
        near_kernel,
        grid=(features // WIDE,),
        out_shape=(shape(COLS * SLOTS, features),) * 2 + (shape(lanes, total),),
        in_specs=[SMEM, tile(total), whole_extra(total, features)],
        out_specs=(tile(COLS * SLOTS),) * 2 + (whole((lanes, total)),),
        compiler_params=params(),
        name="near",
    )(place, rows, rows)


def make_rest(place, rows, pick):
    features = rows.shape[1] - EXTRA
    total = EXPERTS * BOTH
    lanes = EXPERTS * LANES
    return pl.pallas_call(
        rest_kernel,
        grid=(features // WIDE,),
        out_shape=(shape(COLS * SLOTS, features),) * 2 + (shape(total, lanes),) * 2,
        in_specs=[SMEM, tile(total), whole_extra(total, features), whole((lanes, total))],
        out_specs=(tile(COLS * SLOTS),) * 2 + (whole((total, lanes)),) * 2,
        compiler_params=params(),
        name="rest",
    )(place, rows, rows, pick)


def whole_extra(total, features):
    return pl.BlockSpec((total, EXTRA), lambda i: (0, features // EXTRA))


def run_experts(blocks, gates, ups, downs, *before):
    count = len(blocks)
    rows, features = blocks[0].shape
    width = gates[0].shape[1]
    steps = features // WIDE
    first = lambda i: jnp.minimum(i, steps - 1)
    later = lambda i: jnp.maximum(i - steps, 0)
    tall = pl.BlockSpec((WIDE, width), lambda i: (first(i), 0))
    flat = pl.BlockSpec((width, WIDE), lambda i: (0, later(i)))
    token = (8, LANES)

    def body(*refs):
        expert_kernel(steps, count, *refs)

    return pl.pallas_call(
        body,
        grid=(2 * steps,),
        out_shape=(shape(rows, features),) * count + (shape(*token, jnp.int32),),
        in_specs=[pl.BlockSpec((rows, WIDE), lambda i: (0, first(i)))] * count
        + [tall] * 4
        + [flat] * 2
        + [pl.BlockSpec(memory_space=pl.ANY)] * len(before),
        out_specs=(pl.BlockSpec((rows, WIDE), lambda i: (0, later(i))),) * count + (whole(token),),
        scratch_shapes=[
            pltpu.VMEM((count, rows, 2 * width), F32),
            pltpu.VMEM((count, rows, 2 * width), F32),
            pltpu.VMEM((count, rows, 2 * width), BF),
        ],
        compiler_params=params(),
        name="experts",
    )(*blocks, gates[0], gates[1], ups[0], ups[1], downs[0], downs[1], *before)


def make_gather(high, low, blocks, parts, so_far=None, before=()):
    rows, features = blocks[0].shape
    total = high.shape[0]
    last = so_far is not None

    def body(*refs):
        gather_kernel(parts, last, *refs)

    return pl.pallas_call(
        body,
        grid=(features // WIDE,),
        out_shape=shape(total, features, BF if last else F32),
        in_specs=[whole(high.shape), whole(low.shape)]
        + [tile(rows)] * len(blocks)
        + [tile(total)] * last
        + [pl.BlockSpec(memory_space=pl.ANY)] * len(before),
        out_specs=tile(total),
        compiler_params=params(),
        name="gather",
    )(high, low, *blocks, *([so_far] if last else []), *before)


def make_finish(place, meta, rows, fwd, bwd):
    features = fwd.shape[1]
    vmem = pl.BlockSpec(memory_space=pltpu.VMEM)
    return pl.pallas_call(
        finish_kernel,
        out_shape=(shape(ROWS, features),) * 2 + (shape(ROWS, features // RADIX),) * RADIX,
        in_specs=[SMEM] + [vmem] * 4,
        out_specs=(vmem,) * (2 + RADIX),
        compiler_params=params(),
        name="finish",
    )(place, meta, rows, fwd, bwd)


def shifted(block, distance, count):
    route = [(i, i + distance) for i in range(count) if 0 <= i + distance < count]
    return lax.ppermute(block, "pp", route)


def from_other_core(block):
    return lax.ppermute(block, "ep", [(i, i ^ 1) for i in range(lax.axis_size("ep"))])


def tree_start(fwd, bwd, section):
    odd = (section & 1) == 1
    return jnp.where(odd, bwd, fwd), jnp.where(odd, fwd, bwd)


def tree_send(block, step, sections):
    bit = 1 << step
    route = [(s, s - bit) for s in range(bit, sections, 2 * bit)]
    route += [(s, s + bit) for s in range(bit - 1, sections, 2 * bit)]
    return lax.ppermute(block, "pp", route)


def tree_join(held, got, step, section):
    upper = (section & (1 << step)) != 0
    return jnp.where(
        upper, jnp.concatenate([got, held], axis=0), jnp.concatenate([held, got], axis=0)
    )


def scatter_far(parts, section, sections):
    final = sections - 1
    held = parts[0]
    for k in range(1, RADIX):
        got = lax.ppermute(parts[k], "pp", [(final, final - RADIX * k), (0, RADIX * k)])
        here = (section == final - RADIX * k) | (section == RADIX * k)
        held = jnp.where(here, got, held)
    return held


def scatter_near(held, section, sections):
    place = section & (RADIX - 1)
    width = held.shape[1] // RADIX
    blocks = [held[:, m * width : (m + 1) * width] for m in range(RADIX)]
    to_fwd, to_bwd = blocks[RADIX - 1], blocks[0]
    for m in range(1, RADIX):
        sent = jnp.where(place == 0, blocks[m], blocks[RADIX - 1 - m])
        route = [(s, s - m) for s in range(RADIX - 1, sections, RADIX)]
        route += [(s, s + m) for s in range(0, sections, RADIX)]
        got = lax.ppermute(sent, "pp", route)
        to_fwd = jnp.where(place == RADIX - 1 - m, got, to_fwd)
        to_bwd = jnp.where(place == m, got, to_bwd)
    return to_fwd, to_bwd


def body(
    state_fwd,
    state_bwd,
    enter_fwd,
    enter_bwd,
    norm_gain,
    w_gate,
    w_up,
    w_down,
    route_ids,
    route_gates,
):
    sections = lax.axis_size("pp")
    section = lax.axis_index("pp")
    position = lax.axis_index("ep")
    place = jnp.stack([position % 2, position // (2 * COLS), section]).astype(jnp.int32)
    fwd, bwd = state_fwd[0], state_bwd[0]
    features = fwd.shape[1]
    part = features // sections
    ids = route_ids[0, 0].transpose(0, 2, 1)
    gates = route_gates[0, 0].transpose(0, 2, 1)

    own = (w_gate[0], w_up[0], w_down[0])
    sent, meta = make_send(place, fwd, bwd, norm_gain, ids, gates)
    after = lax.optimization_barrier
    passed, meta = after((own, meta))
    weights = tuple(zip(own, (from_other_core(w) for w in passed)))

    rows = exchange(sent)
    send1, send3, pick = make_near(place, rows)
    near, far = hop(send1, 1), hop(send3, 3)
    send0, send2, high, low = make_rest(place, rows, pick)
    last = hop(send2, 2)
    done0, token = run_experts([send0], *weights)
    held, sent = tree_start(enter_fwd[0], enter_bwd[0], section + token[0, 0])
    got = tree_send(sent, 0, sections)
    held = tree_join(held, got, 0, section)
    got = tree_send(held, 1, sections)
    done1, done3, token = run_experts([near, far], *weights, token, got)
    back1, back3 = hop(done1, -1), hop(done3, -3)
    done2, token = run_experts([last], *weights, token)
    back2 = hop(done2, -2)
    held = tree_join(held, got, 1, section + token[0, 0])
    got = tree_send(held, 2, sections)
    held = tree_join(held, got, 2, section)
    begun = make_gather(high, low, [done0, back1, back3], (0, 1, 3))
    gathered = make_gather(high, low, [back2], (2,), begun, (got,))
    got = tree_send(held, 3, sections)
    held = tree_join(held, got, 3, section)
    entered = held.reshape(sections, ROWS, part).transpose(1, 0, 2).reshape(ROWS, features)
    fwd_out, bwd_out, *leaving = make_finish(place, meta, exchange(gathered), fwd, bwd)
    fwd_out, bwd_out, entered = after((fwd_out, bwd_out, entered))

    from_left, from_right = shifted(fwd_out, 1, sections), shifted(bwd_out, -1, sections)
    held = scatter_far(leaving, section, sections)
    held, from_left, from_right = after((held, from_left, from_right))
    leave_fwd, leave_bwd = scatter_near(held, section, sections)
    fwd_next = jnp.where(section == 0, entered, from_left)
    bwd_next = jnp.where(section == sections - 1, entered, from_right)
    return (fwd_next[None], bwd_next[None], leave_fwd[None], leave_bwd[None])


def solution(mesh):
    placed = (
        P("pp", "ep", None),
        P("pp", "ep", None),
        P(None, "ep", "pp"),
        P(None, "ep", "pp"),
        P("pp", None),
        P("pp", None, "ep"),
        P("pp", None, "ep"),
        P("pp", "ep", None),
        P("pp", None, None, "ep", None),
        P("pp", None, None, "ep", None),
    )
    return jax.shard_map(
        body,
        mesh=mesh,
        in_specs=placed,
        out_specs=(
            P("pp", "ep", None),
            P("pp", "ep", None),
            P(None, "ep", "pp"),
            P(None, "ep", "pp"),
        ),
        check_vma=False,
    )
```

time: 164 us -> 155 us (0.945)
  the two profiles are of different devices: /device:TPU:6 before, /device:TPU:32 now
where the time goes in v3:
time: 155 us; the launch traced here: 154 us
  starting transfers between devices  69.3 us (45%)
  waiting for transfers between devices  42.8 us (28%)
  Pallas kernels  28.6 us (18%)
  local copies, waits for them, and re-layouts  9.07 us (6%)
  between operations  2.45 us (2%)
  other arithmetic  1.76 us (1%)
    ppermute x6, starting transfers between devices, hop(): return lax.ppermute(block, 'ep', route)  20.2 us
    ppermute x2, starting transfers between devices, shifted(): return lax.ppermute(block, 'pp', route)  18.9 us
    all_to_all x2, waiting for transfers between devices, exchange(): lax.all_to_all(rows, 'ep', split_axis=0, concat_axis=0, axis_index_groups...  18.5 us
    pallas_call x3, Pallas kernels, run_experts(): pl.pallas_call(body, grid=(2 * steps,), out_shape=(shape(rows, features),...  14.4 us
    ppermute x6, waiting for transfers between devices, hop(): return lax.ppermute(block, 'ep', route)  12.4 us
    ppermute x4, starting transfers between devices, tree_send(): return lax.ppermute(block, 'pp', route)  10.4 us
    all_to_all x2, starting transfers between devices, exchange(): lax.all_to_all(rows, 'ep', split_axis=0, concat_axis=0, axis_index_groups...  8.27 us
    unnamed x36, local copies, waits for them, and re-layouts  7.77 us
  transfers between devices with their start and end apart: 23, of which 8 were waited for; matrix products, arithmetic and copies ran while one was open for 1% of the time, Pallas kernels for 16%

profile of v3, /device:TPU:32, one launch (start us, length us, event | category | flops | bytes accessed | tf_op | source)
XLA Modules:
  0.0 154.0 jit_solution(3823219242138072590)
XLA Ops:
  4.6 1.4 normed.1
  7.1 4.6 %all-to-all-start = ((bf16[4,48,3712]{2,1,0:T(8,128)(2,1)}), bf16[4,48,3712]{2,1,0:T(8,128)(2,1)S(1)}, u32[]{:S(2)}, u32[]{:S(2)}) async-start(bf16[4,48,3712]{2,1,0:T(8,128)(2,1)} %bitcast.53), calls=%async_computation | async-start | bytes 2850816 | tf_op jit(solution)/shard_map/all_to_all | solution.py:50
  11.7 1.9 %collective-permute-start.1 = (bf16[3584,128]{1,0:T(8,128)(2,1)S(1)}, bf16[3584,128]{1,0:T(8,128)(2,1)}, u32[]{:S(2)}, u32[]{:S(2)}) collective-permute-start(bf16[3584,128]{1,0:T(8,128)(2,1)S(1)} %bitcast.40), channel_id=1, source_target_pairs={{0,1},{1,0},{2,3},{3,2},{4,5},{5,4},{6,7},{7,6},{8,9},{9,8},{10,11... | collective-permute-start | bytes 2752520 | tf_op jit(solution)/shard_map/ppermute | solution.py:418
  13.7 2.4 %collective-permute-start.2 = (bf16[3584,128]{1,0:T(8,128)(2,1)S(1)}, bf16[3584,128]{1,0:T(8,128)(2,1)}, u32[]{:S(2)}, u32[]{:S(2)}) collective-permute-start(bf16[3584,128]{1,0:T(8,128)(2,1)S(1)} %bitcast.44), channel_id=1, source_target_pairs={{0,1},{1,0},{2,3},{3,2},{4,5},{5,4},{6,7},{7,6},{8,9},{9,8},{10,11... | collective-permute-start | bytes 2752520 | tf_op jit(solution)/shard_map/ppermute | solution.py:418
  16.1 1.9 %collective-permute-start.3 = (bf16[128,3584]{1,0:T(8,128)(2,1)}, bf16[128,3584]{1,0:T(8,128)(2,1)}, u32[]{:S(2)}, u32[]{:S(2)}) collective-permute-start(bf16[128,3584]{1,0:T(8,128)(2,1)} %bitcast.48), channel_id=1, source_target_pairs={{0,1},{1,0},{2,3},{3,2},{4,5},{5,4},{6,7},{7,6},{8,9},{9,8},{10,11... | collective-permute-start | bytes 2752520 | tf_op jit(solution)/shard_map/ppermute | solution.py:418
  18.0 6.6 %all-to-all-done = bf16[4,48,3712]{2,1,0:T(8,128)(2,1)S(1)} async-done(((bf16[4,48,3712]{2,1,0:T(8,128)(2,1)}), bf16[4,48,3712]{2,1,0:T(8,128)(2,1)S(1)}, u32[]{:S(2)}, u32[]{:S(2)}) %all-to-all-start) | async-done | bytes 1425440 | tf_op jit(solution)/shard_map/all_to_all | solution.py:50
  24.6 2.8 %near.1 = (bf16[120,3584]{1,0:T(8,128)(2,1)}, bf16[120,3584]{1,0:T(8,128)(2,1)}, bf16[512,192]{1,0:T(8,128)(2,1)S(1)}) custom-call(s32[3]{0:T(128)S(1)} %pad_add_fusion.place_ref, bf16[192,3712]{1,0:T(8,128)(2,1)S(1)} %bitcast.36, bf16[192,3712]{1,0:T(8,128)(2,1)S(1)} %bitcast.37), custom_call_target="tpu_custom_call" | custom-call | tf_op jit(solution)/shard_map/near/pallas_call | solution.py:314
  27.4 3.4 %collective-permute-start.4 = (bf16[120,3584]{1,0:T(8,128)(2,1)}, bf16[120,3584]{1,0:T(8,128)(2,1)}, u32[]{:S(2)}, u32[]{:S(2)}) collective-permute-start(bf16[120,3584]{1,0:T(8,128)(2,1)} %get-tuple-element.46), channel_id=1, source_target_pairs={{0,2},{1,9},{2,4},{3,11},{4,6},{5,13},{6,0},{7,15},{8,10},{9,17},{... | collective-permute-start | bytes 2580488 | tf_op jit(solution)/shard_map/ppermute | solution.py:36
  30.8 3.7 %collective-permute-start.5 = (bf16[120,3584]{1,0:T(8,128)(2,1)}, bf16[120,3584]{1,0:T(8,128)(2,1)}, u32[]{:S(2)}, u32[]{:S(2)}) collective-permute-start(bf16[120,3584]{1,0:T(8,128)(2,1)} %get-tuple-element.47), channel_id=1, source_target_pairs={{0,6},{1,25},{2,0},{3,27},{4,2},{5,29},{6,4},{7,31},{8,14},{9,1},{... | collective-permute-start | bytes 2580488 | tf_op jit(solution)/shard_map/ppermute | solution.py:36
  34.5 2.7 %rest.1 = (bf16[120,3584]{1,0:T(8,128)(2,1)S(1)}, bf16[120,3584]{1,0:T(8,128)(2,1)}, bf16[192,512]{1,0:T(8,128)(2,1)S(1)}, bf16[192,512]{1,0:T(8,128)(2,1)S(1)}) custom-call(s32[3]{0:T(128)S(1)} %pad_add_fusion.place_ref, bf16[192,3712]{1,0:T(8,128)(2,1)S(1)} %bitcast.38, bf16[192,3712]{1,0:T(8,128)(2,1)S(1)} %bitcast.39, ...), custom_call_target="tpu_custom_call" | custom-call | tf_op jit(solution)/shard_map/rest/pallas_call | solution.py:329
  37.9 3.7 %collective-permute-start = (bf16[120,3584]{1,0:T(8,128)(2,1)}, bf16[120,3584]{1,0:T(8,128)(2,1)}, u32[]{:S(2)}, u32[]{:S(2)}) collective-permute-start(bf16[120,3584]{1,0:T(8,128)(2,1)} %get-tuple-element.42), channel_id=1, source_target_pairs={{0,4},{1,17},{2,6},{3,19},{4,0},{5,21},{6,2},{7,23},{8,12},{9,25},... | collective-permute-start | bytes 2580488 | tf_op jit(solution)/shard_map/ppermute | solution.py:36
  41.7 3.8 %experts.3 = (bf16[120,3584]{1,0:T(8,128)(2,1)S(1)}, s32[8,128]{1,0:T(8,128)S(1)}) custom-call(bf16[120,3584]{1,0:T(8,128)(2,1)S(1)} %get-tuple-element.48.refs_0_, bf16[3584,128]{1,0:T(8,128)(2,1)S(1)} %bitcast.41, bf16[3584,128]{1,0:T(8,128)(2,1)} %collective-permute-done.1.refs_2_.refs_3_, bf16[3584,128]{1,0:T(8,128)(2,1)S(1)} %bitcast.45, ...), custom_call_target="tpu_custom_call" | custom-call | tf_op jit(solution)/shard_map/experts/pallas_call | solution.py:358
  47.6 4.6 %collective-permute-start.6 = (bf16[24,224]{1,0:T(8,128)(2,1)S(1)}, bf16[24,224]{1,0:T(8,128)(2,1)S(1)}, u32[]{:S(2)}, u32[]{:S(2)}) collective-permute-start(bf16[24,224]{1,0:T(8,128)(2,1)S(1)} %get-tuple-element.75), channel_id=1, source_target_pairs={{32,0},{96,64},{160,128},{224,192},{288,256},{352,320},{416,384},{... | collective-permute-start | bytes 32264 | tf_op jit(solution)/shard_map/ppermute | solution.py:430
  52.3 1.7 %collective-permute-done.6 = bf16[24,224]{1,0:T(8,128)(2,1)S(1)} collective-permute-done((bf16[24,224]{1,0:T(8,128)(2,1)S(1)}, bf16[24,224]{1,0:T(8,128)(2,1)S(1)}, u32[]{:S(2)}, u32[]{:S(2)}) %collective-permute-start.6) | collective-permute-done | bytes 10784 | tf_op jit(solution)/shard_map/ppermute | solution.py:430
  54.0 4.5 %collective-permute-start.7 = (bf16[48,224]{1,0:T(8,128)(2,1)S(1)}, bf16[48,224]{1,0:T(8,128)(2,1)S(1)}, u32[]{:S(2)}, u32[]{:S(2)}) collective-permute-start(bf16[48,224]{1,0:T(8,128)(2,1)S(1)} %maximum_select_fusion.3), channel_id=1, source_target_pairs={{64,0},{192,128},{320,256},{448,384},{32,96},{160,224},{288,352},{... | collective-permute-start | bytes 64520 | tf_op jit(solution)/shard_map/ppermute | solution.py:430
  58.4 1.5 collective-permute-done.7.refs_9_
  59.9 5.9 %experts.4 = (bf16[120,3584]{1,0:T(8,128)(2,1)}, bf16[120,3584]{1,0:T(8,128)(2,1)}, s32[8,128]{1,0:T(8,128)S(1)}) custom-call(bf16[120,3584]{1,0:T(8,128)(2,1)} %collective-permute-done.4.refs_0_, bf16[120,3584]{1,0:T(8,128)(2,1)} %collective-permute-done.5.refs_1_, bf16[3584,128]{1,0:T(8,128)(2,1)S(1)} %bitcast.42, ...), custom_call_target="tpu_custom_call" | custom-call | tf_op jit(solution)/shard_map/experts/pallas_call | solution.py:358
  65.9 3.0 %collective-permute-start.9 = (bf16[120,3584]{1,0:T(8,128)(2,1)}, bf16[120,3584]{1,0:T(8,128)(2,1)}, u32[]{:S(2)}, u32[]{:S(2)}) collective-permute-start(bf16[120,3584]{1,0:T(8,128)(2,1)} %get-tuple-element.53), channel_id=1, source_target_pairs={{0,6},{1,25},{2,0},{3,27},{4,2},{5,29},{6,4},{7,31},{8,14},{9,1},{... | collective-permute-start | bytes 2580488 | tf_op jit(solution)/shard_map/ppermute | solution.py:36
  68.9 2.8 %collective-permute-start.10 = (bf16[120,3584]{1,0:T(8,128)(2,1)}, bf16[120,3584]{1,0:T(8,128)(2,1)}, u32[]{:S(2)}, u32[]{:S(2)}) collective-permute-start(bf16[120,3584]{1,0:T(8,128)(2,1)} %get-tuple-element.54), channel_id=1, source_target_pairs={{0,2},{1,9},{2,4},{3,11},{4,6},{5,13},{6,0},{7,15},{8,10},{9,17},{... | collective-permute-start | bytes 2580488 | tf_op jit(solution)/shard_map/ppermute | solution.py:36
  71.7 4.7 %experts.5 = (bf16[120,3584]{1,0:T(8,128)(2,1)}, s32[8,128]{1,0:T(8,128)S(1)}) custom-call(bf16[120,3584]{1,0:T(8,128)(2,1)} %collective-permute-done.refs_0_, bf16[3584,128]{1,0:T(8,128)(2,1)S(1)} %bitcast.43, bf16[3584,128]{1,0:T(8,128)(2,1)} %collective-permute-done.1.refs_2_.refs_3_, bf16[3584,128]{1,0:T(8,128)(2,1)S(1)} %bitcast.47, ...), custom_call_target="tpu_custom_call" | custom-call | tf_op jit(solution)/shard_map/experts/pallas_call | solution.py:358
  76.4 3.6 %collective-permute-start.8 = (bf16[120,3584]{1,0:T(8,128)(2,1)}, bf16[120,3584]{1,0:T(8,128)(2,1)S(1)}, u32[]{:S(2)}, u32[]{:S(2)}) collective-permute-start(bf16[120,3584]{1,0:T(8,128)(2,1)} %get-tuple-element.51), channel_id=1, source_target_pairs={{0,4},{1,17},{2,6},{3,19},{4,0},{5,21},{6,2},{7,23},{8,12},{9,25},... | collective-permute-start | bytes 2580488 | tf_op jit(solution)/shard_map/ppermute | solution.py:36
  81.9 12.4 %collective-permute-done.10.refs_4_ = bf16[120,3584]{1,0:T(8,128)(2,1)} collective-permute-done((bf16[120,3584]{1,0:T(8,128)(2,1)}, bf16[120,3584]{1,0:T(8,128)(2,1)}, u32[]{:S(2)}, u32[]{:S(2)}) %collective-permute-start.10) | collective-permute-done | bytes 860192 | tf_op jit(solution)/shard_map/ppermute | solution.py:36
  95.5 3.8 %gather.2.refs_3_ = f32[192,3584]{1,0:T(8,128)S(1)} custom-call(bf16[192,512]{1,0:T(8,128)(2,1)S(1)} %get-tuple-element.40.refs_0_, bf16[192,512]{1,0:T(8,128)(2,1)S(1)} %copy-done.8, bf16[120,3584]{1,0:T(8,128)(2,1)S(1)} %copy-done.6, bf16[120,3584]{1,0:T(8,128)(2,1)} %collective-permute-done.9.refs_3_, bf16[120,3584]{1,0:T(8,128)(2,1)} %collective-permute-done.10.refs_4_), custom_call_target="tpu_custom_call" | custom-call | tf_op jit(solution)/shard_map/gather/pallas_call | solution.py:385
  99.3 2.2 %gather.3 = bf16[192,3584]{1,0:T(8,128)(2,1)} custom-call(bf16[192,512]{1,0:T(8,128)(2,1)S(1)} %get-tuple-element.40.refs_0_, bf16[192,512]{1,0:T(8,128)(2,1)S(1)} %copy-done.8, bf16[120,3584]{1,0:T(8,128)(2,1)S(1)} %collective-permute-done.8.refs_2_, f32[192,3584]{1,0:T(8,128)S(1)} %gather.2.refs_3_, bf16[96,224]{1,0:T(8,128)(2,1)S(1)} %collective-permute-done.11.refs_4_), custom_call_target="tpu_custom_call" | custom-call | tf_op jit(solution)/shard_map/gather/pallas_call | solution.py:385
  101.5 3.7 %all-to-all-start.1 = ((bf16[4,48,3584]{2,1,0:T(8,128)(2,1)}), bf16[4,48,3584]{2,1,0:T(8,128)(2,1)S(1)}, u32[]{:S(2)}, u32[]{:S(2)}) async-start(bf16[4,48,3584]{2,1,0:T(8,128)(2,1)} %bitcast.18), calls=%async_computation.1 | async-start | bytes 2752512 | tf_op jit(solution)/shard_map/all_to_all | solution.py:50
  105.9 11.9 %all-to-all-done.1 = bf16[4,48,3584]{2,1,0:T(8,128)(2,1)S(1)} async-done(((bf16[4,48,3584]{2,1,0:T(8,128)(2,1)}), bf16[4,48,3584]{2,1,0:T(8,128)(2,1)S(1)}, u32[]{:S(2)}, u32[]{:S(2)}) %all-to-all-start.1) | async-done | bytes 1376288 | tf_op jit(solution)/shard_map/all_to_all | solution.py:50
  117.8 1.4 finish.1
  121.5 1.9 %collective-permute-start.16 = (bf16[24,3584]{1,0:T(8,128)(2,1)S(1)}, bf16[24,3584]{1,0:T(8,128)(2,1)S(1)}, u32[]{:S(2)}, u32[]{:S(2)}) collective-permute-start(bf16[24,3584]{1,0:T(8,128)(2,1)S(1)} %get-tuple-element.63), channel_id=1, source_target_pairs={{0,32},{32,64},{64,96},{96,128},{128,160},{160,192},{192,224},{224... | collective-permute-start | bytes 516104 | tf_op jit(solution)/shard_map/ppermute | solution.py:414
  123.5 17.0 %collective-permute-start.17 = (bf16[24,3584]{1,0:T(8,128)(2,1)S(1)}, bf16[24,3584]{1,0:T(8,128)(2,1)S(1)}, u32[]{:S(2)}, u32[]{:S(2)}) collective-permute-start(bf16[24,3584]{1,0:T(8,128)(2,1)S(1)} %get-tuple-element.64), channel_id=1, source_target_pairs={{32,0},{64,32},{96,64},{128,96},{160,128},{192,160},{224,192},{256... | collective-permute-start | bytes 516104 | tf_op jit(solution)/shard_map/ppermute | solution.py:414
  140.5 1.6 %collective-permute-done.16 = bf16[24,3584]{1,0:T(8,128)(2,1)S(1)} collective-permute-done((bf16[24,3584]{1,0:T(8,128)(2,1)S(1)}, bf16[24,3584]{1,0:T(8,128)(2,1)S(1)}, u32[]{:S(2)}, u32[]{:S(2)}) %collective-permute-start.16) | collective-permute-done | bytes 172064 | tf_op jit(solution)/shard_map/ppermute | solution.py:414
  142.1 1.4 collective-permute-done.17
  147.6 5.7 %collective-permute-done.19 = bf16[24,224]{1,0:T(8,128)(2,1)S(1)} collective-permute-done((bf16[24,224]{1,0:T(8,128)(2,1)S(1)}, bf16[24,224]{1,0:T(8,128)(2,1)S(1)}, u32[]{:S(2)}, u32[]{:S(2)}) %collective-permute-start.19) | collective-permute-done | bytes 10784 | tf_op jit(solution)/shard_map/ppermute | solution.py:459
  (73 shorter events, 17.4 us)
Async XLA Ops:
  7.1 4.6 %copy-start = (bf16[1,3584,128]{2,1,0:T(8,128)(2,1)S(1)}, bf16[1,3584,128]{2,1,0:T(8,128)(2,1)}, u32[]{:S(2)}) copy-start(bf16[1,3584,128]{2,1,0:T(8,128)(2,1)} %param.15) | copy-start | bytes 2752516
  7.1 6.5 %copy-start.1 = (bf16[1,3584,128]{2,1,0:T(8,128)(2,1)S(1)}, bf16[1,3584,128]{2,1,0:T(8,128)(2,1)}, u32[]{:S(2)}) copy-start(bf16[1,3584,128]{2,1,0:T(8,128)(2,1)} %param.16) | copy-start | bytes 2752516
  7.1 17.5 %all-to-all-start = ((bf16[4,48,3712]{2,1,0:T(8,128)(2,1)}), bf16[4,48,3712]{2,1,0:T(8,128)(2,1)S(1)}, u32[]{:S(2)}, u32[]{:S(2)}) async-start(bf16[4,48,3712]{2,1,0:T(8,128)(2,1)} %bitcast.53), calls=%async_computation | async-start | bytes 2850816 | tf_op jit(solution)/shard_map/all_to_all | solution.py:50
  11.7 26.2 %collective-permute-start.1 = (bf16[3584,128]{1,0:T(8,128)(2,1)S(1)}, bf16[3584,128]{1,0:T(8,128)(2,1)}, u32[]{:S(2)}, u32[]{:S(2)}) collective-permute-start(bf16[3584,128]{1,0:T(8,128)(2,1)S(1)} %bitcast.40), channel_id=1, source_target_pairs={{0,1},{1,0},{2,3},{3,2},{4,5},{5,4},{6,7},{7,6},{8,9},{9,8},{10,11... | collective-permute-start | bytes 2752520 | tf_op jit(solution)/shard_map/ppermute | solution.py:418
  13.7 28.0 %collective-permute-start.2 = (bf16[3584,128]{1,0:T(8,128)(2,1)S(1)}, bf16[3584,128]{1,0:T(8,128)(2,1)}, u32[]{:S(2)}, u32[]{:S(2)}) collective-permute-start(bf16[3584,128]{1,0:T(8,128)(2,1)S(1)} %bitcast.44), channel_id=1, source_target_pairs={{0,1},{1,0},{2,3},{3,2},{4,5},{5,4},{6,7},{7,6},{8,9},{9,8},{10,11... | collective-permute-start | bytes 2752520 | tf_op jit(solution)/shard_map/ppermute | solution.py:418
  16.1 25.6 %collective-permute-start.3 = (bf16[128,3584]{1,0:T(8,128)(2,1)}, bf16[128,3584]{1,0:T(8,128)(2,1)}, u32[]{:S(2)}, u32[]{:S(2)}) collective-permute-start(bf16[128,3584]{1,0:T(8,128)(2,1)} %bitcast.48), channel_id=1, source_target_pairs={{0,1},{1,0},{2,3},{3,2},{4,5},{5,4},{6,7},{7,6},{8,9},{9,8},{10,11... | collective-permute-start | bytes 2752520 | tf_op jit(solution)/shard_map/ppermute | solution.py:418
  27.4 32.5 %collective-permute-start.4 = (bf16[120,3584]{1,0:T(8,128)(2,1)}, bf16[120,3584]{1,0:T(8,128)(2,1)}, u32[]{:S(2)}, u32[]{:S(2)}) collective-permute-start(bf16[120,3584]{1,0:T(8,128)(2,1)} %get-tuple-element.46), channel_id=1, source_target_pairs={{0,2},{1,9},{2,4},{3,11},{4,6},{5,13},{6,0},{7,15},{8,10},{9,17},{... | collective-permute-start | bytes 2580488 | tf_op jit(solution)/shard_map/ppermute | solution.py:36
  30.8 29.1 %collective-permute-start.5 = (bf16[120,3584]{1,0:T(8,128)(2,1)}, bf16[120,3584]{1,0:T(8,128)(2,1)}, u32[]{:S(2)}, u32[]{:S(2)}) collective-permute-start(bf16[120,3584]{1,0:T(8,128)(2,1)} %get-tuple-element.47), channel_id=1, source_target_pairs={{0,6},{1,25},{2,0},{3,27},{4,2},{5,29},{6,4},{7,31},{8,14},{9,1},{... | collective-permute-start | bytes 2580488 | tf_op jit(solution)/shard_map/ppermute | solution.py:36
  34.5 7.2 %copy-start.2 = (bf16[1,128,3584]{2,1,0:T(8,128)(2,1)S(1)}, bf16[1,128,3584]{2,1,0:T(8,128)(2,1)}, u32[]{:S(2)}) copy-start(bf16[1,128,3584]{2,1,0:T(8,128)(2,1)} %param.17) | copy-start | bytes 2752516
  37.9 33.8 %collective-permute-start = (bf16[120,3584]{1,0:T(8,128)(2,1)}, bf16[120,3584]{1,0:T(8,128)(2,1)}, u32[]{:S(2)}, u32[]{:S(2)}) collective-permute-start(bf16[120,3584]{1,0:T(8,128)(2,1)} %get-tuple-element.42), channel_id=1, source_target_pairs={{0,4},{1,17},{2,6},{3,19},{4,0},{5,21},{6,2},{7,23},{8,12},{9,25},... | collective-permute-start | bytes 2580488 | tf_op jit(solution)/shard_map/ppermute | solution.py:36
  41.7 5.9 %copy-start.16 = (bf16[1,24,224]{2,1,0:T(8,128)(2,1)S(1)}, bf16[1,24,224]{2,1,0:T(8,128)(2,1)}, u32[]{:S(2)}) copy-start(bf16[1,24,224]{2,1,0:T(8,128)(2,1)} %param.12) | copy-start | bytes 32260
  41.7 5.9 %copy-start.17 = (bf16[1,24,224]{2,1,0:T(8,128)(2,1)S(1)}, bf16[1,24,224]{2,1,0:T(8,128)(2,1)}, u32[]{:S(2)}) copy-start(bf16[1,24,224]{2,1,0:T(8,128)(2,1)} %param.13) | copy-start | bytes 32260
  41.7 18.2 %copy-start.3 = (bf16[1,128,3584]{2,1,0:T(8,128)(2,1)S(1)}, bf16[1,128,3584]{2,1,0:T(8,128)(2,1)}, u32[]{:S(2)}) copy-start(bf16[1,128,3584]{2,1,0:T(8,128)(2,1)} %param.17) | copy-start | bytes 2752516
  47.6 6.3 %collective-permute-start.6 = (bf16[24,224]{1,0:T(8,128)(2,1)S(1)}, bf16[24,224]{1,0:T(8,128)(2,1)S(1)}, u32[]{:S(2)}, u32[]{:S(2)}) collective-permute-start(bf16[24,224]{1,0:T(8,128)(2,1)S(1)} %get-tuple-element.75), channel_id=1, source_target_pairs={{32,0},{96,64},{160,128},{224,192},{288,256},{352,320},{416,384},{... | collective-permute-start | bytes 32264 | tf_op jit(solution)/shard_map/ppermute | solution.py:430
  54.0 6.0 %collective-permute-start.7 = (bf16[48,224]{1,0:T(8,128)(2,1)S(1)}, bf16[48,224]{1,0:T(8,128)(2,1)S(1)}, u32[]{:S(2)}, u32[]{:S(2)}) collective-permute-start(bf16[48,224]{1,0:T(8,128)(2,1)S(1)} %maximum_select_fusion.3), channel_id=1, source_target_pairs={{64,0},{192,128},{320,256},{448,384},{32,96},{160,224},{288,352},{... | collective-permute-start | bytes 64520 | tf_op jit(solution)/shard_map/ppermute | solution.py:430
  65.9 16.0 %collective-permute-start.9 = (bf16[120,3584]{1,0:T(8,128)(2,1)}, bf16[120,3584]{1,0:T(8,128)(2,1)}, u32[]{:S(2)}, u32[]{:S(2)}) collective-permute-start(bf16[120,3584]{1,0:T(8,128)(2,1)} %get-tuple-element.53), channel_id=1, source_target_pairs={{0,6},{1,25},{2,0},{3,27},{4,2},{5,29},{6,4},{7,31},{8,14},{9,1},{... | collective-permute-start | bytes 2580488 | tf_op jit(solution)/shard_map/ppermute | solution.py:36
  68.9 25.4 %collective-permute-start.10 = (bf16[120,3584]{1,0:T(8,128)(2,1)}, bf16[120,3584]{1,0:T(8,128)(2,1)}, u32[]{:S(2)}, u32[]{:S(2)}) collective-permute-start(bf16[120,3584]{1,0:T(8,128)(2,1)} %get-tuple-element.54), channel_id=1, source_target_pairs={{0,2},{1,9},{2,4},{3,11},{4,6},{5,13},{6,0},{7,15},{8,10},{9,17},{... | collective-permute-start | bytes 2580488 | tf_op jit(solution)/shard_map/ppermute | solution.py:36
  71.7 22.6 %copy-start.8 = (bf16[192,512]{1,0:T(8,128)(2,1)S(1)}, bf16[192,512]{1,0:T(8,128)(2,1)}, u32[]{:S(2)}) copy-start(bf16[192,512]{1,0:T(8,128)(2,1)} %copy-done.7) | copy-start | bytes 589828
  76.4 22.9 %collective-permute-start.8 = (bf16[120,3584]{1,0:T(8,128)(2,1)}, bf16[120,3584]{1,0:T(8,128)(2,1)S(1)}, u32[]{:S(2)}, u32[]{:S(2)}) collective-permute-start(bf16[120,3584]{1,0:T(8,128)(2,1)} %get-tuple-element.51), channel_id=1, source_target_pairs={{0,4},{1,17},{2,6},{3,19},{4,0},{5,21},{6,2},{7,23},{8,12},{9,25},... | collective-permute-start | bytes 2580488 | tf_op jit(solution)/shard_map/ppermute | solution.py:36
  81.2 18.1 %collective-permute-start.11 = (bf16[96,224]{1,0:T(8,128)(2,1)S(1)}, bf16[96,224]{1,0:T(8,128)(2,1)S(1)}, u32[]{:S(2)}, u32[]{:S(2)}) collective-permute-start(bf16[96,224]{1,0:T(8,128)(2,1)S(1)} %maximum_select_fusion.2), channel_id=1, source_target_pairs={{128,0},{384,256},{96,224},{352,480},{129,1},{385,257},{97,225},{3... | collective-permute-start | bytes 129032 | tf_op jit(solution)/shard_map/ppermute | solution.py:430
  101.5 16.3 %copy-start.10 = (bf16[1,24,3584]{2,1,0:T(8,128)(2,1)S(1)}, bf16[1,24,3584]{2,1,0:T(8,128)(2,1)}, u32[]{:S(2)}) copy-start(bf16[1,24,3584]{2,1,0:T(8,128)(2,1)} %param.10) | copy-start | bytes 516100
  101.5 16.3 %copy-start.12 = (bf16[1,24,3584]{2,1,0:T(8,128)(2,1)S(1)}, bf16[1,24,3584]{2,1,0:T(8,128)(2,1)}, u32[]{:S(2)}) copy-start(bf16[1,24,3584]{2,1,0:T(8,128)(2,1)} %param.11) | copy-start | bytes 516100
  101.5 16.3 %all-to-all-start.1 = ((bf16[4,48,3584]{2,1,0:T(8,128)(2,1)}), bf16[4,48,3584]{2,1,0:T(8,128)(2,1)S(1)}, u32[]{:S(2)}, u32[]{:S(2)}) async-start(bf16[4,48,3584]{2,1,0:T(8,128)(2,1)} %bitcast.18), calls=%async_computation.1 | async-start | bytes 2752512 | tf_op jit(solution)/shard_map/all_to_all | solution.py:50
  105.2 16.0 %collective-permute-start.12 = (bf16[192,224]{1,0:T(8,128)(2,1)S(1)}, bf16[192,224]{1,0:T(8,128)(2,1)S(1)}, u32[]{:S(2)}, u32[]{:S(2)}) collective-permute-start(bf16[192,224]{1,0:T(8,128)(2,1)S(1)} %maximum_select_fusion.1), channel_id=1, source_target_pairs={{256,0},{224,480},{257,1},{225,481},{258,2},{226,482},{259,3},{227... | collective-permute-start | bytes 258056 | tf_op jit(solution)/shard_map/ppermute | solution.py:430
  119.2 21.3 %collective-permute-start.13 = (bf16[24,896]{1,0:T(8,128)(2,1)S(1)}, bf16[24,896]{1,0:T(8,128)(2,1)S(1)}, u32[]{:S(2)}, u32[]{:S(2)}) collective-permute-start(bf16[24,896]{1,0:T(8,128)(2,1)S(1)} %get-tuple-element.59), channel_id=1, source_target_pairs={{480,96},{0,384},{481,97},{1,385},{482,98},{2,386},{483,99},{3,387... | collective-permute-start | bytes 129032 | tf_op jit(solution)/shard_map/ppermute | solution.py:444
  119.8 20.7 %collective-permute-start.14 = (bf16[24,896]{1,0:T(8,128)(2,1)S(1)}, bf16[24,896]{1,0:T(8,128)(2,1)S(1)}, u32[]{:S(2)}, u32[]{:S(2)}) collective-permute-start(bf16[24,896]{1,0:T(8,128)(2,1)S(1)} %get-tuple-element.60), channel_id=1, source_target_pairs={{480,224},{0,256},{481,225},{1,257},{482,226},{2,258},{483,227},{3... | collective-permute-start | bytes 129032 | tf_op jit(solution)/shard_map/ppermute | solution.py:444
  120.5 20.0 %collective-permute-start.15 = (bf16[24,896]{1,0:T(8,128)(2,1)S(1)}, bf16[24,896]{1,0:T(8,128)(2,1)S(1)}, u32[]{:S(2)}, u32[]{:S(2)}) collective-permute-start(bf16[24,896]{1,0:T(8,128)(2,1)S(1)} %get-tuple-element.61), channel_id=1, source_target_pairs={{480,352},{0,128},{481,353},{1,129},{482,354},{2,130},{483,355},{3... | collective-permute-start | bytes 129032 | tf_op jit(solution)/shard_map/ppermute | solution.py:444
  121.5 20.6 %collective-permute-start.16 = (bf16[24,3584]{1,0:T(8,128)(2,1)S(1)}, bf16[24,3584]{1,0:T(8,128)(2,1)S(1)}, u32[]{:S(2)}, u32[]{:S(2)}) collective-permute-start(bf16[24,3584]{1,0:T(8,128)(2,1)S(1)} %get-tuple-element.63), channel_id=1, source_target_pairs={{0,32},{32,64},{64,96},{96,128},{128,160},{160,192},{192,224},{224... | collective-permute-start | bytes 516104 | tf_op jit(solution)/shard_map/ppermute | solution.py:414
  123.5 20.1 %collective-permute-start.17 = (bf16[24,3584]{1,0:T(8,128)(2,1)S(1)}, bf16[24,3584]{1,0:T(8,128)(2,1)S(1)}, u32[]{:S(2)}, u32[]{:S(2)}) collective-permute-start(bf16[24,3584]{1,0:T(8,128)(2,1)S(1)} %get-tuple-element.64), channel_id=1, source_target_pairs={{32,0},{64,32},{96,64},{128,96},{160,128},{192,160},{224,192},{256... | collective-permute-start | bytes 516104 | tf_op jit(solution)/shard_map/ppermute | solution.py:414
  143.6 4.0 %collective-permute-start.18 = (bf16[24,224]{1,0:T(8,128)(2,1)S(1)}, bf16[24,224]{1,0:T(8,128)(2,1)S(1)}, u32[]{:S(2)}, u32[]{:S(2)}) collective-permute-start(bf16[24,224]{1,0:T(8,128)(2,1)S(1)} %get-tuple-element.74), channel_id=1, source_target_pairs={{96,0},{224,128},{352,256},{480,384},{0,96},{128,224},{256,352},{3... | collective-permute-start | bytes 32264 | tf_op jit(solution)/shard_map/ppermute | solution.py:459
  144.3 9.0 %collective-permute-start.19 = (bf16[24,224]{1,0:T(8,128)(2,1)S(1)}, bf16[24,224]{1,0:T(8,128)(2,1)S(1)}, u32[]{:S(2)}, u32[]{:S(2)}) collective-permute-start(bf16[24,224]{1,0:T(8,128)(2,1)S(1)} %get-tuple-element.73), channel_id=1, source_target_pairs={{96,32},{224,160},{352,288},{480,416},{0,64},{128,192},{256,320},{... | collective-permute-start | bytes 32264 | tf_op jit(solution)/shard_map/ppermute | solution.py:459
  145.6 7.7 %collective-permute-start.20 = (bf16[24,224]{1,0:T(8,128)(2,1)S(1)}, bf16[24,224]{1,0:T(8,128)(2,1)S(1)}, u32[]{:S(2)}, u32[]{:S(2)}) collective-permute-start(bf16[24,224]{1,0:T(8,128)(2,1)S(1)} %get-tuple-element.72), channel_id=1, source_target_pairs={{96,64},{224,192},{352,320},{480,448},{0,32},{128,160},{256,288},{... | collective-permute-start | bytes 32264 | tf_op jit(solution)/shard_map/ppermute | solution.py:459
  (9 other events, 7.7 us)

commit v4 on v3

--- a/solution.py
+++ b/solution.py
@@ -17,7 +17,6 @@
 EXTRA = 128
 WIDE = 1792
 CHUNK = 512
-RADIX = 4
 LANES = 128
 
 
@@ -168,7 +167,7 @@
 
 
 def rest_kernel(
-    place_ref, rows_ref, extra_ref, pick_ref, own_ref, second_ref, high_ref, low_ref
+    place_ref, rows_ref, extra_ref, pick_ref, own_ref, second_ref, back_ref
 ):
     @pl.when(pl.program_id(0) == 0)
     def _():
@@ -179,15 +178,17 @@
             here = column == target
             high_m = jnp.where(here, high, high_m)
             low_m = jnp.where(here, low, low_m)
-        high_ref[...] = high_m.astype(BF)
-        low_ref[...] = low_m.astype(BF)
+        back_ref[:, : EXPERTS * LANES] = high_m.astype(BF)
+        back_ref[:, EXPERTS * LANES :] = low_m.astype(BF)
 
     move(pick_ref, rows_ref, (0, 2), (own_ref, second_ref))
 
 
 def expert_kernel(steps, count, *refs):
     rows_refs = refs[:count]
-    g0_ref, g1_ref, u0_ref, u1_ref, d0_ref, d1_ref = refs[count : count + 6]
+    g0_ref, u0_ref, d0_ref, g1_ref, u1_ref, d1_ref = refs[count : count + 6]
+    features = d0_ref.shape[1]
+    width = g0_ref.shape[1]
     token_ref, gate_acc, up_acc, hid_ref = refs[-4:]
     out_refs = refs[-4 - count : -4]
     step = pl.program_id(0)
@@ -218,12 +219,13 @@
 
     @pl.when(step >= steps)
     def _():
-        down = jnp.concatenate([d0_ref[...], d1_ref[...]], axis=0)
+        other = [d1_ref[i * width : (i + 1) * width, :] for i in range(features // width)]
+        down = jnp.concatenate([d0_ref[...], jnp.concatenate(other, axis=1)], axis=0)
         for i, out_ref in enumerate(out_refs):
             out_ref[...] = dot(hid_ref[i], down).astype(BF)
 
 
-def gather_kernel(parts, last, high_ref, low_ref, *refs):
+def gather_kernel(parts, last, back_ref, *refs):
     rows_refs, so_far_ref, out_ref = refs[: len(parts)], refs[len(parts)], refs[-1]
     width = rows_refs[0].shape[1]
     used = COLS * SLOTS
@@ -231,13 +233,14 @@
         cut = slice(start, min(start + CHUNK, width))
         total = so_far_ref[:, cut] if last else 0.0
         for part, ref in zip(parts, rows_refs):
-            lanes = slice(part * LANES, part * LANES + used)
+            high = slice(part * LANES, part * LANES + used)
+            low = slice((EXPERTS + part) * LANES, (EXPERTS + part) * LANES + used)
             rows = ref[:, cut]
-            total += dot(high_ref[:, lanes], rows) + dot(low_ref[:, lanes], rows)
+            total += dot(back_ref[:, high], rows) + dot(back_ref[:, low], rows)
         out_ref[:, cut] = total.astype(out_ref.dtype)
 
 
-def finish_kernel(place_ref, meta_ref, rows_ref, fwd_ref, bwd_ref, of_ref, ob_ref, *leave_refs):
+def finish_kernel(place_ref, meta_ref, rows_ref, fwd_ref, bwd_ref, _, of_ref, ob_ref):
     meta = meta_ref[...]
     total = EXPERTS * BOTH
     column = iota((BOTH, total), 1)
@@ -255,24 +258,47 @@
     on_first = place_ref[0] == 0
     high = jnp.where(on_first, high, ones).astype(BF)
     low = jnp.where(on_first, low, 0.0).astype(BF)
-    width = fwd_ref.shape[1] // RADIX
-    for part in range(RADIX):
-        cut = slice(part * width, (part + 1) * width)
+    width = fwd_ref.shape[1]
+    for start in range(0, width, CHUNK):
+        cut = slice(start, min(start + CHUNK, width))
         rows = rows_ref[:, cut]
         mixture = dot(high, rows) + dot(low, rows)
         of_ref[:, cut] = (fwd_ref[:, cut].astype(F32) + mixture[:ROWS]).astype(BF)
         ob_ref[:, cut] = (bwd_ref[:, cut].astype(F32) + mixture[ROWS:]).astype(BF)
-    for part in range(RADIX):
-        up = slice(part * width, (part + 1) * width)
-        down = slice((RADIX - 1 - part) * width, (RADIX - part) * width)
-
-        @pl.when(place_ref[2] == 0)
+
+
+def ends_kernel(place_ref, left_ref, right_ref, fwd_ref, bwd_ref, out_ref):
+    count, _, part = out_ref.shape
+    at_start = place_ref[2] == 0
+    for r in range(count):
+        near, far = [slice(j * part, (j + 1) * part) for j in (r, 2 * count - 1 - r)]
+
+        @pl.when(at_start)
         def _():
-            leave_refs[part][...] = ob_ref[:, up]
-
-        @pl.when(place_ref[2] != 0)
+            out_ref[r, :ROWS, :] = left_ref[:, near]
+            out_ref[r, ROWS:, :] = bwd_ref[:, near]
+
+        @pl.when(jnp.logical_not(at_start))
         def _():
-            leave_refs[part][...] = of_ref[:, down]
+            out_ref[r, :ROWS, :] = fwd_ref[:, far]
+            out_ref[r, ROWS:, :] = right_ref[:, far]
+
+
+def entered_kernel(place_ref, held_ref, got_ref, out_ref):
+    count, _, part = held_ref.shape
+    at_start = place_ref[2] == 0
+    for r in range(count):
+        near, far = [slice(j * part, (j + 1) * part) for j in (r, 2 * count - 1 - r)]
+
+        @pl.when(at_start)
+        def _():
+            out_ref[:, near] = held_ref[r, :ROWS, :]
+            out_ref[:, far] = got_ref[r]
+
+        @pl.when(jnp.logical_not(at_start))
+        def _():
+            out_ref[:, near] = got_ref[r]
+            out_ref[:, far] = held_ref[r, ROWS:, :]
 
 
 SMEM = pl.BlockSpec(memory_space=pltpu.SMEM)
@@ -322,6 +348,28 @@
     )(place, rows, rows)
 
 
+def pack_kernel(gate_ref, up_ref, down_ref, _, out_ref):
+    features, width = gate_ref.shape
+    out_ref[:features, :] = gate_ref[...]
+    out_ref[features : 2 * features, :] = up_ref[...]
+    for i in range(features // width):
+        at = 2 * features + i * width
+        out_ref[at : at + width, :] = down_ref[:, i * width : (i + 1) * width]
+
+
+def make_pack(gate, up, down, before):
+    features, width = gate.shape
+    vmem = pl.BlockSpec(memory_space=pltpu.VMEM)
+    return pl.pallas_call(
+        pack_kernel,
+        out_shape=shape(3 * features, width),
+        in_specs=[vmem] * 3 + [pl.BlockSpec(memory_space=pl.ANY)],
+        out_specs=vmem,
+        compiler_params=params(),
+        name="pack",
+    )(gate, up, down, before)
+
+
 def make_rest(place, rows, pick):
     features = rows.shape[1] - EXTRA
     total = EXPERTS * BOTH
@@ -329,9 +377,10 @@
     return pl.pallas_call(
         rest_kernel,
         grid=(features // WIDE,),
-        out_shape=(shape(COLS * SLOTS, features),) * 2 + (shape(total, lanes),) * 2,
+        out_shape=(shape(COLS * SLOTS, features),) * 2
+        + (shape(total, 2 * lanes),),
         in_specs=[SMEM, tile(total), whole_extra(total, features), whole((lanes, total))],
-        out_specs=(tile(COLS * SLOTS),) * 2 + (whole((total, lanes)),) * 2,
+        out_specs=(tile(COLS * SLOTS),) * 2 + (whole((total, 2 * lanes)),),
         compiler_params=params(),
         name="rest",
     )(place, rows, rows, pick)
@@ -341,14 +390,19 @@
     return pl.BlockSpec((total, EXTRA), lambda i: (0, features // EXTRA))
 
 
-def run_experts(blocks, gates, ups, downs, *before):
+def run_experts(blocks, own, packed, *before):
     count = len(blocks)
     rows, features = blocks[0].shape
-    width = gates[0].shape[1]
+    width = own[0].shape[1]
     steps = features // WIDE
     first = lambda i: jnp.minimum(i, steps - 1)
     later = lambda i: jnp.maximum(i - steps, 0)
     tall = pl.BlockSpec((WIDE, width), lambda i: (first(i), 0))
+    parts = [
+        tall,
+        pl.BlockSpec((WIDE, width), lambda i: (steps + first(i), 0)),
+        pl.BlockSpec((WIDE, width), lambda i: (2 * steps + later(i), 0)),
+    ]
     flat = pl.BlockSpec((width, WIDE), lambda i: (0, later(i)))
     token = (8, LANES)
 
@@ -360,8 +414,8 @@
         grid=(2 * steps,),
         out_shape=(shape(rows, features),) * count + (shape(*token, jnp.int32),),
         in_specs=[pl.BlockSpec((rows, WIDE), lambda i: (0, first(i)))] * count
-        + [tall] * 4
-        + [flat] * 2
+        + [tall, tall, flat]
+        + parts
         + [pl.BlockSpec(memory_space=pl.ANY)] * len(before),
         out_specs=(pl.BlockSpec((rows, WIDE), lambda i: (0, later(i))),) * count + (whole(token),),
         scratch_shapes=[
@@ -371,12 +425,12 @@
         ],
         compiler_params=params(),
         name="experts",
-    )(*blocks, gates[0], gates[1], ups[0], ups[1], downs[0], downs[1], *before)
-
-
-def make_gather(high, low, blocks, parts, so_far=None, before=()):
+    )(*blocks, *own, packed, packed, packed, *before)
+
+
+def make_gather(back, blocks, parts, so_far=None, before=()):
     rows, features = blocks[0].shape
-    total = high.shape[0]
+    total = back.shape[0]
     last = so_far is not None
 
     def body(*refs):
@@ -386,80 +440,72 @@
         body,
         grid=(features // WIDE,),
         out_shape=shape(total, features, BF if last else F32),
-        in_specs=[whole(high.shape), whole(low.shape)]
+        in_specs=[whole(back.shape)]
         + [tile(rows)] * len(blocks)
         + [tile(total)] * last
         + [pl.BlockSpec(memory_space=pl.ANY)] * len(before),
         out_specs=tile(total),
         compiler_params=params(),
         name="gather",
-    )(high, low, *blocks, *([so_far] if last else []), *before)
-
-
-def make_finish(place, meta, rows, fwd, bwd):
+    )(back, *blocks, *([so_far] if last else []), *before)
+
+
+def make_finish(place, meta, rows, fwd, bwd, before):
     features = fwd.shape[1]
     vmem = pl.BlockSpec(memory_space=pltpu.VMEM)
     return pl.pallas_call(
         finish_kernel,
-        out_shape=(shape(ROWS, features),) * 2 + (shape(ROWS, features // RADIX),) * RADIX,
-        in_specs=[SMEM] + [vmem] * 4,
-        out_specs=(vmem,) * (2 + RADIX),
+        out_shape=(shape(ROWS, features),) * 2,
+        in_specs=[SMEM] + [vmem] * 4 + [pl.BlockSpec(memory_space=pl.ANY)],
+        out_specs=(vmem,) * 2,
         compiler_params=params(),
         name="finish",
-    )(place, meta, rows, fwd, bwd)
+    )(place, meta, rows, fwd, bwd, before)
+
+
+def make_simple(kernel, out, place, *arrays):
+    vmem = pl.BlockSpec(memory_space=pltpu.VMEM)
+    return pl.pallas_call(
+        kernel,
+        out_shape=jax.ShapeDtypeStruct(out, BF),
+        in_specs=[SMEM] + [vmem] * len(arrays),
+        out_specs=vmem,
+        compiler_params=params(),
+        name="blocks",
+    )(place, *arrays)
 
 
 def shifted(block, distance, count):
-    route = [(i, i + distance) for i in range(count) if 0 <= i + distance < count]
-    return lax.ppermute(block, "pp", route)
+    return lax.ppermute(block, "pp", [(i, (i + distance) % count) for i in range(count)])
+
+
+def mirrored(pairs, sections):
+    return pairs + [(sections - 1 - i, sections - 1 - j) for i, j in pairs]
 
 
 def from_other_core(block):
     return lax.ppermute(block, "ep", [(i, i ^ 1) for i in range(lax.axis_size("ep"))])
 
 
-def tree_start(fwd, bwd, section):
-    odd = (section & 1) == 1
-    return jnp.where(odd, bwd, fwd), jnp.where(odd, fwd, bwd)
-
-
-def tree_send(block, step, sections):
+def inward(held, step, sections):
     bit = 1 << step
-    route = [(s, s - bit) for s in range(bit, sections, 2 * bit)]
-    route += [(s, s + bit) for s in range(bit - 1, sections, 2 * bit)]
-    return lax.ppermute(block, "pp", route)
-
-
-def tree_join(held, got, step, section):
-    upper = (section & (1 << step)) != 0
-    return jnp.where(
-        upper, jnp.concatenate([got, held], axis=0), jnp.concatenate([held, got], axis=0)
-    )
-
-
-def scatter_far(parts, section, sections):
-    final = sections - 1
-    held = parts[0]
-    for k in range(1, RADIX):
-        got = lax.ppermute(parts[k], "pp", [(final, final - RADIX * k), (0, RADIX * k)])
-        here = (section == final - RADIX * k) | (section == RADIX * k)
-        held = jnp.where(here, got, held)
-    return held
-
-
-def scatter_near(held, section, sections):
-    place = section & (RADIX - 1)
-    width = held.shape[1] // RADIX
-    blocks = [held[:, m * width : (m + 1) * width] for m in range(RADIX)]
-    to_fwd, to_bwd = blocks[RADIX - 1], blocks[0]
-    for m in range(1, RADIX):
-        sent = jnp.where(place == 0, blocks[m], blocks[RADIX - 1 - m])
-        route = [(s, s - m) for s in range(RADIX - 1, sections, RADIX)]
-        route += [(s, s + m) for s in range(0, sections, RADIX)]
-        got = lax.ppermute(sent, "pp", route)
-        to_fwd = jnp.where(place == RADIX - 1 - m, got, to_fwd)
-        to_bwd = jnp.where(place == m, got, to_bwd)
-    return to_fwd, to_bwd
+    pairs = [(i, i - bit) for i in range(bit, sections // 2, 2 * bit)]
+    got = lax.ppermute(held, "pp", mirrored(pairs, sections))
+    return jnp.concatenate([held, got], axis=0), got
+
+
+def outward(own, place, sections):
+    def move(block, *pairs):
+        return lax.ppermute(block, "pp", mirrored(list(pairs), sections))
+
+    a = move(own[2:8], (0, 2))
+    b = move(jnp.where(place == 0, own[1:5], a[2:6]), (0, 1), (2, 4))
+    c = move(jnp.where(place == 2, a[1:3], b[2:4]), (2, 3), (4, 6))
+    d = move(jnp.where(place == 4, b[1:2], c[1:2]), (4, 5), (6, 7))
+    mine = own[0]
+    for at, block in ((1, b), (2, a), (3, c), (4, b), (5, d), (6, c), (7, d)):
+        mine = jnp.where(place == at, block[0], mine)
+    return mine
 
 
 def body(
@@ -484,44 +530,41 @@
     ids = route_ids[0, 0].transpose(0, 2, 1)
     gates = route_gates[0, 0].transpose(0, 2, 1)
 
-    own = (w_gate[0], w_up[0], w_down[0])
     sent, meta = make_send(place, fwd, bwd, norm_gain, ids, gates)
-    after = lax.optimization_barrier
-    passed, meta = after((own, meta))
-    weights = tuple(zip(own, (from_other_core(w) for w in passed)))
-
     rows = exchange(sent)
     send1, send3, pick = make_near(place, rows)
     near, far = hop(send1, 1), hop(send3, 3)
-    send0, send2, high, low = make_rest(place, rows, pick)
+    own = (w_gate[0], w_up[0], w_down[0])
+    weights = own, from_other_core(make_pack(*own, pick))
+    send0, send2, back = make_rest(place, rows, pick)
     last = hop(send2, 2)
-    done0, token = run_experts([send0], *weights)
-    held, sent = tree_start(enter_fwd[0], enter_bwd[0], section + token[0, 0])
-    got = tree_send(sent, 0, sections)
-    held = tree_join(held, got, 0, section)
-    got = tree_send(held, 1, sections)
-    done1, done3, token = run_experts([near, far], *weights, token, got)
+    done0, done1, done3, token = run_experts([send0, near, far], *weights)
     back1, back3 = hop(done1, -1), hop(done3, -3)
     done2, token = run_experts([last], *weights, token)
     back2 = hop(done2, -2)
-    held = tree_join(held, got, 1, section + token[0, 0])
-    got = tree_send(held, 2, sections)
-    held = tree_join(held, got, 2, section)
-    begun = make_gather(high, low, [done0, back1, back3], (0, 1, 3))
-    gathered = make_gather(high, low, [back2], (2,), begun, (got,))
-    got = tree_send(held, 3, sections)
-    held = tree_join(held, got, 3, section)
-    entered = held.reshape(sections, ROWS, part).transpose(1, 0, 2).reshape(ROWS, features)
-    fwd_out, bwd_out, *leaving = make_finish(place, meta, exchange(gathered), fwd, bwd)
-    fwd_out, bwd_out, entered = after((fwd_out, bwd_out, entered))
+
+    half = sections // 2
+    entering = jnp.concatenate([enter_fwd, enter_bwd], axis=1)
+    entering = jnp.where(section + token[0, 0] >= 0, entering, 0)
+    held, _ = inward(entering, 0, sections)
+    held, got = inward(held, 1, sections)
+    begun = make_gather(back, [done0, back1, back3], (0, 1, 3))
+    gathered = make_gather(back, [back2], (2,), begun, (got,))
+    held, got = inward(held, 2, sections)
+    fwd_out, bwd_out = make_finish(place, meta, exchange(gathered), fwd, bwd, got)
+    at_start = section == 0
+    passed_on = jnp.where(at_start, held[:, ROWS:], held[:, :ROWS])
+    got = lax.ppermute(passed_on, "pp", [(0, sections - 1), (sections - 1, 0)])
+    entered = make_simple(entered_kernel, (ROWS, features), place, held, got)
 
     from_left, from_right = shifted(fwd_out, 1, sections), shifted(bwd_out, -1, sections)
-    held = scatter_far(leaving, section, sections)
-    held, from_left, from_right = after((held, from_left, from_right))
-    leave_fwd, leave_bwd = scatter_near(held, section, sections)
-    fwd_next = jnp.where(section == 0, entered, from_left)
+    ends = make_simple(
+        ends_kernel, (half, BOTH, part), place, from_left, from_right, fwd_out, bwd_out
+    )
+    mine = outward(ends, jnp.minimum(section, sections - 1 - section), sections)
+    fwd_next = jnp.where(at_start, entered, from_left)
     bwd_next = jnp.where(section == sections - 1, entered, from_right)
-    return (fwd_next[None], bwd_next[None], leave_fwd[None], leave_bwd[None])
+    return (fwd_next[None], bwd_next[None], mine[None, :ROWS], mine[None, ROWS:])
 
 
 def solution(mesh):

time: 155 us -> 147 us (0.948)
  the two profiles are of different devices: /device:TPU:32 before, /device:TPU:6 now
where the time goes in v4:
time: 147 us
  starting transfers between devices  49.6 us (34%)
  waiting for transfers between devices  49.4 us (34%)
  Pallas kernels  22.6 us (15%)
  blocking collectives  17.2 us (12%)
  local copies, waits for them, and re-layouts  5.08 us (3%)
  between operations  1.71 us (1%)
    ppermute x6, waiting for transfers between devices, hop(): return lax.ppermute(block, 'ep', route)  26.3 us
    ppermute x6, starting transfers between devices, hop(): return lax.ppermute(block, 'ep', route)  19 us
    all_to_all x1, blocking collectives, exchange(): lax.all_to_all(rows, 'ep', split_axis=0, concat_axis=0, axis_index_groups...  17.2 us
    ppermute x3, waiting for transfers between devices, inward(): got = lax.ppermute(held, 'pp', mirrored(pairs, sections))  13.5 us
    ppermute x2, starting transfers between devices, shifted(): lax.ppermute(block, 'pp', [(i, (i + distance) % count) for i in range(cou...  9.79 us
    pallas_call x2, Pallas kernels, run_experts(): pl.pallas_call(body, grid=(2 * steps,), out_shape=(shape(rows, features),...  7.88 us
    ppermute x1, starting transfers between devices, body(): got = lax.ppermute(passed_on, 'pp', [(0, sections - 1), (sections - 1, 0)])  7.45 us
    pallas_call x2, Pallas kernels, make_gather(): pl.pallas_call(body, grid=(features // WIDE,), out_shape=shape(total, fea...  5.73 us
  transfers between devices with their start and end apart: 18, of which 10 were waited for; matrix products, arithmetic and copies ran while one was open for 1% of the time, Pallas kernels for 9%

profile of v4, /device:TPU:6, one launch (start us, length us, event | category | flops | bytes accessed | tf_op | source)
XLA Modules:
  0.0 146.5 jit_solution(1293358596630507520)
XLA Ops:
  4.6 1.4 normed.1
  6.0 17.2 %all_to_all.22 = bf16[4,48,3712]{2,1,0:T(8,128)(2,1)S(1)} all-to-all(bf16[4,48,3712]{2,1,0:T(8,128)(2,1)S(1)} %bitcast.71), channel_id=1, replica_groups={{0,8,16,24},{2,10,18,26},{4,12,20,28},{6,14,22,30},{1,3,5,7},{9,11,13,1..., dimensions={0} | all-to-all | bytes 2850816 | tf_op jit(solution)/shard_map/all_to_all | solution.py:49
  23.2 1.9 %near.1 = (bf16[120,3584]{1,0:T(8,128)(2,1)S(1)}, bf16[120,3584]{1,0:T(8,128)(2,1)S(1)}, bf16[512,192]{1,0:T(8,128)(2,1)S(1)}) custom-call(s32[3]{0:T(128)S(1)} %pad_add_fusion.place_ref, bf16[192,3712]{1,0:T(8,128)(2,1)S(1)} %bitcast.57, bf16[192,3712]{1,0:T(8,128)(2,1)S(1)} %bitcast.58), custom_call_target="tpu_custom_call" | custom-call | tf_op jit(solution)/shard_map/near/pallas_call | solution.py:340
  25.5 1.9 %collective-permute-start.1 = (bf16[10752,128]{1,0:T(8,128)(2,1)S(1)}, bf16[10752,128]{1,0:T(8,128)(2,1)S(1)}, u32[]{:S(2)}, u32[]{:S(2)}) collective-permute-start(bf16[10752,128]{1,0:T(8,128)(2,1)S(1)} %pack.1), channel_id=1, source_target_pairs={{0,1},{1,0},{2,3},{3,2},{4,5},{5,4},{6,7},{7,6},{8,9},{9,8},{10,11... | collective-permute-start | bytes 8257544 | tf_op jit(solution)/shard_map/ppermute | solution.py:487
  27.4 5.9 %collective-permute-start.2 = (bf16[120,3584]{1,0:T(8,128)(2,1)S(1)}, bf16[120,3584]{1,0:T(8,128)(2,1)S(1)}, u32[]{:S(2)}, u32[]{:S(2)}) collective-permute-start(bf16[120,3584]{1,0:T(8,128)(2,1)S(1)} %get-tuple-element.24), channel_id=1, source_target_pairs={{0,2},{1,9},{2,4},{3,11},{4,6},{5,13},{6,0},{7,15},{8,10},{9,17},{... | collective-permute-start | bytes 2580488 | tf_op jit(solution)/shard_map/ppermute | solution.py:35
  33.3 1.9 %collective-permute-start.3 = (bf16[120,3584]{1,0:T(8,128)(2,1)S(1)}, bf16[120,3584]{1,0:T(8,128)(2,1)S(1)}, u32[]{:S(2)}, u32[]{:S(2)}) collective-permute-start(bf16[120,3584]{1,0:T(8,128)(2,1)S(1)} %get-tuple-element.25), channel_id=1, source_target_pairs={{0,6},{1,25},{2,0},{3,27},{4,2},{5,29},{6,4},{7,31},{8,14},{9,1},{... | collective-permute-start | bytes 2580488 | tf_op jit(solution)/shard_map/ppermute | solution.py:35
  35.3 2.0 %rest.1 = (bf16[120,3584]{1,0:T(8,128)(2,1)S(1)}, bf16[120,3584]{1,0:T(8,128)(2,1)S(1)}, bf16[192,1024]{1,0:T(8,128)(2,1)S(1)}) custom-call(s32[3]{0:T(128)S(1)} %pad_add_fusion.place_ref, bf16[192,3712]{1,0:T(8,128)(2,1)S(1)} %bitcast.59, bf16[192,3712]{1,0:T(8,128)(2,1)S(1)} %bitcast.60, bf16[512,192]{1,0:T(8,128)(2,1)S(1)} %get-tuple-element.21.pick_ref._), custom_call_target="tpu_custom_call" | custom-call | tf_op jit(solution)/shard_map/rest/pallas_call | solution.py:377
  37.3 3.4 %collective-permute-start = (bf16[120,3584]{1,0:T(8,128)(2,1)S(1)}, bf16[120,3584]{1,0:T(8,128)(2,1)S(1)}, u32[]{:S(2)}, u32[]{:S(2)}) collective-permute-start(bf16[120,3584]{1,0:T(8,128)(2,1)S(1)} %get-tuple-element.22), channel_id=1, source_target_pairs={{0,4},{1,17},{2,6},{3,19},{4,0},{5,21},{6,2},{7,23},{8,12},{9,25},... | collective-permute-start | bytes 2580488 | tf_op jit(solution)/shard_map/ppermute | solution.py:35
  40.7 2.9 %collective-permute-done.2.refs_1_ = bf16[120,3584]{1,0:T(8,128)(2,1)S(1)} collective-permute-done((bf16[120,3584]{1,0:T(8,128)(2,1)S(1)}, bf16[120,3584]{1,0:T(8,128)(2,1)S(1)}, u32[]{:S(2)}, u32[]{:S(2)}) %collective-permute-start.2) | collective-permute-done | bytes 860192 | tf_op jit(solution)/shard_map/ppermute | solution.py:35
  43.6 14.8 %collective-permute-done.3.refs_2_ = bf16[120,3584]{1,0:T(8,128)(2,1)S(1)} collective-permute-done((bf16[120,3584]{1,0:T(8,128)(2,1)S(1)}, bf16[120,3584]{1,0:T(8,128)(2,1)S(1)}, u32[]{:S(2)}, u32[]{:S(2)}) %collective-permute-start.3) | collective-permute-done | bytes 860192 | tf_op jit(solution)/shard_map/ppermute | solution.py:35
  58.4 5.2 %experts.2 = (bf16[120,3584]{1,0:T(8,128)(2,1)S(1)}, bf16[120,3584]{1,0:T(8,128)(2,1)}, bf16[120,3584]{1,0:T(8,128)(2,1)}, s32[8,128]{1,0:T(8,128)S(1)}) custom-call(bf16[120,3584]{1,0:T(8,128)(2,1)S(1)} %get-tuple-element.23.refs_0_, bf16[120,3584]{1,0:T(8,128)(2,1)S(1)} %collective-permute-done.2.refs_1_, ...), custom_call_target="tpu_custom_call" | custom-call | tf_op jit(solution)/shard_map/experts/pallas_call | solution.py:412
  63.7 1.9 %collective-permute-start.10 = (bf16[120,3584]{1,0:T(8,128)(2,1)}, bf16[120,3584]{1,0:T(8,128)(2,1)S(1)}, u32[]{:S(2)}, u32[]{:S(2)}) collective-permute-start(bf16[120,3584]{1,0:T(8,128)(2,1)} %get-tuple-element.33), channel_id=1, source_target_pairs={{0,2},{1,9},{2,4},{3,11},{4,6},{5,13},{6,0},{7,15},{8,10},{9,17},{... | collective-permute-start | bytes 2580488 | tf_op jit(solution)/shard_map/ppermute | solution.py:35
  65.6 3.9 %collective-permute-start.9 = (bf16[120,3584]{1,0:T(8,128)(2,1)}, bf16[120,3584]{1,0:T(8,128)(2,1)S(1)}, u32[]{:S(2)}, u32[]{:S(2)}) collective-permute-start(bf16[120,3584]{1,0:T(8,128)(2,1)} %get-tuple-element.32), channel_id=1, source_target_pairs={{0,6},{1,25},{2,0},{3,27},{4,2},{5,29},{6,4},{7,31},{8,14},{9,1},{... | collective-permute-start | bytes 2580488 | tf_op jit(solution)/shard_map/ppermute | solution.py:35
  69.6 2.6 %experts.3 = (bf16[120,3584]{1,0:T(8,128)(2,1)}, s32[8,128]{1,0:T(8,128)S(1)}) custom-call(bf16[120,3584]{1,0:T(8,128)(2,1)S(1)} %collective-permute-done.refs_0_, bf16[3584,128]{1,0:T(8,128)(2,1)S(1)} %bitcast.63, bf16[3584,128]{1,0:T(8,128)(2,1)S(1)} %bitcast.66, bf16[128,3584]{1,0:T(8,128)(2,1)S(1)} %bitcast.69, ...), custom_call_target="tpu_custom_call" | custom-call | tf_op jit(solution)/shard_map/experts/pallas_call | solution.py:412
  72.2 1.9 %collective-permute-start.8 = (bf16[120,3584]{1,0:T(8,128)(2,1)}, bf16[120,3584]{1,0:T(8,128)(2,1)}, u32[]{:S(2)}, u32[]{:S(2)}) collective-permute-start(bf16[120,3584]{1,0:T(8,128)(2,1)} %get-tuple-element.30), channel_id=1, source_target_pairs={{0,4},{1,17},{2,6},{3,19},{4,0},{5,21},{6,2},{7,23},{8,12},{9,25},... | collective-permute-start | bytes 2580488 | tf_op jit(solution)/shard_map/ppermute | solution.py:35
  76.6 4.4 %collective-permute-done.4 = bf16[1,48,224]{2,1,0:T(8,128)(2,1)S(1)} collective-permute-done((bf16[1,48,224]{2,1,0:T(8,128)(2,1)S(1)}, bf16[1,48,224]{2,1,0:T(8,128)(2,1)S(1)}, u32[]{:S(2)}, u32[]{:S(2)}) %collective-permute-start.4) | collective-permute-done | bytes 21536 | tf_op jit(solution)/shard_map/ppermute | solution.py:493
  81.1 1.3 collective-permute-start.5
  82.4 8.5 %collective-permute-done.9.refs_2_ = bf16[120,3584]{1,0:T(8,128)(2,1)S(1)} collective-permute-done((bf16[120,3584]{1,0:T(8,128)(2,1)}, bf16[120,3584]{1,0:T(8,128)(2,1)S(1)}, u32[]{:S(2)}, u32[]{:S(2)}) %collective-permute-start.9) | collective-permute-done | bytes 860192 | tf_op jit(solution)/shard_map/ppermute | solution.py:35
  90.9 2.8 %gather.2.refs_2_ = f32[192,3584]{1,0:T(8,128)S(1)} custom-call(bf16[192,1024]{1,0:T(8,128)(2,1)S(1)} %get-tuple-element.29.refs_0_, bf16[120,3584]{1,0:T(8,128)(2,1)S(1)} %get-tuple-element.31.refs_1_, bf16[120,3584]{1,0:T(8,128)(2,1)S(1)} %collective-permute-done.9.refs_2_, bf16[120,3584]{1,0:T(8,128)(2,1)S(1)} %collective-permute-done.10.refs_3_), custom_call_target="tpu_custom_call" | custom-call | tf_op jit(solution)/shard_map/gather/pallas_call | solution.py:439
  93.7 2.9 %gather.3 = bf16[192,3584]{1,0:T(8,128)(2,1)} custom-call(bf16[192,1024]{1,0:T(8,128)(2,1)S(1)} %get-tuple-element.29.refs_0_, bf16[120,3584]{1,0:T(8,128)(2,1)} %collective-permute-done.8.refs_1_, f32[192,3584]{1,0:T(8,128)S(1)} %gather.2.refs_2_, bf16[2,48,224]{2,1,0:T(8,128)(2,1)S(1)} %collective-permute-done.5.refs_3_), custom_call_target="tpu_custom_call" | custom-call | tf_op jit(solution)/shard_map/gather/pallas_call | solution.py:439
  96.7 3.7 %all-to-all-start.1 = ((bf16[4,48,3584]{2,1,0:T(8,128)(2,1)}), bf16[4,48,3584]{2,1,0:T(8,128)(2,1)S(1)}, u32[]{:S(2)}, u32[]{:S(2)}) async-start(bf16[4,48,3584]{2,1,0:T(8,128)(2,1)} %bitcast.15), calls=%async_computation.1 | async-start | bytes 2752512 | tf_op jit(solution)/shard_map/all_to_all | solution.py:49
  101.7 9.1 %collective-permute-done.6._ = bf16[4,48,224]{2,1,0:T(8,128)(2,1)S(1)} collective-permute-done((bf16[4,48,224]{2,1,0:T(8,128)(2,1)S(1)}, bf16[4,48,224]{2,1,0:T(8,128)(2,1)S(1)}, u32[]{:S(2)}, u32[]{:S(2)}) %collective-permute-start.6) | collective-permute-done | bytes 86048 | tf_op jit(solution)/shard_map/ppermute | solution.py:493
  110.8 2.2 %all-to-all-done.1 = bf16[4,48,3584]{2,1,0:T(8,128)(2,1)S(1)} async-done(((bf16[4,48,3584]{2,1,0:T(8,128)(2,1)}), bf16[4,48,3584]{2,1,0:T(8,128)(2,1)S(1)}, u32[]{:S(2)}, u32[]{:S(2)}) %all-to-all-start.1) | async-done | bytes 1376288 | tf_op jit(solution)/shard_map/all_to_all | solution.py:49
  114.2 1.9 %collective-permute-start.11 = (bf16[24,3584]{1,0:T(8,128)(2,1)S(1)}, bf16[24,3584]{1,0:T(8,128)(2,1)S(1)}, u32[]{:S(2)}, u32[]{:S(2)}) collective-permute-start(bf16[24,3584]{1,0:T(8,128)(2,1)S(1)} %get-tuple-element.34.fwd_ref), channel_id=1, source_target_pairs={{0,32},{32,64},{64,96},{96,128},{128,160},{160,192},{192,224},{224... | collective-permute-start | bytes 516104 | tf_op jit(solution)/shard_map/ppermute | solution.py:479
  116.2 7.9 %collective-permute-start.12 = (bf16[24,3584]{1,0:T(8,128)(2,1)S(1)}, bf16[24,3584]{1,0:T(8,128)(2,1)S(1)}, u32[]{:S(2)}, u32[]{:S(2)}) collective-permute-start(bf16[24,3584]{1,0:T(8,128)(2,1)S(1)} %get-tuple-element.35.bwd_ref), channel_id=1, source_target_pairs={{0,480},{32,0},{64,32},{96,64},{128,96},{160,128},{192,160},{224,1... | collective-permute-start | bytes 516104 | tf_op jit(solution)/shard_map/ppermute | solution.py:479
  124.0 1.4 collective-permute-done.11.left_ref
  125.5 1.5 collective-permute-done.12.right_ref
  128.0 1.3 collective-permute-start.13
  129.4 2.6 %collective-permute-done.13 = bf16[6,48,224]{2,1,0:T(8,128)(2,1)S(1)} collective-permute-done((bf16[6,48,224]{2,1,0:T(8,128)(2,1)S(1)}, bf16[6,48,224]{2,1,0:T(8,128)(2,1)S(1)}, u32[]{:S(2)}, u32[]{:S(2)}) %collective-permute-start.13) | collective-permute-done | bytes 129056 | tf_op jit(solution)/shard_map/ppermute | solution.py:499
  132.0 1.3 collective-permute-start.14
  133.3 7.5 %collective-permute-start.7 = (bf16[8,24,224]{2,1,0:T(8,128)(2,1)S(1)}, bf16[8,24,224]{2,1,0:T(8,128)(2,1)S(1)}, u32[]{:S(2)}, u32[]{:S(2)}) collective-permute-start(bf16[8,24,224]{2,1,0:T(8,128)(2,1)S(1)} %slice_select_fusion.1), channel_id=1, source_target_pairs={{0,480},{480,0},{1,481},{481,1},{2,482},{482,2},{3,483},{483,3},{4... | collective-permute-start | bytes 258056 | tf_op jit(solution)/shard_map/ppermute | solution.py:557
  141.5 1.9 %collective-permute-done.7.got_ref = bf16[8,24,224]{2,1,0:T(8,128)(2,1)S(1)} collective-permute-done((bf16[8,24,224]{2,1,0:T(8,128)(2,1)S(1)}, bf16[8,24,224]{2,1,0:T(8,128)(2,1)S(1)}, u32[]{:S(2)}, u32[]{:S(2)}) %collective-permute-start.7) | collective-permute-done | bytes 86048 | tf_op jit(solution)/shard_map/ppermute | solution.py:557
  (54 shorter events, 13.7 us)
Async XLA Ops:
  0.7 0.9 copy-start.3
  1.6 0.9 copy-start.5
  2.6 0.7 copy-start.7
  3.3 0.7 copy-start.8
  4.0 0.7 copy-start.9
  23.2 1.9 %copy-start = (bf16[1,3584,128]{2,1,0:T(8,128)(2,1)S(1)}, bf16[1,3584,128]{2,1,0:T(8,128)(2,1)}, u32[]{:S(2)}) copy-start(bf16[1,3584,128]{2,1,0:T(8,128)(2,1)} %param.15) | copy-start | bytes 2752516
  23.2 2.0 %copy-start.1 = (bf16[1,3584,128]{2,1,0:T(8,128)(2,1)S(1)}, bf16[1,3584,128]{2,1,0:T(8,128)(2,1)}, u32[]{:S(2)}) copy-start(bf16[1,3584,128]{2,1,0:T(8,128)(2,1)} %param.16) | copy-start | bytes 2752516
  23.2 2.0 %copy-start.2 = (bf16[1,128,3584]{2,1,0:T(8,128)(2,1)S(1)}, bf16[1,128,3584]{2,1,0:T(8,128)(2,1)}, u32[]{:S(2)}) copy-start(bf16[1,128,3584]{2,1,0:T(8,128)(2,1)} %param.17) | copy-start | bytes 2752516
  25.5 33.0 %collective-permute-start.1 = (bf16[10752,128]{1,0:T(8,128)(2,1)S(1)}, bf16[10752,128]{1,0:T(8,128)(2,1)S(1)}, u32[]{:S(2)}, u32[]{:S(2)}) collective-permute-start(bf16[10752,128]{1,0:T(8,128)(2,1)S(1)} %pack.1), channel_id=1, source_target_pairs={{0,1},{1,0},{2,3},{3,2},{4,5},{5,4},{6,7},{7,6},{8,9},{9,8},{10,11... | collective-permute-start | bytes 8257544 | tf_op jit(solution)/shard_map/ppermute | solution.py:487
  27.4 16.2 %collective-permute-start.2 = (bf16[120,3584]{1,0:T(8,128)(2,1)S(1)}, bf16[120,3584]{1,0:T(8,128)(2,1)S(1)}, u32[]{:S(2)}, u32[]{:S(2)}) collective-permute-start(bf16[120,3584]{1,0:T(8,128)(2,1)S(1)} %get-tuple-element.24), channel_id=1, source_target_pairs={{0,2},{1,9},{2,4},{3,11},{4,6},{5,13},{6,0},{7,15},{8,10},{9,17},{... | collective-permute-start | bytes 2580488 | tf_op jit(solution)/shard_map/ppermute | solution.py:35
  33.3 25.1 %collective-permute-start.3 = (bf16[120,3584]{1,0:T(8,128)(2,1)S(1)}, bf16[120,3584]{1,0:T(8,128)(2,1)S(1)}, u32[]{:S(2)}, u32[]{:S(2)}) collective-permute-start(bf16[120,3584]{1,0:T(8,128)(2,1)S(1)} %get-tuple-element.25), channel_id=1, source_target_pairs={{0,6},{1,25},{2,0},{3,27},{4,2},{5,29},{6,4},{7,31},{8,14},{9,1},{... | collective-permute-start | bytes 2580488 | tf_op jit(solution)/shard_map/ppermute | solution.py:35
  37.3 32.2 %collective-permute-start = (bf16[120,3584]{1,0:T(8,128)(2,1)S(1)}, bf16[120,3584]{1,0:T(8,128)(2,1)S(1)}, u32[]{:S(2)}, u32[]{:S(2)}) collective-permute-start(bf16[120,3584]{1,0:T(8,128)(2,1)S(1)} %get-tuple-element.22), channel_id=1, source_target_pairs={{0,4},{1,17},{2,6},{3,19},{4,0},{5,21},{6,2},{7,23},{8,12},{9,25},... | collective-permute-start | bytes 2580488 | tf_op jit(solution)/shard_map/ppermute | solution.py:35
  63.7 18.7 %collective-permute-start.10 = (bf16[120,3584]{1,0:T(8,128)(2,1)}, bf16[120,3584]{1,0:T(8,128)(2,1)S(1)}, u32[]{:S(2)}, u32[]{:S(2)}) collective-permute-start(bf16[120,3584]{1,0:T(8,128)(2,1)} %get-tuple-element.33), channel_id=1, source_target_pairs={{0,2},{1,9},{2,4},{3,11},{4,6},{5,13},{6,0},{7,15},{8,10},{9,17},{... | collective-permute-start | bytes 2580488 | tf_op jit(solution)/shard_map/ppermute | solution.py:35
  65.6 25.3 %collective-permute-start.9 = (bf16[120,3584]{1,0:T(8,128)(2,1)}, bf16[120,3584]{1,0:T(8,128)(2,1)S(1)}, u32[]{:S(2)}, u32[]{:S(2)}) collective-permute-start(bf16[120,3584]{1,0:T(8,128)(2,1)} %get-tuple-element.32), channel_id=1, source_target_pairs={{0,6},{1,25},{2,0},{3,27},{4,2},{5,29},{6,4},{7,31},{8,14},{9,1},{... | collective-permute-start | bytes 2580488 | tf_op jit(solution)/shard_map/ppermute | solution.py:35
  69.5 5.7 %copy-start.10 = (bf16[1,24,224]{2,1,0:T(8,128)(2,1)S(1)}, bf16[1,24,224]{2,1,0:T(8,128)(2,1)}, u32[]{:S(2)}) copy-start(bf16[1,24,224]{2,1,0:T(8,128)(2,1)} %param.13) | copy-start | bytes 32260
  69.6 5.7 %copy-start.11 = (bf16[1,24,224]{2,1,0:T(8,128)(2,1)S(1)}, bf16[1,24,224]{2,1,0:T(8,128)(2,1)}, u32[]{:S(2)}) copy-start(bf16[1,24,224]{2,1,0:T(8,128)(2,1)} %param.12) | copy-start | bytes 32260
  72.2 21.5 %collective-permute-start.8 = (bf16[120,3584]{1,0:T(8,128)(2,1)}, bf16[120,3584]{1,0:T(8,128)(2,1)}, u32[]{:S(2)}, u32[]{:S(2)}) collective-permute-start(bf16[120,3584]{1,0:T(8,128)(2,1)} %get-tuple-element.30), channel_id=1, source_target_pairs={{0,4},{1,17},{2,6},{3,19},{4,0},{5,21},{6,2},{7,23},{8,12},{9,25},... | collective-permute-start | bytes 2580488 | tf_op jit(solution)/shard_map/ppermute | solution.py:35
  75.3 5.7 %collective-permute-start.4 = (bf16[1,48,224]{2,1,0:T(8,128)(2,1)S(1)}, bf16[1,48,224]{2,1,0:T(8,128)(2,1)S(1)}, u32[]{:S(2)}, u32[]{:S(2)}) collective-permute-start(bf16[1,48,224]{2,1,0:T(8,128)(2,1)S(1)} %maximum_select_fusion), channel_id=1, source_target_pairs={{32,0},{96,64},{160,128},{224,192},{448,480},{384,416},{320,352},{... | collective-permute-start | bytes 64520 | tf_op jit(solution)/shard_map/ppermute | solution.py:493
  81.1 12.7 %collective-permute-start.5 = (bf16[2,48,224]{2,1,0:T(8,128)(2,1)S(1)}, bf16[2,48,224]{2,1,0:T(8,128)(2,1)S(1)}, u32[]{:S(2)}, u32[]{:S(2)}) collective-permute-start(bf16[2,48,224]{2,1,0:T(8,128)(2,1)S(1)} %pad_maximum_fusion.2), channel_id=1, source_target_pairs={{64,0},{192,128},{416,480},{288,352},{65,1},{193,129},{417,481},{2... | collective-permute-start | bytes 129032 | tf_op jit(solution)/shard_map/ppermute | solution.py:493
  96.7 16.3 %copy-start.4 = (bf16[1,24,3584]{2,1,0:T(8,128)(2,1)S(1)}, bf16[1,24,3584]{2,1,0:T(8,128)(2,1)}, u32[]{:S(2)}) copy-start(bf16[1,24,3584]{2,1,0:T(8,128)(2,1)} %param.10) | copy-start | bytes 516100
  96.7 16.3 %copy-start.6 = (bf16[1,24,3584]{2,1,0:T(8,128)(2,1)S(1)}, bf16[1,24,3584]{2,1,0:T(8,128)(2,1)}, u32[]{:S(2)}) copy-start(bf16[1,24,3584]{2,1,0:T(8,128)(2,1)} %param.11) | copy-start | bytes 516100
  96.7 16.3 %all-to-all-start.1 = ((bf16[4,48,3584]{2,1,0:T(8,128)(2,1)}), bf16[4,48,3584]{2,1,0:T(8,128)(2,1)S(1)}, u32[]{:S(2)}, u32[]{:S(2)}) async-start(bf16[4,48,3584]{2,1,0:T(8,128)(2,1)} %bitcast.15), calls=%async_computation.1 | async-start | bytes 2752512 | tf_op jit(solution)/shard_map/all_to_all | solution.py:49
  100.4 10.4 %collective-permute-start.6 = (bf16[4,48,224]{2,1,0:T(8,128)(2,1)S(1)}, bf16[4,48,224]{2,1,0:T(8,128)(2,1)S(1)}, u32[]{:S(2)}, u32[]{:S(2)}) collective-permute-start(bf16[4,48,224]{2,1,0:T(8,128)(2,1)S(1)} %pad_maximum_fusion.1), channel_id=1, source_target_pairs={{128,0},{352,480},{129,1},{353,481},{130,2},{354,482},{131,3},{355... | collective-permute-start | bytes 258056 | tf_op jit(solution)/shard_map/ppermute | solution.py:493
  114.2 11.3 %collective-permute-start.11 = (bf16[24,3584]{1,0:T(8,128)(2,1)S(1)}, bf16[24,3584]{1,0:T(8,128)(2,1)S(1)}, u32[]{:S(2)}, u32[]{:S(2)}) collective-permute-start(bf16[24,3584]{1,0:T(8,128)(2,1)S(1)} %get-tuple-element.34.fwd_ref), channel_id=1, source_target_pairs={{0,32},{32,64},{64,96},{96,128},{128,160},{160,192},{192,224},{224... | collective-permute-start | bytes 516104 | tf_op jit(solution)/shard_map/ppermute | solution.py:479
  116.2 10.8 %collective-permute-start.12 = (bf16[24,3584]{1,0:T(8,128)(2,1)S(1)}, bf16[24,3584]{1,0:T(8,128)(2,1)S(1)}, u32[]{:S(2)}, u32[]{:S(2)}) collective-permute-start(bf16[24,3584]{1,0:T(8,128)(2,1)S(1)} %get-tuple-element.35.bwd_ref), channel_id=1, source_target_pairs={{0,480},{32,0},{64,32},{96,64},{128,96},{160,128},{192,160},{224,1... | collective-permute-start | bytes 516104 | tf_op jit(solution)/shard_map/ppermute | solution.py:479
  128.0 4.0 %collective-permute-start.13 = (bf16[6,48,224]{2,1,0:T(8,128)(2,1)S(1)}, bf16[6,48,224]{2,1,0:T(8,128)(2,1)S(1)}, u32[]{:S(2)}, u32[]{:S(2)}) collective-permute-start(bf16[6,48,224]{2,1,0:T(8,128)(2,1)S(1)} %slice.69), channel_id=1, source_target_pairs={{0,64},{480,416},{1,65},{481,417},{2,66},{482,418},{3,67},{483,419... | collective-permute-start | bytes 387080 | tf_op jit(solution)/shard_map/ppermute | solution.py:499
  132.0 8.8 %collective-permute-start.14 = (bf16[4,48,224]{2,1,0:T(8,128)(2,1)S(1)}, bf16[4,48,224]{2,1,0:T(8,128)(2,1)S(1)}, u32[]{:S(2)}, u32[]{:S(2)}) collective-permute-start(bf16[4,48,224]{2,1,0:T(8,128)(2,1)S(1)} %slice_select_fusion), channel_id=1, source_target_pairs={{0,32},{64,128},{480,448},{416,352},{1,33},{65,129},{481,449},{417... | collective-permute-start | bytes 258056 | tf_op jit(solution)/shard_map/ppermute | solution.py:499
  133.3 10.0 %collective-permute-start.7 = (bf16[8,24,224]{2,1,0:T(8,128)(2,1)S(1)}, bf16[8,24,224]{2,1,0:T(8,128)(2,1)S(1)}, u32[]{:S(2)}, u32[]{:S(2)}) collective-permute-start(bf16[8,24,224]{2,1,0:T(8,128)(2,1)S(1)} %slice_select_fusion.1), channel_id=1, source_target_pairs={{0,480},{480,0},{1,481},{481,1},{2,482},{482,2},{3,483},{483,3},{4... | collective-permute-start | bytes 258056 | tf_op jit(solution)/shard_map/ppermute | solution.py:557
  140.8 3.7 %collective-permute-start.15 = (bf16[2,48,224]{2,1,0:T(8,128)(2,1)S(1)}, bf16[2,48,224]{2,1,0:T(8,128)(2,1)S(1)}, u32[]{:S(2)}, u32[]{:S(2)}) collective-permute-start(bf16[2,48,224]{2,1,0:T(8,128)(2,1)S(1)} %slice_select_fusion.2), channel_id=1, source_target_pairs={{64,96},{128,192},{416,384},{352,288},{65,97},{129,193},{417,385},... | collective-permute-start | bytes 129032 | tf_op jit(solution)/shard_map/ppermute | solution.py:499
  144.5 1.4 collective-permute-start.16

commit v5 on v4

--- a/solution.py
+++ b/solution.py
@@ -119,8 +119,10 @@
     out_ref[:, features:] = dot(pick, meta.astype(BF)).astype(BF)
 
 
-def slot_targets(place_ref, extra):
+def slot_targets(place_ref, rows_ref):
     total = EXPERTS * BOTH
+    features = rows_ref.shape[1] - EXTRA
+    extra = rows_ref[:, features:].astype(F32)
     row = iota((total, 1), 0)
     part = (
         (row >= BOTH).astype(jnp.int32)
@@ -145,84 +147,65 @@
 
 
 def move(pick_ref, rows_ref, parts, out_refs):
-    width = rows_ref.shape[1]
+    width = rows_ref.shape[1] - EXTRA
     for start in range(0, width, CHUNK):
-        cut = slice(start, min(start + CHUNK, width))
+        cut = slice(start, start + CHUNK)
         rows = rows_ref[:, cut]
         for part, out_ref in zip(parts, out_refs):
             moved = dot(pick_ref[part * LANES : (part + 1) * LANES, :], rows)
             out_ref[:, cut] = moved[: COLS * SLOTS].astype(BF)
 
 
-def near_kernel(place_ref, rows_ref, extra_ref, first_ref, third_ref, pick_ref):
-    @pl.when(pl.program_id(0) == 0)
-    def _():
-        column = iota((EXPERTS * BOTH, EXPERTS * LANES), 1)
-        pick = jnp.zeros(column.shape, F32)
-        for target, _, _ in slot_targets(place_ref, extra_ref[...].astype(F32)):
-            pick = jnp.where(column == target, 1.0, pick)
-        pick_ref[...] = pick.T.astype(BF)
-
+def near_kernel(place_ref, rows_ref, first_ref, third_ref, pick_ref, token_ref):
+    token_ref[...] = jnp.zeros_like(token_ref)
+    column = iota((EXPERTS * BOTH, EXPERTS * LANES), 1)
+    pick = jnp.zeros(column.shape, F32)
+    for target, _, _ in slot_targets(place_ref, rows_ref):
+        pick = jnp.where(column == target, 1.0, pick)
+    pick_ref[...] = pick.T.astype(BF)
     move(pick_ref, rows_ref, (1, 3), (first_ref, third_ref))
 
 
-def rest_kernel(
-    place_ref, rows_ref, extra_ref, pick_ref, own_ref, second_ref, back_ref
-):
-    @pl.when(pl.program_id(0) == 0)
-    def _():
-        column = iota((EXPERTS * BOTH, EXPERTS * LANES), 1)
-        high_m = jnp.zeros(column.shape, F32)
-        low_m = jnp.zeros(column.shape, F32)
-        for target, high, low in slot_targets(place_ref, extra_ref[...].astype(F32)):
-            here = column == target
-            high_m = jnp.where(here, high, high_m)
-            low_m = jnp.where(here, low, low_m)
-        back_ref[:, : EXPERTS * LANES] = high_m.astype(BF)
-        back_ref[:, EXPERTS * LANES :] = low_m.astype(BF)
-
-    move(pick_ref, rows_ref, (0, 2), (own_ref, second_ref))
-
-
-def expert_kernel(steps, count, *refs):
+def rest_kernel(place_ref, rows_ref, pick_ref, own_ref, back_ref):
+    column = iota((EXPERTS * BOTH, EXPERTS * LANES), 1)
+    high_m = jnp.zeros(column.shape, F32)
+    low_m = jnp.zeros(column.shape, F32)
+    for target, high, low in slot_targets(place_ref, rows_ref):
+        here = column == target
+        high_m = jnp.where(here, high, high_m)
+        low_m = jnp.where(here, low, low_m)
+    back_ref[:, : EXPERTS * LANES] = high_m.astype(BF)
+    back_ref[:, EXPERTS * LANES :] = low_m.astype(BF)
+    move(pick_ref, rows_ref, (0,), (own_ref,))
+
+
+def far_kernel(rows_ref, pick_ref, *refs):
+    move(pick_ref, rows_ref, (2,), refs[-1:])
+
+
+def expert_kernel(count, *refs):
     rows_refs = refs[:count]
-    g0_ref, u0_ref, d0_ref, g1_ref, u1_ref, d1_ref = refs[count : count + 6]
-    features = d0_ref.shape[1]
-    width = g0_ref.shape[1]
-    token_ref, gate_acc, up_acc, hid_ref = refs[-4:]
-    out_refs = refs[-4 - count : -4]
-    step = pl.program_id(0)
+    gate_ref, up_ref, down_ref, other_ref = refs[count : count + 4]
+    out_refs, token_ref = refs[-1 - count : -1], refs[-1]
     token_ref[...] = jnp.zeros_like(token_ref)
-
-    @pl.when(step < steps)
-    def _():
-        gate_w = jnp.concatenate([g0_ref[...], g1_ref[...]], axis=1)
-        up_w = jnp.concatenate([u0_ref[...], u1_ref[...]], axis=1)
-        for i, rows_ref in enumerate(rows_refs):
-            gate = dot(rows_ref[...], gate_w)
-            up = dot(rows_ref[...], up_w)
-
-            @pl.when(step == 0)
-            def _():
-                gate_acc[i] = gate
-                up_acc[i] = up
-
-            @pl.when(step > 0)
-            def _():
-                gate_acc[i] += gate
-                up_acc[i] += up
-
-    @pl.when(step == steps - 1)
-    def _():
-        gate = gate_acc[...]
-        hid_ref[...] = (gate / (1.0 + jnp.exp(-gate)) * up_acc[...]).astype(BF)
-
-    @pl.when(step >= steps)
-    def _():
-        other = [d1_ref[i * width : (i + 1) * width, :] for i in range(features // width)]
-        down = jnp.concatenate([d0_ref[...], jnp.concatenate(other, axis=1)], axis=0)
-        for i, out_ref in enumerate(out_refs):
-            out_ref[...] = dot(hid_ref[i], down).astype(BF)
+    features, width = gate_ref.shape
+    hidden = []
+    for rows_ref in rows_refs:
+        gate, up = 0.0, 0.0
+        for start in range(0, features, WIDE):
+            cut = slice(start, start + WIDE)
+            more = slice(features + start, features + start + WIDE)
+            rows = rows_ref[:, cut]
+            gate += dot(rows, jnp.concatenate([gate_ref[cut, :], other_ref[cut, :]], axis=1))
+            up += dot(rows, jnp.concatenate([up_ref[cut, :], other_ref[more, :]], axis=1))
+        hidden.append((gate / (1.0 + jnp.exp(-gate)) * up).astype(BF))
+    for start in range(0, features, CHUNK):
+        cut = slice(start, start + CHUNK)
+        at = [2 * features + start + i * width for i in range(CHUNK // width)]
+        other = jnp.concatenate([other_ref[i : i + width, :] for i in at], axis=1)
+        down = jnp.concatenate([down_ref[:, cut], other], axis=0)
+        for rows, out_ref in zip(hidden, out_refs):
+            out_ref[:, cut] = dot(rows, down).astype(BF)
 
 
 def gather_kernel(parts, last, back_ref, *refs):
@@ -308,12 +291,8 @@
     return pltpu.CompilerParams(vmem_limit_bytes=mib * 1024 * 1024)
 
 
-def whole(shape):
-    return pl.BlockSpec(shape, lambda i: (0,) * len(shape))
-
-
-def tile(rows, width=WIDE):
-    return pl.BlockSpec((rows, width), lambda i: (0, i))
+VMEM = pl.BlockSpec(memory_space=pltpu.VMEM)
+ANY = pl.BlockSpec(memory_space=pl.ANY)
 
 
 def shape(rows, columns, dtype=BF):
@@ -322,12 +301,11 @@
 
 def make_send(place, fwd, bwd, gain, ids, gates):
     features = fwd.shape[1]
-    vmem = pl.BlockSpec(memory_space=pltpu.VMEM)
     return pl.pallas_call(
         send_kernel,
         out_shape=(shape(EXPERTS * BOTH, features + EXTRA), shape(BOTH, EXTRA, F32)),
-        in_specs=[SMEM] + [vmem] * 5,
-        out_specs=(vmem, vmem),
+        in_specs=[SMEM] + [VMEM] * 5,
+        out_specs=(VMEM, VMEM),
         compiler_params=params(),
         name="normed",
     )(place, fwd, bwd, gain, ids, gates)
@@ -336,16 +314,15 @@
 def make_near(place, rows):
     features = rows.shape[1] - EXTRA
     total = EXPERTS * BOTH
-    lanes = EXPERTS * LANES
     return pl.pallas_call(
         near_kernel,
-        grid=(features // WIDE,),
-        out_shape=(shape(COLS * SLOTS, features),) * 2 + (shape(lanes, total),),
-        in_specs=[SMEM, tile(total), whole_extra(total, features)],
-        out_specs=(tile(COLS * SLOTS),) * 2 + (whole((lanes, total)),),
+        out_shape=(shape(COLS * SLOTS, features),) * 2
+        + (shape(EXPERTS * LANES, total), shape(8, LANES, jnp.int32)),
+        in_specs=[SMEM, VMEM],
+        out_specs=(VMEM,) * 4,
         compiler_params=params(),
         name="near",
-    )(place, rows, rows)
+    )(place, rows)
 
 
 def pack_kernel(gate_ref, up_ref, down_ref, _, out_ref):
@@ -359,12 +336,11 @@
 
 def make_pack(gate, up, down, before):
     features, width = gate.shape
-    vmem = pl.BlockSpec(memory_space=pltpu.VMEM)
     return pl.pallas_call(
         pack_kernel,
         out_shape=shape(3 * features, width),
-        in_specs=[vmem] * 3 + [pl.BlockSpec(memory_space=pl.ANY)],
-        out_specs=vmem,
+        in_specs=[VMEM] * 3 + [ANY],
+        out_specs=VMEM,
         compiler_params=params(),
         name="pack",
     )(gate, up, down, before)
@@ -372,64 +348,48 @@
 
 def make_rest(place, rows, pick):
     features = rows.shape[1] - EXTRA
-    total = EXPERTS * BOTH
-    lanes = EXPERTS * LANES
     return pl.pallas_call(
         rest_kernel,
-        grid=(features // WIDE,),
-        out_shape=(shape(COLS * SLOTS, features),) * 2
-        + (shape(total, 2 * lanes),),
-        in_specs=[SMEM, tile(total), whole_extra(total, features), whole((lanes, total))],
-        out_specs=(tile(COLS * SLOTS),) * 2 + (whole((total, 2 * lanes)),),
+        out_shape=(
+            shape(COLS * SLOTS, features),
+            shape(EXPERTS * BOTH, 2 * EXPERTS * LANES),
+        ),
+        in_specs=[SMEM, VMEM, VMEM],
+        out_specs=(VMEM, VMEM),
         compiler_params=params(),
         name="rest",
-    )(place, rows, rows, pick)
-
-
-def whole_extra(total, features):
-    return pl.BlockSpec((total, EXTRA), lambda i: (0, features // EXTRA))
+    )(place, rows, pick)
+
+
+def make_far(rows, pick, *before):
+    return pl.pallas_call(
+        far_kernel,
+        out_shape=shape(COLS * SLOTS, rows.shape[1] - EXTRA),
+        in_specs=[VMEM, VMEM] + [ANY] * len(before),
+        out_specs=VMEM,
+        compiler_params=params(),
+        name="far",
+    )(rows, pick, *before)
 
 
 def run_experts(blocks, own, packed, *before):
     count = len(blocks)
-    rows, features = blocks[0].shape
-    width = own[0].shape[1]
-    steps = features // WIDE
-    first = lambda i: jnp.minimum(i, steps - 1)
-    later = lambda i: jnp.maximum(i - steps, 0)
-    tall = pl.BlockSpec((WIDE, width), lambda i: (first(i), 0))
-    parts = [
-        tall,
-        pl.BlockSpec((WIDE, width), lambda i: (steps + first(i), 0)),
-        pl.BlockSpec((WIDE, width), lambda i: (2 * steps + later(i), 0)),
-    ]
-    flat = pl.BlockSpec((width, WIDE), lambda i: (0, later(i)))
-    token = (8, LANES)
 
     def body(*refs):
-        expert_kernel(steps, count, *refs)
+        expert_kernel(count, *refs)
 
     return pl.pallas_call(
         body,
-        grid=(2 * steps,),
-        out_shape=(shape(rows, features),) * count + (shape(*token, jnp.int32),),
-        in_specs=[pl.BlockSpec((rows, WIDE), lambda i: (0, first(i)))] * count
-        + [tall, tall, flat]
-        + parts
-        + [pl.BlockSpec(memory_space=pl.ANY)] * len(before),
-        out_specs=(pl.BlockSpec((rows, WIDE), lambda i: (0, later(i))),) * count + (whole(token),),
-        scratch_shapes=[
-            pltpu.VMEM((count, rows, 2 * width), F32),
-            pltpu.VMEM((count, rows, 2 * width), F32),
-            pltpu.VMEM((count, rows, 2 * width), BF),
-        ],
+        out_shape=(shape(*blocks[0].shape),) * count + (shape(8, LANES, jnp.int32),),
+        in_specs=[VMEM] * (count + 4) + [ANY] * len(before),
+        out_specs=(VMEM,) * (count + 1),
         compiler_params=params(),
         name="experts",
-    )(*blocks, *own, packed, packed, packed, *before)
+    )(*blocks, *own, packed, *before)
 
 
 def make_gather(back, blocks, parts, so_far=None, before=()):
-    rows, features = blocks[0].shape
+    features = blocks[0].shape[1]
     total = back.shape[0]
     last = so_far is not None
 
@@ -438,13 +398,9 @@
 
     return pl.pallas_call(
         body,
-        grid=(features // WIDE,),
         out_shape=shape(total, features, BF if last else F32),
-        in_specs=[whole(back.shape)]
-        + [tile(rows)] * len(blocks)
-        + [tile(total)] * last
-        + [pl.BlockSpec(memory_space=pl.ANY)] * len(before),
-        out_specs=tile(total),
+        in_specs=[VMEM] * (1 + len(blocks) + last) + [ANY] * len(before),
+        out_specs=VMEM,
         compiler_params=params(),
         name="gather",
     )(back, *blocks, *([so_far] if last else []), *before)
@@ -452,24 +408,22 @@
 
 def make_finish(place, meta, rows, fwd, bwd, before):
     features = fwd.shape[1]
-    vmem = pl.BlockSpec(memory_space=pltpu.VMEM)
     return pl.pallas_call(
         finish_kernel,
         out_shape=(shape(ROWS, features),) * 2,
-        in_specs=[SMEM] + [vmem] * 4 + [pl.BlockSpec(memory_space=pl.ANY)],
-        out_specs=(vmem,) * 2,
+        in_specs=[SMEM] + [VMEM] * 4 + [ANY],
+        out_specs=(VMEM,) * 2,
         compiler_params=params(),
         name="finish",
     )(place, meta, rows, fwd, bwd, before)
 
 
 def make_simple(kernel, out, place, *arrays):
-    vmem = pl.BlockSpec(memory_space=pltpu.VMEM)
     return pl.pallas_call(
         kernel,
         out_shape=jax.ShapeDtypeStruct(out, BF),
-        in_specs=[SMEM] + [vmem] * len(arrays),
-        out_specs=vmem,
+        in_specs=[SMEM] + [VMEM] * len(arrays),
+        out_specs=VMEM,
         compiler_params=params(),
         name="blocks",
     )(place, *arrays)
@@ -532,31 +486,29 @@
 
     sent, meta = make_send(place, fwd, bwd, norm_gain, ids, gates)
     rows = exchange(sent)
-    send1, send3, pick = make_near(place, rows)
+    send1, send3, pick, token = make_near(place, rows)
     near, far = hop(send1, 1), hop(send3, 3)
     own = (w_gate[0], w_up[0], w_down[0])
     weights = own, from_other_core(make_pack(*own, pick))
-    send0, send2, back = make_rest(place, rows, pick)
-    last = hop(send2, 2)
+    send0, back = make_rest(place, rows, pick)
+    last = hop(make_far(rows, pick, near, far, back), 2)
+
+    half = sections // 2
+    at_start = section == 0
+    entering = jnp.concatenate([enter_fwd, enter_bwd], axis=1)
+    held, got = inward(entering, 0, sections)
     done0, done1, done3, token = run_experts([send0, near, far], *weights)
     back1, back3 = hop(done1, -1), hop(done3, -3)
     done2, token = run_experts([last], *weights, token)
     back2 = hop(done2, -2)
-
-    half = sections // 2
-    entering = jnp.concatenate([enter_fwd, enter_bwd], axis=1)
-    entering = jnp.where(section + token[0, 0] >= 0, entering, 0)
-    held, _ = inward(entering, 0, sections)
-    held, got = inward(held, 1, sections)
+    held, got0 = inward(held, 1, sections)
+    held, got = inward(held, 2, sections)
     begun = make_gather(back, [done0, back1, back3], (0, 1, 3))
     gathered = make_gather(back, [back2], (2,), begun, (got,))
-    held, got = inward(held, 2, sections)
-    fwd_out, bwd_out = make_finish(place, meta, exchange(gathered), fwd, bwd, got)
-    at_start = section == 0
     passed_on = jnp.where(at_start, held[:, ROWS:], held[:, :ROWS])
     got = lax.ppermute(passed_on, "pp", [(0, sections - 1), (sections - 1, 0)])
     entered = make_simple(entered_kernel, (ROWS, features), place, held, got)
-
+    fwd_out, bwd_out = make_finish(place, meta, exchange(gathered), fwd, bwd, entered)
     from_left, from_right = shifted(fwd_out, 1, sections), shifted(bwd_out, -1, sections)
     ends = make_simple(
         ends_kernel, (half, BOTH, part), place, from_left, from_right, fwd_out, bwd_out

time: 147 us -> 147 us (level)
  the two profiles are of different devices: /device:TPU:6 before, /device:TPU:160 now
where the time goes in v5:
time: 147 us; the launch traced here: 146 us
  waiting for transfers between devices  64.5 us (44%)
  starting transfers between devices  41.3 us (28%)
  blocking collectives  17.3 us (12%)
  Pallas kernels  16.4 us (11%)
  local copies, waits for them, and re-layouts  4.57 us (3%)
    ppermute x4, waiting for transfers between devices, move(): return lax.ppermute(block, 'pp', mirrored(list(pairs), sections))  25.7 us
    ppermute x6, starting transfers between devices, hop(): return lax.ppermute(block, 'ep', route)  22.3 us
    ppermute x6, waiting for transfers between devices, hop(): return lax.ppermute(block, 'ep', route)  21.2 us
    all_to_all x1, blocking collectives, exchange(): lax.all_to_all(rows, 'ep', split_axis=0, concat_axis=0, axis_index_groups...  17.3 us
    all_to_all x1, waiting for transfers between devices, exchange(): lax.all_to_all(rows, 'ep', split_axis=0, concat_axis=0, axis_index_groups...  10.7 us
    ppermute x2, starting transfers between devices, shifted(): lax.ppermute(block, 'pp', [(i, (i + distance) % count) for i in range(cou...  6.09 us
    ppermute x2, waiting for transfers between devices, shifted(): lax.ppermute(block, 'pp', [(i, (i + distance) % count) for i in range(cou...  5.37 us
    pallas_call x2, Pallas kernels, make_gather(): pl.pallas_call(body, out_shape=shape(total, features, BF if last else F32...  4.31 us
  transfers between devices with their start and end apart: 18, of which 9 were waited for; matrix products, arithmetic and copies ran while one was open for 1% of the time, Pallas kernels for 6%

profile of v5, /device:TPU:160, one launch (start us, length us, event | category | flops | bytes accessed | tf_op | source)
XLA Modules:
  0.0 146.2 jit_solution(7526560706934049809)
XLA Ops:
  4.6 1.4 normed.1
  6.1 17.3 %all_to_all.22 = bf16[4,48,3712]{2,1,0:T(8,128)(2,1)S(1)} all-to-all(bf16[4,48,3712]{2,1,0:T(8,128)(2,1)S(1)} %bitcast.69), channel_id=1, replica_groups={{0,8,16,24},{2,10,18,26},{4,12,20,28},{6,14,22,30},{1,3,5,7},{9,11,13,1..., dimensions={0} | all-to-all | bytes 2850816 | tf_op jit(solution)/shard_map/all_to_all | solution.py:49
  23.4 1.5 %near.1 = (bf16[120,3584]{1,0:T(8,128)(2,1)S(1)}, bf16[120,3584]{1,0:T(8,128)(2,1)S(1)}, bf16[512,192]{1,0:T(8,128)(2,1)S(1)}, s32[8,128]{1,0:T(8,128)}) custom-call(s32[3]{0:T(128)S(1)} %pad_add_fusion.place_ref, bf16[192,3712]{1,0:T(8,128)(2,1)S(1)} %bitcast.56), custom_call_target="tpu_custom_call" | custom-call | tf_op jit(solution)/shard_map/near/pallas_call | solution.py:317
  25.2 1.9 %collective-permute-start.7 = (bf16[10752,128]{1,0:T(8,128)(2,1)S(1)}, bf16[10752,128]{1,0:T(8,128)(2,1)S(1)}, u32[]{:S(2)}, u32[]{:S(2)}) collective-permute-start(bf16[10752,128]{1,0:T(8,128)(2,1)S(1)} %pack.1), channel_id=1, source_target_pairs={{0,1},{1,0},{2,3},{3,2},{4,5},{5,4},{6,7},{7,6},{8,9},{9,8},{10,11... | collective-permute-start | bytes 8257544 | tf_op jit(solution)/shard_map/ppermute | solution.py:441
  27.1 3.4 %collective-permute-start.4 = (bf16[120,3584]{1,0:T(8,128)(2,1)S(1)}, bf16[120,3584]{1,0:T(8,128)(2,1)S(1)}, u32[]{:S(2)}, u32[]{:S(2)}) collective-permute-start(bf16[120,3584]{1,0:T(8,128)(2,1)S(1)} %get-tuple-element.22), channel_id=1, source_target_pairs={{0,2},{1,9},{2,4},{3,11},{4,6},{5,13},{6,0},{7,15},{8,10},{9,17},{... | collective-permute-start | bytes 2580488 | tf_op jit(solution)/shard_map/ppermute | solution.py:35
  30.5 3.7 %collective-permute-start.5 = (bf16[120,3584]{1,0:T(8,128)(2,1)S(1)}, bf16[120,3584]{1,0:T(8,128)(2,1)S(1)}, u32[]{:S(2)}, u32[]{:S(2)}) collective-permute-start(bf16[120,3584]{1,0:T(8,128)(2,1)S(1)} %get-tuple-element.23), channel_id=1, source_target_pairs={{0,6},{1,25},{2,0},{3,27},{4,2},{5,29},{6,4},{7,31},{8,14},{9,1},{... | collective-permute-start | bytes 2580488 | tf_op jit(solution)/shard_map/ppermute | solution.py:35
  34.2 1.1 rest.1
  35.3 7.7 %collective-permute-done.4.refs_0_.refs_1_ = bf16[120,3584]{1,0:T(8,128)(2,1)S(1)} collective-permute-done((bf16[120,3584]{1,0:T(8,128)(2,1)S(1)}, bf16[120,3584]{1,0:T(8,128)(2,1)S(1)}, u32[]{:S(2)}, u32[]{:S(2)}) %collective-permute-start.4) | collective-permute-done | bytes 860192 | tf_op jit(solution)/shard_map/ppermute | solution.py:35
  43.0 2.2 %collective-permute-done.5.refs_1_.refs_2_ = bf16[120,3584]{1,0:T(8,128)(2,1)S(1)} collective-permute-done((bf16[120,3584]{1,0:T(8,128)(2,1)S(1)}, bf16[120,3584]{1,0:T(8,128)(2,1)S(1)}, u32[]{:S(2)}, u32[]{:S(2)}) %collective-permute-start.5) | collective-permute-done | bytes 860192 | tf_op jit(solution)/shard_map/ppermute | solution.py:35
  45.6 4.6 %collective-permute-start.6 = (bf16[120,3584]{1,0:T(8,128)(2,1)S(1)}, bf16[120,3584]{1,0:T(8,128)(2,1)S(1)}, u32[]{:S(2)}, u32[]{:S(2)}) collective-permute-start(bf16[120,3584]{1,0:T(8,128)(2,1)S(1)} %far.1), channel_id=1, source_target_pairs={{0,4},{1,17},{2,6},{3,19},{4,0},{5,21},{6,2},{7,23},{8,12},{9,25},... | collective-permute-start | bytes 2580488 | tf_op jit(solution)/shard_map/ppermute | solution.py:35
  50.2 2.5 %experts.2 = (bf16[120,3584]{1,0:T(8,128)(2,1)S(1)}, bf16[120,3584]{1,0:T(8,128)(2,1)S(1)}, bf16[120,3584]{1,0:T(8,128)(2,1)S(1)}, s32[8,128]{1,0:T(8,128)S(1)}) custom-call(bf16[120,3584]{1,0:T(8,128)(2,1)S(1)} %get-tuple-element.24.refs_0_, bf16[120,3584]{1,0:T(8,128)(2,1)S(1)} %collective-permute-done.4.refs_0_.refs_1_, ...), custom_call_target="tpu_custom_call" | custom-call | tf_op jit(solution)/shard_map/experts/pallas_call | solution.py:381
  52.7 3.4 %collective-permute-start.9 = (bf16[120,3584]{1,0:T(8,128)(2,1)S(1)}, bf16[120,3584]{1,0:T(8,128)(2,1)S(1)}, u32[]{:S(2)}, u32[]{:S(2)}) collective-permute-start(bf16[120,3584]{1,0:T(8,128)(2,1)S(1)} %get-tuple-element.28), channel_id=1, source_target_pairs={{0,6},{1,25},{2,0},{3,27},{4,2},{5,29},{6,4},{7,31},{8,14},{9,1},{... | collective-permute-start | bytes 2580488 | tf_op jit(solution)/shard_map/ppermute | solution.py:35
  56.1 2.5 %collective-permute-start.10 = (bf16[120,3584]{1,0:T(8,128)(2,1)S(1)}, bf16[120,3584]{1,0:T(8,128)(2,1)S(1)}, u32[]{:S(2)}, u32[]{:S(2)}) collective-permute-start(bf16[120,3584]{1,0:T(8,128)(2,1)S(1)} %get-tuple-element.29), channel_id=1, source_target_pairs={{0,2},{1,9},{2,4},{3,11},{4,6},{5,13},{6,0},{7,15},{8,10},{9,17},{... | collective-permute-start | bytes 2580488 | tf_op jit(solution)/shard_map/ppermute | solution.py:35
  58.6 3.2 %collective-permute-done.6.refs_0_ = bf16[120,3584]{1,0:T(8,128)(2,1)S(1)} collective-permute-done((bf16[120,3584]{1,0:T(8,128)(2,1)S(1)}, bf16[120,3584]{1,0:T(8,128)(2,1)S(1)}, u32[]{:S(2)}, u32[]{:S(2)}) %collective-permute-start.6) | collective-permute-done | bytes 860192 | tf_op jit(solution)/shard_map/ppermute | solution.py:35
  61.8 1.6 %experts.3 = (bf16[120,3584]{1,0:T(8,128)(2,1)S(1)}, s32[8,128]{1,0:T(8,128)}) custom-call(bf16[120,3584]{1,0:T(8,128)(2,1)S(1)} %collective-permute-done.6.refs_0_, bf16[3584,128]{1,0:T(8,128)(2,1)S(1)} %bitcast.61, bf16[3584,128]{1,0:T(8,128)(2,1)S(1)} %bitcast.64, bf16[128,3584]{1,0:T(8,128)(2,1)S(1)} %bitcast.67, ...), custom_call_target="tpu_custom_call" | custom-call | tf_op jit(solution)/shard_map/experts/pallas_call | solution.py:381
  63.3 4.7 %collective-permute-start.8 = (bf16[120,3584]{1,0:T(8,128)(2,1)S(1)}, bf16[120,3584]{1,0:T(8,128)(2,1)S(1)}, u32[]{:S(2)}, u32[]{:S(2)}) collective-permute-start(bf16[120,3584]{1,0:T(8,128)(2,1)S(1)} %get-tuple-element.26), channel_id=1, source_target_pairs={{0,4},{1,17},{2,6},{3,19},{4,0},{5,21},{6,2},{7,23},{8,12},{9,25},... | collective-permute-start | bytes 2580488 | tf_op jit(solution)/shard_map/ppermute | solution.py:35
  68.1 2.0 %collective-permute-start = (bf16[1,48,224]{2,1,0:T(8,128)(2,1)S(1)}, bf16[1,48,224]{2,1,0:T(8,128)(2,1)S(1)}, u32[]{:S(2)}, u32[]{:S(2)}) collective-permute-start(bf16[1,48,224]{2,1,0:T(8,128)(2,1)S(1)} %constant_dynamic-update-slice_fusion), channel_id=1, source_target_pairs={{32,0},{96,64},{160,128},{224,192},{448,480},{384,416},{320,352},{... | collective-permute-start | bytes 64520 | tf_op jit(solution)/shard_map/ppermute | solution.py:447
  70.1 1.5 %collective-permute-done = bf16[1,48,224]{2,1,0:T(8,128)(2,1)S(1)} collective-permute-done((bf16[1,48,224]{2,1,0:T(8,128)(2,1)S(1)}, bf16[1,48,224]{2,1,0:T(8,128)(2,1)S(1)}, u32[]{:S(2)}, u32[]{:S(2)}) %collective-permute-start) | collective-permute-done | bytes 21536 | tf_op jit(solution)/shard_map/ppermute | solution.py:447
  73.1 8.1 %collective-permute-done.10.refs_3_ = bf16[120,3584]{1,0:T(8,128)(2,1)S(1)} collective-permute-done((bf16[120,3584]{1,0:T(8,128)(2,1)S(1)}, bf16[120,3584]{1,0:T(8,128)(2,1)S(1)}, u32[]{:S(2)}, u32[]{:S(2)}) %collective-permute-start.10) | collective-permute-done | bytes 860192 | tf_op jit(solution)/shard_map/ppermute | solution.py:35
  81.2 2.3 %gather.2.refs_2_ = f32[192,3584]{1,0:T(8,128)S(1)} custom-call(bf16[192,1024]{1,0:T(8,128)(2,1)S(1)} %get-tuple-element.21.refs_2_.refs_0_, bf16[120,3584]{1,0:T(8,128)(2,1)S(1)} %get-tuple-element.27.refs_1_, bf16[120,3584]{1,0:T(8,128)(2,1)S(1)} %collective-permute-done.9.refs_2_, bf16[120,3584]{1,0:T(8,128)(2,1)S(1)} %collective-permute-done.10.refs_3_), custom_call_target="tpu_custom_call" | custom-call | tf_op jit(solution)/shard_map/gather/pallas_call | solution.py:399
  83.5 2.0 %gather.3 = bf16[192,3584]{1,0:T(8,128)(2,1)} custom-call(bf16[192,1024]{1,0:T(8,128)(2,1)S(1)} %get-tuple-element.21.refs_2_.refs_0_, bf16[120,3584]{1,0:T(8,128)(2,1)S(1)} %collective-permute-done.8.refs_1_, f32[192,3584]{1,0:T(8,128)S(1)} %gather.2.refs_2_, bf16[4,48,224]{2,1,0:T(8,128)(2,1)S(1)} %collective-permute-done.2.refs_3_), custom_call_target="tpu_custom_call" | custom-call | tf_op jit(solution)/shard_map/gather/pallas_call | solution.py:399
  85.5 3.7 %all-to-all-start.1 = ((bf16[4,48,3584]{2,1,0:T(8,128)(2,1)}), bf16[4,48,3584]{2,1,0:T(8,128)(2,1)S(1)}, u32[]{:S(2)}, u32[]{:S(2)}) async-start(bf16[4,48,3584]{2,1,0:T(8,128)(2,1)} %bitcast.14), calls=%async_computation.1 | async-start | bytes 2752512 | tf_op jit(solution)/shard_map/all_to_all | solution.py:49
  90.0 1.1 blocks.2._
  91.1 10.7 %all-to-all-done.1 = bf16[4,48,3584]{2,1,0:T(8,128)(2,1)S(1)} async-done(((bf16[4,48,3584]{2,1,0:T(8,128)(2,1)}), bf16[4,48,3584]{2,1,0:T(8,128)(2,1)S(1)}, u32[]{:S(2)}, u32[]{:S(2)}) %all-to-all-start.1) | async-done | bytes 1376288 | tf_op jit(solution)/shard_map/all_to_all | solution.py:49
  101.8 1.3 finish.1
  103.1 4.2 %collective-permute-start.12 = (bf16[24,3584]{1,0:T(8,128)(2,1)S(1)}, bf16[24,3584]{1,0:T(8,128)(2,1)S(1)}, u32[]{:S(2)}, u32[]{:S(2)}) collective-permute-start(bf16[24,3584]{1,0:T(8,128)(2,1)S(1)} %get-tuple-element.31.bwd_ref), channel_id=1, source_target_pairs={{0,480},{32,0},{64,32},{96,64},{128,96},{160,128},{192,160},{224,1... | collective-permute-start | bytes 516104 | tf_op jit(solution)/shard_map/ppermute | solution.py:433
  107.3 1.9 %collective-permute-start.11 = (bf16[24,3584]{1,0:T(8,128)(2,1)S(1)}, bf16[24,3584]{1,0:T(8,128)(2,1)S(1)}, u32[]{:S(2)}, u32[]{:S(2)}) collective-permute-start(bf16[24,3584]{1,0:T(8,128)(2,1)S(1)} %get-tuple-element.30.fwd_ref), channel_id=1, source_target_pairs={{0,32},{32,64},{64,96},{96,128},{128,160},{160,192},{192,224},{224... | collective-permute-start | bytes 516104 | tf_op jit(solution)/shard_map/ppermute | solution.py:433
  109.2 1.2 collective-permute-done.12.right_ref
  110.4 4.2 %collective-permute-done.11.left_ref = bf16[24,3584]{1,0:T(8,128)(2,1)S(1)} collective-permute-done((bf16[24,3584]{1,0:T(8,128)(2,1)S(1)}, bf16[24,3584]{1,0:T(8,128)(2,1)S(1)}, u32[]{:S(2)}, u32[]{:S(2)}) %collective-permute-start.11) | collective-permute-done | bytes 172064 | tf_op jit(solution)/shard_map/ppermute | solution.py:433
  114.6 1.0 blocks.3
  117.8 1.3 collective-permute-start.16
  119.8 25.7 %collective-permute-done.16 = bf16[1,48,224]{2,1,0:T(8,128)(2,1)S(1)} collective-permute-done((bf16[1,48,224]{2,1,0:T(8,128)(2,1)S(1)}, bf16[1,48,224]{2,1,0:T(8,128)(2,1)S(1)}, u32[]{:S(2)}, u32[]{:S(2)}) %collective-permute-start.16) | collective-permute-done | bytes 21536 | tf_op jit(solution)/shard_map/ppermute | solution.py:453
  (55 shorter events, 10.2 us)
Async XLA Ops:
  0.7 0.9 copy-start.3
  1.7 0.9 copy-start.5
  2.6 0.7 copy-start.7
  3.3 0.7 copy-start.8
  4.0 0.7 copy-start.9
  6.0 18.8 %copy-start.1 = (bf16[1,3584,128]{2,1,0:T(8,128)(2,1)S(1)}, bf16[1,3584,128]{2,1,0:T(8,128)(2,1)}, u32[]{:S(2)}) copy-start(bf16[1,3584,128]{2,1,0:T(8,128)(2,1)} %param.16) | copy-start | bytes 2752516
  6.1 18.8 %copy-start.2 = (bf16[1,128,3584]{2,1,0:T(8,128)(2,1)S(1)}, bf16[1,128,3584]{2,1,0:T(8,128)(2,1)}, u32[]{:S(2)}) copy-start(bf16[1,128,3584]{2,1,0:T(8,128)(2,1)} %param.17) | copy-start | bytes 2752516
  23.4 1.5 %copy-start = (bf16[1,3584,128]{2,1,0:T(8,128)(2,1)S(1)}, bf16[1,3584,128]{2,1,0:T(8,128)(2,1)}, u32[]{:S(2)}) copy-start(bf16[1,3584,128]{2,1,0:T(8,128)(2,1)} %param.15) | copy-start | bytes 2752516
  25.2 25.1 %collective-permute-start.7 = (bf16[10752,128]{1,0:T(8,128)(2,1)S(1)}, bf16[10752,128]{1,0:T(8,128)(2,1)S(1)}, u32[]{:S(2)}, u32[]{:S(2)}) collective-permute-start(bf16[10752,128]{1,0:T(8,128)(2,1)S(1)} %pack.1), channel_id=1, source_target_pairs={{0,1},{1,0},{2,3},{3,2},{4,5},{5,4},{6,7},{7,6},{8,9},{9,8},{10,11... | collective-permute-start | bytes 8257544 | tf_op jit(solution)/shard_map/ppermute | solution.py:441
  27.1 15.9 %collective-permute-start.4 = (bf16[120,3584]{1,0:T(8,128)(2,1)S(1)}, bf16[120,3584]{1,0:T(8,128)(2,1)S(1)}, u32[]{:S(2)}, u32[]{:S(2)}) collective-permute-start(bf16[120,3584]{1,0:T(8,128)(2,1)S(1)} %get-tuple-element.22), channel_id=1, source_target_pairs={{0,2},{1,9},{2,4},{3,11},{4,6},{5,13},{6,0},{7,15},{8,10},{9,17},{... | collective-permute-start | bytes 2580488 | tf_op jit(solution)/shard_map/ppermute | solution.py:35
  30.5 14.7 %collective-permute-start.5 = (bf16[120,3584]{1,0:T(8,128)(2,1)S(1)}, bf16[120,3584]{1,0:T(8,128)(2,1)S(1)}, u32[]{:S(2)}, u32[]{:S(2)}) collective-permute-start(bf16[120,3584]{1,0:T(8,128)(2,1)S(1)} %get-tuple-element.23), channel_id=1, source_target_pairs={{0,6},{1,25},{2,0},{3,27},{4,2},{5,29},{6,4},{7,31},{8,14},{9,1},{... | collective-permute-start | bytes 2580488 | tf_op jit(solution)/shard_map/ppermute | solution.py:35
  45.6 16.2 %collective-permute-start.6 = (bf16[120,3584]{1,0:T(8,128)(2,1)S(1)}, bf16[120,3584]{1,0:T(8,128)(2,1)S(1)}, u32[]{:S(2)}, u32[]{:S(2)}) collective-permute-start(bf16[120,3584]{1,0:T(8,128)(2,1)S(1)} %far.1), channel_id=1, source_target_pairs={{0,4},{1,17},{2,6},{3,19},{4,0},{5,21},{6,2},{7,23},{8,12},{9,25},... | collective-permute-start | bytes 2580488 | tf_op jit(solution)/shard_map/ppermute | solution.py:35
  52.7 20.3 %collective-permute-start.9 = (bf16[120,3584]{1,0:T(8,128)(2,1)S(1)}, bf16[120,3584]{1,0:T(8,128)(2,1)S(1)}, u32[]{:S(2)}, u32[]{:S(2)}) collective-permute-start(bf16[120,3584]{1,0:T(8,128)(2,1)S(1)} %get-tuple-element.28), channel_id=1, source_target_pairs={{0,6},{1,25},{2,0},{3,27},{4,2},{5,29},{6,4},{7,31},{8,14},{9,1},{... | collective-permute-start | bytes 2580488 | tf_op jit(solution)/shard_map/ppermute | solution.py:35
  56.1 25.1 %collective-permute-start.10 = (bf16[120,3584]{1,0:T(8,128)(2,1)S(1)}, bf16[120,3584]{1,0:T(8,128)(2,1)S(1)}, u32[]{:S(2)}, u32[]{:S(2)}) collective-permute-start(bf16[120,3584]{1,0:T(8,128)(2,1)S(1)} %get-tuple-element.29), channel_id=1, source_target_pairs={{0,2},{1,9},{2,4},{3,11},{4,6},{5,13},{6,0},{7,15},{8,10},{9,17},{... | collective-permute-start | bytes 2580488 | tf_op jit(solution)/shard_map/ppermute | solution.py:35
  61.8 6.3 %copy-start.10 = (bf16[1,24,224]{2,1,0:T(8,128)(2,1)S(1)}, bf16[1,24,224]{2,1,0:T(8,128)(2,1)}, u32[]{:S(2)}) copy-start(bf16[1,24,224]{2,1,0:T(8,128)(2,1)} %param.12) | copy-start | bytes 32260
  61.8 6.3 %copy-start.11 = (bf16[1,24,224]{2,1,0:T(8,128)(2,1)S(1)}, bf16[1,24,224]{2,1,0:T(8,128)(2,1)}, u32[]{:S(2)}) copy-start(bf16[1,24,224]{2,1,0:T(8,128)(2,1)} %param.13) | copy-start | bytes 32260
  63.3 20.2 %collective-permute-start.8 = (bf16[120,3584]{1,0:T(8,128)(2,1)S(1)}, bf16[120,3584]{1,0:T(8,128)(2,1)S(1)}, u32[]{:S(2)}, u32[]{:S(2)}) collective-permute-start(bf16[120,3584]{1,0:T(8,128)(2,1)S(1)} %get-tuple-element.26), channel_id=1, source_target_pairs={{0,4},{1,17},{2,6},{3,19},{4,0},{5,21},{6,2},{7,23},{8,12},{9,25},... | collective-permute-start | bytes 2580488 | tf_op jit(solution)/shard_map/ppermute | solution.py:35
  68.1 3.5 %collective-permute-start = (bf16[1,48,224]{2,1,0:T(8,128)(2,1)S(1)}, bf16[1,48,224]{2,1,0:T(8,128)(2,1)S(1)}, u32[]{:S(2)}, u32[]{:S(2)}) collective-permute-start(bf16[1,48,224]{2,1,0:T(8,128)(2,1)S(1)} %constant_dynamic-update-slice_fusion), channel_id=1, source_target_pairs={{32,0},{96,64},{160,128},{224,192},{448,480},{384,416},{320,352},{... | collective-permute-start | bytes 64520 | tf_op jit(solution)/shard_map/ppermute | solution.py:447
  71.7 0.7 collective-permute-start.1
  72.4 11.1 %collective-permute-start.2 = (bf16[4,48,224]{2,1,0:T(8,128)(2,1)S(1)}, bf16[4,48,224]{2,1,0:T(8,128)(2,1)S(1)}, u32[]{:S(2)}, u32[]{:S(2)}) collective-permute-start(bf16[4,48,224]{2,1,0:T(8,128)(2,1)S(1)} %pad_maximum_fusion.1), channel_id=1, source_target_pairs={{128,0},{352,480},{129,1},{353,481},{130,2},{354,482},{131,3},{355... | collective-permute-start | bytes 258056 | tf_op jit(solution)/shard_map/ppermute | solution.py:447
  85.5 16.3 %copy-start.4 = (bf16[1,24,3584]{2,1,0:T(8,128)(2,1)S(1)}, bf16[1,24,3584]{2,1,0:T(8,128)(2,1)}, u32[]{:S(2)}) copy-start(bf16[1,24,3584]{2,1,0:T(8,128)(2,1)} %param.10) | copy-start | bytes 516100
  85.5 16.3 %copy-start.6 = (bf16[1,24,3584]{2,1,0:T(8,128)(2,1)S(1)}, bf16[1,24,3584]{2,1,0:T(8,128)(2,1)}, u32[]{:S(2)}) copy-start(bf16[1,24,3584]{2,1,0:T(8,128)(2,1)} %param.11) | copy-start | bytes 516100
  85.5 16.3 %all-to-all-start.1 = ((bf16[4,48,3584]{2,1,0:T(8,128)(2,1)}), bf16[4,48,3584]{2,1,0:T(8,128)(2,1)S(1)}, u32[]{:S(2)}, u32[]{:S(2)}) async-start(bf16[4,48,3584]{2,1,0:T(8,128)(2,1)} %bitcast.14), calls=%async_computation.1 | async-start | bytes 2752512 | tf_op jit(solution)/shard_map/all_to_all | solution.py:49
  89.3 0.7 collective-permute-start.3
  103.1 7.3 %collective-permute-start.12 = (bf16[24,3584]{1,0:T(8,128)(2,1)S(1)}, bf16[24,3584]{1,0:T(8,128)(2,1)S(1)}, u32[]{:S(2)}, u32[]{:S(2)}) collective-permute-start(bf16[24,3584]{1,0:T(8,128)(2,1)S(1)} %get-tuple-element.31.bwd_ref), channel_id=1, source_target_pairs={{0,480},{32,0},{64,32},{96,64},{128,96},{160,128},{192,160},{224,1... | collective-permute-start | bytes 516104 | tf_op jit(solution)/shard_map/ppermute | solution.py:433
  107.3 7.3 %collective-permute-start.11 = (bf16[24,3584]{1,0:T(8,128)(2,1)S(1)}, bf16[24,3584]{1,0:T(8,128)(2,1)S(1)}, u32[]{:S(2)}, u32[]{:S(2)}) collective-permute-start(bf16[24,3584]{1,0:T(8,128)(2,1)S(1)} %get-tuple-element.30.fwd_ref), channel_id=1, source_target_pairs={{0,32},{32,64},{64,96},{96,128},{128,160},{160,192},{192,224},{224... | collective-permute-start | bytes 516104 | tf_op jit(solution)/shard_map/ppermute | solution.py:433
  115.6 0.7 collective-permute-start.13
  116.3 0.7 collective-permute-start.14
  117.1 0.7 collective-permute-start.15
  117.8 27.8 %collective-permute-start.16 = (bf16[1,48,224]{2,1,0:T(8,128)(2,1)S(1)}, bf16[1,48,224]{2,1,0:T(8,128)(2,1)S(1)}, u32[]{:S(2)}, u32[]{:S(2)}) collective-permute-start(bf16[1,48,224]{2,1,0:T(8,128)(2,1)S(1)} %slice_select_fusion.3), channel_id=1, source_target_pairs={{128,160},{192,224},{352,320},{288,256},{129,161},{193,225},{353,3... | collective-permute-start | bytes 64520 | tf_op jit(solution)/shard_map/ppermute | solution.py:453

commit v6 on v5

--- a/solution.py
+++ b/solution.py
@@ -223,7 +223,7 @@
         out_ref[:, cut] = total.astype(out_ref.dtype)
 
 
-def finish_kernel(place_ref, meta_ref, rows_ref, fwd_ref, bwd_ref, _, of_ref, ob_ref):
+def finish_kernel(place_ref, meta_ref, rows_ref, fwd_ref, bwd_ref, of_ref, ob_ref):
     meta = meta_ref[...]
     total = EXPERTS * BOTH
     column = iota((BOTH, total), 1)
@@ -406,16 +406,16 @@
     )(back, *blocks, *([so_far] if last else []), *before)
 
 
-def make_finish(place, meta, rows, fwd, bwd, before):
+def make_finish(place, meta, rows, fwd, bwd):
     features = fwd.shape[1]
     return pl.pallas_call(
         finish_kernel,
         out_shape=(shape(ROWS, features),) * 2,
-        in_specs=[SMEM] + [VMEM] * 4 + [ANY],
+        in_specs=[SMEM] + [VMEM] * 4,
         out_specs=(VMEM,) * 2,
         compiler_params=params(),
         name="finish",
-    )(place, meta, rows, fwd, bwd, before)
+    )(place, meta, rows, fwd, bwd)
 
 
 def make_simple(kernel, out, place, *arrays):
@@ -452,14 +452,12 @@
     def move(block, *pairs):
         return lax.ppermute(block, "pp", mirrored(list(pairs), sections))
 
-    a = move(own[2:8], (0, 2))
-    b = move(jnp.where(place == 0, own[1:5], a[2:6]), (0, 1), (2, 4))
-    c = move(jnp.where(place == 2, a[1:3], b[2:4]), (2, 3), (4, 6))
-    d = move(jnp.where(place == 4, b[1:2], c[1:2]), (4, 5), (6, 7))
-    mine = own[0]
-    for at, block in ((1, b), (2, a), (3, c), (4, b), (5, d), (6, c), (7, d)):
-        mine = jnp.where(place == at, block[0], mine)
-    return mine
+    a = move(own[4:8], (0, 4))
+    b = move(jnp.where(place == 0, own[2:4], a[2:4]), (0, 2), (4, 6))
+    c = jnp.where(place == 0, own[1:2], jnp.where(place == 4, a[1:2], b[1:2]))
+    c = move(c, (0, 1), (2, 3), (4, 5), (6, 7))
+    mine = jnp.where(place == 0, own[0], jnp.where(place == 4, a[0], b[0]))
+    return jnp.where((place & 1) == 1, c[0], mine)
 
 
 def body(
@@ -501,14 +499,14 @@
     back1, back3 = hop(done1, -1), hop(done3, -3)
     done2, token = run_experts([last], *weights, token)
     back2 = hop(done2, -2)
-    held, got0 = inward(held, 1, sections)
-    held, got = inward(held, 2, sections)
+    held, got = inward(held, 1, sections)
     begun = make_gather(back, [done0, back1, back3], (0, 1, 3))
     gathered = make_gather(back, [back2], (2,), begun, (got,))
+    held, _ = inward(held, 2, sections)
     passed_on = jnp.where(at_start, held[:, ROWS:], held[:, :ROWS])
     got = lax.ppermute(passed_on, "pp", [(0, sections - 1), (sections - 1, 0)])
     entered = make_simple(entered_kernel, (ROWS, features), place, held, got)
-    fwd_out, bwd_out = make_finish(place, meta, exchange(gathered), fwd, bwd, entered)
+    fwd_out, bwd_out = make_finish(place, meta, exchange(gathered), fwd, bwd)
     from_left, from_right = shifted(fwd_out, 1, sections), shifted(bwd_out, -1, sections)
     ends = make_simple(
         ends_kernel, (half, BOTH, part), place, from_left, from_right, fwd_out, bwd_out

time: 147 us -> 140 us (0.952)
  the two profiles are of different devices: /device:TPU:160 before, /device:TPU:32 now
where the time goes in v6:
time: 140 us; the launch traced here: 139 us
  waiting for transfers between devices  55.8 us (40%)
  starting transfers between devices  42.7 us (30%)
  blocking collectives  17.3 us (12%)
  Pallas kernels  16.4 us (12%)
  local copies, waits for them, and re-layouts  4.57 us (3%)
    ppermute x6, starting transfers between devices, hop(): return lax.ppermute(block, 'ep', route)  22.3 us
    ppermute x6, waiting for transfers between devices, hop(): return lax.ppermute(block, 'ep', route)  20 us
    all_to_all x1, blocking collectives, exchange(): lax.all_to_all(rows, 'ep', split_axis=0, concat_axis=0, axis_index_groups...  17.3 us
    all_to_all x1, waiting for transfers between devices, exchange(): lax.all_to_all(rows, 'ep', split_axis=0, concat_axis=0, axis_index_groups...  11.9 us
    ppermute x2, waiting for transfers between devices, shifted(): lax.ppermute(block, 'pp', [(i, (i + distance) % count) for i in range(cou...  11.5 us
    ppermute x3, waiting for transfers between devices, move(): return lax.ppermute(block, 'pp', mirrored(list(pairs), sections))  10.9 us
    ppermute x2, starting transfers between devices, shifted(): lax.ppermute(block, 'pp', [(i, (i + distance) % count) for i in range(cou...  6.3 us
    ppermute x3, starting transfers between devices, inward(): got = lax.ppermute(held, 'pp', mirrored(pairs, sections))  5.25 us
  transfers between devices with their start and end apart: 17, of which 9 were waited for; matrix products, arithmetic and copies ran while one was open for 1% of the time, Pallas kernels for 7%

profile of v6, /device:TPU:32, one launch (start us, length us, event | category | flops | bytes accessed | tf_op | source)
XLA Modules:
  0.0 138.8 jit_solution(16698271268964817200)
XLA Ops:
  0.7 0.9 copy-done.3
  4.6 1.4 normed.1
  6.1 17.3 %all_to_all.22 = bf16[4,48,3712]{2,1,0:T(8,128)(2,1)S(1)} all-to-all(bf16[4,48,3712]{2,1,0:T(8,128)(2,1)S(1)} %bitcast.35), channel_id=1, replica_groups={{0,8,16,24},{2,10,18,26},{4,12,20,28},{6,14,22,30},{1,3,5,7},{9,11,13,1..., dimensions={0} | all-to-all | bytes 2850816 | tf_op jit(solution)/shard_map/all_to_all | solution.py:49
  23.4 1.5 %near.1 = (bf16[120,3584]{1,0:T(8,128)(2,1)S(1)}, bf16[120,3584]{1,0:T(8,128)(2,1)S(1)}, bf16[512,192]{1,0:T(8,128)(2,1)S(1)}, s32[8,128]{1,0:T(8,128)}) custom-call(s32[3]{0:T(128)S(1)} %pad_add_fusion.place_ref, bf16[192,3712]{1,0:T(8,128)(2,1)S(1)} %bitcast.22), custom_call_target="tpu_custom_call" | custom-call | tf_op jit(solution)/shard_map/near/pallas_call | solution.py:317
  25.2 1.9 %collective-permute-start.7 = (bf16[10752,128]{1,0:T(8,128)(2,1)S(1)}, bf16[10752,128]{1,0:T(8,128)(2,1)S(1)}, u32[]{:S(2)}, u32[]{:S(2)}) collective-permute-start(bf16[10752,128]{1,0:T(8,128)(2,1)S(1)} %pack.1), channel_id=1, source_target_pairs={{0,1},{1,0},{2,3},{3,2},{4,5},{5,4},{6,7},{7,6},{8,9},{9,8},{10,11... | collective-permute-start | bytes 8257544 | tf_op jit(solution)/shard_map/ppermute | solution.py:441
  27.1 3.4 %collective-permute-start.4 = (bf16[120,3584]{1,0:T(8,128)(2,1)S(1)}, bf16[120,3584]{1,0:T(8,128)(2,1)S(1)}, u32[]{:S(2)}, u32[]{:S(2)}) collective-permute-start(bf16[120,3584]{1,0:T(8,128)(2,1)S(1)} %get-tuple-element.22), channel_id=1, source_target_pairs={{0,2},{1,9},{2,4},{3,11},{4,6},{5,13},{6,0},{7,15},{8,10},{9,17},{... | collective-permute-start | bytes 2580488 | tf_op jit(solution)/shard_map/ppermute | solution.py:35
  30.5 3.7 %collective-permute-start.5 = (bf16[120,3584]{1,0:T(8,128)(2,1)S(1)}, bf16[120,3584]{1,0:T(8,128)(2,1)S(1)}, u32[]{:S(2)}, u32[]{:S(2)}) collective-permute-start(bf16[120,3584]{1,0:T(8,128)(2,1)S(1)} %get-tuple-element.23), channel_id=1, source_target_pairs={{0,6},{1,25},{2,0},{3,27},{4,2},{5,29},{6,4},{7,31},{8,14},{9,1},{... | collective-permute-start | bytes 2580488 | tf_op jit(solution)/shard_map/ppermute | solution.py:35
  34.2 1.1 rest.1
  35.3 7.7 %collective-permute-done.4.refs_0_.refs_1_ = bf16[120,3584]{1,0:T(8,128)(2,1)S(1)} collective-permute-done((bf16[120,3584]{1,0:T(8,128)(2,1)S(1)}, bf16[120,3584]{1,0:T(8,128)(2,1)S(1)}, u32[]{:S(2)}, u32[]{:S(2)}) %collective-permute-start.4) | collective-permute-done | bytes 860192 | tf_op jit(solution)/shard_map/ppermute | solution.py:35
  43.0 2.2 %collective-permute-done.5.refs_1_.refs_2_ = bf16[120,3584]{1,0:T(8,128)(2,1)S(1)} collective-permute-done((bf16[120,3584]{1,0:T(8,128)(2,1)S(1)}, bf16[120,3584]{1,0:T(8,128)(2,1)S(1)}, u32[]{:S(2)}, u32[]{:S(2)}) %collective-permute-start.5) | collective-permute-done | bytes 860192 | tf_op jit(solution)/shard_map/ppermute | solution.py:35
  45.6 4.7 %collective-permute-start.6 = (bf16[120,3584]{1,0:T(8,128)(2,1)S(1)}, bf16[120,3584]{1,0:T(8,128)(2,1)S(1)}, u32[]{:S(2)}, u32[]{:S(2)}) collective-permute-start(bf16[120,3584]{1,0:T(8,128)(2,1)S(1)} %far.1), channel_id=1, source_target_pairs={{0,4},{1,17},{2,6},{3,19},{4,0},{5,21},{6,2},{7,23},{8,12},{9,25},... | collective-permute-start | bytes 2580488 | tf_op jit(solution)/shard_map/ppermute | solution.py:35
  50.3 2.5 %experts.2 = (bf16[120,3584]{1,0:T(8,128)(2,1)S(1)}, bf16[120,3584]{1,0:T(8,128)(2,1)S(1)}, bf16[120,3584]{1,0:T(8,128)(2,1)S(1)}, s32[8,128]{1,0:T(8,128)S(1)}) custom-call(bf16[120,3584]{1,0:T(8,128)(2,1)S(1)} %get-tuple-element.24.refs_0_, bf16[120,3584]{1,0:T(8,128)(2,1)S(1)} %collective-permute-done.4.refs_0_.refs_1_, ...), custom_call_target="tpu_custom_call" | custom-call | tf_op jit(solution)/shard_map/experts/pallas_call | solution.py:381
  52.8 3.3 %collective-permute-start.9 = (bf16[120,3584]{1,0:T(8,128)(2,1)S(1)}, bf16[120,3584]{1,0:T(8,128)(2,1)S(1)}, u32[]{:S(2)}, u32[]{:S(2)}) collective-permute-start(bf16[120,3584]{1,0:T(8,128)(2,1)S(1)} %get-tuple-element.28), channel_id=1, source_target_pairs={{0,6},{1,25},{2,0},{3,27},{4,2},{5,29},{6,4},{7,31},{8,14},{9,1},{... | collective-permute-start | bytes 2580488 | tf_op jit(solution)/shard_map/ppermute | solution.py:35
  56.1 2.5 %collective-permute-start.10 = (bf16[120,3584]{1,0:T(8,128)(2,1)S(1)}, bf16[120,3584]{1,0:T(8,128)(2,1)S(1)}, u32[]{:S(2)}, u32[]{:S(2)}) collective-permute-start(bf16[120,3584]{1,0:T(8,128)(2,1)S(1)} %get-tuple-element.29), channel_id=1, source_target_pairs={{0,2},{1,9},{2,4},{3,11},{4,6},{5,13},{6,0},{7,15},{8,10},{9,17},{... | collective-permute-start | bytes 2580488 | tf_op jit(solution)/shard_map/ppermute | solution.py:35
  58.6 3.2 %collective-permute-done.6.refs_0_ = bf16[120,3584]{1,0:T(8,128)(2,1)S(1)} collective-permute-done((bf16[120,3584]{1,0:T(8,128)(2,1)S(1)}, bf16[120,3584]{1,0:T(8,128)(2,1)S(1)}, u32[]{:S(2)}, u32[]{:S(2)}) %collective-permute-start.6) | collective-permute-done | bytes 860192 | tf_op jit(solution)/shard_map/ppermute | solution.py:35
  61.8 1.6 %experts.3 = (bf16[120,3584]{1,0:T(8,128)(2,1)S(1)}, s32[8,128]{1,0:T(8,128)}) custom-call(bf16[120,3584]{1,0:T(8,128)(2,1)S(1)} %collective-permute-done.6.refs_0_, bf16[3584,128]{1,0:T(8,128)(2,1)S(1)} %bitcast.27, bf16[3584,128]{1,0:T(8,128)(2,1)S(1)} %bitcast.30, bf16[128,3584]{1,0:T(8,128)(2,1)S(1)} %bitcast.33, ...), custom_call_target="tpu_custom_call" | custom-call | tf_op jit(solution)/shard_map/experts/pallas_call | solution.py:381
  63.3 4.7 %collective-permute-start.8 = (bf16[120,3584]{1,0:T(8,128)(2,1)S(1)}, bf16[120,3584]{1,0:T(8,128)(2,1)S(1)}, u32[]{:S(2)}, u32[]{:S(2)}) collective-permute-start(bf16[120,3584]{1,0:T(8,128)(2,1)S(1)} %get-tuple-element.26), channel_id=1, source_target_pairs={{0,4},{1,17},{2,6},{3,19},{4,0},{5,21},{6,2},{7,23},{8,12},{9,25},... | collective-permute-start | bytes 2580488 | tf_op jit(solution)/shard_map/ppermute | solution.py:35
  68.1 3.9 %collective-permute-start = (bf16[1,48,224]{2,1,0:T(8,128)(2,1)S(1)}, bf16[1,48,224]{2,1,0:T(8,128)(2,1)S(1)}, u32[]{:S(2)}, u32[]{:S(2)}) collective-permute-start(bf16[1,48,224]{2,1,0:T(8,128)(2,1)S(1)} %constant_dynamic-update-slice_fusion), channel_id=1, source_target_pairs={{32,0},{96,64},{160,128},{224,192},{448,480},{384,416},{320,352},{... | collective-permute-start | bytes 64520 | tf_op jit(solution)/shard_map/ppermute | solution.py:447
  72.0 1.5 %collective-permute-done = bf16[1,48,224]{2,1,0:T(8,128)(2,1)S(1)} collective-permute-done((bf16[1,48,224]{2,1,0:T(8,128)(2,1)S(1)}, bf16[1,48,224]{2,1,0:T(8,128)(2,1)S(1)}, u32[]{:S(2)}, u32[]{:S(2)}) %collective-permute-start) | collective-permute-done | bytes 21536 | tf_op jit(solution)/shard_map/ppermute | solution.py:447
  74.2 6.9 %collective-permute-done.10.refs_3_ = bf16[120,3584]{1,0:T(8,128)(2,1)S(1)} collective-permute-done((bf16[120,3584]{1,0:T(8,128)(2,1)S(1)}, bf16[120,3584]{1,0:T(8,128)(2,1)S(1)}, u32[]{:S(2)}, u32[]{:S(2)}) %collective-permute-start.10) | collective-permute-done | bytes 860192 | tf_op jit(solution)/shard_map/ppermute | solution.py:35
  81.2 2.3 %gather.2.refs_2_ = f32[192,3584]{1,0:T(8,128)S(1)} custom-call(bf16[192,1024]{1,0:T(8,128)(2,1)S(1)} %get-tuple-element.21.refs_2_.refs_0_, bf16[120,3584]{1,0:T(8,128)(2,1)S(1)} %get-tuple-element.27.refs_1_, bf16[120,3584]{1,0:T(8,128)(2,1)S(1)} %collective-permute-done.9.refs_2_, bf16[120,3584]{1,0:T(8,128)(2,1)S(1)} %collective-permute-done.10.refs_3_), custom_call_target="tpu_custom_call" | custom-call | tf_op jit(solution)/shard_map/gather/pallas_call | solution.py:399
  83.5 2.0 %gather.3 = bf16[192,3584]{1,0:T(8,128)(2,1)} custom-call(bf16[192,1024]{1,0:T(8,128)(2,1)S(1)} %get-tuple-element.21.refs_2_.refs_0_, bf16[120,3584]{1,0:T(8,128)(2,1)S(1)} %collective-permute-done.8.refs_1_, f32[192,3584]{1,0:T(8,128)S(1)} %gather.2.refs_2_, bf16[2,48,224]{2,1,0:T(8,128)(2,1)S(1)} %collective-permute-done.1.refs_3_), custom_call_target="tpu_custom_call" | custom-call | tf_op jit(solution)/shard_map/gather/pallas_call | solution.py:399
  85.5 3.7 %all-to-all-start.1 = ((bf16[4,48,3584]{2,1,0:T(8,128)(2,1)}), bf16[4,48,3584]{2,1,0:T(8,128)(2,1)S(1)}, u32[]{:S(2)}, u32[]{:S(2)}) async-start(bf16[4,48,3584]{2,1,0:T(8,128)(2,1)} %bitcast.14), calls=%async_computation.1 | async-start | bytes 2752512 | tf_op jit(solution)/shard_map/all_to_all | solution.py:49
  89.9 11.9 %all-to-all-done.1 = bf16[4,48,3584]{2,1,0:T(8,128)(2,1)S(1)} async-done(((bf16[4,48,3584]{2,1,0:T(8,128)(2,1)}), bf16[4,48,3584]{2,1,0:T(8,128)(2,1)S(1)}, u32[]{:S(2)}, u32[]{:S(2)}) %all-to-all-start.1) | async-done | bytes 1376288 | tf_op jit(solution)/shard_map/all_to_all | solution.py:49
  101.8 1.3 finish.1
  103.1 4.4 %collective-permute-start.12 = (bf16[24,3584]{1,0:T(8,128)(2,1)S(1)}, bf16[24,3584]{1,0:T(8,128)(2,1)S(1)}, u32[]{:S(2)}, u32[]{:S(2)}) collective-permute-start(bf16[24,3584]{1,0:T(8,128)(2,1)S(1)} %get-tuple-element.31.bwd_ref), channel_id=1, source_target_pairs={{0,480},{32,0},{64,32},{96,64},{128,96},{160,128},{192,160},{224,1... | collective-permute-start | bytes 516104 | tf_op jit(solution)/shard_map/ppermute | solution.py:433
  107.5 1.9 %collective-permute-start.11 = (bf16[24,3584]{1,0:T(8,128)(2,1)S(1)}, bf16[24,3584]{1,0:T(8,128)(2,1)S(1)}, u32[]{:S(2)}, u32[]{:S(2)}) collective-permute-start(bf16[24,3584]{1,0:T(8,128)(2,1)S(1)} %get-tuple-element.30.fwd_ref), channel_id=1, source_target_pairs={{0,32},{32,64},{64,96},{96,128},{128,160},{160,192},{192,224},{224... | collective-permute-start | bytes 516104 | tf_op jit(solution)/shard_map/ppermute | solution.py:433
  110.4 10.6 %collective-permute-done.11.left_ref = bf16[24,3584]{1,0:T(8,128)(2,1)S(1)} collective-permute-done((bf16[24,3584]{1,0:T(8,128)(2,1)S(1)}, bf16[24,3584]{1,0:T(8,128)(2,1)S(1)}, u32[]{:S(2)}, u32[]{:S(2)}) %collective-permute-start.11) | collective-permute-done | bytes 172064 | tf_op jit(solution)/shard_map/ppermute | solution.py:433
  120.9 1.0 blocks.3
  124.1 1.1 blocks.2
  125.2 1.3 collective-permute-start.15
  127.3 10.9 %collective-permute-done.15 = bf16[1,48,224]{2,1,0:T(8,128)(2,1)S(1)} collective-permute-done((bf16[1,48,224]{2,1,0:T(8,128)(2,1)S(1)}, bf16[1,48,224]{2,1,0:T(8,128)(2,1)S(1)}, u32[]{:S(2)}, u32[]{:S(2)}) %collective-permute-start.15) | collective-permute-done | bytes 21536 | tf_op jit(solution)/shard_map/ppermute | solution.py:453
  (52 shorter events, 9.6 us)
Async XLA Ops:
  0.7 0.9 copy-start.3
  1.7 0.9 copy-start.5
  2.6 0.7 copy-start.7
  3.3 0.7 copy-start.8
  4.0 0.7 copy-start.9
  6.0 18.8 %copy-start.1 = (bf16[1,3584,128]{2,1,0:T(8,128)(2,1)S(1)}, bf16[1,3584,128]{2,1,0:T(8,128)(2,1)}, u32[]{:S(2)}) copy-start(bf16[1,3584,128]{2,1,0:T(8,128)(2,1)} %param.16) | copy-start | bytes 2752516
  6.1 18.8 %copy-start.2 = (bf16[1,128,3584]{2,1,0:T(8,128)(2,1)S(1)}, bf16[1,128,3584]{2,1,0:T(8,128)(2,1)}, u32[]{:S(2)}) copy-start(bf16[1,128,3584]{2,1,0:T(8,128)(2,1)} %param.17) | copy-start | bytes 2752516
  23.4 1.5 %copy-start = (bf16[1,3584,128]{2,1,0:T(8,128)(2,1)S(1)}, bf16[1,3584,128]{2,1,0:T(8,128)(2,1)}, u32[]{:S(2)}) copy-start(bf16[1,3584,128]{2,1,0:T(8,128)(2,1)} %param.15) | copy-start | bytes 2752516
  25.2 25.1 %collective-permute-start.7 = (bf16[10752,128]{1,0:T(8,128)(2,1)S(1)}, bf16[10752,128]{1,0:T(8,128)(2,1)S(1)}, u32[]{:S(2)}, u32[]{:S(2)}) collective-permute-start(bf16[10752,128]{1,0:T(8,128)(2,1)S(1)} %pack.1), channel_id=1, source_target_pairs={{0,1},{1,0},{2,3},{3,2},{4,5},{5,4},{6,7},{7,6},{8,9},{9,8},{10,11... | collective-permute-start | bytes 8257544 | tf_op jit(solution)/shard_map/ppermute | solution.py:441
  27.1 15.9 %collective-permute-start.4 = (bf16[120,3584]{1,0:T(8,128)(2,1)S(1)}, bf16[120,3584]{1,0:T(8,128)(2,1)S(1)}, u32[]{:S(2)}, u32[]{:S(2)}) collective-permute-start(bf16[120,3584]{1,0:T(8,128)(2,1)S(1)} %get-tuple-element.22), channel_id=1, source_target_pairs={{0,2},{1,9},{2,4},{3,11},{4,6},{5,13},{6,0},{7,15},{8,10},{9,17},{... | collective-permute-start | bytes 2580488 | tf_op jit(solution)/shard_map/ppermute | solution.py:35
  30.5 14.7 %collective-permute-start.5 = (bf16[120,3584]{1,0:T(8,128)(2,1)S(1)}, bf16[120,3584]{1,0:T(8,128)(2,1)S(1)}, u32[]{:S(2)}, u32[]{:S(2)}) collective-permute-start(bf16[120,3584]{1,0:T(8,128)(2,1)S(1)} %get-tuple-element.23), channel_id=1, source_target_pairs={{0,6},{1,25},{2,0},{3,27},{4,2},{5,29},{6,4},{7,31},{8,14},{9,1},{... | collective-permute-start | bytes 2580488 | tf_op jit(solution)/shard_map/ppermute | solution.py:35
  45.6 16.2 %collective-permute-start.6 = (bf16[120,3584]{1,0:T(8,128)(2,1)S(1)}, bf16[120,3584]{1,0:T(8,128)(2,1)S(1)}, u32[]{:S(2)}, u32[]{:S(2)}) collective-permute-start(bf16[120,3584]{1,0:T(8,128)(2,1)S(1)} %far.1), channel_id=1, source_target_pairs={{0,4},{1,17},{2,6},{3,19},{4,0},{5,21},{6,2},{7,23},{8,12},{9,25},... | collective-permute-start | bytes 2580488 | tf_op jit(solution)/shard_map/ppermute | solution.py:35
  52.8 21.5 %collective-permute-start.9 = (bf16[120,3584]{1,0:T(8,128)(2,1)S(1)}, bf16[120,3584]{1,0:T(8,128)(2,1)S(1)}, u32[]{:S(2)}, u32[]{:S(2)}) collective-permute-start(bf16[120,3584]{1,0:T(8,128)(2,1)S(1)} %get-tuple-element.28), channel_id=1, source_target_pairs={{0,6},{1,25},{2,0},{3,27},{4,2},{5,29},{6,4},{7,31},{8,14},{9,1},{... | collective-permute-start | bytes 2580488 | tf_op jit(solution)/shard_map/ppermute | solution.py:35
  56.1 25.1 %collective-permute-start.10 = (bf16[120,3584]{1,0:T(8,128)(2,1)S(1)}, bf16[120,3584]{1,0:T(8,128)(2,1)S(1)}, u32[]{:S(2)}, u32[]{:S(2)}) collective-permute-start(bf16[120,3584]{1,0:T(8,128)(2,1)S(1)} %get-tuple-element.29), channel_id=1, source_target_pairs={{0,2},{1,9},{2,4},{3,11},{4,6},{5,13},{6,0},{7,15},{8,10},{9,17},{... | collective-permute-start | bytes 2580488 | tf_op jit(solution)/shard_map/ppermute | solution.py:35
  61.8 6.3 %copy-start.10 = (bf16[1,24,224]{2,1,0:T(8,128)(2,1)S(1)}, bf16[1,24,224]{2,1,0:T(8,128)(2,1)}, u32[]{:S(2)}) copy-start(bf16[1,24,224]{2,1,0:T(8,128)(2,1)} %param.12) | copy-start | bytes 32260
  61.8 6.3 %copy-start.11 = (bf16[1,24,224]{2,1,0:T(8,128)(2,1)S(1)}, bf16[1,24,224]{2,1,0:T(8,128)(2,1)}, u32[]{:S(2)}) copy-start(bf16[1,24,224]{2,1,0:T(8,128)(2,1)} %param.13) | copy-start | bytes 32260
  63.3 20.2 %collective-permute-start.8 = (bf16[120,3584]{1,0:T(8,128)(2,1)S(1)}, bf16[120,3584]{1,0:T(8,128)(2,1)S(1)}, u32[]{:S(2)}, u32[]{:S(2)}) collective-permute-start(bf16[120,3584]{1,0:T(8,128)(2,1)S(1)} %get-tuple-element.26), channel_id=1, source_target_pairs={{0,4},{1,17},{2,6},{3,19},{4,0},{5,21},{6,2},{7,23},{8,12},{9,25},... | collective-permute-start | bytes 2580488 | tf_op jit(solution)/shard_map/ppermute | solution.py:35
  68.1 5.4 %collective-permute-start = (bf16[1,48,224]{2,1,0:T(8,128)(2,1)S(1)}, bf16[1,48,224]{2,1,0:T(8,128)(2,1)S(1)}, u32[]{:S(2)}, u32[]{:S(2)}) collective-permute-start(bf16[1,48,224]{2,1,0:T(8,128)(2,1)S(1)} %constant_dynamic-update-slice_fusion), channel_id=1, source_target_pairs={{32,0},{96,64},{160,128},{224,192},{448,480},{384,416},{320,352},{... | collective-permute-start | bytes 64520 | tf_op jit(solution)/shard_map/ppermute | solution.py:447
  73.6 9.9 %collective-permute-start.1 = (bf16[2,48,224]{2,1,0:T(8,128)(2,1)S(1)}, bf16[2,48,224]{2,1,0:T(8,128)(2,1)S(1)}, u32[]{:S(2)}, u32[]{:S(2)}) collective-permute-start(bf16[2,48,224]{2,1,0:T(8,128)(2,1)S(1)} %pad_maximum_fusion.2), channel_id=1, source_target_pairs={{64,0},{192,128},{416,480},{288,352},{65,1},{193,129},{417,481},{2... | collective-permute-start | bytes 129032 | tf_op jit(solution)/shard_map/ppermute | solution.py:447
  85.5 16.3 %copy-start.4 = (bf16[1,24,3584]{2,1,0:T(8,128)(2,1)S(1)}, bf16[1,24,3584]{2,1,0:T(8,128)(2,1)}, u32[]{:S(2)}) copy-start(bf16[1,24,3584]{2,1,0:T(8,128)(2,1)} %param.10) | copy-start | bytes 516100
  85.5 16.3 %copy-start.6 = (bf16[1,24,3584]{2,1,0:T(8,128)(2,1)S(1)}, bf16[1,24,3584]{2,1,0:T(8,128)(2,1)}, u32[]{:S(2)}) copy-start(bf16[1,24,3584]{2,1,0:T(8,128)(2,1)} %param.11) | copy-start | bytes 516100
  85.5 16.3 %all-to-all-start.1 = ((bf16[4,48,3584]{2,1,0:T(8,128)(2,1)}), bf16[4,48,3584]{2,1,0:T(8,128)(2,1)S(1)}, u32[]{:S(2)}, u32[]{:S(2)}) async-start(bf16[4,48,3584]{2,1,0:T(8,128)(2,1)} %bitcast.14), calls=%async_computation.1 | async-start | bytes 2752512 | tf_op jit(solution)/shard_map/all_to_all | solution.py:49
  89.2 20.2 %collective-permute-start.2 = (bf16[4,48,224]{2,1,0:T(8,128)(2,1)S(1)}, bf16[4,48,224]{2,1,0:T(8,128)(2,1)S(1)}, u32[]{:S(2)}, u32[]{:S(2)}) collective-permute-start(bf16[4,48,224]{2,1,0:T(8,128)(2,1)S(1)} %pad_maximum_fusion.1), channel_id=1, source_target_pairs={{128,0},{352,480},{129,1},{353,481},{130,2},{354,482},{131,3},{355... | collective-permute-start | bytes 258056 | tf_op jit(solution)/shard_map/ppermute | solution.py:447
  103.1 7.3 %collective-permute-start.12 = (bf16[24,3584]{1,0:T(8,128)(2,1)S(1)}, bf16[24,3584]{1,0:T(8,128)(2,1)S(1)}, u32[]{:S(2)}, u32[]{:S(2)}) collective-permute-start(bf16[24,3584]{1,0:T(8,128)(2,1)S(1)} %get-tuple-element.31.bwd_ref), channel_id=1, source_target_pairs={{0,480},{32,0},{64,32},{96,64},{128,96},{160,128},{192,160},{224,1... | collective-permute-start | bytes 516104 | tf_op jit(solution)/shard_map/ppermute | solution.py:433
  107.5 13.5 %collective-permute-start.11 = (bf16[24,3584]{1,0:T(8,128)(2,1)S(1)}, bf16[24,3584]{1,0:T(8,128)(2,1)S(1)}, u32[]{:S(2)}, u32[]{:S(2)}) collective-permute-start(bf16[24,3584]{1,0:T(8,128)(2,1)S(1)} %get-tuple-element.30.fwd_ref), channel_id=1, source_target_pairs={{0,32},{32,64},{64,96},{96,128},{128,160},{160,192},{192,224},{224... | collective-permute-start | bytes 516104 | tf_op jit(solution)/shard_map/ppermute | solution.py:433
  122.0 1.4 collective-permute-start.13
  122.7 1.4 %collective-permute-start.3 = (bf16[8,24,224]{2,1,0:T(8,128)(2,1)S(1)}, bf16[8,24,224]{2,1,0:T(8,128)(2,1)S(1)}, u32[]{:S(2)}, u32[]{:S(2)}) collective-permute-start(bf16[8,24,224]{2,1,0:T(8,128)(2,1)S(1)} %slice_select_fusion), channel_id=1, source_target_pairs={{0,480},{480,0},{1,481},{481,1},{2,482},{482,2},{3,483},{483,3},{4... | collective-permute-start | bytes 258056 | tf_op jit(solution)/shard_map/ppermute | solution.py:507
  123.4 1.8 %collective-permute-start.14 = (bf16[2,48,224]{2,1,0:T(8,128)(2,1)S(1)}, bf16[2,48,224]{2,1,0:T(8,128)(2,1)S(1)}, u32[]{:S(2)}, u32[]{:S(2)}) collective-permute-start(bf16[2,48,224]{2,1,0:T(8,128)(2,1)S(1)} %slice_select_fusion.1), channel_id=1, source_target_pairs={{0,64},{128,192},{480,416},{352,288},{1,65},{129,193},{481,417},{3... | collective-permute-start | bytes 129032 | tf_op jit(solution)/shard_map/ppermute | solution.py:453
  125.2 12.9 %collective-permute-start.15 = (bf16[1,48,224]{2,1,0:T(8,128)(2,1)S(1)}, bf16[1,48,224]{2,1,0:T(8,128)(2,1)S(1)}, u32[]{:S(2)}, u32[]{:S(2)}) collective-permute-start(bf16[1,48,224]{2,1,0:T(8,128)(2,1)S(1)} %fusion.2), channel_id=1, source_target_pairs={{0,32},{64,96},{128,160},{192,224},{480,448},{416,384},{352,320},{... | collective-permute-start | bytes 64520 | tf_op jit(solution)/shard_map/ppermute | solution.py:453

commit v7 on v6

--- a/solution.py
+++ b/solution.py
@@ -223,7 +223,9 @@
         out_ref[:, cut] = total.astype(out_ref.dtype)
 
 
-def finish_kernel(place_ref, meta_ref, rows_ref, fwd_ref, bwd_ref, of_ref, ob_ref):
+def finish_kernel(direction, place_ref, meta_ref, rows_ref, own_ref, *refs):
+    out_ref = refs[-1]
+    mine = slice(direction * ROWS, (direction + 1) * ROWS)
     meta = meta_ref[...]
     total = EXPERTS * BOTH
     column = iota((BOTH, total), 1)
@@ -239,18 +241,17 @@
         same = same | (column == row + part * BOTH)
     ones = jnp.where(same, 1.0, 0.0)
     on_first = place_ref[0] == 0
-    high = jnp.where(on_first, high, ones).astype(BF)
-    low = jnp.where(on_first, low, 0.0).astype(BF)
-    width = fwd_ref.shape[1]
+    high = jnp.where(on_first, high, ones)[mine].astype(BF)
+    low = jnp.where(on_first, low, 0.0)[mine].astype(BF)
+    width = own_ref.shape[1]
     for start in range(0, width, CHUNK):
         cut = slice(start, min(start + CHUNK, width))
         rows = rows_ref[:, cut]
         mixture = dot(high, rows) + dot(low, rows)
-        of_ref[:, cut] = (fwd_ref[:, cut].astype(F32) + mixture[:ROWS]).astype(BF)
-        ob_ref[:, cut] = (bwd_ref[:, cut].astype(F32) + mixture[ROWS:]).astype(BF)
-
-
-def ends_kernel(place_ref, left_ref, right_ref, fwd_ref, bwd_ref, out_ref):
+        out_ref[:, cut] = (own_ref[:, cut].astype(F32) + mixture).astype(BF)
+
+
+def ends_kernel(place_ref, right_ref, left_ref, fwd_ref, bwd_ref, _, out_ref):
     count, _, part = out_ref.shape
     at_start = place_ref[2] == 0
     for r in range(count):
@@ -406,27 +407,29 @@
     )(back, *blocks, *([so_far] if last else []), *before)
 
 
-def make_finish(place, meta, rows, fwd, bwd):
-    features = fwd.shape[1]
-    return pl.pallas_call(
-        finish_kernel,
-        out_shape=(shape(ROWS, features),) * 2,
-        in_specs=[SMEM] + [VMEM] * 4,
-        out_specs=(VMEM,) * 2,
+def make_finish(direction, place, meta, rows, own, *before):
+    def body(*refs):
+        finish_kernel(direction, *refs)
+
+    return pl.pallas_call(
+        body,
+        out_shape=shape(*own.shape),
+        in_specs=[SMEM] + [VMEM] * 3 + [ANY] * len(before),
+        out_specs=VMEM,
         compiler_params=params(),
         name="finish",
-    )(place, meta, rows, fwd, bwd)
-
-
-def make_simple(kernel, out, place, *arrays):
+    )(place, meta, rows, own, *before)
+
+
+def make_simple(kernel, out, place, *arrays, before=()):
     return pl.pallas_call(
         kernel,
         out_shape=jax.ShapeDtypeStruct(out, BF),
-        in_specs=[SMEM] + [VMEM] * len(arrays),
+        in_specs=[SMEM] + [VMEM] * len(arrays) + [ANY] * len(before),
         out_specs=VMEM,
         compiler_params=params(),
         name="blocks",
-    )(place, *arrays)
+    )(place, *arrays, *before)
 
 
 def shifted(block, distance, count):
@@ -505,11 +508,16 @@
     held, _ = inward(held, 2, sections)
     passed_on = jnp.where(at_start, held[:, ROWS:], held[:, :ROWS])
     got = lax.ppermute(passed_on, "pp", [(0, sections - 1), (sections - 1, 0)])
-    entered = make_simple(entered_kernel, (ROWS, features), place, held, got)
-    fwd_out, bwd_out = make_finish(place, meta, exchange(gathered), fwd, bwd)
-    from_left, from_right = shifted(fwd_out, 1, sections), shifted(bwd_out, -1, sections)
+    rows = exchange(gathered)
+    fwd_out = make_finish(0, place, meta, rows, fwd)
+    bwd_out = make_finish(1, place, meta, rows, bwd, fwd_out)
+    from_right = shifted(bwd_out, -1, sections)
+    from_left = shifted(fwd_out, 1, sections)
+    entered = make_simple(
+        entered_kernel, (ROWS, features), place, held, got
+    )
     ends = make_simple(
-        ends_kernel, (half, BOTH, part), place, from_left, from_right, fwd_out, bwd_out
+        ends_kernel, (half, BOTH, part), place, from_right, from_left, fwd_out, bwd_out, before=(got,)
     )
     mine = outward(ends, jnp.minimum(section, sections - 1 - section), sections)
     fwd_next = jnp.where(at_start, entered, from_left)

time: 140 us -> 138 us (0.986)
  the two profiles are of different devices: /device:TPU:32 before, /device:TPU:256 now
where the time goes in v7:
time: 138 us; the launch traced here: 137 us
  waiting for transfers between devices  52.6 us (38%)
  starting transfers between devices  42.6 us (31%)
  Pallas kernels  17.6 us (13%)
  blocking collectives  17.3 us (13%)
  local copies, waits for them, and re-layouts  4.6 us (3%)
    ppermute x6, starting transfers between devices, hop(): return lax.ppermute(block, 'ep', route)  22.3 us
    ppermute x6, waiting for transfers between devices, hop(): return lax.ppermute(block, 'ep', route)  21 us
    all_to_all x1, blocking collectives, exchange(): lax.all_to_all(rows, 'ep', split_axis=0, concat_axis=0, axis_index_groups...  17.3 us
    ppermute x3, waiting for transfers between devices, move(): return lax.ppermute(block, 'pp', mirrored(list(pairs), sections))  16 us
    all_to_all x1, waiting for transfers between devices, exchange(): lax.all_to_all(rows, 'ep', split_axis=0, concat_axis=0, axis_index_groups...  11.7 us
    ppermute x2, starting transfers between devices, shifted(): lax.ppermute(block, 'pp', [(i, (i + distance) % count) for i in range(cou...  7.08 us
    ppermute x3, starting transfers between devices, inward(): got = lax.ppermute(held, 'pp', mirrored(pairs, sections))  4.4 us
    pallas_call x2, Pallas kernels, make_gather(): pl.pallas_call(body, out_shape=shape(total, features, BF if last else F32...  4.28 us
  transfers between devices with their start and end apart: 17, of which 8 were waited for; matrix products, arithmetic and copies ran while one was open for 1% of the time, Pallas kernels for 7%

profile of v7, /device:TPU:256, one launch (start us, length us, event | category | flops | bytes accessed | tf_op | source)
XLA Modules:
  0.0 136.9 jit_solution(17931568257879173609)
XLA Ops:
  4.6 1.4 %normed.1 = (bf16[192,3712]{1,0:T(8,128)(2,1)S(1)}, f32[48,128]{1,0:T(8,128)S(1)}) custom-call(s32[3]{0:T(128)S(1)} %pad_add_fusion.place_ref.refs_0_, bf16[24,3584]{1,0:T(8,128)(2,1)S(1)} %bitcast.37, bf16[24,3584]{1,0:T(8,128)(2,1)S(1)} %bitcast.39, f32[1,3584]{1,0:T(1,128)S(1)} %copy-done.7, s32[2,2,24]{2,1,0:T(2,128)S(1)} %bitcast.41, ...), custom_call_target="tpu_custom_call" | custom-call | tf_op jit(solution)/shard_map/normed/pallas_call | solution.py:305
  6.1 17.3 %all_to_all.22 = bf16[4,48,3712]{2,1,0:T(8,128)(2,1)S(1)} all-to-all(bf16[4,48,3712]{2,1,0:T(8,128)(2,1)S(1)} %bitcast.36), channel_id=1, replica_groups={{0,8,16,24},{2,10,18,26},{4,12,20,28},{6,14,22,30},{1,3,5,7},{9,11,13,1..., dimensions={0} | all-to-all | bytes 2850816 | tf_op jit(solution)/shard_map/all_to_all | solution.py:49
  23.4 1.5 %near.1 = (bf16[120,3584]{1,0:T(8,128)(2,1)S(1)}, bf16[120,3584]{1,0:T(8,128)(2,1)S(1)}, bf16[512,192]{1,0:T(8,128)(2,1)S(1)}, s32[8,128]{1,0:T(8,128)}) custom-call(s32[3]{0:T(128)S(1)} %pad_add_fusion.place_ref.refs_0_, bf16[192,3712]{1,0:T(8,128)(2,1)S(1)} %bitcast.22), custom_call_target="tpu_custom_call" | custom-call | tf_op jit(solution)/shard_map/near/pallas_call | solution.py:318
  25.2 1.9 %collective-permute-start.7 = (bf16[10752,128]{1,0:T(8,128)(2,1)S(1)}, bf16[10752,128]{1,0:T(8,128)(2,1)S(1)}, u32[]{:S(2)}, u32[]{:S(2)}) collective-permute-start(bf16[10752,128]{1,0:T(8,128)(2,1)S(1)} %pack.1), channel_id=1, source_target_pairs={{0,1},{1,0},{2,3},{3,2},{4,5},{5,4},{6,7},{7,6},{8,9},{9,8},{10,11... | collective-permute-start | bytes 8257544 | tf_op jit(solution)/shard_map/ppermute | solution.py:444
  27.1 3.4 %collective-permute-start.4 = (bf16[120,3584]{1,0:T(8,128)(2,1)S(1)}, bf16[120,3584]{1,0:T(8,128)(2,1)S(1)}, u32[]{:S(2)}, u32[]{:S(2)}) collective-permute-start(bf16[120,3584]{1,0:T(8,128)(2,1)S(1)} %get-tuple-element.20), channel_id=1, source_target_pairs={{0,2},{1,9},{2,4},{3,11},{4,6},{5,13},{6,0},{7,15},{8,10},{9,17},{... | collective-permute-start | bytes 2580488 | tf_op jit(solution)/shard_map/ppermute | solution.py:35
  30.5 3.7 %collective-permute-start.5 = (bf16[120,3584]{1,0:T(8,128)(2,1)S(1)}, bf16[120,3584]{1,0:T(8,128)(2,1)S(1)}, u32[]{:S(2)}, u32[]{:S(2)}) collective-permute-start(bf16[120,3584]{1,0:T(8,128)(2,1)S(1)} %get-tuple-element.21), channel_id=1, source_target_pairs={{0,6},{1,25},{2,0},{3,27},{4,2},{5,29},{6,4},{7,31},{8,14},{9,1},{... | collective-permute-start | bytes 2580488 | tf_op jit(solution)/shard_map/ppermute | solution.py:35
  34.2 1.1 rest.1
  35.3 7.7 %collective-permute-done.4.refs_0_.refs_1_ = bf16[120,3584]{1,0:T(8,128)(2,1)S(1)} collective-permute-done((bf16[120,3584]{1,0:T(8,128)(2,1)S(1)}, bf16[120,3584]{1,0:T(8,128)(2,1)S(1)}, u32[]{:S(2)}, u32[]{:S(2)}) %collective-permute-start.4) | collective-permute-done | bytes 860192 | tf_op jit(solution)/shard_map/ppermute | solution.py:35
  43.0 2.2 %collective-permute-done.5.refs_1_.refs_2_ = bf16[120,3584]{1,0:T(8,128)(2,1)S(1)} collective-permute-done((bf16[120,3584]{1,0:T(8,128)(2,1)S(1)}, bf16[120,3584]{1,0:T(8,128)(2,1)S(1)}, u32[]{:S(2)}, u32[]{:S(2)}) %collective-permute-start.5) | collective-permute-done | bytes 860192 | tf_op jit(solution)/shard_map/ppermute | solution.py:35
  45.6 4.6 %collective-permute-start.6 = (bf16[120,3584]{1,0:T(8,128)(2,1)S(1)}, bf16[120,3584]{1,0:T(8,128)(2,1)S(1)}, u32[]{:S(2)}, u32[]{:S(2)}) collective-permute-start(bf16[120,3584]{1,0:T(8,128)(2,1)S(1)} %far.1), channel_id=1, source_target_pairs={{0,4},{1,17},{2,6},{3,19},{4,0},{5,21},{6,2},{7,23},{8,12},{9,25},... | collective-permute-start | bytes 2580488 | tf_op jit(solution)/shard_map/ppermute | solution.py:35
  50.2 2.5 %experts.2 = (bf16[120,3584]{1,0:T(8,128)(2,1)S(1)}, bf16[120,3584]{1,0:T(8,128)(2,1)S(1)}, bf16[120,3584]{1,0:T(8,128)(2,1)S(1)}, s32[8,128]{1,0:T(8,128)S(1)}) custom-call(bf16[120,3584]{1,0:T(8,128)(2,1)S(1)} %get-tuple-element.22.refs_0_, bf16[120,3584]{1,0:T(8,128)(2,1)S(1)} %collective-permute-done.4.refs_0_.refs_1_, ...), custom_call_target="tpu_custom_call" | custom-call | tf_op jit(solution)/shard_map/experts/pallas_call | solution.py:382
  52.7 3.4 %collective-permute-start.9 = (bf16[120,3584]{1,0:T(8,128)(2,1)S(1)}, bf16[120,3584]{1,0:T(8,128)(2,1)S(1)}, u32[]{:S(2)}, u32[]{:S(2)}) collective-permute-start(bf16[120,3584]{1,0:T(8,128)(2,1)S(1)} %get-tuple-element.26), channel_id=1, source_target_pairs={{0,6},{1,25},{2,0},{3,27},{4,2},{5,29},{6,4},{7,31},{8,14},{9,1},{... | collective-permute-start | bytes 2580488 | tf_op jit(solution)/shard_map/ppermute | solution.py:35
  56.1 2.5 %collective-permute-start.10 = (bf16[120,3584]{1,0:T(8,128)(2,1)S(1)}, bf16[120,3584]{1,0:T(8,128)(2,1)S(1)}, u32[]{:S(2)}, u32[]{:S(2)}) collective-permute-start(bf16[120,3584]{1,0:T(8,128)(2,1)S(1)} %get-tuple-element.27), channel_id=1, source_target_pairs={{0,2},{1,9},{2,4},{3,11},{4,6},{5,13},{6,0},{7,15},{8,10},{9,17},{... | collective-permute-start | bytes 2580488 | tf_op jit(solution)/shard_map/ppermute | solution.py:35
  58.6 3.2 %collective-permute-done.6.refs_0_ = bf16[120,3584]{1,0:T(8,128)(2,1)S(1)} collective-permute-done((bf16[120,3584]{1,0:T(8,128)(2,1)S(1)}, bf16[120,3584]{1,0:T(8,128)(2,1)S(1)}, u32[]{:S(2)}, u32[]{:S(2)}) %collective-permute-start.6) | collective-permute-done | bytes 860192 | tf_op jit(solution)/shard_map/ppermute | solution.py:35
  61.8 1.6 %experts.3 = (bf16[120,3584]{1,0:T(8,128)(2,1)S(1)}, s32[8,128]{1,0:T(8,128)}) custom-call(bf16[120,3584]{1,0:T(8,128)(2,1)S(1)} %collective-permute-done.6.refs_0_, bf16[3584,128]{1,0:T(8,128)(2,1)S(1)} %bitcast.29, bf16[3584,128]{1,0:T(8,128)(2,1)S(1)} %bitcast.32, bf16[128,3584]{1,0:T(8,128)(2,1)S(1)} %bitcast.35, ...), custom_call_target="tpu_custom_call" | custom-call | tf_op jit(solution)/shard_map/experts/pallas_call | solution.py:382
  63.3 4.7 %collective-permute-start.8 = (bf16[120,3584]{1,0:T(8,128)(2,1)S(1)}, bf16[120,3584]{1,0:T(8,128)(2,1)S(1)}, u32[]{:S(2)}, u32[]{:S(2)}) collective-permute-start(bf16[120,3584]{1,0:T(8,128)(2,1)S(1)} %get-tuple-element.24), channel_id=1, source_target_pairs={{0,4},{1,17},{2,6},{3,19},{4,0},{5,21},{6,2},{7,23},{8,12},{9,25},... | collective-permute-start | bytes 2580488 | tf_op jit(solution)/shard_map/ppermute | solution.py:35
  68.1 2.9 %collective-permute-start = (bf16[1,48,224]{2,1,0:T(8,128)(2,1)S(1)}, bf16[1,48,224]{2,1,0:T(8,128)(2,1)S(1)}, u32[]{:S(2)}, u32[]{:S(2)}) collective-permute-start(bf16[1,48,224]{2,1,0:T(8,128)(2,1)S(1)} %constant_dynamic-update-slice_fusion), channel_id=1, source_target_pairs={{32,0},{96,64},{160,128},{224,192},{448,480},{384,416},{320,352},{... | collective-permute-start | bytes 64520 | tf_op jit(solution)/shard_map/ppermute | solution.py:450
  71.1 1.5 %collective-permute-done = bf16[1,48,224]{2,1,0:T(8,128)(2,1)S(1)} collective-permute-done((bf16[1,48,224]{2,1,0:T(8,128)(2,1)S(1)}, bf16[1,48,224]{2,1,0:T(8,128)(2,1)S(1)}, u32[]{:S(2)}, u32[]{:S(2)}) %collective-permute-start) | collective-permute-done | bytes 21536 | tf_op jit(solution)/shard_map/ppermute | solution.py:450
  73.3 7.9 %collective-permute-done.10.refs_3_ = bf16[120,3584]{1,0:T(8,128)(2,1)S(1)} collective-permute-done((bf16[120,3584]{1,0:T(8,128)(2,1)S(1)}, bf16[120,3584]{1,0:T(8,128)(2,1)S(1)}, u32[]{:S(2)}, u32[]{:S(2)}) %collective-permute-start.10) | collective-permute-done | bytes 860192 | tf_op jit(solution)/shard_map/ppermute | solution.py:35
  81.2 2.3 %gather.2.refs_2_ = f32[192,3584]{1,0:T(8,128)S(1)} custom-call(bf16[192,1024]{1,0:T(8,128)(2,1)S(1)} %get-tuple-element.19.refs_2_.refs_0_, bf16[120,3584]{1,0:T(8,128)(2,1)S(1)} %get-tuple-element.25.refs_1_, bf16[120,3584]{1,0:T(8,128)(2,1)S(1)} %collective-permute-done.9.refs_2_, bf16[120,3584]{1,0:T(8,128)(2,1)S(1)} %collective-permute-done.10.refs_3_), custom_call_target="tpu_custom_call" | custom-call | tf_op jit(solution)/shard_map/gather/pallas_call | solution.py:400
  83.5 2.0 %gather.3 = bf16[192,3584]{1,0:T(8,128)(2,1)} custom-call(bf16[192,1024]{1,0:T(8,128)(2,1)S(1)} %get-tuple-element.19.refs_2_.refs_0_, bf16[120,3584]{1,0:T(8,128)(2,1)S(1)} %collective-permute-done.8.refs_1_, f32[192,3584]{1,0:T(8,128)S(1)} %gather.2.refs_2_, bf16[2,48,224]{2,1,0:T(8,128)(2,1)S(1)} %collective-permute-done.1.refs_3_), custom_call_target="tpu_custom_call" | custom-call | tf_op jit(solution)/shard_map/gather/pallas_call | solution.py:400
  85.5 3.7 %all-to-all-start.1 = ((bf16[4,48,3584]{2,1,0:T(8,128)(2,1)}), bf16[4,48,3584]{2,1,0:T(8,128)(2,1)S(1)}, u32[]{:S(2)}, u32[]{:S(2)}) async-start(bf16[4,48,3584]{2,1,0:T(8,128)(2,1)} %bitcast.14), calls=%async_computation.1 | async-start | bytes 2752512 | tf_op jit(solution)/shard_map/all_to_all | solution.py:49
  90.1 11.7 %all-to-all-done.1 = bf16[4,48,3584]{2,1,0:T(8,128)(2,1)S(1)} async-done(((bf16[4,48,3584]{2,1,0:T(8,128)(2,1)}), bf16[4,48,3584]{2,1,0:T(8,128)(2,1)S(1)}, u32[]{:S(2)}, u32[]{:S(2)}) %all-to-all-start.1) | async-done | bytes 1376288 | tf_op jit(solution)/shard_map/all_to_all | solution.py:49
  101.8 1.2 finish.2.refs_4_.fwd_ref
  103.1 1.2 finish.3.bwd_ref
  104.4 2.9 %collective-permute-start.11 = (bf16[24,3584]{1,0:T(8,128)(2,1)S(1)}, bf16[24,3584]{1,0:T(8,128)(2,1)S(1)}, u32[]{:S(2)}, u32[]{:S(2)}) collective-permute-start(bf16[24,3584]{1,0:T(8,128)(2,1)S(1)} %finish.2.refs_4_.fwd_ref), channel_id=1, source_target_pairs={{0,32},{32,64},{64,96},{96,128},{128,160},{160,192},{192,224},{224... | collective-permute-start | bytes 516104 | tf_op jit(solution)/shard_map/ppermute | solution.py:436
  107.3 4.1 %collective-permute-start.12 = (bf16[24,3584]{1,0:T(8,128)(2,1)S(1)}, bf16[24,3584]{1,0:T(8,128)(2,1)S(1)}, u32[]{:S(2)}, u32[]{:S(2)}) collective-permute-start(bf16[24,3584]{1,0:T(8,128)(2,1)S(1)} %finish.3.bwd_ref), channel_id=1, source_target_pairs={{0,480},{32,0},{64,32},{96,64},{128,96},{160,128},{192,160},{224,1... | collective-permute-start | bytes 516104 | tf_op jit(solution)/shard_map/ppermute | solution.py:436
  112.2 2.4 %collective-permute-done.12.right_ref = bf16[24,3584]{1,0:T(8,128)(2,1)S(1)} collective-permute-done((bf16[24,3584]{1,0:T(8,128)(2,1)S(1)}, bf16[24,3584]{1,0:T(8,128)(2,1)S(1)}, u32[]{:S(2)}, u32[]{:S(2)}) %collective-permute-start.12) | collective-permute-done | bytes 172064 | tf_op jit(solution)/shard_map/ppermute | solution.py:436
  114.6 1.0 blocks.3
  117.1 1.1 blocks.2
  118.2 1.3 collective-permute-start.15
  120.3 16.0 %collective-permute-done.15 = bf16[1,48,224]{2,1,0:T(8,128)(2,1)S(1)} collective-permute-done((bf16[1,48,224]{2,1,0:T(8,128)(2,1)S(1)}, bf16[1,48,224]{2,1,0:T(8,128)(2,1)S(1)}, u32[]{:S(2)}, u32[]{:S(2)}) %collective-permute-start.15) | collective-permute-done | bytes 21536 | tf_op jit(solution)/shard_map/ppermute | solution.py:456
  (53 shorter events, 9.7 us)
Async XLA Ops:
  0.7 0.9 copy-start.3
  1.7 0.9 copy-start.5
  2.6 0.7 copy-start.7
  3.3 0.7 copy-start.8
  4.0 0.7 copy-start.9
  6.0 18.8 %copy-start.1 = (bf16[1,3584,128]{2,1,0:T(8,128)(2,1)S(1)}, bf16[1,3584,128]{2,1,0:T(8,128)(2,1)}, u32[]{:S(2)}) copy-start(bf16[1,3584,128]{2,1,0:T(8,128)(2,1)} %param.16) | copy-start | bytes 2752516
  6.1 18.8 %copy-start.2 = (bf16[1,128,3584]{2,1,0:T(8,128)(2,1)S(1)}, bf16[1,128,3584]{2,1,0:T(8,128)(2,1)}, u32[]{:S(2)}) copy-start(bf16[1,128,3584]{2,1,0:T(8,128)(2,1)} %param.17) | copy-start | bytes 2752516
  23.4 1.5 %copy-start = (bf16[1,3584,128]{2,1,0:T(8,128)(2,1)S(1)}, bf16[1,3584,128]{2,1,0:T(8,128)(2,1)}, u32[]{:S(2)}) copy-start(bf16[1,3584,128]{2,1,0:T(8,128)(2,1)} %param.15) | copy-start | bytes 2752516
  25.2 25.1 %collective-permute-start.7 = (bf16[10752,128]{1,0:T(8,128)(2,1)S(1)}, bf16[10752,128]{1,0:T(8,128)(2,1)S(1)}, u32[]{:S(2)}, u32[]{:S(2)}) collective-permute-start(bf16[10752,128]{1,0:T(8,128)(2,1)S(1)} %pack.1), channel_id=1, source_target_pairs={{0,1},{1,0},{2,3},{3,2},{4,5},{5,4},{6,7},{7,6},{8,9},{9,8},{10,11... | collective-permute-start | bytes 8257544 | tf_op jit(solution)/shard_map/ppermute | solution.py:444
  27.1 15.9 %collective-permute-start.4 = (bf16[120,3584]{1,0:T(8,128)(2,1)S(1)}, bf16[120,3584]{1,0:T(8,128)(2,1)S(1)}, u32[]{:S(2)}, u32[]{:S(2)}) collective-permute-start(bf16[120,3584]{1,0:T(8,128)(2,1)S(1)} %get-tuple-element.20), channel_id=1, source_target_pairs={{0,2},{1,9},{2,4},{3,11},{4,6},{5,13},{6,0},{7,15},{8,10},{9,17},{... | collective-permute-start | bytes 2580488 | tf_op jit(solution)/shard_map/ppermute | solution.py:35
  30.5 14.7 %collective-permute-start.5 = (bf16[120,3584]{1,0:T(8,128)(2,1)S(1)}, bf16[120,3584]{1,0:T(8,128)(2,1)S(1)}, u32[]{:S(2)}, u32[]{:S(2)}) collective-permute-start(bf16[120,3584]{1,0:T(8,128)(2,1)S(1)} %get-tuple-element.21), channel_id=1, source_target_pairs={{0,6},{1,25},{2,0},{3,27},{4,2},{5,29},{6,4},{7,31},{8,14},{9,1},{... | collective-permute-start | bytes 2580488 | tf_op jit(solution)/shard_map/ppermute | solution.py:35
  45.6 16.2 %collective-permute-start.6 = (bf16[120,3584]{1,0:T(8,128)(2,1)S(1)}, bf16[120,3584]{1,0:T(8,128)(2,1)S(1)}, u32[]{:S(2)}, u32[]{:S(2)}) collective-permute-start(bf16[120,3584]{1,0:T(8,128)(2,1)S(1)} %far.1), channel_id=1, source_target_pairs={{0,4},{1,17},{2,6},{3,19},{4,0},{5,21},{6,2},{7,23},{8,12},{9,25},... | collective-permute-start | bytes 2580488 | tf_op jit(solution)/shard_map/ppermute | solution.py:35
  52.7 20.5 %collective-permute-start.9 = (bf16[120,3584]{1,0:T(8,128)(2,1)S(1)}, bf16[120,3584]{1,0:T(8,128)(2,1)S(1)}, u32[]{:S(2)}, u32[]{:S(2)}) collective-permute-start(bf16[120,3584]{1,0:T(8,128)(2,1)S(1)} %get-tuple-element.26), channel_id=1, source_target_pairs={{0,6},{1,25},{2,0},{3,27},{4,2},{5,29},{6,4},{7,31},{8,14},{9,1},{... | collective-permute-start | bytes 2580488 | tf_op jit(solution)/shard_map/ppermute | solution.py:35
  56.1 25.1 %collective-permute-start.10 = (bf16[120,3584]{1,0:T(8,128)(2,1)S(1)}, bf16[120,3584]{1,0:T(8,128)(2,1)S(1)}, u32[]{:S(2)}, u32[]{:S(2)}) collective-permute-start(bf16[120,3584]{1,0:T(8,128)(2,1)S(1)} %get-tuple-element.27), channel_id=1, source_target_pairs={{0,2},{1,9},{2,4},{3,11},{4,6},{5,13},{6,0},{7,15},{8,10},{9,17},{... | collective-permute-start | bytes 2580488 | tf_op jit(solution)/shard_map/ppermute | solution.py:35
  61.8 6.3 %copy-start.10 = (bf16[1,24,224]{2,1,0:T(8,128)(2,1)S(1)}, bf16[1,24,224]{2,1,0:T(8,128)(2,1)}, u32[]{:S(2)}) copy-start(bf16[1,24,224]{2,1,0:T(8,128)(2,1)} %param.12) | copy-start | bytes 32260
  61.8 6.3 %copy-start.11 = (bf16[1,24,224]{2,1,0:T(8,128)(2,1)S(1)}, bf16[1,24,224]{2,1,0:T(8,128)(2,1)}, u32[]{:S(2)}) copy-start(bf16[1,24,224]{2,1,0:T(8,128)(2,1)} %param.13) | copy-start | bytes 32260
  63.3 20.2 %collective-permute-start.8 = (bf16[120,3584]{1,0:T(8,128)(2,1)S(1)}, bf16[120,3584]{1,0:T(8,128)(2,1)S(1)}, u32[]{:S(2)}, u32[]{:S(2)}) collective-permute-start(bf16[120,3584]{1,0:T(8,128)(2,1)S(1)} %get-tuple-element.24), channel_id=1, source_target_pairs={{0,4},{1,17},{2,6},{3,19},{4,0},{5,21},{6,2},{7,23},{8,12},{9,25},... | collective-permute-start | bytes 2580488 | tf_op jit(solution)/shard_map/ppermute | solution.py:35
  68.1 4.4 %collective-permute-start = (bf16[1,48,224]{2,1,0:T(8,128)(2,1)S(1)}, bf16[1,48,224]{2,1,0:T(8,128)(2,1)S(1)}, u32[]{:S(2)}, u32[]{:S(2)}) collective-permute-start(bf16[1,48,224]{2,1,0:T(8,128)(2,1)S(1)} %constant_dynamic-update-slice_fusion), channel_id=1, source_target_pairs={{32,0},{96,64},{160,128},{224,192},{448,480},{384,416},{320,352},{... | collective-permute-start | bytes 64520 | tf_op jit(solution)/shard_map/ppermute | solution.py:450
  72.6 10.9 %collective-permute-start.1 = (bf16[2,48,224]{2,1,0:T(8,128)(2,1)S(1)}, bf16[2,48,224]{2,1,0:T(8,128)(2,1)S(1)}, u32[]{:S(2)}, u32[]{:S(2)}) collective-permute-start(bf16[2,48,224]{2,1,0:T(8,128)(2,1)S(1)} %pad_maximum_fusion.2), channel_id=1, source_target_pairs={{64,0},{192,128},{416,480},{288,352},{65,1},{193,129},{417,481},{2... | collective-permute-start | bytes 129032 | tf_op jit(solution)/shard_map/ppermute | solution.py:450
  85.5 16.3 %copy-start.4 = (bf16[1,24,3584]{2,1,0:T(8,128)(2,1)S(1)}, bf16[1,24,3584]{2,1,0:T(8,128)(2,1)}, u32[]{:S(2)}) copy-start(bf16[1,24,3584]{2,1,0:T(8,128)(2,1)} %param.10) | copy-start | bytes 516100
  85.5 16.3 %all-to-all-start.1 = ((bf16[4,48,3584]{2,1,0:T(8,128)(2,1)}), bf16[4,48,3584]{2,1,0:T(8,128)(2,1)S(1)}, u32[]{:S(2)}, u32[]{:S(2)}) async-start(bf16[4,48,3584]{2,1,0:T(8,128)(2,1)} %bitcast.14), calls=%async_computation.1 | async-start | bytes 2752512 | tf_op jit(solution)/shard_map/all_to_all | solution.py:49
  89.2 13.9 %copy-start.6 = (bf16[1,24,3584]{2,1,0:T(8,128)(2,1)S(1)}, bf16[1,24,3584]{2,1,0:T(8,128)(2,1)}, u32[]{:S(2)}) copy-start(bf16[1,24,3584]{2,1,0:T(8,128)(2,1)} %param.11) | copy-start | bytes 516100
  89.2 0.8 collective-permute-start.2
  104.4 10.3 %collective-permute-start.11 = (bf16[24,3584]{1,0:T(8,128)(2,1)S(1)}, bf16[24,3584]{1,0:T(8,128)(2,1)S(1)}, u32[]{:S(2)}, u32[]{:S(2)}) collective-permute-start(bf16[24,3584]{1,0:T(8,128)(2,1)S(1)} %finish.2.refs_4_.fwd_ref), channel_id=1, source_target_pairs={{0,32},{32,64},{64,96},{96,128},{128,160},{160,192},{192,224},{224... | collective-permute-start | bytes 516104 | tf_op jit(solution)/shard_map/ppermute | solution.py:436
  107.3 7.3 %collective-permute-start.12 = (bf16[24,3584]{1,0:T(8,128)(2,1)S(1)}, bf16[24,3584]{1,0:T(8,128)(2,1)S(1)}, u32[]{:S(2)}, u32[]{:S(2)}) collective-permute-start(bf16[24,3584]{1,0:T(8,128)(2,1)S(1)} %finish.3.bwd_ref), channel_id=1, source_target_pairs={{0,480},{32,0},{64,32},{96,64},{128,96},{160,128},{192,160},{224,1... | collective-permute-start | bytes 516104 | tf_op jit(solution)/shard_map/ppermute | solution.py:436
  111.5 0.7 collective-permute-start.3
  115.7 0.7 collective-permute-start.13
  116.4 1.8 %collective-permute-start.14 = (bf16[2,48,224]{2,1,0:T(8,128)(2,1)S(1)}, bf16[2,48,224]{2,1,0:T(8,128)(2,1)S(1)}, u32[]{:S(2)}, u32[]{:S(2)}) collective-permute-start(bf16[2,48,224]{2,1,0:T(8,128)(2,1)S(1)} %slice_select_fusion.1), channel_id=1, source_target_pairs={{0,64},{128,192},{480,416},{352,288},{1,65},{129,193},{481,417},{3... | collective-permute-start | bytes 129032 | tf_op jit(solution)/shard_map/ppermute | solution.py:456
  118.2 18.0 %collective-permute-start.15 = (bf16[1,48,224]{2,1,0:T(8,128)(2,1)S(1)}, bf16[1,48,224]{2,1,0:T(8,128)(2,1)S(1)}, u32[]{:S(2)}, u32[]{:S(2)}) collective-permute-start(bf16[1,48,224]{2,1,0:T(8,128)(2,1)S(1)} %fusion.2), channel_id=1, source_target_pairs={{0,32},{64,96},{128,160},{192,224},{480,448},{416,384},{352,320},{... | collective-permute-start | bytes 64520 | tf_op jit(solution)/shard_map/ppermute | solution.py:456

commit v8 on v7

--- a/solution.py
+++ b/solution.py
@@ -166,7 +166,7 @@
     move(pick_ref, rows_ref, (1, 3), (first_ref, third_ref))
 
 
-def rest_kernel(place_ref, rows_ref, pick_ref, own_ref, back_ref):
+def rest_kernel(place_ref, rows_ref, pick_ref, _, own_ref, back_ref):
     column = iota((EXPERTS * BOTH, EXPERTS * LANES), 1)
     high_m = jnp.zeros(column.shape, F32)
     low_m = jnp.zeros(column.shape, F32)
@@ -251,20 +251,32 @@
         out_ref[:, cut] = (own_ref[:, cut].astype(F32) + mixture).astype(BF)
 
 
-def ends_kernel(place_ref, right_ref, left_ref, fwd_ref, bwd_ref, _, out_ref):
+def ends_fwd_kernel(place_ref, left_ref, fwd_ref, out_ref):
     count, _, part = out_ref.shape
-    at_start = place_ref[2] == 0
     for r in range(count):
         near, far = [slice(j * part, (j + 1) * part) for j in (r, 2 * count - 1 - r)]
 
-        @pl.when(at_start)
+        @pl.when(place_ref[2] == 0)
         def _():
-            out_ref[r, :ROWS, :] = left_ref[:, near]
+            out_ref[r] = left_ref[:, near]
+
+        @pl.when(place_ref[2] != 0)
+        def _():
+            out_ref[r] = fwd_ref[:, far]
+
+
+def ends_kernel(place_ref, fwds_ref, right_ref, bwd_ref, out_ref):
+    count, _, part = out_ref.shape
+    for r in range(count):
+        near, far = [slice(j * part, (j + 1) * part) for j in (r, 2 * count - 1 - r)]
+        out_ref[r, :ROWS, :] = fwds_ref[r]
+
+        @pl.when(place_ref[2] == 0)
+        def _():
             out_ref[r, ROWS:, :] = bwd_ref[:, near]
 
-        @pl.when(jnp.logical_not(at_start))
+        @pl.when(place_ref[2] != 0)
         def _():
-            out_ref[r, :ROWS, :] = fwd_ref[:, far]
             out_ref[r, ROWS:, :] = right_ref[:, far]
 
 
@@ -347,7 +359,7 @@
     )(gate, up, down, before)
 
 
-def make_rest(place, rows, pick):
+def make_rest(place, rows, pick, before):
     features = rows.shape[1] - EXTRA
     return pl.pallas_call(
         rest_kernel,
@@ -355,11 +367,11 @@
             shape(COLS * SLOTS, features),
             shape(EXPERTS * BOTH, 2 * EXPERTS * LANES),
         ),
-        in_specs=[SMEM, VMEM, VMEM],
+        in_specs=[SMEM, VMEM, VMEM, ANY],
         out_specs=(VMEM, VMEM),
         compiler_params=params(),
         name="rest",
-    )(place, rows, pick)
+    )(place, rows, pick, before)
 
 
 def make_far(rows, pick, *before):
@@ -444,11 +456,12 @@
     return lax.ppermute(block, "ep", [(i, i ^ 1) for i in range(lax.axis_size("ep"))])
 
 
-def inward(held, step, sections):
-    bit = 1 << step
-    pairs = [(i, i - bit) for i in range(bit, sections // 2, 2 * bit)]
-    got = lax.ppermute(held, "pp", mirrored(pairs, sections))
-    return jnp.concatenate([held, got], axis=0), got
+def inward(held, bit, radix, sections):
+    got = []
+    for k in range(1, radix):
+        pairs = [(i + k * bit, i) for i in range(0, sections // 2, radix * bit)]
+        got.append(lax.ppermute(held, "pp", mirrored(pairs, sections)))
+    return jnp.concatenate([held] + got, axis=0), got[-1]
 
 
 def outward(own, place, sections):
@@ -491,34 +504,32 @@
     near, far = hop(send1, 1), hop(send3, 3)
     own = (w_gate[0], w_up[0], w_down[0])
     weights = own, from_other_core(make_pack(*own, pick))
-    send0, back = make_rest(place, rows, pick)
-    last = hop(make_far(rows, pick, near, far, back), 2)
-
-    half = sections // 2
-    at_start = section == 0
-    entering = jnp.concatenate([enter_fwd, enter_bwd], axis=1)
-    held, got = inward(entering, 0, sections)
-    done0, done1, done3, token = run_experts([send0, near, far], *weights)
+    send0, back = make_rest(place, rows, pick, weights[1])
+    done0, token = run_experts([send0], *weights)
+    last = hop(make_far(rows, pick, token), 2)
+    done1, done3, token = run_experts([near, far], *weights)
     back1, back3 = hop(done1, -1), hop(done3, -3)
     done2, token = run_experts([last], *weights, token)
     back2 = hop(done2, -2)
-    held, got = inward(held, 1, sections)
+
+    half = sections // 2
+    at_start = section == 0
+    held, _ = inward(jnp.concatenate([enter_fwd, enter_bwd], axis=1), 1, 4, sections)
+    held, got = inward(held, 4, 2, sections)
     begun = make_gather(back, [done0, back1, back3], (0, 1, 3))
     gathered = make_gather(back, [back2], (2,), begun, (got,))
-    held, _ = inward(held, 2, sections)
     passed_on = jnp.where(at_start, held[:, ROWS:], held[:, :ROWS])
     got = lax.ppermute(passed_on, "pp", [(0, sections - 1), (sections - 1, 0)])
     rows = exchange(gathered)
-    fwd_out = make_finish(0, place, meta, rows, fwd)
+    fwd_out = make_finish(0, place, meta, rows, fwd, got)
     bwd_out = make_finish(1, place, meta, rows, bwd, fwd_out)
     from_right = shifted(bwd_out, -1, sections)
     from_left = shifted(fwd_out, 1, sections)
     entered = make_simple(
         entered_kernel, (ROWS, features), place, held, got
     )
-    ends = make_simple(
-        ends_kernel, (half, BOTH, part), place, from_right, from_left, fwd_out, bwd_out, before=(got,)
-    )
+    fwds = make_simple(ends_fwd_kernel, (half, ROWS, part), place, from_left, fwd_out)
+    ends = make_simple(ends_kernel, (half, BOTH, part), place, fwds, from_right, bwd_out)
     mine = outward(ends, jnp.minimum(section, sections - 1 - section), sections)
     fwd_next = jnp.where(at_start, entered, from_left)
     bwd_next = jnp.where(section == sections - 1, entered, from_right)

time: 138 us -> 143 us (1.036)
  starting transfers between devices: 42.6 us -> 47.8 us
    ppermute x3 -> x4, starting transfers between devices: 4.4 us -> 10.2 us  [inward(): got.append(lax.ppermute(held, 'pp', mirrored(pairs, sections)))]
    ppermute x6, waiting for transfers between devices: 21 us -> 19.6 us  [hop(): return lax.ppermute(block, 'ep', route)]
    pallas_call x2 -> x3, Pallas kernels: 2.15 us -> 3.12 us  [make_simple(): pl.pallas_call(kernel, out_shape=jax.ShapeDtypeStruct(out, BF), in_specs=...]
    pallas_call x2 -> x3, Pallas kernels: 4.04 us -> 4.34 us  [run_experts(): pl.pallas_call(body, out_shape=(shape(*blocks[0].shape),) * count + (shap...]
    unnamed x25 -> x28, local copies, waits for them, and re-layouts: 3.98 us -> 3.97 us
  transfers between devices with their start and end apart: 17 -> 18, of which waited for: 8 -> 8; matrix products, arithmetic and copies ran while one was open for 1% -> 1% of each run, Pallas kernels for 7% -> 8%
where the time goes in v8:
time: 143 us; the launch traced here: 142 us
  waiting for transfers between devices  51.4 us (36%)
  starting transfers between devices  47.8 us (33%)
  Pallas kernels  18.9 us (13%)
  blocking collectives  17.3 us (12%)
  local copies, waits for them, and re-layouts  4.6 us (3%)
    ppermute x6, starting transfers between devices, hop(): return lax.ppermute(block, 'ep', route)  21.6 us
    ppermute x6, waiting for transfers between devices, hop(): return lax.ppermute(block, 'ep', route)  19.6 us
    all_to_all x1, blocking collectives, exchange(): lax.all_to_all(rows, 'ep', split_axis=0, concat_axis=0, axis_index_groups...  17.3 us
    ppermute x3, waiting for transfers between devices, move(): return lax.ppermute(block, 'pp', mirrored(list(pairs), sections))  16.3 us
    all_to_all x1, waiting for transfers between devices, exchange(): lax.all_to_all(rows, 'ep', split_axis=0, concat_axis=0, axis_index_groups...  11.8 us
    ppermute x4, starting transfers between devices, inward(): got.append(lax.ppermute(held, 'pp', mirrored(pairs, sections)))  10.2 us
    ppermute x2, starting transfers between devices, shifted(): lax.ppermute(block, 'pp', [(i, (i + distance) % count) for i in range(cou...  7.11 us
    pallas_call x3, Pallas kernels, run_experts(): pl.pallas_call(body, out_shape=(shape(*blocks[0].shape),) * count + (shap...  4.34 us
  transfers between devices with their start and end apart: 18, of which 8 were waited for; matrix products, arithmetic and copies ran while one was open for 1% of the time, Pallas kernels for 8%

profile of v8, /device:TPU:256, one launch (start us, length us, event | category | flops | bytes accessed | tf_op | source)
XLA Modules:
  0.0 142.1 jit_solution(9330100408742532770)
XLA Ops:
  4.6 1.4 normed.1
  6.1 17.3 %all_to_all.22 = bf16[4,48,3712]{2,1,0:T(8,128)(2,1)S(1)} all-to-all(bf16[4,48,3712]{2,1,0:T(8,128)(2,1)S(1)} %bitcast.39), channel_id=1, replica_groups={{0,8,16,24},{2,10,18,26},{4,12,20,28},{6,14,22,30},{1,3,5,7},{9,11,13,1..., dimensions={0} | all-to-all | bytes 2850816 | tf_op jit(solution)/shard_map/all_to_all | solution.py:49
  23.4 1.5 %near.1 = (bf16[120,3584]{1,0:T(8,128)(2,1)S(1)}, bf16[120,3584]{1,0:T(8,128)(2,1)S(1)}, bf16[512,192]{1,0:T(8,128)(2,1)S(1)}, s32[8,128]{1,0:T(8,128)}) custom-call(s32[3]{0:T(128)S(1)} %pad_add_fusion.place_ref.refs_0_, bf16[192,3712]{1,0:T(8,128)(2,1)S(1)} %bitcast.22), custom_call_target="tpu_custom_call" | custom-call | tf_op jit(solution)/shard_map/near/pallas_call | solution.py:330
  25.2 1.9 %collective-permute-start.5 = (bf16[10752,128]{1,0:T(8,128)(2,1)S(1)}, bf16[10752,128]{1,0:T(8,128)(2,1)S(1)}, u32[]{:S(2)}, u32[]{:S(2)}) collective-permute-start(bf16[10752,128]{1,0:T(8,128)(2,1)S(1)} %pack.1), channel_id=1, source_target_pairs={{0,1},{1,0},{2,3},{3,2},{4,5},{5,4},{6,7},{7,6},{8,9},{9,8},{10,11... | collective-permute-start | bytes 8257544 | tf_op jit(solution)/shard_map/ppermute | solution.py:456
  27.1 3.4 %collective-permute-start.7 = (bf16[120,3584]{1,0:T(8,128)(2,1)S(1)}, bf16[120,3584]{1,0:T(8,128)(2,1)S(1)}, u32[]{:S(2)}, u32[]{:S(2)}) collective-permute-start(bf16[120,3584]{1,0:T(8,128)(2,1)S(1)} %get-tuple-element.23), channel_id=1, source_target_pairs={{0,2},{1,9},{2,4},{3,11},{4,6},{5,13},{6,0},{7,15},{8,10},{9,17},{... | collective-permute-start | bytes 2580488 | tf_op jit(solution)/shard_map/ppermute | solution.py:35
  30.5 3.7 %collective-permute-start.8 = (bf16[120,3584]{1,0:T(8,128)(2,1)S(1)}, bf16[120,3584]{1,0:T(8,128)(2,1)S(1)}, u32[]{:S(2)}, u32[]{:S(2)}) collective-permute-start(bf16[120,3584]{1,0:T(8,128)(2,1)S(1)} %get-tuple-element.24), channel_id=1, source_target_pairs={{0,6},{1,25},{2,0},{3,27},{4,2},{5,29},{6,4},{7,31},{8,14},{9,1},{... | collective-permute-start | bytes 2580488 | tf_op jit(solution)/shard_map/ppermute | solution.py:35
  34.2 1.1 rest.1
  35.3 1.1 experts.3
  36.8 3.7 %collective-permute-start.6 = (bf16[120,3584]{1,0:T(8,128)(2,1)S(1)}, bf16[120,3584]{1,0:T(8,128)(2,1)S(1)}, u32[]{:S(2)}, u32[]{:S(2)}) collective-permute-start(bf16[120,3584]{1,0:T(8,128)(2,1)S(1)} %far.1), channel_id=1, source_target_pairs={{0,4},{1,17},{2,6},{3,19},{4,0},{5,21},{6,2},{7,23},{8,12},{9,25},... | collective-permute-start | bytes 2580488 | tf_op jit(solution)/shard_map/ppermute | solution.py:35
  40.5 2.5 %collective-permute-done.7.refs_0_ = bf16[120,3584]{1,0:T(8,128)(2,1)S(1)} collective-permute-done((bf16[120,3584]{1,0:T(8,128)(2,1)S(1)}, bf16[120,3584]{1,0:T(8,128)(2,1)S(1)}, u32[]{:S(2)}, u32[]{:S(2)}) %collective-permute-start.7) | collective-permute-done | bytes 860192 | tf_op jit(solution)/shard_map/ppermute | solution.py:35
  43.0 10.7 %collective-permute-done.8.refs_1_ = bf16[120,3584]{1,0:T(8,128)(2,1)S(1)} collective-permute-done((bf16[120,3584]{1,0:T(8,128)(2,1)S(1)}, bf16[120,3584]{1,0:T(8,128)(2,1)S(1)}, u32[]{:S(2)}, u32[]{:S(2)}) %collective-permute-start.8) | collective-permute-done | bytes 860192 | tf_op jit(solution)/shard_map/ppermute | solution.py:35
  53.7 1.7 %experts.4 = (bf16[120,3584]{1,0:T(8,128)(2,1)S(1)}, bf16[120,3584]{1,0:T(8,128)(2,1)S(1)}, s32[8,128]{1,0:T(8,128)S(1)}) custom-call(bf16[120,3584]{1,0:T(8,128)(2,1)S(1)} %collective-permute-done.7.refs_0_, bf16[120,3584]{1,0:T(8,128)(2,1)S(1)} %collective-permute-done.8.refs_1_, bf16[3584,128]{1,0:T(8,128)(2,1)S(1)} %bitcast.27, ...), custom_call_target="tpu_custom_call" | custom-call | tf_op jit(solution)/shard_map/experts/pallas_call | solution.py:394
  55.4 5.6 %collective-permute-start.10 = (bf16[120,3584]{1,0:T(8,128)(2,1)S(1)}, bf16[120,3584]{1,0:T(8,128)(2,1)S(1)}, u32[]{:S(2)}, u32[]{:S(2)}) collective-permute-start(bf16[120,3584]{1,0:T(8,128)(2,1)S(1)} %get-tuple-element.28), channel_id=1, source_target_pairs={{0,6},{1,25},{2,0},{3,27},{4,2},{5,29},{6,4},{7,31},{8,14},{9,1},{... | collective-permute-start | bytes 2580488 | tf_op jit(solution)/shard_map/ppermute | solution.py:35
  61.0 1.9 %collective-permute-start.11 = (bf16[120,3584]{1,0:T(8,128)(2,1)S(1)}, bf16[120,3584]{1,0:T(8,128)(2,1)S(1)}, u32[]{:S(2)}, u32[]{:S(2)}) collective-permute-start(bf16[120,3584]{1,0:T(8,128)(2,1)S(1)} %get-tuple-element.29), channel_id=1, source_target_pairs={{0,2},{1,9},{2,4},{3,11},{4,6},{5,13},{6,0},{7,15},{8,10},{9,17},{... | collective-permute-start | bytes 2580488 | tf_op jit(solution)/shard_map/ppermute | solution.py:35
  62.9 1.6 %experts.5 = (bf16[120,3584]{1,0:T(8,128)(2,1)S(1)}, s32[8,128]{1,0:T(8,128)}) custom-call(bf16[120,3584]{1,0:T(8,128)(2,1)S(1)} %collective-permute-done.6.refs_0_, bf16[3584,128]{1,0:T(8,128)(2,1)S(1)} %bitcast.28, bf16[3584,128]{1,0:T(8,128)(2,1)S(1)} %bitcast.32, bf16[128,3584]{1,0:T(8,128)(2,1)S(1)} %bitcast.36, ...), custom_call_target="tpu_custom_call" | custom-call | tf_op jit(solution)/shard_map/experts/pallas_call | solution.py:394
  64.5 3.4 %collective-permute-start.9 = (bf16[120,3584]{1,0:T(8,128)(2,1)S(1)}, bf16[120,3584]{1,0:T(8,128)(2,1)S(1)}, u32[]{:S(2)}, u32[]{:S(2)}) collective-permute-start(bf16[120,3584]{1,0:T(8,128)(2,1)S(1)} %get-tuple-element.26), channel_id=1, source_target_pairs={{0,4},{1,17},{2,6},{3,19},{4,0},{5,21},{6,2},{7,23},{8,12},{9,25},... | collective-permute-start | bytes 2580488 | tf_op jit(solution)/shard_map/ppermute | solution.py:35
  69.3 8.2 %collective-permute-start.2 = (bf16[1,48,224]{2,1,0:T(8,128)(2,1)S(1)}, bf16[1,48,224]{2,1,0:T(8,128)(2,1)S(1)}, u32[]{:S(2)}, u32[]{:S(2)}) collective-permute-start(bf16[1,48,224]{2,1,0:T(8,128)(2,1)S(1)} %get-tuple-element.34), channel_id=1, source_target_pairs={{96,0},{224,128},{384,480},{256,352},{97,1},{225,129},{385,481},{2... | collective-permute-start | bytes 64520 | tf_op jit(solution)/shard_map/ppermute | solution.py:463
  77.5 1.5 %collective-permute-done.2 = bf16[1,48,224]{2,1,0:T(8,128)(2,1)S(1)} collective-permute-done((bf16[1,48,224]{2,1,0:T(8,128)(2,1)S(1)}, bf16[1,48,224]{2,1,0:T(8,128)(2,1)S(1)}, u32[]{:S(2)}, u32[]{:S(2)}) %collective-permute-start.2) | collective-permute-done | bytes 21536 | tf_op jit(solution)/shard_map/ppermute | solution.py:463
  79.7 6.4 %collective-permute-done.11.refs_3_ = bf16[120,3584]{1,0:T(8,128)(2,1)S(1)} collective-permute-done((bf16[120,3584]{1,0:T(8,128)(2,1)S(1)}, bf16[120,3584]{1,0:T(8,128)(2,1)S(1)}, u32[]{:S(2)}, u32[]{:S(2)}) %collective-permute-start.11) | collective-permute-done | bytes 860192 | tf_op jit(solution)/shard_map/ppermute | solution.py:35
  86.1 2.3 %gather.2.refs_2_ = f32[192,3584]{1,0:T(8,128)S(1)} custom-call(bf16[192,1024]{1,0:T(8,128)(2,1)S(1)} %get-tuple-element.20.refs_0_, bf16[120,3584]{1,0:T(8,128)(2,1)S(1)} %get-tuple-element.27.refs_1_, bf16[120,3584]{1,0:T(8,128)(2,1)S(1)} %collective-permute-done.10.refs_2_, bf16[120,3584]{1,0:T(8,128)(2,1)S(1)} %collective-permute-done.11.refs_3_), custom_call_target="tpu_custom_call" | custom-call | tf_op jit(solution)/shard_map/gather/pallas_call | solution.py:412
  88.4 2.0 %gather.3 = bf16[192,3584]{1,0:T(8,128)(2,1)} custom-call(bf16[192,1024]{1,0:T(8,128)(2,1)S(1)} %get-tuple-element.20.refs_0_, bf16[120,3584]{1,0:T(8,128)(2,1)S(1)} %collective-permute-done.9.refs_1_, f32[192,3584]{1,0:T(8,128)S(1)} %gather.2.refs_2_, bf16[4,48,224]{2,1,0:T(8,128)(2,1)S(1)} %collective-permute-done.3.refs_3_), custom_call_target="tpu_custom_call" | custom-call | tf_op jit(solution)/shard_map/gather/pallas_call | solution.py:412
  90.4 3.7 %all-to-all-start.1 = ((bf16[4,48,3584]{2,1,0:T(8,128)(2,1)}), bf16[4,48,3584]{2,1,0:T(8,128)(2,1)S(1)}, u32[]{:S(2)}, u32[]{:S(2)}) async-start(bf16[4,48,3584]{2,1,0:T(8,128)(2,1)} %bitcast.14), calls=%async_computation.1 | async-start | bytes 2752512 | tf_op jit(solution)/shard_map/all_to_all | solution.py:49
  94.9 11.8 %all-to-all-done.1 = bf16[4,48,3584]{2,1,0:T(8,128)(2,1)S(1)} async-done(((bf16[4,48,3584]{2,1,0:T(8,128)(2,1)}), bf16[4,48,3584]{2,1,0:T(8,128)(2,1)S(1)}, u32[]{:S(2)}, u32[]{:S(2)}) %all-to-all-start.1) | async-done | bytes 1376288 | tf_op jit(solution)/shard_map/all_to_all | solution.py:49
  106.7 1.2 finish.2.refs_4_.fwd_ref
  108.0 3.0 %collective-permute-start.12 = (bf16[24,3584]{1,0:T(8,128)(2,1)S(1)}, bf16[24,3584]{1,0:T(8,128)(2,1)S(1)}, u32[]{:S(2)}, u32[]{:S(2)}) collective-permute-start(bf16[24,3584]{1,0:T(8,128)(2,1)S(1)} %finish.2.refs_4_.fwd_ref), channel_id=1, source_target_pairs={{0,32},{32,64},{64,96},{96,128},{128,160},{160,192},{192,224},{224... | collective-permute-start | bytes 516104 | tf_op jit(solution)/shard_map/ppermute | solution.py:448
  110.9 1.2 finish.3.bwd_ref
  112.2 4.2 %collective-permute-start.13 = (bf16[24,3584]{1,0:T(8,128)(2,1)S(1)}, bf16[24,3584]{1,0:T(8,128)(2,1)S(1)}, u32[]{:S(2)}, u32[]{:S(2)}) collective-permute-start(bf16[24,3584]{1,0:T(8,128)(2,1)S(1)} %finish.3.bwd_ref), channel_id=1, source_target_pairs={{0,480},{32,0},{64,32},{96,64},{128,96},{160,128},{192,160},{224,1... | collective-permute-start | bytes 516104 | tf_op jit(solution)/shard_map/ppermute | solution.py:448
  117.5 2.0 %collective-permute-done.13.right_ref = bf16[24,3584]{1,0:T(8,128)(2,1)S(1)} collective-permute-done((bf16[24,3584]{1,0:T(8,128)(2,1)S(1)}, bf16[24,3584]{1,0:T(8,128)(2,1)S(1)}, u32[]{:S(2)}, u32[]{:S(2)}) %collective-permute-start.13) | collective-permute-done | bytes 172064 | tf_op jit(solution)/shard_map/ppermute | solution.py:448
  119.5 1.0 blocks.5
  121.9 1.1 blocks.3
  123.1 1.3 collective-permute-start.16
  125.2 16.3 %collective-permute-done.16 = bf16[1,48,224]{2,1,0:T(8,128)(2,1)S(1)} collective-permute-done((bf16[1,48,224]{2,1,0:T(8,128)(2,1)S(1)}, bf16[1,48,224]{2,1,0:T(8,128)(2,1)S(1)}, u32[]{:S(2)}, u32[]{:S(2)}) %collective-permute-start.16) | collective-permute-done | bytes 21536 | tf_op jit(solution)/shard_map/ppermute | solution.py:469
  (59 shorter events, 11.3 us)
Async XLA Ops:
  0.7 0.9 copy-start.3
  1.7 0.9 copy-start.5
  2.6 0.7 copy-start.7
  3.3 0.7 copy-start.8
  4.0 0.7 copy-start.9
  6.0 18.8 %copy-start.1 = (bf16[1,3584,128]{2,1,0:T(8,128)(2,1)S(1)}, bf16[1,3584,128]{2,1,0:T(8,128)(2,1)}, u32[]{:S(2)}) copy-start(bf16[1,3584,128]{2,1,0:T(8,128)(2,1)} %param.16) | copy-start | bytes 2752516
  6.1 18.8 %copy-start.2 = (bf16[1,128,3584]{2,1,0:T(8,128)(2,1)S(1)}, bf16[1,128,3584]{2,1,0:T(8,128)(2,1)}, u32[]{:S(2)}) copy-start(bf16[1,128,3584]{2,1,0:T(8,128)(2,1)} %param.17) | copy-start | bytes 2752516
  23.4 1.5 %copy-start = (bf16[1,3584,128]{2,1,0:T(8,128)(2,1)S(1)}, bf16[1,3584,128]{2,1,0:T(8,128)(2,1)}, u32[]{:S(2)}) copy-start(bf16[1,3584,128]{2,1,0:T(8,128)(2,1)} %param.15) | copy-start | bytes 2752516
  25.2 9.0 %collective-permute-start.5 = (bf16[10752,128]{1,0:T(8,128)(2,1)S(1)}, bf16[10752,128]{1,0:T(8,128)(2,1)S(1)}, u32[]{:S(2)}, u32[]{:S(2)}) collective-permute-start(bf16[10752,128]{1,0:T(8,128)(2,1)S(1)} %pack.1), channel_id=1, source_target_pairs={{0,1},{1,0},{2,3},{3,2},{4,5},{5,4},{6,7},{7,6},{8,9},{9,8},{10,11... | collective-permute-start | bytes 8257544 | tf_op jit(solution)/shard_map/ppermute | solution.py:456
  27.1 15.9 %collective-permute-start.7 = (bf16[120,3584]{1,0:T(8,128)(2,1)S(1)}, bf16[120,3584]{1,0:T(8,128)(2,1)S(1)}, u32[]{:S(2)}, u32[]{:S(2)}) collective-permute-start(bf16[120,3584]{1,0:T(8,128)(2,1)S(1)} %get-tuple-element.23), channel_id=1, source_target_pairs={{0,2},{1,9},{2,4},{3,11},{4,6},{5,13},{6,0},{7,15},{8,10},{9,17},{... | collective-permute-start | bytes 2580488 | tf_op jit(solution)/shard_map/ppermute | solution.py:35
  30.5 23.2 %collective-permute-start.8 = (bf16[120,3584]{1,0:T(8,128)(2,1)S(1)}, bf16[120,3584]{1,0:T(8,128)(2,1)S(1)}, u32[]{:S(2)}, u32[]{:S(2)}) collective-permute-start(bf16[120,3584]{1,0:T(8,128)(2,1)S(1)} %get-tuple-element.24), channel_id=1, source_target_pairs={{0,6},{1,25},{2,0},{3,27},{4,2},{5,29},{6,4},{7,31},{8,14},{9,1},{... | collective-permute-start | bytes 2580488 | tf_op jit(solution)/shard_map/ppermute | solution.py:35
  36.8 26.1 %collective-permute-start.6 = (bf16[120,3584]{1,0:T(8,128)(2,1)S(1)}, bf16[120,3584]{1,0:T(8,128)(2,1)S(1)}, u32[]{:S(2)}, u32[]{:S(2)}) collective-permute-start(bf16[120,3584]{1,0:T(8,128)(2,1)S(1)} %far.1), channel_id=1, source_target_pairs={{0,4},{1,17},{2,6},{3,19},{4,0},{5,21},{6,2},{7,23},{8,12},{9,25},... | collective-permute-start | bytes 2580488 | tf_op jit(solution)/shard_map/ppermute | solution.py:35
  55.4 24.3 %collective-permute-start.10 = (bf16[120,3584]{1,0:T(8,128)(2,1)S(1)}, bf16[120,3584]{1,0:T(8,128)(2,1)S(1)}, u32[]{:S(2)}, u32[]{:S(2)}) collective-permute-start(bf16[120,3584]{1,0:T(8,128)(2,1)S(1)} %get-tuple-element.28), channel_id=1, source_target_pairs={{0,6},{1,25},{2,0},{3,27},{4,2},{5,29},{6,4},{7,31},{8,14},{9,1},{... | collective-permute-start | bytes 2580488 | tf_op jit(solution)/shard_map/ppermute | solution.py:35
  61.0 25.1 %collective-permute-start.11 = (bf16[120,3584]{1,0:T(8,128)(2,1)S(1)}, bf16[120,3584]{1,0:T(8,128)(2,1)S(1)}, u32[]{:S(2)}, u32[]{:S(2)}) collective-permute-start(bf16[120,3584]{1,0:T(8,128)(2,1)S(1)} %get-tuple-element.29), channel_id=1, source_target_pairs={{0,2},{1,9},{2,4},{3,11},{4,6},{5,13},{6,0},{7,15},{8,10},{9,17},{... | collective-permute-start | bytes 2580488 | tf_op jit(solution)/shard_map/ppermute | solution.py:35
  62.9 5.0 %copy-start.10 = (bf16[1,24,224]{2,1,0:T(8,128)(2,1)S(1)}, bf16[1,24,224]{2,1,0:T(8,128)(2,1)}, u32[]{:S(2)}) copy-start(bf16[1,24,224]{2,1,0:T(8,128)(2,1)} %param.12) | copy-start | bytes 32260
  62.9 5.0 %copy-start.11 = (bf16[1,24,224]{2,1,0:T(8,128)(2,1)S(1)}, bf16[1,24,224]{2,1,0:T(8,128)(2,1)}, u32[]{:S(2)}) copy-start(bf16[1,24,224]{2,1,0:T(8,128)(2,1)} %param.13) | copy-start | bytes 32260
  64.5 23.9 %collective-permute-start.9 = (bf16[120,3584]{1,0:T(8,128)(2,1)S(1)}, bf16[120,3584]{1,0:T(8,128)(2,1)S(1)}, u32[]{:S(2)}, u32[]{:S(2)}) collective-permute-start(bf16[120,3584]{1,0:T(8,128)(2,1)S(1)} %get-tuple-element.26), channel_id=1, source_target_pairs={{0,4},{1,17},{2,6},{3,19},{4,0},{5,21},{6,2},{7,23},{8,12},{9,25},... | collective-permute-start | bytes 2580488 | tf_op jit(solution)/shard_map/ppermute | solution.py:35
  67.9 1.3 collective-permute-start
  68.6 8.9 %collective-permute-start.1 = (bf16[1,48,224]{2,1,0:T(8,128)(2,1)S(1)}, bf16[1,48,224]{2,1,0:T(8,128)(2,1)S(1)}, u32[]{:S(2)}, u32[]{:S(2)}) collective-permute-start(bf16[1,48,224]{2,1,0:T(8,128)(2,1)S(1)} %get-tuple-element.34), channel_id=1, source_target_pairs={{64,0},{192,128},{416,480},{288,352},{65,1},{193,129},{417,481},{2... | collective-permute-start | bytes 64520 | tf_op jit(solution)/shard_map/ppermute | solution.py:463
  69.3 9.7 %collective-permute-start.2 = (bf16[1,48,224]{2,1,0:T(8,128)(2,1)S(1)}, bf16[1,48,224]{2,1,0:T(8,128)(2,1)S(1)}, u32[]{:S(2)}, u32[]{:S(2)}) collective-permute-start(bf16[1,48,224]{2,1,0:T(8,128)(2,1)S(1)} %get-tuple-element.34), channel_id=1, source_target_pairs={{96,0},{224,128},{384,480},{256,352},{97,1},{225,129},{385,481},{2... | collective-permute-start | bytes 64520 | tf_op jit(solution)/shard_map/ppermute | solution.py:463
  79.0 9.4 %collective-permute-start.3 = (bf16[4,48,224]{2,1,0:T(8,128)(2,1)S(1)}, bf16[4,48,224]{2,1,0:T(8,128)(2,1)S(1)}, u32[]{:S(2)}, u32[]{:S(2)}) collective-permute-start(bf16[4,48,224]{2,1,0:T(8,128)(2,1)S(1)} %pad_maximum_fusion), channel_id=1, source_target_pairs={{128,0},{352,480},{129,1},{353,481},{130,2},{354,482},{131,3},{355... | collective-permute-start | bytes 258056 | tf_op jit(solution)/shard_map/ppermute | solution.py:463
  90.4 16.3 %copy-start.4 = (bf16[1,24,3584]{2,1,0:T(8,128)(2,1)S(1)}, bf16[1,24,3584]{2,1,0:T(8,128)(2,1)}, u32[]{:S(2)}) copy-start(bf16[1,24,3584]{2,1,0:T(8,128)(2,1)} %param.10) | copy-start | bytes 516100
  90.4 16.3 %all-to-all-start.1 = ((bf16[4,48,3584]{2,1,0:T(8,128)(2,1)}), bf16[4,48,3584]{2,1,0:T(8,128)(2,1)S(1)}, u32[]{:S(2)}, u32[]{:S(2)}) async-start(bf16[4,48,3584]{2,1,0:T(8,128)(2,1)} %bitcast.14), calls=%async_computation.1 | async-start | bytes 2752512 | tf_op jit(solution)/shard_map/all_to_all | solution.py:49
  94.1 16.8 %copy-start.6 = (bf16[1,24,3584]{2,1,0:T(8,128)(2,1)S(1)}, bf16[1,24,3584]{2,1,0:T(8,128)(2,1)}, u32[]{:S(2)}) copy-start(bf16[1,24,3584]{2,1,0:T(8,128)(2,1)} %param.11) | copy-start | bytes 516100
  94.2 0.7 collective-permute-start.4
  108.0 8.5 %collective-permute-start.12 = (bf16[24,3584]{1,0:T(8,128)(2,1)S(1)}, bf16[24,3584]{1,0:T(8,128)(2,1)S(1)}, u32[]{:S(2)}, u32[]{:S(2)}) collective-permute-start(bf16[24,3584]{1,0:T(8,128)(2,1)S(1)} %finish.2.refs_4_.fwd_ref), channel_id=1, source_target_pairs={{0,32},{32,64},{64,96},{96,128},{128,160},{160,192},{192,224},{224... | collective-permute-start | bytes 516104 | tf_op jit(solution)/shard_map/ppermute | solution.py:448
  112.2 7.3 %collective-permute-start.13 = (bf16[24,3584]{1,0:T(8,128)(2,1)S(1)}, bf16[24,3584]{1,0:T(8,128)(2,1)S(1)}, u32[]{:S(2)}, u32[]{:S(2)}) collective-permute-start(bf16[24,3584]{1,0:T(8,128)(2,1)S(1)} %finish.3.bwd_ref), channel_id=1, source_target_pairs={{0,480},{32,0},{64,32},{96,64},{128,96},{160,128},{192,160},{224,1... | collective-permute-start | bytes 516104 | tf_op jit(solution)/shard_map/ppermute | solution.py:448
  120.6 0.7 collective-permute-start.14
  121.3 1.8 %collective-permute-start.15 = (bf16[2,48,224]{2,1,0:T(8,128)(2,1)S(1)}, bf16[2,48,224]{2,1,0:T(8,128)(2,1)S(1)}, u32[]{:S(2)}, u32[]{:S(2)}) collective-permute-start(bf16[2,48,224]{2,1,0:T(8,128)(2,1)S(1)} %slice_select_fusion.1), channel_id=1, source_target_pairs={{0,64},{128,192},{480,416},{352,288},{1,65},{129,193},{481,417},{3... | collective-permute-start | bytes 129032 | tf_op jit(solution)/shard_map/ppermute | solution.py:469
  123.1 18.3 %collective-permute-start.16 = (bf16[1,48,224]{2,1,0:T(8,128)(2,1)S(1)}, bf16[1,48,224]{2,1,0:T(8,128)(2,1)S(1)}, u32[]{:S(2)}, u32[]{:S(2)}) collective-permute-start(bf16[1,48,224]{2,1,0:T(8,128)(2,1)S(1)} %fusion.2), channel_id=1, source_target_pairs={{0,32},{64,96},{128,160},{192,224},{480,448},{416,384},{352,320},{... | collective-permute-start | bytes 64520 | tf_op jit(solution)/shard_map/ppermute | solution.py:469

commit v9 on v8

--- a/solution.py
+++ b/solution.py
@@ -251,6 +251,11 @@
         out_ref[:, cut] = (own_ref[:, cut].astype(F32) + mixture).astype(BF)
 
 
+def enter_kernel(place_ref, fwd_ref, bwd_ref, _, out_ref):
+    out_ref[:, :ROWS, :] = fwd_ref[...]
+    out_ref[:, ROWS:, :] = bwd_ref[...]
+
+
 def ends_fwd_kernel(place_ref, left_ref, fwd_ref, out_ref):
     count, _, part = out_ref.shape
     for r in range(count):
@@ -468,12 +473,13 @@
     def move(block, *pairs):
         return lax.ppermute(block, "pp", mirrored(list(pairs), sections))
 
+    first = move(own[1:2], (0, 1))
     a = move(own[4:8], (0, 4))
-    b = move(jnp.where(place == 0, own[2:4], a[2:4]), (0, 2), (4, 6))
-    c = jnp.where(place == 0, own[1:2], jnp.where(place == 4, a[1:2], b[1:2]))
-    c = move(c, (0, 1), (2, 3), (4, 5), (6, 7))
+    b = jnp.where(place == 0, own[2:4], jnp.where(place == 1, first, a[2:4]))
+    b = move(b, (0, 2), (4, 6))
+    c = move(jnp.where(place == 4, a[1:2], b[1:2]), (2, 3), (4, 5), (6, 7))
     mine = jnp.where(place == 0, own[0], jnp.where(place == 4, a[0], b[0]))
-    return jnp.where((place & 1) == 1, c[0], mine)
+    return jnp.where((place & 1) == 1, jnp.where(place == 1, first[0], c[0]), mine)
 
 
 def body(
@@ -506,15 +512,19 @@
     weights = own, from_other_core(make_pack(*own, pick))
     send0, back = make_rest(place, rows, pick, weights[1])
     done0, token = run_experts([send0], *weights)
-    last = hop(make_far(rows, pick, token), 2)
+    half = sections // 2
+    at_start = section == 0
+    entering = make_simple(
+        enter_kernel, (1, BOTH, part), place, enter_fwd, enter_bwd, before=(weights[1],)
+    )
+    held, got = inward(entering, 1, 2, sections)
+    last = hop(make_far(rows, pick, near, far, got, token), 2)
     done1, done3, token = run_experts([near, far], *weights)
     back1, back3 = hop(done1, -1), hop(done3, -3)
     done2, token = run_experts([last], *weights, token)
     back2 = hop(done2, -2)
 
-    half = sections // 2
-    at_start = section == 0
-    held, _ = inward(jnp.concatenate([enter_fwd, enter_bwd], axis=1), 1, 4, sections)
+    held, _ = inward(held, 2, 2, sections)
     held, got = inward(held, 4, 2, sections)
     begun = make_gather(back, [done0, back1, back3], (0, 1, 3))
     gathered = make_gather(back, [back2], (2,), begun, (got,))

time: 143 us -> 137 us (0.958)
  starting transfers between devices: 47.8 us -> 43.2 us
  waiting for transfers between devices: 51.4 us -> 49.5 us
    ppermute x4 -> x3, starting transfers between devices: 10.2 us -> 4.25 us  [inward(): got.append(lax.ppermute(held, 'pp', mirrored(pairs, sections)))]
    ppermute x4 -> x3, waiting for transfers between devices: 1.5 us -> 0.01 us  [inward(): got.append(lax.ppermute(held, 'pp', mirrored(pairs, sections)))]
    ppermute x3 -> x4, waiting for transfers between devices: 16.3 us -> 15.3 us  [move(): return lax.ppermute(block, 'pp', mirrored(list(pairs), sections))]
    ppermute x3 -> x4, starting transfers between devices: 2.62 us -> 3.29 us  [move(): return lax.ppermute(block, 'pp', mirrored(list(pairs), sections))]
    pallas_call x3 -> x4, Pallas kernels: 3.12 us -> 3.66 us  [make_simple(): pl.pallas_call(kernel, out_shape=jax.ShapeDtypeStruct(out, BF), in_specs=...]
    unnamed x28 -> x24, local copies, waits for them, and re-layouts: 3.97 us -> 3.95 us
  transfers between devices with their start and end apart: 18 -> 18, of which waited for: 8 -> 9; matrix products, arithmetic and copies ran while one was open for 1% -> 1% of each run, Pallas kernels for 8% -> 9%
where the time goes in v9:
time: 137 us; the launch traced here: 136 us
  waiting for transfers between devices  49.5 us (36%)
  starting transfers between devices  43.2 us (32%)
  Pallas kernels  19.4 us (14%)
  blocking collectives  17.3 us (13%)
  local copies, waits for them, and re-layouts  4.58 us (3%)
    ppermute x6, starting transfers between devices, hop(): return lax.ppermute(block, 'ep', route)  22.3 us
    ppermute x6, waiting for transfers between devices, hop(): return lax.ppermute(block, 'ep', route)  20.2 us
    all_to_all x1, blocking collectives, exchange(): lax.all_to_all(rows, 'ep', split_axis=0, concat_axis=0, axis_index_groups...  17.3 us
    ppermute x4, waiting for transfers between devices, move(): return lax.ppermute(block, 'pp', mirrored(list(pairs), sections))  15.3 us
    all_to_all x1, waiting for transfers between devices, exchange(): lax.all_to_all(rows, 'ep', split_axis=0, concat_axis=0, axis_index_groups...  11.8 us
    ppermute x2, starting transfers between devices, shifted(): lax.ppermute(block, 'pp', [(i, (i + distance) % count) for i in range(cou...  7.11 us
    pallas_call x2, Pallas kernels, make_gather(): pl.pallas_call(body, out_shape=shape(total, features, BF if last else F32...  4.31 us
    pallas_call x3, Pallas kernels, run_experts(): pl.pallas_call(body, out_shape=(shape(*blocks[0].shape),) * count + (shap...  4.26 us
  transfers between devices with their start and end apart: 18, of which 9 were waited for; matrix products, arithmetic and copies ran while one was open for 1% of the time, Pallas kernels for 9%

profile of v9, /device:TPU:256, one launch (start us, length us, event | category | flops | bytes accessed | tf_op | source)
XLA Modules:
  0.0 136.1 jit_solution(7946008691589691986)
XLA Ops:
  4.6 1.4 %normed.1 = (bf16[192,3712]{1,0:T(8,128)(2,1)S(1)}, f32[48,128]{1,0:T(8,128)S(1)}) custom-call(s32[3]{0:T(128)S(1)} %pad_add_fusion.place_ref.refs_0_, bf16[24,3584]{1,0:T(8,128)(2,1)S(1)} %bitcast.54, bf16[24,3584]{1,0:T(8,128)(2,1)S(1)} %bitcast.56, f32[1,3584]{1,0:T(1,128)S(1)} %copy-done.7, s32[2,2,24]{2,1,0:T(2,128)S(1)} %bitcast.58, ...), custom_call_target="tpu_custom_call" | custom-call | tf_op jit(solution)/shard_map/normed/pallas_call | solution.py:322
  6.1 17.3 %all_to_all.22 = bf16[4,48,3712]{2,1,0:T(8,128)(2,1)S(1)} all-to-all(bf16[4,48,3712]{2,1,0:T(8,128)(2,1)S(1)} %bitcast.53), channel_id=1, replica_groups={{0,8,16,24},{2,10,18,26},{4,12,20,28},{6,14,22,30},{1,3,5,7},{9,11,13,1..., dimensions={0} | all-to-all | bytes 2850816 | tf_op jit(solution)/shard_map/all_to_all | solution.py:49
  23.4 1.5 %near.1 = (bf16[120,3584]{1,0:T(8,128)(2,1)S(1)}, bf16[120,3584]{1,0:T(8,128)(2,1)S(1)}, bf16[512,192]{1,0:T(8,128)(2,1)S(1)}, s32[8,128]{1,0:T(8,128)}) custom-call(s32[3]{0:T(128)S(1)} %pad_add_fusion.place_ref.refs_0_, bf16[192,3712]{1,0:T(8,128)(2,1)S(1)} %bitcast.36), custom_call_target="tpu_custom_call" | custom-call | tf_op jit(solution)/shard_map/near/pallas_call | solution.py:335
  25.2 1.9 %collective-permute-start = (bf16[10752,128]{1,0:T(8,128)(2,1)S(1)}, bf16[10752,128]{1,0:T(8,128)(2,1)S(1)}, u32[]{:S(2)}, u32[]{:S(2)}) collective-permute-start(bf16[10752,128]{1,0:T(8,128)(2,1)S(1)} %pack.1), channel_id=1, source_target_pairs={{0,1},{1,0},{2,3},{3,2},{4,5},{5,4},{6,7},{7,6},{8,9},{9,8},{10,11... | collective-permute-start | bytes 8257544 | tf_op jit(solution)/shard_map/ppermute | solution.py:461
  27.1 3.4 %collective-permute-start.5 = (bf16[120,3584]{1,0:T(8,128)(2,1)S(1)}, bf16[120,3584]{1,0:T(8,128)(2,1)S(1)}, u32[]{:S(2)}, u32[]{:S(2)}) collective-permute-start(bf16[120,3584]{1,0:T(8,128)(2,1)S(1)} %get-tuple-element.21), channel_id=1, source_target_pairs={{0,2},{1,9},{2,4},{3,11},{4,6},{5,13},{6,0},{7,15},{8,10},{9,17},{... | collective-permute-start | bytes 2580488 | tf_op jit(solution)/shard_map/ppermute | solution.py:35
  30.5 3.7 %collective-permute-start.6 = (bf16[120,3584]{1,0:T(8,128)(2,1)S(1)}, bf16[120,3584]{1,0:T(8,128)(2,1)S(1)}, u32[]{:S(2)}, u32[]{:S(2)}) collective-permute-start(bf16[120,3584]{1,0:T(8,128)(2,1)S(1)} %get-tuple-element.22), channel_id=1, source_target_pairs={{0,6},{1,25},{2,0},{3,27},{4,2},{5,29},{6,4},{7,31},{8,14},{9,1},{... | collective-permute-start | bytes 2580488 | tf_op jit(solution)/shard_map/ppermute | solution.py:35
  34.8 2.9 %collective-permute-start.1 = (bf16[1,48,224]{2,1,0:T(8,128)(2,1)S(1)}, bf16[1,48,224]{2,1,0:T(8,128)(2,1)S(1)}, u32[]{:S(2)}, u32[]{:S(2)}) collective-permute-start(bf16[1,48,224]{2,1,0:T(8,128)(2,1)S(1)} %blocks.4), channel_id=1, source_target_pairs={{32,0},{96,64},{160,128},{224,192},{448,480},{384,416},{320,352},{... | collective-permute-start | bytes 64520 | tf_op jit(solution)/shard_map/ppermute | solution.py:468
  37.7 1.1 rest.1
  38.8 1.0 experts.3
  39.9 3.1 %collective-permute-done.5.refs_0_ = bf16[120,3584]{1,0:T(8,128)(2,1)S(1)} collective-permute-done((bf16[120,3584]{1,0:T(8,128)(2,1)S(1)}, bf16[120,3584]{1,0:T(8,128)(2,1)S(1)}, u32[]{:S(2)}, u32[]{:S(2)}) %collective-permute-start.5) | collective-permute-done | bytes 860192 | tf_op jit(solution)/shard_map/ppermute | solution.py:35
  43.0 2.2 %collective-permute-done.6.refs_1_ = bf16[120,3584]{1,0:T(8,128)(2,1)S(1)} collective-permute-done((bf16[120,3584]{1,0:T(8,128)(2,1)S(1)}, bf16[120,3584]{1,0:T(8,128)(2,1)S(1)}, u32[]{:S(2)}, u32[]{:S(2)}) %collective-permute-start.6) | collective-permute-done | bytes 860192 | tf_op jit(solution)/shard_map/ppermute | solution.py:35
  45.6 4.6 %collective-permute-start.7 = (bf16[120,3584]{1,0:T(8,128)(2,1)S(1)}, bf16[120,3584]{1,0:T(8,128)(2,1)S(1)}, u32[]{:S(2)}, u32[]{:S(2)}) collective-permute-start(bf16[120,3584]{1,0:T(8,128)(2,1)S(1)} %far.1), channel_id=1, source_target_pairs={{0,4},{1,17},{2,6},{3,19},{4,0},{5,21},{6,2},{7,23},{8,12},{9,25},... | collective-permute-start | bytes 2580488 | tf_op jit(solution)/shard_map/ppermute | solution.py:35
  50.3 1.7 %experts.4 = (bf16[120,3584]{1,0:T(8,128)(2,1)S(1)}, bf16[120,3584]{1,0:T(8,128)(2,1)S(1)}, s32[8,128]{1,0:T(8,128)S(1)}) custom-call(bf16[120,3584]{1,0:T(8,128)(2,1)S(1)} %collective-permute-done.5.refs_0_, bf16[120,3584]{1,0:T(8,128)(2,1)S(1)} %collective-permute-done.6.refs_1_, bf16[3584,128]{1,0:T(8,128)(2,1)S(1)} %bitcast.41, ...), custom_call_target="tpu_custom_call" | custom-call | tf_op jit(solution)/shard_map/experts/pallas_call | solution.py:399
  52.0 3.3 %collective-permute-start.9 = (bf16[120,3584]{1,0:T(8,128)(2,1)S(1)}, bf16[120,3584]{1,0:T(8,128)(2,1)S(1)}, u32[]{:S(2)}, u32[]{:S(2)}) collective-permute-start(bf16[120,3584]{1,0:T(8,128)(2,1)S(1)} %get-tuple-element.28), channel_id=1, source_target_pairs={{0,6},{1,25},{2,0},{3,27},{4,2},{5,29},{6,4},{7,31},{8,14},{9,1},{... | collective-permute-start | bytes 2580488 | tf_op jit(solution)/shard_map/ppermute | solution.py:35
  55.3 2.5 %collective-permute-start.10 = (bf16[120,3584]{1,0:T(8,128)(2,1)S(1)}, bf16[120,3584]{1,0:T(8,128)(2,1)S(1)}, u32[]{:S(2)}, u32[]{:S(2)}) collective-permute-start(bf16[120,3584]{1,0:T(8,128)(2,1)S(1)} %get-tuple-element.29), channel_id=1, source_target_pairs={{0,2},{1,9},{2,4},{3,11},{4,6},{5,13},{6,0},{7,15},{8,10},{9,17},{... | collective-permute-start | bytes 2580488 | tf_op jit(solution)/shard_map/ppermute | solution.py:35
  57.8 4.0 %collective-permute-done.7.refs_0_ = bf16[120,3584]{1,0:T(8,128)(2,1)S(1)} collective-permute-done((bf16[120,3584]{1,0:T(8,128)(2,1)S(1)}, bf16[120,3584]{1,0:T(8,128)(2,1)S(1)}, u32[]{:S(2)}, u32[]{:S(2)}) %collective-permute-start.7) | collective-permute-done | bytes 860192 | tf_op jit(solution)/shard_map/ppermute | solution.py:35
  61.8 1.5 %experts.5 = (bf16[120,3584]{1,0:T(8,128)(2,1)S(1)}, s32[8,128]{1,0:T(8,128)}) custom-call(bf16[120,3584]{1,0:T(8,128)(2,1)S(1)} %collective-permute-done.7.refs_0_, bf16[3584,128]{1,0:T(8,128)(2,1)S(1)} %bitcast.42, bf16[3584,128]{1,0:T(8,128)(2,1)S(1)} %bitcast.46, bf16[128,3584]{1,0:T(8,128)(2,1)S(1)} %bitcast.50, ...), custom_call_target="tpu_custom_call" | custom-call | tf_op jit(solution)/shard_map/experts/pallas_call | solution.py:399
  63.3 4.7 %collective-permute-start.8 = (bf16[120,3584]{1,0:T(8,128)(2,1)S(1)}, bf16[120,3584]{1,0:T(8,128)(2,1)S(1)}, u32[]{:S(2)}, u32[]{:S(2)}) collective-permute-start(bf16[120,3584]{1,0:T(8,128)(2,1)S(1)} %get-tuple-element.26), channel_id=1, source_target_pairs={{0,4},{1,17},{2,6},{3,19},{4,0},{5,21},{6,2},{7,23},{8,12},{9,25},... | collective-permute-start | bytes 2580488 | tf_op jit(solution)/shard_map/ppermute | solution.py:35
  69.5 1.8 %collective-permute-done.9.refs_2_ = bf16[120,3584]{1,0:T(8,128)(2,1)S(1)} collective-permute-done((bf16[120,3584]{1,0:T(8,128)(2,1)S(1)}, bf16[120,3584]{1,0:T(8,128)(2,1)S(1)}, u32[]{:S(2)}, u32[]{:S(2)}) %collective-permute-start.9) | collective-permute-done | bytes 860192 | tf_op jit(solution)/shard_map/ppermute | solution.py:35
  71.3 9.1 %collective-permute-done.10.refs_3_ = bf16[120,3584]{1,0:T(8,128)(2,1)S(1)} collective-permute-done((bf16[120,3584]{1,0:T(8,128)(2,1)S(1)}, bf16[120,3584]{1,0:T(8,128)(2,1)S(1)}, u32[]{:S(2)}, u32[]{:S(2)}) %collective-permute-start.10) | collective-permute-done | bytes 860192 | tf_op jit(solution)/shard_map/ppermute | solution.py:35
  80.4 2.3 %gather.2.refs_2_ = f32[192,3584]{1,0:T(8,128)S(1)} custom-call(bf16[192,1024]{1,0:T(8,128)(2,1)S(1)} %get-tuple-element.20.refs_0_, bf16[120,3584]{1,0:T(8,128)(2,1)S(1)} %get-tuple-element.27.refs_1_, bf16[120,3584]{1,0:T(8,128)(2,1)S(1)} %collective-permute-done.9.refs_2_, bf16[120,3584]{1,0:T(8,128)(2,1)S(1)} %collective-permute-done.10.refs_3_), custom_call_target="tpu_custom_call" | custom-call | tf_op jit(solution)/shard_map/gather/pallas_call | solution.py:417
  82.7 2.0 %gather.3 = bf16[192,3584]{1,0:T(8,128)(2,1)} custom-call(bf16[192,1024]{1,0:T(8,128)(2,1)S(1)} %get-tuple-element.20.refs_0_, bf16[120,3584]{1,0:T(8,128)(2,1)S(1)} %collective-permute-done.8.refs_1_, f32[192,3584]{1,0:T(8,128)S(1)} %gather.2.refs_2_, bf16[4,48,224]{2,1,0:T(8,128)(2,1)S(1)} %collective-permute-done.3.refs_3_), custom_call_target="tpu_custom_call" | custom-call | tf_op jit(solution)/shard_map/gather/pallas_call | solution.py:417
  84.8 3.7 %all-to-all-start.1 = ((bf16[4,48,3584]{2,1,0:T(8,128)(2,1)}), bf16[4,48,3584]{2,1,0:T(8,128)(2,1)S(1)}, u32[]{:S(2)}, u32[]{:S(2)}) async-start(bf16[4,48,3584]{2,1,0:T(8,128)(2,1)} %bitcast.14), calls=%async_computation.1 | async-start | bytes 2752512 | tf_op jit(solution)/shard_map/all_to_all | solution.py:49
  89.2 11.8 %all-to-all-done.1 = bf16[4,48,3584]{2,1,0:T(8,128)(2,1)S(1)} async-done(((bf16[4,48,3584]{2,1,0:T(8,128)(2,1)}), bf16[4,48,3584]{2,1,0:T(8,128)(2,1)S(1)}, u32[]{:S(2)}, u32[]{:S(2)}) %all-to-all-start.1) | async-done | bytes 1376288 | tf_op jit(solution)/shard_map/all_to_all | solution.py:49
  101.1 1.2 finish.2.refs_4_.fwd_ref
  102.3 3.0 %collective-permute-start.11 = (bf16[24,3584]{1,0:T(8,128)(2,1)S(1)}, bf16[24,3584]{1,0:T(8,128)(2,1)S(1)}, u32[]{:S(2)}, u32[]{:S(2)}) collective-permute-start(bf16[24,3584]{1,0:T(8,128)(2,1)S(1)} %finish.2.refs_4_.fwd_ref), channel_id=1, source_target_pairs={{0,32},{32,64},{64,96},{96,128},{128,160},{160,192},{192,224},{224... | collective-permute-start | bytes 516104 | tf_op jit(solution)/shard_map/ppermute | solution.py:453
  105.3 1.2 finish.3.bwd_ref
  106.5 4.2 %collective-permute-start.12 = (bf16[24,3584]{1,0:T(8,128)(2,1)S(1)}, bf16[24,3584]{1,0:T(8,128)(2,1)S(1)}, u32[]{:S(2)}, u32[]{:S(2)}) collective-permute-start(bf16[24,3584]{1,0:T(8,128)(2,1)S(1)} %finish.3.bwd_ref), channel_id=1, source_target_pairs={{0,480},{32,0},{64,32},{96,64},{128,96},{160,128},{192,160},{224,1... | collective-permute-start | bytes 516104 | tf_op jit(solution)/shard_map/ppermute | solution.py:453
  111.8 2.0 %collective-permute-done.12.right_ref = bf16[24,3584]{1,0:T(8,128)(2,1)S(1)} collective-permute-done((bf16[24,3584]{1,0:T(8,128)(2,1)S(1)}, bf16[24,3584]{1,0:T(8,128)(2,1)S(1)}, u32[]{:S(2)}, u32[]{:S(2)}) %collective-permute-start.12) | collective-permute-done | bytes 172064 | tf_op jit(solution)/shard_map/ppermute | solution.py:453
  117.0 1.1 blocks.5
  118.1 1.3 collective-permute-start.16
  120.2 15.3 %collective-permute-done.16 = bf16[1,48,224]{2,1,0:T(8,128)(2,1)S(1)} collective-permute-done((bf16[1,48,224]{2,1,0:T(8,128)(2,1)S(1)}, bf16[1,48,224]{2,1,0:T(8,128)(2,1)S(1)}, u32[]{:S(2)}, u32[]{:S(2)}) %collective-permute-start.16) | collective-permute-done | bytes 21536 | tf_op jit(solution)/shard_map/ppermute | solution.py:474
  (57 shorter events, 12.9 us)
Async XLA Ops:
  0.7 0.9 copy-start.3
  1.7 0.9 copy-start.5
  2.6 0.7 copy-start.7
  3.3 0.7 copy-start.10
  4.0 0.7 copy-start.11
  6.0 18.8 %copy-start.1 = (bf16[1,3584,128]{2,1,0:T(8,128)(2,1)S(1)}, bf16[1,3584,128]{2,1,0:T(8,128)(2,1)}, u32[]{:S(2)}) copy-start(bf16[1,3584,128]{2,1,0:T(8,128)(2,1)} %param.16) | copy-start | bytes 2752516
  6.1 18.8 %copy-start.2 = (bf16[1,128,3584]{2,1,0:T(8,128)(2,1)S(1)}, bf16[1,128,3584]{2,1,0:T(8,128)(2,1)}, u32[]{:S(2)}) copy-start(bf16[1,128,3584]{2,1,0:T(8,128)(2,1)} %param.17) | copy-start | bytes 2752516
  23.4 1.5 %copy-start = (bf16[1,3584,128]{2,1,0:T(8,128)(2,1)S(1)}, bf16[1,3584,128]{2,1,0:T(8,128)(2,1)}, u32[]{:S(2)}) copy-start(bf16[1,3584,128]{2,1,0:T(8,128)(2,1)} %param.15) | copy-start | bytes 2752516
  24.9 9.3 %copy-start.8 = (bf16[1,24,224]{2,1,0:T(8,128)(2,1)S(1)}, bf16[1,24,224]{2,1,0:T(8,128)(2,1)}, u32[]{:S(2)}) copy-start(bf16[1,24,224]{2,1,0:T(8,128)(2,1)} %fwd_ref.1) | copy-start | bytes 32260
  24.9 9.3 %copy-start.9 = (bf16[1,24,224]{2,1,0:T(8,128)(2,1)S(1)}, bf16[1,24,224]{2,1,0:T(8,128)(2,1)}, u32[]{:S(2)}) copy-start(bf16[1,24,224]{2,1,0:T(8,128)(2,1)} %bwd_ref.1) | copy-start | bytes 32260
  25.2 9.0 %collective-permute-start = (bf16[10752,128]{1,0:T(8,128)(2,1)S(1)}, bf16[10752,128]{1,0:T(8,128)(2,1)S(1)}, u32[]{:S(2)}, u32[]{:S(2)}) collective-permute-start(bf16[10752,128]{1,0:T(8,128)(2,1)S(1)} %pack.1), channel_id=1, source_target_pairs={{0,1},{1,0},{2,3},{3,2},{4,5},{5,4},{6,7},{7,6},{8,9},{9,8},{10,11... | collective-permute-start | bytes 8257544 | tf_op jit(solution)/shard_map/ppermute | solution.py:461
  27.1 15.9 %collective-permute-start.5 = (bf16[120,3584]{1,0:T(8,128)(2,1)S(1)}, bf16[120,3584]{1,0:T(8,128)(2,1)S(1)}, u32[]{:S(2)}, u32[]{:S(2)}) collective-permute-start(bf16[120,3584]{1,0:T(8,128)(2,1)S(1)} %get-tuple-element.21), channel_id=1, source_target_pairs={{0,2},{1,9},{2,4},{3,11},{4,6},{5,13},{6,0},{7,15},{8,10},{9,17},{... | collective-permute-start | bytes 2580488 | tf_op jit(solution)/shard_map/ppermute | solution.py:35
  30.5 14.7 %collective-permute-start.6 = (bf16[120,3584]{1,0:T(8,128)(2,1)S(1)}, bf16[120,3584]{1,0:T(8,128)(2,1)S(1)}, u32[]{:S(2)}, u32[]{:S(2)}) collective-permute-start(bf16[120,3584]{1,0:T(8,128)(2,1)S(1)} %get-tuple-element.22), channel_id=1, source_target_pairs={{0,6},{1,25},{2,0},{3,27},{4,2},{5,29},{6,4},{7,31},{8,14},{9,1},{... | collective-permute-start | bytes 2580488 | tf_op jit(solution)/shard_map/ppermute | solution.py:35
  34.8 10.4 %collective-permute-start.1 = (bf16[1,48,224]{2,1,0:T(8,128)(2,1)S(1)}, bf16[1,48,224]{2,1,0:T(8,128)(2,1)S(1)}, u32[]{:S(2)}, u32[]{:S(2)}) collective-permute-start(bf16[1,48,224]{2,1,0:T(8,128)(2,1)S(1)} %blocks.4), channel_id=1, source_target_pairs={{32,0},{96,64},{160,128},{224,192},{448,480},{384,416},{320,352},{... | collective-permute-start | bytes 64520 | tf_op jit(solution)/shard_map/ppermute | solution.py:468
  45.6 16.2 %collective-permute-start.7 = (bf16[120,3584]{1,0:T(8,128)(2,1)S(1)}, bf16[120,3584]{1,0:T(8,128)(2,1)S(1)}, u32[]{:S(2)}, u32[]{:S(2)}) collective-permute-start(bf16[120,3584]{1,0:T(8,128)(2,1)S(1)} %far.1), channel_id=1, source_target_pairs={{0,4},{1,17},{2,6},{3,19},{4,0},{5,21},{6,2},{7,23},{8,12},{9,25},... | collective-permute-start | bytes 2580488 | tf_op jit(solution)/shard_map/ppermute | solution.py:35
  52.0 19.4 %collective-permute-start.9 = (bf16[120,3584]{1,0:T(8,128)(2,1)S(1)}, bf16[120,3584]{1,0:T(8,128)(2,1)S(1)}, u32[]{:S(2)}, u32[]{:S(2)}) collective-permute-start(bf16[120,3584]{1,0:T(8,128)(2,1)S(1)} %get-tuple-element.28), channel_id=1, source_target_pairs={{0,6},{1,25},{2,0},{3,27},{4,2},{5,29},{6,4},{7,31},{8,14},{9,1},{... | collective-permute-start | bytes 2580488 | tf_op jit(solution)/shard_map/ppermute | solution.py:35
  55.3 25.1 %collective-permute-start.10 = (bf16[120,3584]{1,0:T(8,128)(2,1)S(1)}, bf16[120,3584]{1,0:T(8,128)(2,1)S(1)}, u32[]{:S(2)}, u32[]{:S(2)}) collective-permute-start(bf16[120,3584]{1,0:T(8,128)(2,1)S(1)} %get-tuple-element.29), channel_id=1, source_target_pairs={{0,2},{1,9},{2,4},{3,11},{4,6},{5,13},{6,0},{7,15},{8,10},{9,17},{... | collective-permute-start | bytes 2580488 | tf_op jit(solution)/shard_map/ppermute | solution.py:35
  63.3 19.4 %collective-permute-start.8 = (bf16[120,3584]{1,0:T(8,128)(2,1)S(1)}, bf16[120,3584]{1,0:T(8,128)(2,1)S(1)}, u32[]{:S(2)}, u32[]{:S(2)}) collective-permute-start(bf16[120,3584]{1,0:T(8,128)(2,1)S(1)} %get-tuple-element.26), channel_id=1, source_target_pairs={{0,4},{1,17},{2,6},{3,19},{4,0},{5,21},{6,2},{7,23},{8,12},{9,25},... | collective-permute-start | bytes 2580488 | tf_op jit(solution)/shard_map/ppermute | solution.py:35
  68.1 0.7 collective-permute-start.2
  68.8 13.9 %collective-permute-start.3 = (bf16[4,48,224]{2,1,0:T(8,128)(2,1)S(1)}, bf16[4,48,224]{2,1,0:T(8,128)(2,1)S(1)}, u32[]{:S(2)}, u32[]{:S(2)}) collective-permute-start(bf16[4,48,224]{2,1,0:T(8,128)(2,1)S(1)} %pad_maximum_fusion.1), channel_id=1, source_target_pairs={{128,0},{352,480},{129,1},{353,481},{130,2},{354,482},{131,3},{355... | collective-permute-start | bytes 258056 | tf_op jit(solution)/shard_map/ppermute | solution.py:468
  84.8 16.3 %copy-start.4 = (bf16[1,24,3584]{2,1,0:T(8,128)(2,1)S(1)}, bf16[1,24,3584]{2,1,0:T(8,128)(2,1)}, u32[]{:S(2)}) copy-start(bf16[1,24,3584]{2,1,0:T(8,128)(2,1)} %param.10) | copy-start | bytes 516100
  84.8 16.3 %all-to-all-start.1 = ((bf16[4,48,3584]{2,1,0:T(8,128)(2,1)}), bf16[4,48,3584]{2,1,0:T(8,128)(2,1)S(1)}, u32[]{:S(2)}, u32[]{:S(2)}) async-start(bf16[4,48,3584]{2,1,0:T(8,128)(2,1)} %bitcast.14), calls=%async_computation.1 | async-start | bytes 2752512 | tf_op jit(solution)/shard_map/all_to_all | solution.py:49
  88.4 16.8 %copy-start.6 = (bf16[1,24,3584]{2,1,0:T(8,128)(2,1)S(1)}, bf16[1,24,3584]{2,1,0:T(8,128)(2,1)}, u32[]{:S(2)}) copy-start(bf16[1,24,3584]{2,1,0:T(8,128)(2,1)} %param.11) | copy-start | bytes 516100
  88.5 0.7 collective-permute-start.4
  102.3 8.5 %collective-permute-start.11 = (bf16[24,3584]{1,0:T(8,128)(2,1)S(1)}, bf16[24,3584]{1,0:T(8,128)(2,1)S(1)}, u32[]{:S(2)}, u32[]{:S(2)}) collective-permute-start(bf16[24,3584]{1,0:T(8,128)(2,1)S(1)} %finish.2.refs_4_.fwd_ref), channel_id=1, source_target_pairs={{0,32},{32,64},{64,96},{96,128},{128,160},{160,192},{192,224},{224... | collective-permute-start | bytes 516104 | tf_op jit(solution)/shard_map/ppermute | solution.py:453
  106.5 7.3 %collective-permute-start.12 = (bf16[24,3584]{1,0:T(8,128)(2,1)S(1)}, bf16[24,3584]{1,0:T(8,128)(2,1)S(1)}, u32[]{:S(2)}, u32[]{:S(2)}) collective-permute-start(bf16[24,3584]{1,0:T(8,128)(2,1)S(1)} %finish.3.bwd_ref), channel_id=1, source_target_pairs={{0,480},{32,0},{64,32},{96,64},{128,96},{160,128},{192,160},{224,1... | collective-permute-start | bytes 516104 | tf_op jit(solution)/shard_map/ppermute | solution.py:453
  114.9 1.4 %collective-permute-start.14 = (bf16[4,48,224]{2,1,0:T(8,128)(2,1)S(1)}, bf16[4,48,224]{2,1,0:T(8,128)(2,1)S(1)}, u32[]{:S(2)}, u32[]{:S(2)}) collective-permute-start(bf16[4,48,224]{2,1,0:T(8,128)(2,1)S(1)} %slice.55), channel_id=1, source_target_pairs={{0,128},{480,352},{1,129},{481,353},{2,130},{482,354},{3,131},{483... | collective-permute-start | bytes 258056 | tf_op jit(solution)/shard_map/ppermute | solution.py:474
  115.6 0.7 collective-permute-start.13
  116.3 1.8 %collective-permute-start.15 = (bf16[2,48,224]{2,1,0:T(8,128)(2,1)S(1)}, bf16[2,48,224]{2,1,0:T(8,128)(2,1)S(1)}, u32[]{:S(2)}, u32[]{:S(2)}) collective-permute-start(bf16[2,48,224]{2,1,0:T(8,128)(2,1)S(1)} %fusion), channel_id=1, source_target_pairs={{0,64},{128,192},{480,416},{352,288},{1,65},{129,193},{481,417},{3... | collective-permute-start | bytes 129032 | tf_op jit(solution)/shard_map/ppermute | solution.py:474
  118.1 17.3 %collective-permute-start.16 = (bf16[1,48,224]{2,1,0:T(8,128)(2,1)S(1)}, bf16[1,48,224]{2,1,0:T(8,128)(2,1)S(1)}, u32[]{:S(2)}, u32[]{:S(2)}) collective-permute-start(bf16[1,48,224]{2,1,0:T(8,128)(2,1)S(1)} %slice_select_fusion.3), channel_id=1, source_target_pairs={{64,96},{128,160},{192,224},{416,384},{352,320},{288,256},{65,97},... | collective-permute-start | bytes 64520 | tf_op jit(solution)/shard_map/ppermute | solution.py:474

commit v10 on v9

--- a/solution.py
+++ b/solution.py
@@ -223,9 +223,7 @@
         out_ref[:, cut] = total.astype(out_ref.dtype)
 
 
-def finish_kernel(direction, place_ref, meta_ref, rows_ref, own_ref, *refs):
-    out_ref = refs[-1]
-    mine = slice(direction * ROWS, (direction + 1) * ROWS)
+def finish_kernel(place_ref, meta_ref, rows_ref, fwd_ref, bwd_ref, _, of_ref, ob_ref, leave_ref):
     meta = meta_ref[...]
     total = EXPERTS * BOTH
     column = iota((BOTH, total), 1)
@@ -241,14 +239,19 @@
         same = same | (column == row + part * BOTH)
     ones = jnp.where(same, 1.0, 0.0)
     on_first = place_ref[0] == 0
-    high = jnp.where(on_first, high, ones)[mine].astype(BF)
-    low = jnp.where(on_first, low, 0.0)[mine].astype(BF)
-    width = own_ref.shape[1]
+    high = jnp.where(on_first, high, ones).astype(BF)
+    low = jnp.where(on_first, low, 0.0).astype(BF)
+    at_start = place_ref[2] == 0
+    width = fwd_ref.shape[1]
     for start in range(0, width, CHUNK):
         cut = slice(start, min(start + CHUNK, width))
         rows = rows_ref[:, cut]
         mixture = dot(high, rows) + dot(low, rows)
-        out_ref[:, cut] = (own_ref[:, cut].astype(F32) + mixture).astype(BF)
+        forward = fwd_ref[:, cut].astype(F32) + mixture[:ROWS]
+        backward = bwd_ref[:, cut].astype(F32) + mixture[ROWS:]
+        of_ref[:, cut] = forward.astype(BF)
+        ob_ref[:, cut] = backward.astype(BF)
+        leave_ref[:, cut] = jnp.where(at_start, backward, forward).astype(BF)
 
 
 def enter_kernel(place_ref, fwd_ref, bwd_ref, _, out_ref):
@@ -256,33 +259,20 @@
     out_ref[:, ROWS:, :] = bwd_ref[...]
 
 
-def ends_fwd_kernel(place_ref, left_ref, fwd_ref, out_ref):
+def ends_kernel(place_ref, own_ref, other_ref, out_ref):
     count, _, part = out_ref.shape
     for r in range(count):
         near, far = [slice(j * part, (j + 1) * part) for j in (r, 2 * count - 1 - r)]
 
         @pl.when(place_ref[2] == 0)
         def _():
-            out_ref[r] = left_ref[:, near]
+            out_ref[r, :ROWS, :] = other_ref[:, near]
+            out_ref[r, ROWS:, :] = own_ref[:, near]
 
         @pl.when(place_ref[2] != 0)
         def _():
-            out_ref[r] = fwd_ref[:, far]
-
-
-def ends_kernel(place_ref, fwds_ref, right_ref, bwd_ref, out_ref):
-    count, _, part = out_ref.shape
-    for r in range(count):
-        near, far = [slice(j * part, (j + 1) * part) for j in (r, 2 * count - 1 - r)]
-        out_ref[r, :ROWS, :] = fwds_ref[r]
-
-        @pl.when(place_ref[2] == 0)
-        def _():
-            out_ref[r, ROWS:, :] = bwd_ref[:, near]
-
-        @pl.when(place_ref[2] != 0)
-        def _():
-            out_ref[r, ROWS:, :] = right_ref[:, far]
+            out_ref[r, :ROWS, :] = own_ref[:, far]
+            out_ref[r, ROWS:, :] = other_ref[:, far]
 
 
 def entered_kernel(place_ref, held_ref, got_ref, out_ref):
@@ -424,18 +414,15 @@
     )(back, *blocks, *([so_far] if last else []), *before)
 
 
-def make_finish(direction, place, meta, rows, own, *before):
-    def body(*refs):
-        finish_kernel(direction, *refs)
-
-    return pl.pallas_call(
-        body,
-        out_shape=shape(*own.shape),
-        in_specs=[SMEM] + [VMEM] * 3 + [ANY] * len(before),
-        out_specs=VMEM,
+def make_finish(place, meta, rows, fwd, bwd, before):
+    return pl.pallas_call(
+        finish_kernel,
+        out_shape=(shape(*fwd.shape),) * 3,
+        in_specs=[SMEM] + [VMEM] * 4 + [ANY],
+        out_specs=(VMEM,) * 3,
         compiler_params=params(),
         name="finish",
-    )(place, meta, rows, own, *before)
+    )(place, meta, rows, fwd, bwd, before)
 
 
 def make_simple(kernel, out, place, *arrays, before=()):
@@ -450,7 +437,12 @@
 
 
 def shifted(block, distance, count):
-    return lax.ppermute(block, "pp", [(i, (i + distance) % count) for i in range(count)])
+    route = [(i, i + distance) for i in range(count) if 0 <= i + distance < count]
+    return lax.ppermute(block, "pp", route)
+
+
+def swapped(block, count):
+    return lax.ppermute(block, "pp", [(0, count - 1), (count - 1, 0)])
 
 
 def mirrored(pairs, sections):
@@ -473,13 +465,11 @@
     def move(block, *pairs):
         return lax.ppermute(block, "pp", mirrored(list(pairs), sections))
 
-    first = move(own[1:2], (0, 1))
-    a = move(own[4:8], (0, 4))
-    b = jnp.where(place == 0, own[2:4], jnp.where(place == 1, first, a[2:4]))
-    b = move(b, (0, 2), (4, 6))
-    c = move(jnp.where(place == 4, a[1:2], b[1:2]), (2, 3), (4, 5), (6, 7))
-    mine = jnp.where(place == 0, own[0], jnp.where(place == 4, a[0], b[0]))
-    return jnp.where((place & 1) == 1, jnp.where(place == 1, first[0], c[0]), mine)
+    to4, to6, to2 = [move(own[r : r + 2], (0, r)) for r in (4, 6, 2)]
+    pair = jnp.where(place >= 6, to6, jnp.where(place >= 4, to4, to2))
+    pair = jnp.where(place < 2, own[:2], pair)
+    odd = move(pair[1:], (0, 1), (2, 3), (4, 5), (6, 7))
+    return jnp.where((place & 1) == 1, odd[0], pair[0])
 
 
 def body(
@@ -529,18 +519,14 @@
     begun = make_gather(back, [done0, back1, back3], (0, 1, 3))
     gathered = make_gather(back, [back2], (2,), begun, (got,))
     passed_on = jnp.where(at_start, held[:, ROWS:], held[:, :ROWS])
-    got = lax.ppermute(passed_on, "pp", [(0, sections - 1), (sections - 1, 0)])
+    got = swapped(passed_on, sections)
     rows = exchange(gathered)
-    fwd_out = make_finish(0, place, meta, rows, fwd, got)
-    bwd_out = make_finish(1, place, meta, rows, bwd, fwd_out)
-    from_right = shifted(bwd_out, -1, sections)
-    from_left = shifted(fwd_out, 1, sections)
-    entered = make_simple(
-        entered_kernel, (ROWS, features), place, held, got
-    )
-    fwds = make_simple(ends_fwd_kernel, (half, ROWS, part), place, from_left, fwd_out)
-    ends = make_simple(ends_kernel, (half, BOTH, part), place, fwds, from_right, bwd_out)
+    fwd_out, bwd_out, leaving = make_finish(place, meta, rows, fwd, bwd, got)
+    entered = make_simple(entered_kernel, (ROWS, features), place, held, got)
+    other = swapped(leaving, sections)
+    ends = make_simple(ends_kernel, (half, BOTH, part), place, leaving, other)
     mine = outward(ends, jnp.minimum(section, sections - 1 - section), sections)
+    from_left, from_right = shifted(fwd_out, 1, sections), shifted(bwd_out, -1, sections)
     fwd_next = jnp.where(at_start, entered, from_left)
     bwd_next = jnp.where(section == sections - 1, entered, from_right)
     return (fwd_next[None], bwd_next[None], mine[None, :ROWS], mine[None, ROWS:])

time: 137 us -> 137 us (level)
  the two profiles are of different devices: /device:TPU:256 before, /device:TPU:32 now
where the time goes in v10:
time: 137 us
  starting transfers between devices  61.9 us (45%)
  waiting for transfers between devices  33.5 us (24%)
  blocking collectives  17.3 us (13%)
  Pallas kernels  17.2 us (13%)
  local copies, waits for them, and re-layouts  4.57 us (3%)
    ppermute x2, starting transfers between devices, shifted(): return lax.ppermute(block, 'pp', route)  22.6 us
    ppermute x6, starting transfers between devices, hop(): return lax.ppermute(block, 'ep', route)  22.2 us
    ppermute x6, waiting for transfers between devices, hop(): return lax.ppermute(block, 'ep', route)  17.6 us
    all_to_all x1, blocking collectives, exchange(): lax.all_to_all(rows, 'ep', split_axis=0, concat_axis=0, axis_index_groups...  17.3 us
    all_to_all x1, waiting for transfers between devices, exchange(): lax.all_to_all(rows, 'ep', split_axis=0, concat_axis=0, axis_index_groups...  11.8 us
    ppermute x3, starting transfers between devices, inward(): got.append(lax.ppermute(held, 'pp', mirrored(pairs, sections)))  6.89 us
    pallas_call x2, Pallas kernels, make_gather(): pl.pallas_call(body, out_shape=shape(total, features, BF if last else F32...  4.31 us
    pallas_call x3, Pallas kernels, run_experts(): pl.pallas_call(body, out_shape=(shape(*blocks[0].shape),) * count + (shap...  4.27 us
  transfers between devices with their start and end apart: 19, of which 7 were waited for; matrix products, arithmetic and copies ran while one was open for 1% of the time, Pallas kernels for 7%

profile of v10, /device:TPU:32, one launch (start us, length us, event | category | flops | bytes accessed | tf_op | source)
XLA Modules:
  0.0 136.6 jit_solution(6347371319716840509)
XLA Ops:
  0.7 0.9 copy-done.3
  1.7 0.9 copy-done.5
  4.6 1.4 %normed.1 = (bf16[192,3712]{1,0:T(8,128)(2,1)S(1)}, f32[48,128]{1,0:T(8,128)S(1)}) custom-call(s32[3]{0:T(128)S(1)} %pad_add_fusion.place_ref, bf16[24,3584]{1,0:T(8,128)(2,1)S(1)} %bitcast.39, bf16[24,3584]{1,0:T(8,128)(2,1)S(1)} %bitcast.41, f32[1,3584]{1,0:T(1,128)S(1)} %copy-done.7, s32[2,2,24]{2,1,0:T(2,128)S(1)} %bitcast.43, f32[2,2,24]{2,1,0:T(2,128)S(1)} %bitcast.44), custom_call_target="tpu_custom_call" | custom-call | tf_op jit(solution)/shard_map/normed/pallas_call | solution.py:312
  6.1 17.3 %all_to_all.22 = bf16[4,48,3712]{2,1,0:T(8,128)(2,1)S(1)} all-to-all(bf16[4,48,3712]{2,1,0:T(8,128)(2,1)S(1)} %bitcast.38), channel_id=1, replica_groups={{0,8,16,24},{2,10,18,26},{4,12,20,28},{6,14,22,30},{1,3,5,7},{9,11,13,1..., dimensions={0} | all-to-all | bytes 2850816 | tf_op jit(solution)/shard_map/all_to_all | solution.py:49
  23.4 1.5 %near.1 = (bf16[120,3584]{1,0:T(8,128)(2,1)S(1)}, bf16[120,3584]{1,0:T(8,128)(2,1)S(1)}, bf16[512,192]{1,0:T(8,128)(2,1)S(1)}, s32[8,128]{1,0:T(8,128)}) custom-call(s32[3]{0:T(128)S(1)} %pad_add_fusion.place_ref, bf16[192,3712]{1,0:T(8,128)(2,1)S(1)} %bitcast.22), custom_call_target="tpu_custom_call" | custom-call | tf_op jit(solution)/shard_map/near/pallas_call | solution.py:325
  25.2 1.9 %collective-permute-start = (bf16[10752,128]{1,0:T(8,128)(2,1)S(1)}, bf16[10752,128]{1,0:T(8,128)(2,1)S(1)}, u32[]{:S(2)}, u32[]{:S(2)}) collective-permute-start(bf16[10752,128]{1,0:T(8,128)(2,1)S(1)} %pack.1), channel_id=1, source_target_pairs={{0,1},{1,0},{2,3},{3,2},{4,5},{5,4},{6,7},{7,6},{8,9},{9,8},{10,11... | collective-permute-start | bytes 8257544 | tf_op jit(solution)/shard_map/ppermute | solution.py:453
  27.1 3.4 %collective-permute-start.5 = (bf16[120,3584]{1,0:T(8,128)(2,1)S(1)}, bf16[120,3584]{1,0:T(8,128)(2,1)S(1)}, u32[]{:S(2)}, u32[]{:S(2)}) collective-permute-start(bf16[120,3584]{1,0:T(8,128)(2,1)S(1)} %get-tuple-element.24), channel_id=1, source_target_pairs={{0,2},{1,9},{2,4},{3,11},{4,6},{5,13},{6,0},{7,15},{8,10},{9,17},{... | collective-permute-start | bytes 2580488 | tf_op jit(solution)/shard_map/ppermute | solution.py:35
  30.5 3.7 %collective-permute-start.6 = (bf16[120,3584]{1,0:T(8,128)(2,1)S(1)}, bf16[120,3584]{1,0:T(8,128)(2,1)S(1)}, u32[]{:S(2)}, u32[]{:S(2)}) collective-permute-start(bf16[120,3584]{1,0:T(8,128)(2,1)S(1)} %get-tuple-element.25), channel_id=1, source_target_pairs={{0,6},{1,25},{2,0},{3,27},{4,2},{5,29},{6,4},{7,31},{8,14},{9,1},{... | collective-permute-start | bytes 2580488 | tf_op jit(solution)/shard_map/ppermute | solution.py:35
  34.8 5.6 %collective-permute-start.1 = (bf16[1,48,224]{2,1,0:T(8,128)(2,1)S(1)}, bf16[1,48,224]{2,1,0:T(8,128)(2,1)S(1)}, u32[]{:S(2)}, u32[]{:S(2)}) collective-permute-start(bf16[1,48,224]{2,1,0:T(8,128)(2,1)S(1)} %blocks.3), channel_id=1, source_target_pairs={{32,0},{96,64},{160,128},{224,192},{448,480},{384,416},{320,352},{... | collective-permute-start | bytes 64520 | tf_op jit(solution)/shard_map/ppermute | solution.py:460
  40.3 1.1 rest.1
  41.5 1.0 experts.3
  43.0 2.2 %collective-permute-done.6.refs_1_ = bf16[120,3584]{1,0:T(8,128)(2,1)S(1)} collective-permute-done((bf16[120,3584]{1,0:T(8,128)(2,1)S(1)}, bf16[120,3584]{1,0:T(8,128)(2,1)S(1)}, u32[]{:S(2)}, u32[]{:S(2)}) %collective-permute-start.6) | collective-permute-done | bytes 860192 | tf_op jit(solution)/shard_map/ppermute | solution.py:35
  45.6 4.6 %collective-permute-start.7 = (bf16[120,3584]{1,0:T(8,128)(2,1)S(1)}, bf16[120,3584]{1,0:T(8,128)(2,1)S(1)}, u32[]{:S(2)}, u32[]{:S(2)}) collective-permute-start(bf16[120,3584]{1,0:T(8,128)(2,1)S(1)} %far.1), channel_id=1, source_target_pairs={{0,4},{1,17},{2,6},{3,19},{4,0},{5,21},{6,2},{7,23},{8,12},{9,25},... | collective-permute-start | bytes 2580488 | tf_op jit(solution)/shard_map/ppermute | solution.py:35
  50.3 1.7 %experts.4 = (bf16[120,3584]{1,0:T(8,128)(2,1)S(1)}, bf16[120,3584]{1,0:T(8,128)(2,1)S(1)}, s32[8,128]{1,0:T(8,128)S(1)}) custom-call(bf16[120,3584]{1,0:T(8,128)(2,1)S(1)} %collective-permute-done.5.refs_0_, bf16[120,3584]{1,0:T(8,128)(2,1)S(1)} %collective-permute-done.6.refs_1_, bf16[3584,128]{1,0:T(8,128)(2,1)S(1)} %bitcast.27, ...), custom_call_target="tpu_custom_call" | custom-call | tf_op jit(solution)/shard_map/experts/pallas_call | solution.py:389
  52.0 3.3 %collective-permute-start.9 = (bf16[120,3584]{1,0:T(8,128)(2,1)S(1)}, bf16[120,3584]{1,0:T(8,128)(2,1)S(1)}, u32[]{:S(2)}, u32[]{:S(2)}) collective-permute-start(bf16[120,3584]{1,0:T(8,128)(2,1)S(1)} %get-tuple-element.31), channel_id=1, source_target_pairs={{0,6},{1,25},{2,0},{3,27},{4,2},{5,29},{6,4},{7,31},{8,14},{9,1},{... | collective-permute-start | bytes 2580488 | tf_op jit(solution)/shard_map/ppermute | solution.py:35
  55.3 2.5 %collective-permute-start.10 = (bf16[120,3584]{1,0:T(8,128)(2,1)S(1)}, bf16[120,3584]{1,0:T(8,128)(2,1)S(1)}, u32[]{:S(2)}, u32[]{:S(2)}) collective-permute-start(bf16[120,3584]{1,0:T(8,128)(2,1)S(1)} %get-tuple-element.32), channel_id=1, source_target_pairs={{0,2},{1,9},{2,4},{3,11},{4,6},{5,13},{6,0},{7,15},{8,10},{9,17},{... | collective-permute-start | bytes 2580488 | tf_op jit(solution)/shard_map/ppermute | solution.py:35
  57.8 4.0 %collective-permute-done.7.refs_0_ = bf16[120,3584]{1,0:T(8,128)(2,1)S(1)} collective-permute-done((bf16[120,3584]{1,0:T(8,128)(2,1)S(1)}, bf16[120,3584]{1,0:T(8,128)(2,1)S(1)}, u32[]{:S(2)}, u32[]{:S(2)}) %collective-permute-start.7) | collective-permute-done | bytes 860192 | tf_op jit(solution)/shard_map/ppermute | solution.py:35
  61.8 1.5 %experts.5 = (bf16[120,3584]{1,0:T(8,128)(2,1)S(1)}, s32[8,128]{1,0:T(8,128)}) custom-call(bf16[120,3584]{1,0:T(8,128)(2,1)S(1)} %collective-permute-done.7.refs_0_, bf16[3584,128]{1,0:T(8,128)(2,1)S(1)} %bitcast.28, bf16[3584,128]{1,0:T(8,128)(2,1)S(1)} %bitcast.32, bf16[128,3584]{1,0:T(8,128)(2,1)S(1)} %bitcast.36, ...), custom_call_target="tpu_custom_call" | custom-call | tf_op jit(solution)/shard_map/experts/pallas_call | solution.py:389
  63.3 4.7 %collective-permute-start.8 = (bf16[120,3584]{1,0:T(8,128)(2,1)S(1)}, bf16[120,3584]{1,0:T(8,128)(2,1)S(1)}, u32[]{:S(2)}, u32[]{:S(2)}) collective-permute-start(bf16[120,3584]{1,0:T(8,128)(2,1)S(1)} %get-tuple-element.29), channel_id=1, source_target_pairs={{0,4},{1,17},{2,6},{3,19},{4,0},{5,21},{6,2},{7,23},{8,12},{9,25},... | collective-permute-start | bytes 2580488 | tf_op jit(solution)/shard_map/ppermute | solution.py:35
  69.5 1.9 %collective-permute-done.9.refs_2_ = bf16[120,3584]{1,0:T(8,128)(2,1)S(1)} collective-permute-done((bf16[120,3584]{1,0:T(8,128)(2,1)S(1)}, bf16[120,3584]{1,0:T(8,128)(2,1)S(1)}, u32[]{:S(2)}, u32[]{:S(2)}) %collective-permute-start.9) | collective-permute-done | bytes 860192 | tf_op jit(solution)/shard_map/ppermute | solution.py:35
  71.3 9.1 %collective-permute-done.10.refs_3_ = bf16[120,3584]{1,0:T(8,128)(2,1)S(1)} collective-permute-done((bf16[120,3584]{1,0:T(8,128)(2,1)S(1)}, bf16[120,3584]{1,0:T(8,128)(2,1)S(1)}, u32[]{:S(2)}, u32[]{:S(2)}) %collective-permute-start.10) | collective-permute-done | bytes 860192 | tf_op jit(solution)/shard_map/ppermute | solution.py:35
  80.4 2.3 %gather.2.refs_2_ = f32[192,3584]{1,0:T(8,128)S(1)} custom-call(bf16[192,1024]{1,0:T(8,128)(2,1)S(1)} %get-tuple-element.23.refs_0_, bf16[120,3584]{1,0:T(8,128)(2,1)S(1)} %get-tuple-element.30.refs_1_, bf16[120,3584]{1,0:T(8,128)(2,1)S(1)} %collective-permute-done.9.refs_2_, bf16[120,3584]{1,0:T(8,128)(2,1)S(1)} %collective-permute-done.10.refs_3_), custom_call_target="tpu_custom_call" | custom-call | tf_op jit(solution)/shard_map/gather/pallas_call | solution.py:407
  82.7 2.0 %gather.3 = bf16[192,3584]{1,0:T(8,128)(2,1)} custom-call(bf16[192,1024]{1,0:T(8,128)(2,1)S(1)} %get-tuple-element.23.refs_0_, bf16[120,3584]{1,0:T(8,128)(2,1)S(1)} %collective-permute-done.8.refs_1_, f32[192,3584]{1,0:T(8,128)S(1)} %gather.2.refs_2_, bf16[4,48,224]{2,1,0:T(8,128)(2,1)S(1)} %collective-permute-done.3.refs_3_), custom_call_target="tpu_custom_call" | custom-call | tf_op jit(solution)/shard_map/gather/pallas_call | solution.py:407
  84.8 3.7 %all-to-all-start.1 = ((bf16[4,48,3584]{2,1,0:T(8,128)(2,1)}), bf16[4,48,3584]{2,1,0:T(8,128)(2,1)S(1)}, u32[]{:S(2)}, u32[]{:S(2)}) async-start(bf16[4,48,3584]{2,1,0:T(8,128)(2,1)} %bitcast.14), calls=%async_computation.1 | async-start | bytes 2752512 | tf_op jit(solution)/shard_map/all_to_all | solution.py:49
  89.2 11.8 %all-to-all-done.1 = bf16[4,48,3584]{2,1,0:T(8,128)(2,1)S(1)} async-done(((bf16[4,48,3584]{2,1,0:T(8,128)(2,1)}), bf16[4,48,3584]{2,1,0:T(8,128)(2,1)S(1)}, u32[]{:S(2)}, u32[]{:S(2)}) %all-to-all-start.1) | async-done | bytes 1376288 | tf_op jit(solution)/shard_map/all_to_all | solution.py:49
  101.1 1.3 finish.1
  103.0 1.0 blocks.5
  106.1 1.1 blocks.4
  107.2 20.7 %collective-permute-start.12 = (bf16[24,3584]{1,0:T(8,128)(2,1)S(1)}, bf16[24,3584]{1,0:T(8,128)(2,1)S(1)}, u32[]{:S(2)}, u32[]{:S(2)}) collective-permute-start(bf16[24,3584]{1,0:T(8,128)(2,1)S(1)} %get-tuple-element.34), channel_id=1, source_target_pairs={{32,0},{64,32},{96,64},{128,96},{160,128},{192,160},{224,192},{256... | collective-permute-start | bytes 516104 | tf_op jit(solution)/shard_map/ppermute | solution.py:441
  127.9 1.9 %collective-permute-start.11 = (bf16[24,3584]{1,0:T(8,128)(2,1)S(1)}, bf16[24,3584]{1,0:T(8,128)(2,1)S(1)}, u32[]{:S(2)}, u32[]{:S(2)}) collective-permute-start(bf16[24,3584]{1,0:T(8,128)(2,1)S(1)} %get-tuple-element.33), channel_id=1, source_target_pairs={{0,32},{32,64},{64,96},{96,128},{128,160},{160,192},{192,224},{224... | collective-permute-start | bytes 516104 | tf_op jit(solution)/shard_map/ppermute | solution.py:441
  129.9 1.3 collective-permute-start.17
  131.2 4.0 %collective-permute-done.11 = bf16[24,3584]{1,0:T(8,128)(2,1)S(1)} collective-permute-done((bf16[24,3584]{1,0:T(8,128)(2,1)S(1)}, bf16[24,3584]{1,0:T(8,128)(2,1)S(1)}, u32[]{:S(2)}, u32[]{:S(2)}) %collective-permute-start.11) | collective-permute-done | bytes 172064 | tf_op jit(solution)/shard_map/ppermute | solution.py:441
  (56 shorter events, 10.1 us)
Async XLA Ops:
  0.7 0.9 copy-start.3
  1.7 0.9 copy-start.5
  2.6 0.7 copy-start.7
  3.3 0.7 copy-start.10
  4.0 0.7 copy-start.11
  6.0 18.8 %copy-start.1 = (bf16[1,3584,128]{2,1,0:T(8,128)(2,1)S(1)}, bf16[1,3584,128]{2,1,0:T(8,128)(2,1)}, u32[]{:S(2)}) copy-start(bf16[1,3584,128]{2,1,0:T(8,128)(2,1)} %param.16) | copy-start | bytes 2752516
  6.1 18.8 %copy-start.2 = (bf16[1,128,3584]{2,1,0:T(8,128)(2,1)S(1)}, bf16[1,128,3584]{2,1,0:T(8,128)(2,1)}, u32[]{:S(2)}) copy-start(bf16[1,128,3584]{2,1,0:T(8,128)(2,1)} %param.17) | copy-start | bytes 2752516
  23.4 1.5 %copy-start = (bf16[1,3584,128]{2,1,0:T(8,128)(2,1)S(1)}, bf16[1,3584,128]{2,1,0:T(8,128)(2,1)}, u32[]{:S(2)}) copy-start(bf16[1,3584,128]{2,1,0:T(8,128)(2,1)} %param.15) | copy-start | bytes 2752516
  24.9 9.3 %copy-start.8 = (bf16[1,24,224]{2,1,0:T(8,128)(2,1)S(1)}, bf16[1,24,224]{2,1,0:T(8,128)(2,1)}, u32[]{:S(2)}) copy-start(bf16[1,24,224]{2,1,0:T(8,128)(2,1)} %fwd_ref.1) | copy-start | bytes 32260
  24.9 9.3 %copy-start.9 = (bf16[1,24,224]{2,1,0:T(8,128)(2,1)S(1)}, bf16[1,24,224]{2,1,0:T(8,128)(2,1)}, u32[]{:S(2)}) copy-start(bf16[1,24,224]{2,1,0:T(8,128)(2,1)} %bwd_ref.1) | copy-start | bytes 32260
  25.2 9.0 %collective-permute-start = (bf16[10752,128]{1,0:T(8,128)(2,1)S(1)}, bf16[10752,128]{1,0:T(8,128)(2,1)S(1)}, u32[]{:S(2)}, u32[]{:S(2)}) collective-permute-start(bf16[10752,128]{1,0:T(8,128)(2,1)S(1)} %pack.1), channel_id=1, source_target_pairs={{0,1},{1,0},{2,3},{3,2},{4,5},{5,4},{6,7},{7,6},{8,9},{9,8},{10,11... | collective-permute-start | bytes 8257544 | tf_op jit(solution)/shard_map/ppermute | solution.py:453
  27.1 15.9 %collective-permute-start.5 = (bf16[120,3584]{1,0:T(8,128)(2,1)S(1)}, bf16[120,3584]{1,0:T(8,128)(2,1)S(1)}, u32[]{:S(2)}, u32[]{:S(2)}) collective-permute-start(bf16[120,3584]{1,0:T(8,128)(2,1)S(1)} %get-tuple-element.24), channel_id=1, source_target_pairs={{0,2},{1,9},{2,4},{3,11},{4,6},{5,13},{6,0},{7,15},{8,10},{9,17},{... | collective-permute-start | bytes 2580488 | tf_op jit(solution)/shard_map/ppermute | solution.py:35
  30.5 14.7 %collective-permute-start.6 = (bf16[120,3584]{1,0:T(8,128)(2,1)S(1)}, bf16[120,3584]{1,0:T(8,128)(2,1)S(1)}, u32[]{:S(2)}, u32[]{:S(2)}) collective-permute-start(bf16[120,3584]{1,0:T(8,128)(2,1)S(1)} %get-tuple-element.25), channel_id=1, source_target_pairs={{0,6},{1,25},{2,0},{3,27},{4,2},{5,29},{6,4},{7,31},{8,14},{9,1},{... | collective-permute-start | bytes 2580488 | tf_op jit(solution)/shard_map/ppermute | solution.py:35
  34.8 10.4 %collective-permute-start.1 = (bf16[1,48,224]{2,1,0:T(8,128)(2,1)S(1)}, bf16[1,48,224]{2,1,0:T(8,128)(2,1)S(1)}, u32[]{:S(2)}, u32[]{:S(2)}) collective-permute-start(bf16[1,48,224]{2,1,0:T(8,128)(2,1)S(1)} %blocks.3), channel_id=1, source_target_pairs={{32,0},{96,64},{160,128},{224,192},{448,480},{384,416},{320,352},{... | collective-permute-start | bytes 64520 | tf_op jit(solution)/shard_map/ppermute | solution.py:460
  45.6 16.2 %collective-permute-start.7 = (bf16[120,3584]{1,0:T(8,128)(2,1)S(1)}, bf16[120,3584]{1,0:T(8,128)(2,1)S(1)}, u32[]{:S(2)}, u32[]{:S(2)}) collective-permute-start(bf16[120,3584]{1,0:T(8,128)(2,1)S(1)} %far.1), channel_id=1, source_target_pairs={{0,4},{1,17},{2,6},{3,19},{4,0},{5,21},{6,2},{7,23},{8,12},{9,25},... | collective-permute-start | bytes 2580488 | tf_op jit(solution)/shard_map/ppermute | solution.py:35
  52.0 19.4 %collective-permute-start.9 = (bf16[120,3584]{1,0:T(8,128)(2,1)S(1)}, bf16[120,3584]{1,0:T(8,128)(2,1)S(1)}, u32[]{:S(2)}, u32[]{:S(2)}) collective-permute-start(bf16[120,3584]{1,0:T(8,128)(2,1)S(1)} %get-tuple-element.31), channel_id=1, source_target_pairs={{0,6},{1,25},{2,0},{3,27},{4,2},{5,29},{6,4},{7,31},{8,14},{9,1},{... | collective-permute-start | bytes 2580488 | tf_op jit(solution)/shard_map/ppermute | solution.py:35
  55.3 25.1 %collective-permute-start.10 = (bf16[120,3584]{1,0:T(8,128)(2,1)S(1)}, bf16[120,3584]{1,0:T(8,128)(2,1)S(1)}, u32[]{:S(2)}, u32[]{:S(2)}) collective-permute-start(bf16[120,3584]{1,0:T(8,128)(2,1)S(1)} %get-tuple-element.32), channel_id=1, source_target_pairs={{0,2},{1,9},{2,4},{3,11},{4,6},{5,13},{6,0},{7,15},{8,10},{9,17},{... | collective-permute-start | bytes 2580488 | tf_op jit(solution)/shard_map/ppermute | solution.py:35
  63.3 19.4 %collective-permute-start.8 = (bf16[120,3584]{1,0:T(8,128)(2,1)S(1)}, bf16[120,3584]{1,0:T(8,128)(2,1)S(1)}, u32[]{:S(2)}, u32[]{:S(2)}) collective-permute-start(bf16[120,3584]{1,0:T(8,128)(2,1)S(1)} %get-tuple-element.29), channel_id=1, source_target_pairs={{0,4},{1,17},{2,6},{3,19},{4,0},{5,21},{6,2},{7,23},{8,12},{9,25},... | collective-permute-start | bytes 2580488 | tf_op jit(solution)/shard_map/ppermute | solution.py:35
  68.1 0.7 collective-permute-start.2
  68.8 13.9 %collective-permute-start.3 = (bf16[4,48,224]{2,1,0:T(8,128)(2,1)S(1)}, bf16[4,48,224]{2,1,0:T(8,128)(2,1)S(1)}, u32[]{:S(2)}, u32[]{:S(2)}) collective-permute-start(bf16[4,48,224]{2,1,0:T(8,128)(2,1)S(1)} %pad_maximum_fusion.1), channel_id=1, source_target_pairs={{128,0},{352,480},{129,1},{353,481},{130,2},{354,482},{131,3},{355... | collective-permute-start | bytes 258056 | tf_op jit(solution)/shard_map/ppermute | solution.py:460
  84.8 16.3 %copy-start.4 = (bf16[1,24,3584]{2,1,0:T(8,128)(2,1)S(1)}, bf16[1,24,3584]{2,1,0:T(8,128)(2,1)}, u32[]{:S(2)}) copy-start(bf16[1,24,3584]{2,1,0:T(8,128)(2,1)} %param.10) | copy-start | bytes 516100
  84.8 16.3 %copy-start.6 = (bf16[1,24,3584]{2,1,0:T(8,128)(2,1)S(1)}, bf16[1,24,3584]{2,1,0:T(8,128)(2,1)}, u32[]{:S(2)}) copy-start(bf16[1,24,3584]{2,1,0:T(8,128)(2,1)} %param.11) | copy-start | bytes 516100
  84.8 16.3 %all-to-all-start.1 = ((bf16[4,48,3584]{2,1,0:T(8,128)(2,1)}), bf16[4,48,3584]{2,1,0:T(8,128)(2,1)S(1)}, u32[]{:S(2)}, u32[]{:S(2)}) async-start(bf16[4,48,3584]{2,1,0:T(8,128)(2,1)} %bitcast.14), calls=%async_computation.1 | async-start | bytes 2752512 | tf_op jit(solution)/shard_map/all_to_all | solution.py:49
  88.5 0.7 collective-permute-start.4
  102.3 0.7 collective-permute-start.13
  104.1 25.7 %collective-permute-start.14 = (bf16[2,48,224]{2,1,0:T(8,128)(2,1)S(1)}, bf16[2,48,224]{2,1,0:T(8,128)(2,1)S(1)}, u32[]{:S(2)}, u32[]{:S(2)}) collective-permute-start(bf16[2,48,224]{2,1,0:T(8,128)(2,1)S(1)} %get-tuple-element.38), channel_id=1, source_target_pairs={{0,192},{480,288},{1,193},{481,289},{2,194},{482,290},{3,195},{483... | collective-permute-start | bytes 129032 | tf_op jit(solution)/shard_map/ppermute | solution.py:466
  104.8 25.1 %collective-permute-start.15 = (bf16[2,48,224]{2,1,0:T(8,128)(2,1)S(1)}, bf16[2,48,224]{2,1,0:T(8,128)(2,1)S(1)}, u32[]{:S(2)}, u32[]{:S(2)}) collective-permute-start(bf16[2,48,224]{2,1,0:T(8,128)(2,1)S(1)} %get-tuple-element.37), channel_id=1, source_target_pairs={{0,128},{480,352},{1,129},{481,353},{2,130},{482,354},{3,131},{483... | collective-permute-start | bytes 129032 | tf_op jit(solution)/shard_map/ppermute | solution.py:466
  105.4 24.4 %collective-permute-start.16 = (bf16[2,48,224]{2,1,0:T(8,128)(2,1)S(1)}, bf16[2,48,224]{2,1,0:T(8,128)(2,1)S(1)}, u32[]{:S(2)}, u32[]{:S(2)}) collective-permute-start(bf16[2,48,224]{2,1,0:T(8,128)(2,1)S(1)} %get-tuple-element.36), channel_id=1, source_target_pairs={{0,64},{480,416},{1,65},{481,417},{2,66},{482,418},{3,67},{483,419... | collective-permute-start | bytes 129032 | tf_op jit(solution)/shard_map/ppermute | solution.py:466
  107.2 24.0 %collective-permute-start.12 = (bf16[24,3584]{1,0:T(8,128)(2,1)S(1)}, bf16[24,3584]{1,0:T(8,128)(2,1)S(1)}, u32[]{:S(2)}, u32[]{:S(2)}) collective-permute-start(bf16[24,3584]{1,0:T(8,128)(2,1)S(1)} %get-tuple-element.34), channel_id=1, source_target_pairs={{32,0},{64,32},{96,64},{128,96},{160,128},{192,160},{224,192},{256... | collective-permute-start | bytes 516104 | tf_op jit(solution)/shard_map/ppermute | solution.py:441
  127.9 7.3 %collective-permute-start.11 = (bf16[24,3584]{1,0:T(8,128)(2,1)S(1)}, bf16[24,3584]{1,0:T(8,128)(2,1)S(1)}, u32[]{:S(2)}, u32[]{:S(2)}) collective-permute-start(bf16[24,3584]{1,0:T(8,128)(2,1)S(1)} %get-tuple-element.33), channel_id=1, source_target_pairs={{0,32},{32,64},{64,96},{96,128},{128,160},{160,192},{192,224},{224... | collective-permute-start | bytes 516104 | tf_op jit(solution)/shard_map/ppermute | solution.py:441
  129.9 6.1 %collective-permute-start.17 = (bf16[1,48,224]{2,1,0:T(8,128)(2,1)S(1)}, bf16[1,48,224]{2,1,0:T(8,128)(2,1)S(1)}, u32[]{:S(2)}, u32[]{:S(2)}) collective-permute-start(bf16[1,48,224]{2,1,0:T(8,128)(2,1)S(1)} %slice.48), channel_id=1, source_target_pairs={{0,32},{64,96},{128,160},{192,224},{480,448},{416,384},{352,320},{... | collective-permute-start | bytes 64520 | tf_op jit(solution)/shard_map/ppermute | solution.py:466

commit v11 on v10

--- a/solution.py
+++ b/solution.py
@@ -223,7 +223,7 @@
         out_ref[:, cut] = total.astype(out_ref.dtype)
 
 
-def finish_kernel(place_ref, meta_ref, rows_ref, fwd_ref, bwd_ref, _, of_ref, ob_ref, leave_ref):
+def finish_kernel(place_ref, meta_ref, rows_ref, fwd_ref, bwd_ref, _, toward_ref, away_ref):
     meta = meta_ref[...]
     total = EXPERTS * BOTH
     column = iota((BOTH, total), 1)
@@ -241,7 +241,7 @@
     on_first = place_ref[0] == 0
     high = jnp.where(on_first, high, ones).astype(BF)
     low = jnp.where(on_first, low, 0.0).astype(BF)
-    at_start = place_ref[2] == 0
+    lower = place_ref[3] == 1
     width = fwd_ref.shape[1]
     for start in range(0, width, CHUNK):
         cut = slice(start, min(start + CHUNK, width))
@@ -249,9 +249,8 @@
         mixture = dot(high, rows) + dot(low, rows)
         forward = fwd_ref[:, cut].astype(F32) + mixture[:ROWS]
         backward = bwd_ref[:, cut].astype(F32) + mixture[ROWS:]
-        of_ref[:, cut] = forward.astype(BF)
-        ob_ref[:, cut] = backward.astype(BF)
-        leave_ref[:, cut] = jnp.where(at_start, backward, forward).astype(BF)
+        toward_ref[:, cut] = jnp.where(lower, backward, forward).astype(BF)
+        away_ref[:, cut] = jnp.where(lower, forward, backward).astype(BF)
 
 
 def enter_kernel(place_ref, fwd_ref, bwd_ref, _, out_ref):
@@ -259,7 +258,7 @@
     out_ref[:, ROWS:, :] = bwd_ref[...]
 
 
-def ends_kernel(place_ref, own_ref, other_ref, out_ref):
+def ends_kernel(place_ref, own_ref, other_ref, _, out_ref):
     count, _, part = out_ref.shape
     for r in range(count):
         near, far = [slice(j * part, (j + 1) * part) for j in (r, 2 * count - 1 - r)]
@@ -417,9 +416,9 @@
 def make_finish(place, meta, rows, fwd, bwd, before):
     return pl.pallas_call(
         finish_kernel,
-        out_shape=(shape(*fwd.shape),) * 3,
+        out_shape=(shape(*fwd.shape),) * 2,
         in_specs=[SMEM] + [VMEM] * 4 + [ANY],
-        out_specs=(VMEM,) * 3,
+        out_specs=(VMEM,) * 2,
         compiler_params=params(),
         name="finish",
     )(place, meta, rows, fwd, bwd, before)
@@ -436,9 +435,8 @@
     )(place, *arrays, *before)
 
 
-def shifted(block, distance, count):
-    route = [(i, i + distance) for i in range(count) if 0 <= i + distance < count]
-    return lax.ppermute(block, "pp", route)
+def move_pp(block, pairs, sections):
+    return lax.ppermute(block, "pp", mirrored(pairs, sections))
 
 
 def swapped(block, count):
@@ -487,7 +485,9 @@
     sections = lax.axis_size("pp")
     section = lax.axis_index("pp")
     position = lax.axis_index("ep")
-    place = jnp.stack([position % 2, position // (2 * COLS), section]).astype(jnp.int32)
+    half = sections // 2
+    lower = section < half
+    place = jnp.stack([position % 2, position // (2 * COLS), section, lower]).astype(jnp.int32)
     fwd, bwd = state_fwd[0], state_bwd[0]
     features = fwd.shape[1]
     part = features // sections
@@ -502,7 +502,6 @@
     weights = own, from_other_core(make_pack(*own, pick))
     send0, back = make_rest(place, rows, pick, weights[1])
     done0, token = run_experts([send0], *weights)
-    half = sections // 2
     at_start = section == 0
     entering = make_simple(
         enter_kernel, (1, BOTH, part), place, enter_fwd, enter_bwd, before=(weights[1],)
@@ -521,14 +520,18 @@
     passed_on = jnp.where(at_start, held[:, ROWS:], held[:, :ROWS])
     got = swapped(passed_on, sections)
     rows = exchange(gathered)
-    fwd_out, bwd_out, leaving = make_finish(place, meta, rows, fwd, bwd, got)
+    toward, away = make_finish(place, meta, rows, fwd, bwd, got)
     entered = make_simple(entered_kernel, (ROWS, features), place, held, got)
-    other = swapped(leaving, sections)
-    ends = make_simple(ends_kernel, (half, BOTH, part), place, leaving, other)
+    inner = move_pp(toward, [(i, i - 1) for i in range(1, half)], sections)
+    other = swapped(toward, sections)
+    ends = make_simple(ends_kernel, (half, BOTH, part), place, toward, other, before=(inner,))
     mine = outward(ends, jnp.minimum(section, sections - 1 - section), sections)
-    from_left, from_right = shifted(fwd_out, 1, sections), shifted(bwd_out, -1, sections)
-    fwd_next = jnp.where(at_start, entered, from_left)
-    bwd_next = jnp.where(section == sections - 1, entered, from_right)
+    outer = move_pp(away, [(i, i + 1) for i in range(half - 1)], sections)
+    middle = move_pp(away, [(half - 1, half)], sections)
+    inner = jnp.where((section == half - 1) | (section == half), middle, inner)
+    outer = jnp.where(at_start | (section == sections - 1), entered, outer)
+    fwd_next = jnp.where(lower, outer, inner)
+    bwd_next = jnp.where(lower, inner, outer)
     return (fwd_next[None], bwd_next[None], mine[None, :ROWS], mine[None, ROWS:])
 
 

time: 137 us -> 134 us (0.978)
  starting transfers between devices: 61.9 us -> 48.9 us
  waiting for transfers between devices: 33.5 us -> 43.3 us
    ppermute x2 -> x3, starting transfers between devices: 22.6 us -> 9.52 us  [move_pp(): return lax.ppermute(block, 'pp', mirrored(pairs, sections))]
    ppermute x2 -> x3, waiting for transfers between devices: 4 us -> 13.8 us  [move_pp(): return lax.ppermute(block, 'pp', mirrored(pairs, sections))]
  transfers between devices with their start and end apart: 19 -> 20, of which waited for: 7 -> 8; matrix products, arithmetic and copies ran while one was open for 1% -> 1% of each run, Pallas kernels for 7% -> 7%
where the time goes in v11:
time: 134 us; the launch traced here: 133 us
  starting transfers between devices  48.9 us (36%)
  waiting for transfers between devices  43.3 us (32%)
  blocking collectives  17.3 us (13%)
  Pallas kernels  17.2 us (13%)
  local copies, waits for them, and re-layouts  4.57 us (3%)
    ppermute x6, starting transfers between devices, hop(): return lax.ppermute(block, 'ep', route)  22.3 us
    ppermute x6, waiting for transfers between devices, hop(): return lax.ppermute(block, 'ep', route)  17.6 us
    all_to_all x1, blocking collectives, exchange(): lax.all_to_all(rows, 'ep', split_axis=0, concat_axis=0, axis_index_groups...  17.3 us
    ppermute x3, waiting for transfers between devices, move_pp(): return lax.ppermute(block, 'pp', mirrored(pairs, sections))  13.8 us
    all_to_all x1, waiting for transfers between devices, exchange(): lax.all_to_all(rows, 'ep', split_axis=0, concat_axis=0, axis_index_groups...  11.8 us
    ppermute x3, starting transfers between devices, move_pp(): return lax.ppermute(block, 'pp', mirrored(pairs, sections))  9.52 us
    ppermute x3, starting transfers between devices, inward(): got.append(lax.ppermute(held, 'pp', mirrored(pairs, sections)))  6.89 us
    pallas_call x2, Pallas kernels, make_gather(): pl.pallas_call(body, out_shape=shape(total, features, BF if last else F32...  4.33 us
  transfers between devices with their start and end apart: 20, of which 8 were waited for; matrix products, arithmetic and copies ran while one was open for 1% of the time, Pallas kernels for 7%

profile of v11, /device:TPU:32, one launch (start us, length us, event | category | flops | bytes accessed | tf_op | source)
XLA Modules:
  0.0 133.4 jit_solution(5454259014326526169)
XLA Ops:
  0.7 0.9 copy-done.3
  4.6 1.4 %normed.1 = (bf16[192,3712]{1,0:T(8,128)(2,1)S(1)}, f32[48,128]{1,0:T(8,128)S(1)}) custom-call(s32[4]{0:T(128)S(1)} %pad_add_fusion.place_ref, bf16[24,3584]{1,0:T(8,128)(2,1)S(1)} %bitcast.40, bf16[24,3584]{1,0:T(8,128)(2,1)S(1)} %bitcast.42, f32[1,3584]{1,0:T(1,128)S(1)} %copy-done.7, s32[2,2,24]{2,1,0:T(2,128)S(1)} %bitcast.44, f32[2,2,24]{2,1,0:T(2,128)S(1)} %bitcast.45), custom_call_target="tpu_custom_call" | custom-call | tf_op jit(solution)/shard_map/normed/pallas_call | solution.py:311
  6.1 17.3 %all_to_all.22 = bf16[4,48,3712]{2,1,0:T(8,128)(2,1)S(1)} all-to-all(bf16[4,48,3712]{2,1,0:T(8,128)(2,1)S(1)} %bitcast.39), channel_id=1, replica_groups={{0,8,16,24},{2,10,18,26},{4,12,20,28},{6,14,22,30},{1,3,5,7},{9,11,13,1..., dimensions={0} | all-to-all | bytes 2850816 | tf_op jit(solution)/shard_map/all_to_all | solution.py:49
  23.4 1.5 %near.1 = (bf16[120,3584]{1,0:T(8,128)(2,1)S(1)}, bf16[120,3584]{1,0:T(8,128)(2,1)S(1)}, bf16[512,192]{1,0:T(8,128)(2,1)S(1)}, s32[8,128]{1,0:T(8,128)}) custom-call(s32[4]{0:T(128)S(1)} %pad_add_fusion.place_ref, bf16[192,3712]{1,0:T(8,128)(2,1)S(1)} %bitcast.23), custom_call_target="tpu_custom_call" | custom-call | tf_op jit(solution)/shard_map/near/pallas_call | solution.py:324
  25.2 1.9 %collective-permute-start = (bf16[10752,128]{1,0:T(8,128)(2,1)S(1)}, bf16[10752,128]{1,0:T(8,128)(2,1)S(1)}, u32[]{:S(2)}, u32[]{:S(2)}) collective-permute-start(bf16[10752,128]{1,0:T(8,128)(2,1)S(1)} %pack.1), channel_id=1, source_target_pairs={{0,1},{1,0},{2,3},{3,2},{4,5},{5,4},{6,7},{7,6},{8,9},{9,8},{10,11... | collective-permute-start | bytes 8257544 | tf_op jit(solution)/shard_map/ppermute | solution.py:451
  27.1 3.4 %collective-permute-start.5 = (bf16[120,3584]{1,0:T(8,128)(2,1)S(1)}, bf16[120,3584]{1,0:T(8,128)(2,1)S(1)}, u32[]{:S(2)}, u32[]{:S(2)}) collective-permute-start(bf16[120,3584]{1,0:T(8,128)(2,1)S(1)} %get-tuple-element.23), channel_id=1, source_target_pairs={{0,2},{1,9},{2,4},{3,11},{4,6},{5,13},{6,0},{7,15},{8,10},{9,17},{... | collective-permute-start | bytes 2580488 | tf_op jit(solution)/shard_map/ppermute | solution.py:35
  30.5 3.7 %collective-permute-start.6 = (bf16[120,3584]{1,0:T(8,128)(2,1)S(1)}, bf16[120,3584]{1,0:T(8,128)(2,1)S(1)}, u32[]{:S(2)}, u32[]{:S(2)}) collective-permute-start(bf16[120,3584]{1,0:T(8,128)(2,1)S(1)} %get-tuple-element.24), channel_id=1, source_target_pairs={{0,6},{1,25},{2,0},{3,27},{4,2},{5,29},{6,4},{7,31},{8,14},{9,1},{... | collective-permute-start | bytes 2580488 | tf_op jit(solution)/shard_map/ppermute | solution.py:35
  34.8 5.6 %collective-permute-start.1 = (bf16[1,48,224]{2,1,0:T(8,128)(2,1)S(1)}, bf16[1,48,224]{2,1,0:T(8,128)(2,1)S(1)}, u32[]{:S(2)}, u32[]{:S(2)}) collective-permute-start(bf16[1,48,224]{2,1,0:T(8,128)(2,1)S(1)} %blocks.3), channel_id=1, source_target_pairs={{32,0},{96,64},{160,128},{224,192},{448,480},{384,416},{320,352},{... | collective-permute-start | bytes 64520 | tf_op jit(solution)/shard_map/ppermute | solution.py:458
  40.3 1.1 rest.1
  41.5 1.0 experts.3
  43.0 2.2 %collective-permute-done.6.refs_1_ = bf16[120,3584]{1,0:T(8,128)(2,1)S(1)} collective-permute-done((bf16[120,3584]{1,0:T(8,128)(2,1)S(1)}, bf16[120,3584]{1,0:T(8,128)(2,1)S(1)}, u32[]{:S(2)}, u32[]{:S(2)}) %collective-permute-start.6) | collective-permute-done | bytes 860192 | tf_op jit(solution)/shard_map/ppermute | solution.py:35
  45.6 4.7 %collective-permute-start.7 = (bf16[120,3584]{1,0:T(8,128)(2,1)S(1)}, bf16[120,3584]{1,0:T(8,128)(2,1)S(1)}, u32[]{:S(2)}, u32[]{:S(2)}) collective-permute-start(bf16[120,3584]{1,0:T(8,128)(2,1)S(1)} %far.1), channel_id=1, source_target_pairs={{0,4},{1,17},{2,6},{3,19},{4,0},{5,21},{6,2},{7,23},{8,12},{9,25},... | collective-permute-start | bytes 2580488 | tf_op jit(solution)/shard_map/ppermute | solution.py:35
  50.3 1.7 %experts.4 = (bf16[120,3584]{1,0:T(8,128)(2,1)S(1)}, bf16[120,3584]{1,0:T(8,128)(2,1)S(1)}, s32[8,128]{1,0:T(8,128)S(1)}) custom-call(bf16[120,3584]{1,0:T(8,128)(2,1)S(1)} %collective-permute-done.5.refs_0_, bf16[120,3584]{1,0:T(8,128)(2,1)S(1)} %collective-permute-done.6.refs_1_, bf16[3584,128]{1,0:T(8,128)(2,1)S(1)} %bitcast.28, ...), custom_call_target="tpu_custom_call" | custom-call | tf_op jit(solution)/shard_map/experts/pallas_call | solution.py:388
  52.0 3.3 %collective-permute-start.9 = (bf16[120,3584]{1,0:T(8,128)(2,1)S(1)}, bf16[120,3584]{1,0:T(8,128)(2,1)S(1)}, u32[]{:S(2)}, u32[]{:S(2)}) collective-permute-start(bf16[120,3584]{1,0:T(8,128)(2,1)S(1)} %get-tuple-element.30), channel_id=1, source_target_pairs={{0,6},{1,25},{2,0},{3,27},{4,2},{5,29},{6,4},{7,31},{8,14},{9,1},{... | collective-permute-start | bytes 2580488 | tf_op jit(solution)/shard_map/ppermute | solution.py:35
  55.3 2.5 %collective-permute-start.10 = (bf16[120,3584]{1,0:T(8,128)(2,1)S(1)}, bf16[120,3584]{1,0:T(8,128)(2,1)S(1)}, u32[]{:S(2)}, u32[]{:S(2)}) collective-permute-start(bf16[120,3584]{1,0:T(8,128)(2,1)S(1)} %get-tuple-element.31), channel_id=1, source_target_pairs={{0,2},{1,9},{2,4},{3,11},{4,6},{5,13},{6,0},{7,15},{8,10},{9,17},{... | collective-permute-start | bytes 2580488 | tf_op jit(solution)/shard_map/ppermute | solution.py:35
  57.8 4.0 %collective-permute-done.7.refs_0_ = bf16[120,3584]{1,0:T(8,128)(2,1)S(1)} collective-permute-done((bf16[120,3584]{1,0:T(8,128)(2,1)S(1)}, bf16[120,3584]{1,0:T(8,128)(2,1)S(1)}, u32[]{:S(2)}, u32[]{:S(2)}) %collective-permute-start.7) | collective-permute-done | bytes 860192 | tf_op jit(solution)/shard_map/ppermute | solution.py:35
  61.8 1.5 %experts.5 = (bf16[120,3584]{1,0:T(8,128)(2,1)S(1)}, s32[8,128]{1,0:T(8,128)}) custom-call(bf16[120,3584]{1,0:T(8,128)(2,1)S(1)} %collective-permute-done.7.refs_0_, bf16[3584,128]{1,0:T(8,128)(2,1)S(1)} %bitcast.29, bf16[3584,128]{1,0:T(8,128)(2,1)S(1)} %bitcast.33, bf16[128,3584]{1,0:T(8,128)(2,1)S(1)} %bitcast.37, ...), custom_call_target="tpu_custom_call" | custom-call | tf_op jit(solution)/shard_map/experts/pallas_call | solution.py:388
  63.3 4.7 %collective-permute-start.8 = (bf16[120,3584]{1,0:T(8,128)(2,1)S(1)}, bf16[120,3584]{1,0:T(8,128)(2,1)S(1)}, u32[]{:S(2)}, u32[]{:S(2)}) collective-permute-start(bf16[120,3584]{1,0:T(8,128)(2,1)S(1)} %get-tuple-element.28), channel_id=1, source_target_pairs={{0,4},{1,17},{2,6},{3,19},{4,0},{5,21},{6,2},{7,23},{8,12},{9,25},... | collective-permute-start | bytes 2580488 | tf_op jit(solution)/shard_map/ppermute | solution.py:35
  69.5 1.8 %collective-permute-done.9.refs_2_ = bf16[120,3584]{1,0:T(8,128)(2,1)S(1)} collective-permute-done((bf16[120,3584]{1,0:T(8,128)(2,1)S(1)}, bf16[120,3584]{1,0:T(8,128)(2,1)S(1)}, u32[]{:S(2)}, u32[]{:S(2)}) %collective-permute-start.9) | collective-permute-done | bytes 860192 | tf_op jit(solution)/shard_map/ppermute | solution.py:35
  71.3 9.1 %collective-permute-done.10.refs_3_ = bf16[120,3584]{1,0:T(8,128)(2,1)S(1)} collective-permute-done((bf16[120,3584]{1,0:T(8,128)(2,1)S(1)}, bf16[120,3584]{1,0:T(8,128)(2,1)S(1)}, u32[]{:S(2)}, u32[]{:S(2)}) %collective-permute-start.10) | collective-permute-done | bytes 860192 | tf_op jit(solution)/shard_map/ppermute | solution.py:35
  80.4 2.3 %gather.2.refs_2_ = f32[192,3584]{1,0:T(8,128)S(1)} custom-call(bf16[192,1024]{1,0:T(8,128)(2,1)S(1)} %get-tuple-element.22.refs_0_, bf16[120,3584]{1,0:T(8,128)(2,1)S(1)} %get-tuple-element.29.refs_1_, bf16[120,3584]{1,0:T(8,128)(2,1)S(1)} %collective-permute-done.9.refs_2_, bf16[120,3584]{1,0:T(8,128)(2,1)S(1)} %collective-permute-done.10.refs_3_), custom_call_target="tpu_custom_call" | custom-call | tf_op jit(solution)/shard_map/gather/pallas_call | solution.py:406
  82.7 2.0 %gather.3 = bf16[192,3584]{1,0:T(8,128)(2,1)} custom-call(bf16[192,1024]{1,0:T(8,128)(2,1)S(1)} %get-tuple-element.22.refs_0_, bf16[120,3584]{1,0:T(8,128)(2,1)S(1)} %collective-permute-done.8.refs_1_, f32[192,3584]{1,0:T(8,128)S(1)} %gather.2.refs_2_, bf16[4,48,224]{2,1,0:T(8,128)(2,1)S(1)} %collective-permute-done.3.refs_3_), custom_call_target="tpu_custom_call" | custom-call | tf_op jit(solution)/shard_map/gather/pallas_call | solution.py:406
  84.8 3.7 %all-to-all-start.1 = ((bf16[4,48,3584]{2,1,0:T(8,128)(2,1)}), bf16[4,48,3584]{2,1,0:T(8,128)(2,1)S(1)}, u32[]{:S(2)}, u32[]{:S(2)}) async-start(bf16[4,48,3584]{2,1,0:T(8,128)(2,1)} %bitcast.15), calls=%async_computation.1 | async-start | bytes 2752512 | tf_op jit(solution)/shard_map/all_to_all | solution.py:49
  89.2 11.8 %all-to-all-done.1 = bf16[4,48,3584]{2,1,0:T(8,128)(2,1)S(1)} async-done(((bf16[4,48,3584]{2,1,0:T(8,128)(2,1)}), bf16[4,48,3584]{2,1,0:T(8,128)(2,1)S(1)}, u32[]{:S(2)}, u32[]{:S(2)}) %all-to-all-start.1) | async-done | bytes 1376288 | tf_op jit(solution)/shard_map/all_to_all | solution.py:49
  101.1 1.3 finish.1
  102.3 6.6 %collective-permute-start.13 = (bf16[24,3584]{1,0:T(8,128)(2,1)S(1)}, bf16[24,3584]{1,0:T(8,128)(2,1)S(1)}, u32[]{:S(2)}, u32[]{:S(2)}) collective-permute-start(bf16[24,3584]{1,0:T(8,128)(2,1)S(1)} %get-tuple-element.33.own_ref), channel_id=1, source_target_pairs={{32,0},{64,32},{96,64},{128,96},{160,128},{192,160},{224,192},{448... | collective-permute-start | bytes 516104 | tf_op jit(solution)/shard_map/ppermute | solution.py:439
  109.7 2.2 %collective-permute-done.13._ = bf16[24,3584]{1,0:T(8,128)(2,1)S(1)} collective-permute-done((bf16[24,3584]{1,0:T(8,128)(2,1)S(1)}, bf16[24,3584]{1,0:T(8,128)(2,1)S(1)}, u32[]{:S(2)}, u32[]{:S(2)}) %collective-permute-start.13) | collective-permute-done | bytes 172064 | tf_op jit(solution)/shard_map/ppermute | solution.py:439
  111.9 1.0 blocks.5
  115.0 1.1 blocks.4
  116.1 2.2 %collective-permute-start.11 = (bf16[24,3584]{1,0:T(8,128)(2,1)S(1)}, bf16[24,3584]{1,0:T(8,128)(2,1)S(1)}, u32[]{:S(2)}, u32[]{:S(2)}) collective-permute-start(bf16[24,3584]{1,0:T(8,128)(2,1)S(1)} %get-tuple-element.32), channel_id=1, source_target_pairs={{0,32},{32,64},{64,96},{96,128},{128,160},{160,192},{192,224},{480... | collective-permute-start | bytes 516104 | tf_op jit(solution)/shard_map/ppermute | solution.py:439
  119.1 1.3 collective-permute-start.18
  120.4 11.6 %collective-permute-done.11 = bf16[24,3584]{1,0:T(8,128)(2,1)S(1)} collective-permute-done((bf16[24,3584]{1,0:T(8,128)(2,1)S(1)}, bf16[24,3584]{1,0:T(8,128)(2,1)S(1)}, u32[]{:S(2)}, u32[]{:S(2)}) %collective-permute-start.11) | collective-permute-done | bytes 172064 | tf_op jit(solution)/shard_map/ppermute | solution.py:439
  (58 shorter events, 11.7 us)
Async XLA Ops:
  0.7 0.9 copy-start.3
  1.7 0.9 copy-start.5
  2.6 0.7 copy-start.7
  3.3 0.7 copy-start.10
  4.0 0.7 copy-start.11
  6.0 18.8 %copy-start.1 = (bf16[1,3584,128]{2,1,0:T(8,128)(2,1)S(1)}, bf16[1,3584,128]{2,1,0:T(8,128)(2,1)}, u32[]{:S(2)}) copy-start(bf16[1,3584,128]{2,1,0:T(8,128)(2,1)} %param.16) | copy-start | bytes 2752516
  6.1 18.8 %copy-start.2 = (bf16[1,128,3584]{2,1,0:T(8,128)(2,1)S(1)}, bf16[1,128,3584]{2,1,0:T(8,128)(2,1)}, u32[]{:S(2)}) copy-start(bf16[1,128,3584]{2,1,0:T(8,128)(2,1)} %param.17) | copy-start | bytes 2752516
  23.4 1.5 %copy-start = (bf16[1,3584,128]{2,1,0:T(8,128)(2,1)S(1)}, bf16[1,3584,128]{2,1,0:T(8,128)(2,1)}, u32[]{:S(2)}) copy-start(bf16[1,3584,128]{2,1,0:T(8,128)(2,1)} %param.15) | copy-start | bytes 2752516
  24.9 9.3 %copy-start.8 = (bf16[1,24,224]{2,1,0:T(8,128)(2,1)S(1)}, bf16[1,24,224]{2,1,0:T(8,128)(2,1)}, u32[]{:S(2)}) copy-start(bf16[1,24,224]{2,1,0:T(8,128)(2,1)} %fwd_ref.1) | copy-start | bytes 32260
  24.9 9.3 %copy-start.9 = (bf16[1,24,224]{2,1,0:T(8,128)(2,1)S(1)}, bf16[1,24,224]{2,1,0:T(8,128)(2,1)}, u32[]{:S(2)}) copy-start(bf16[1,24,224]{2,1,0:T(8,128)(2,1)} %bwd_ref.1) | copy-start | bytes 32260
  25.2 9.0 %collective-permute-start = (bf16[10752,128]{1,0:T(8,128)(2,1)S(1)}, bf16[10752,128]{1,0:T(8,128)(2,1)S(1)}, u32[]{:S(2)}, u32[]{:S(2)}) collective-permute-start(bf16[10752,128]{1,0:T(8,128)(2,1)S(1)} %pack.1), channel_id=1, source_target_pairs={{0,1},{1,0},{2,3},{3,2},{4,5},{5,4},{6,7},{7,6},{8,9},{9,8},{10,11... | collective-permute-start | bytes 8257544 | tf_op jit(solution)/shard_map/ppermute | solution.py:451
  27.1 15.9 %collective-permute-start.5 = (bf16[120,3584]{1,0:T(8,128)(2,1)S(1)}, bf16[120,3584]{1,0:T(8,128)(2,1)S(1)}, u32[]{:S(2)}, u32[]{:S(2)}) collective-permute-start(bf16[120,3584]{1,0:T(8,128)(2,1)S(1)} %get-tuple-element.23), channel_id=1, source_target_pairs={{0,2},{1,9},{2,4},{3,11},{4,6},{5,13},{6,0},{7,15},{8,10},{9,17},{... | collective-permute-start | bytes 2580488 | tf_op jit(solution)/shard_map/ppermute | solution.py:35
  30.5 14.7 %collective-permute-start.6 = (bf16[120,3584]{1,0:T(8,128)(2,1)S(1)}, bf16[120,3584]{1,0:T(8,128)(2,1)S(1)}, u32[]{:S(2)}, u32[]{:S(2)}) collective-permute-start(bf16[120,3584]{1,0:T(8,128)(2,1)S(1)} %get-tuple-element.24), channel_id=1, source_target_pairs={{0,6},{1,25},{2,0},{3,27},{4,2},{5,29},{6,4},{7,31},{8,14},{9,1},{... | collective-permute-start | bytes 2580488 | tf_op jit(solution)/shard_map/ppermute | solution.py:35
  34.8 10.4 %collective-permute-start.1 = (bf16[1,48,224]{2,1,0:T(8,128)(2,1)S(1)}, bf16[1,48,224]{2,1,0:T(8,128)(2,1)S(1)}, u32[]{:S(2)}, u32[]{:S(2)}) collective-permute-start(bf16[1,48,224]{2,1,0:T(8,128)(2,1)S(1)} %blocks.3), channel_id=1, source_target_pairs={{32,0},{96,64},{160,128},{224,192},{448,480},{384,416},{320,352},{... | collective-permute-start | bytes 64520 | tf_op jit(solution)/shard_map/ppermute | solution.py:458
  45.6 16.2 %collective-permute-start.7 = (bf16[120,3584]{1,0:T(8,128)(2,1)S(1)}, bf16[120,3584]{1,0:T(8,128)(2,1)S(1)}, u32[]{:S(2)}, u32[]{:S(2)}) collective-permute-start(bf16[120,3584]{1,0:T(8,128)(2,1)S(1)} %far.1), channel_id=1, source_target_pairs={{0,4},{1,17},{2,6},{3,19},{4,0},{5,21},{6,2},{7,23},{8,12},{9,25},... | collective-permute-start | bytes 2580488 | tf_op jit(solution)/shard_map/ppermute | solution.py:35
  52.0 19.4 %collective-permute-start.9 = (bf16[120,3584]{1,0:T(8,128)(2,1)S(1)}, bf16[120,3584]{1,0:T(8,128)(2,1)S(1)}, u32[]{:S(2)}, u32[]{:S(2)}) collective-permute-start(bf16[120,3584]{1,0:T(8,128)(2,1)S(1)} %get-tuple-element.30), channel_id=1, source_target_pairs={{0,6},{1,25},{2,0},{3,27},{4,2},{5,29},{6,4},{7,31},{8,14},{9,1},{... | collective-permute-start | bytes 2580488 | tf_op jit(solution)/shard_map/ppermute | solution.py:35
  55.3 25.1 %collective-permute-start.10 = (bf16[120,3584]{1,0:T(8,128)(2,1)S(1)}, bf16[120,3584]{1,0:T(8,128)(2,1)S(1)}, u32[]{:S(2)}, u32[]{:S(2)}) collective-permute-start(bf16[120,3584]{1,0:T(8,128)(2,1)S(1)} %get-tuple-element.31), channel_id=1, source_target_pairs={{0,2},{1,9},{2,4},{3,11},{4,6},{5,13},{6,0},{7,15},{8,10},{9,17},{... | collective-permute-start | bytes 2580488 | tf_op jit(solution)/shard_map/ppermute | solution.py:35
  63.3 19.4 %collective-permute-start.8 = (bf16[120,3584]{1,0:T(8,128)(2,1)S(1)}, bf16[120,3584]{1,0:T(8,128)(2,1)S(1)}, u32[]{:S(2)}, u32[]{:S(2)}) collective-permute-start(bf16[120,3584]{1,0:T(8,128)(2,1)S(1)} %get-tuple-element.28), channel_id=1, source_target_pairs={{0,4},{1,17},{2,6},{3,19},{4,0},{5,21},{6,2},{7,23},{8,12},{9,25},... | collective-permute-start | bytes 2580488 | tf_op jit(solution)/shard_map/ppermute | solution.py:35
  68.1 0.7 collective-permute-start.2
  68.8 13.9 %collective-permute-start.3 = (bf16[4,48,224]{2,1,0:T(8,128)(2,1)S(1)}, bf16[4,48,224]{2,1,0:T(8,128)(2,1)S(1)}, u32[]{:S(2)}, u32[]{:S(2)}) collective-permute-start(bf16[4,48,224]{2,1,0:T(8,128)(2,1)S(1)} %pad_maximum_fusion.1), channel_id=1, source_target_pairs={{128,0},{352,480},{129,1},{353,481},{130,2},{354,482},{131,3},{355... | collective-permute-start | bytes 258056 | tf_op jit(solution)/shard_map/ppermute | solution.py:458
  84.8 16.3 %copy-start.4 = (bf16[1,24,3584]{2,1,0:T(8,128)(2,1)S(1)}, bf16[1,24,3584]{2,1,0:T(8,128)(2,1)}, u32[]{:S(2)}) copy-start(bf16[1,24,3584]{2,1,0:T(8,128)(2,1)} %param.10) | copy-start | bytes 516100
  84.8 16.3 %copy-start.6 = (bf16[1,24,3584]{2,1,0:T(8,128)(2,1)S(1)}, bf16[1,24,3584]{2,1,0:T(8,128)(2,1)}, u32[]{:S(2)}) copy-start(bf16[1,24,3584]{2,1,0:T(8,128)(2,1)} %param.11) | copy-start | bytes 516100
  84.8 16.3 %all-to-all-start.1 = ((bf16[4,48,3584]{2,1,0:T(8,128)(2,1)}), bf16[4,48,3584]{2,1,0:T(8,128)(2,1)S(1)}, u32[]{:S(2)}, u32[]{:S(2)}) async-start(bf16[4,48,3584]{2,1,0:T(8,128)(2,1)} %bitcast.15), calls=%async_computation.1 | async-start | bytes 2752512 | tf_op jit(solution)/shard_map/all_to_all | solution.py:49
  88.5 0.7 collective-permute-start.4
  102.3 9.6 %collective-permute-start.13 = (bf16[24,3584]{1,0:T(8,128)(2,1)S(1)}, bf16[24,3584]{1,0:T(8,128)(2,1)S(1)}, u32[]{:S(2)}, u32[]{:S(2)}) collective-permute-start(bf16[24,3584]{1,0:T(8,128)(2,1)S(1)} %get-tuple-element.33.own_ref), channel_id=1, source_target_pairs={{32,0},{64,32},{96,64},{128,96},{160,128},{192,160},{224,192},{448... | collective-permute-start | bytes 516104 | tf_op jit(solution)/shard_map/ppermute | solution.py:439
  109.0 2.9 %collective-permute-start.14 = (bf16[24,3584]{1,0:T(8,128)(2,1)S(1)}, bf16[24,3584]{1,0:T(8,128)(2,1)S(1)}, u32[]{:S(2)}, u32[]{:S(2)}) collective-permute-start(bf16[24,3584]{1,0:T(8,128)(2,1)S(1)} %get-tuple-element.33.own_ref), channel_id=1, source_target_pairs={{0,480},{480,0},{1,481},{481,1},{2,482},{482,2},{3,483},{483,3},{4... | collective-permute-start | bytes 516104 | tf_op jit(solution)/shard_map/ppermute | solution.py:443
  113.0 6.1 %collective-permute-start.15 = (bf16[2,48,224]{2,1,0:T(8,128)(2,1)S(1)}, bf16[2,48,224]{2,1,0:T(8,128)(2,1)S(1)}, u32[]{:S(2)}, u32[]{:S(2)}) collective-permute-start(bf16[2,48,224]{2,1,0:T(8,128)(2,1)S(1)} %get-tuple-element.38), channel_id=1, source_target_pairs={{0,192},{480,288},{1,193},{481,289},{2,194},{482,290},{3,195},{483... | collective-permute-start | bytes 129032 | tf_op jit(solution)/shard_map/ppermute | solution.py:464
  113.6 5.4 %collective-permute-start.16 = (bf16[2,48,224]{2,1,0:T(8,128)(2,1)S(1)}, bf16[2,48,224]{2,1,0:T(8,128)(2,1)S(1)}, u32[]{:S(2)}, u32[]{:S(2)}) collective-permute-start(bf16[2,48,224]{2,1,0:T(8,128)(2,1)S(1)} %get-tuple-element.37), channel_id=1, source_target_pairs={{0,128},{480,352},{1,129},{481,353},{2,130},{482,354},{3,131},{483... | collective-permute-start | bytes 129032 | tf_op jit(solution)/shard_map/ppermute | solution.py:464
  114.3 4.7 %collective-permute-start.17 = (bf16[2,48,224]{2,1,0:T(8,128)(2,1)S(1)}, bf16[2,48,224]{2,1,0:T(8,128)(2,1)S(1)}, u32[]{:S(2)}, u32[]{:S(2)}) collective-permute-start(bf16[2,48,224]{2,1,0:T(8,128)(2,1)S(1)} %get-tuple-element.36), channel_id=1, source_target_pairs={{0,64},{480,416},{1,65},{481,417},{2,66},{482,418},{3,67},{483,419... | collective-permute-start | bytes 129032 | tf_op jit(solution)/shard_map/ppermute | solution.py:464
  116.1 15.8 %collective-permute-start.11 = (bf16[24,3584]{1,0:T(8,128)(2,1)S(1)}, bf16[24,3584]{1,0:T(8,128)(2,1)S(1)}, u32[]{:S(2)}, u32[]{:S(2)}) collective-permute-start(bf16[24,3584]{1,0:T(8,128)(2,1)S(1)} %get-tuple-element.32), channel_id=1, source_target_pairs={{0,32},{32,64},{64,96},{96,128},{128,160},{160,192},{192,224},{480... | collective-permute-start | bytes 516104 | tf_op jit(solution)/shard_map/ppermute | solution.py:439
  118.4 13.6 %collective-permute-start.12 = (bf16[24,3584]{1,0:T(8,128)(2,1)S(1)}, bf16[24,3584]{1,0:T(8,128)(2,1)S(1)}, u32[]{:S(2)}, u32[]{:S(2)}) collective-permute-start(bf16[24,3584]{1,0:T(8,128)(2,1)S(1)} %get-tuple-element.32), channel_id=1, source_target_pairs={{224,256},{256,224},{225,257},{257,225},{226,258},{258,226},{227,2... | collective-permute-start | bytes 516104 | tf_op jit(solution)/shard_map/ppermute | solution.py:439
  119.1 13.7 %collective-permute-start.18 = (bf16[1,48,224]{2,1,0:T(8,128)(2,1)S(1)}, bf16[1,48,224]{2,1,0:T(8,128)(2,1)S(1)}, u32[]{:S(2)}, u32[]{:S(2)}) collective-permute-start(bf16[1,48,224]{2,1,0:T(8,128)(2,1)S(1)} %slice.48), channel_id=1, source_target_pairs={{0,32},{64,96},{128,160},{192,224},{480,448},{416,384},{352,320},{... | collective-permute-start | bytes 64520 | tf_op jit(solution)/shard_map/ppermute | solution.py:464

commit v12 on v11

--- a/solution.py
+++ b/solution.py
@@ -258,7 +258,8 @@
     out_ref[:, ROWS:, :] = bwd_ref[...]
 
 
-def ends_kernel(place_ref, own_ref, other_ref, _, out_ref):
+def ends_kernel(place_ref, own_ref, other_ref, *refs):
+    out_ref = refs[-1]
     count, _, part = out_ref.shape
     for r in range(count):
         near, far = [slice(j * part, (j + 1) * part) for j in (r, 2 * count - 1 - r)]
@@ -523,12 +524,15 @@
     toward, away = make_finish(place, meta, rows, fwd, bwd, got)
     entered = make_simple(entered_kernel, (ROWS, features), place, held, got)
     inner = move_pp(toward, [(i, i - 1) for i in range(1, half)], sections)
+    away_low = lax.ppermute(away, "pp", [(i, i + 1) for i in range(half - 1)])
     other = swapped(toward, sections)
-    ends = make_simple(ends_kernel, (half, BOTH, part), place, toward, other, before=(inner,))
+    before = (inner, away_low, entered)
+    ends = make_simple(ends_kernel, (half, BOTH, part), place, toward, other, before=before)
     mine = outward(ends, jnp.minimum(section, sections - 1 - section), sections)
-    outer = move_pp(away, [(i, i + 1) for i in range(half - 1)], sections)
+    away_up = lax.ppermute(away, "pp", [(i, i - 1) for i in range(half + 1, sections)])
     middle = move_pp(away, [(half - 1, half)], sections)
     inner = jnp.where((section == half - 1) | (section == half), middle, inner)
+    outer = jnp.where(lower, away_low, away_up)
     outer = jnp.where(at_start | (section == sections - 1), entered, outer)
     fwd_next = jnp.where(lower, outer, inner)
     bwd_next = jnp.where(lower, inner, outer)

time: 134 us -> 134 us (level)
  the two profiles are of different devices: /device:TPU:32 before, /device:TPU:34 now
where the time goes in v12:
time: 134 us; the launch traced here: 133 us
  starting transfers between devices  49.3 us (37%)
  waiting for transfers between devices  42.5 us (32%)
  blocking collectives  17.3 us (13%)
  Pallas kernels  17.2 us (13%)
  local copies, waits for them, and re-layouts  4.57 us (3%)
    ppermute x6, starting transfers between devices, hop(): return lax.ppermute(block, 'ep', route)  20.1 us
    ppermute x6, waiting for transfers between devices, hop(): return lax.ppermute(block, 'ep', route)  18.8 us
    all_to_all x1, blocking collectives, exchange(): lax.all_to_all(rows, 'ep', split_axis=0, concat_axis=0, axis_index_groups...  17.3 us
    all_to_all x1, waiting for transfers between devices, exchange(): lax.all_to_all(rows, 'ep', split_axis=0, concat_axis=0, axis_index_groups...  11.8 us
    ppermute x2, starting transfers between devices, move_pp(): return lax.ppermute(block, 'pp', mirrored(pairs, sections))  11 us
    ppermute x4, waiting for transfers between devices, move(): return lax.ppermute(block, 'pp', mirrored(list(pairs), sections))  8.31 us
    ppermute x3, starting transfers between devices, inward(): got.append(lax.ppermute(held, 'pp', mirrored(pairs, sections)))  5.41 us
    pallas_call x2, Pallas kernels, make_gather(): pl.pallas_call(body, out_shape=shape(total, features, BF if last else F32...  4.32 us
  transfers between devices with their start and end apart: 21, of which 8 were waited for; matrix products, arithmetic and copies ran while one was open for 1% of the time, Pallas kernels for 7%

profile of v12, /device:TPU:34, one launch (start us, length us, event | category | flops | bytes accessed | tf_op | source)
XLA Modules:
  0.0 133.1 jit_solution(13678804311799629855)
XLA Ops:
  4.6 1.4 %normed.1 = (bf16[192,3712]{1,0:T(8,128)(2,1)S(1)}, f32[48,128]{1,0:T(8,128)S(1)}) custom-call(s32[4]{0:T(128)S(1)} %pad_add_fusion.place_ref, bf16[24,3584]{1,0:T(8,128)(2,1)S(1)} %bitcast.40, bf16[24,3584]{1,0:T(8,128)(2,1)S(1)} %bitcast.42, f32[1,3584]{1,0:T(1,128)S(1)} %copy-done.7, s32[2,2,24]{2,1,0:T(2,128)S(1)} %bitcast.44, f32[2,2,24]{2,1,0:T(2,128)S(1)} %bitcast.45), custom_call_target="tpu_custom_call" | custom-call | tf_op jit(solution)/shard_map/normed/pallas_call | solution.py:312
  6.1 17.3 %all_to_all.22 = bf16[4,48,3712]{2,1,0:T(8,128)(2,1)S(1)} all-to-all(bf16[4,48,3712]{2,1,0:T(8,128)(2,1)S(1)} %bitcast.39), channel_id=1, replica_groups={{0,8,16,24},{2,10,18,26},{4,12,20,28},{6,14,22,30},{1,3,5,7},{9,11,13,1..., dimensions={0} | all-to-all | bytes 2850816 | tf_op jit(solution)/shard_map/all_to_all | solution.py:49
  23.4 1.5 %near.1 = (bf16[120,3584]{1,0:T(8,128)(2,1)S(1)}, bf16[120,3584]{1,0:T(8,128)(2,1)S(1)}, bf16[512,192]{1,0:T(8,128)(2,1)S(1)}, s32[8,128]{1,0:T(8,128)}) custom-call(s32[4]{0:T(128)S(1)} %pad_add_fusion.place_ref, bf16[192,3712]{1,0:T(8,128)(2,1)S(1)} %bitcast.23), custom_call_target="tpu_custom_call" | custom-call | tf_op jit(solution)/shard_map/near/pallas_call | solution.py:325
  25.2 1.9 %collective-permute-start = (bf16[10752,128]{1,0:T(8,128)(2,1)S(1)}, bf16[10752,128]{1,0:T(8,128)(2,1)S(1)}, u32[]{:S(2)}, u32[]{:S(2)}) collective-permute-start(bf16[10752,128]{1,0:T(8,128)(2,1)S(1)} %pack.1), channel_id=1, source_target_pairs={{0,1},{1,0},{2,3},{3,2},{4,5},{5,4},{6,7},{7,6},{8,9},{9,8},{10,11... | collective-permute-start | bytes 8257544 | tf_op jit(solution)/shard_map/ppermute | solution.py:452
  27.1 3.4 %collective-permute-start.5 = (bf16[120,3584]{1,0:T(8,128)(2,1)S(1)}, bf16[120,3584]{1,0:T(8,128)(2,1)S(1)}, u32[]{:S(2)}, u32[]{:S(2)}) collective-permute-start(bf16[120,3584]{1,0:T(8,128)(2,1)S(1)} %get-tuple-element.23), channel_id=1, source_target_pairs={{0,2},{1,9},{2,4},{3,11},{4,6},{5,13},{6,0},{7,15},{8,10},{9,17},{... | collective-permute-start | bytes 2580488 | tf_op jit(solution)/shard_map/ppermute | solution.py:35
  30.5 2.4 %collective-permute-start.6 = (bf16[120,3584]{1,0:T(8,128)(2,1)S(1)}, bf16[120,3584]{1,0:T(8,128)(2,1)S(1)}, u32[]{:S(2)}, u32[]{:S(2)}) collective-permute-start(bf16[120,3584]{1,0:T(8,128)(2,1)S(1)} %get-tuple-element.24), channel_id=1, source_target_pairs={{0,6},{1,25},{2,0},{3,27},{4,2},{5,29},{6,4},{7,31},{8,14},{9,1},{... | collective-permute-start | bytes 2580488 | tf_op jit(solution)/shard_map/ppermute | solution.py:35
  33.6 4.1 %collective-permute-start.1 = (bf16[1,48,224]{2,1,0:T(8,128)(2,1)S(1)}, bf16[1,48,224]{2,1,0:T(8,128)(2,1)S(1)}, u32[]{:S(2)}, u32[]{:S(2)}) collective-permute-start(bf16[1,48,224]{2,1,0:T(8,128)(2,1)S(1)} %blocks.3), channel_id=1, source_target_pairs={{32,0},{96,64},{160,128},{224,192},{448,480},{384,416},{320,352},{... | collective-permute-start | bytes 64520 | tf_op jit(solution)/shard_map/ppermute | solution.py:459
  37.7 1.1 rest.1
  38.8 1.0 experts.3
  39.8 2.0 %collective-permute-done.5.refs_0_ = bf16[120,3584]{1,0:T(8,128)(2,1)S(1)} collective-permute-done((bf16[120,3584]{1,0:T(8,128)(2,1)S(1)}, bf16[120,3584]{1,0:T(8,128)(2,1)S(1)}, u32[]{:S(2)}, u32[]{:S(2)}) %collective-permute-start.5) | collective-permute-done | bytes 860192 | tf_op jit(solution)/shard_map/ppermute | solution.py:35
  41.8 3.4 %collective-permute-done.6.refs_1_ = bf16[120,3584]{1,0:T(8,128)(2,1)S(1)} collective-permute-done((bf16[120,3584]{1,0:T(8,128)(2,1)S(1)}, bf16[120,3584]{1,0:T(8,128)(2,1)S(1)}, u32[]{:S(2)}, u32[]{:S(2)}) %collective-permute-start.6) | collective-permute-done | bytes 860192 | tf_op jit(solution)/shard_map/ppermute | solution.py:35
  45.6 4.2 %collective-permute-start.7 = (bf16[120,3584]{1,0:T(8,128)(2,1)S(1)}, bf16[120,3584]{1,0:T(8,128)(2,1)S(1)}, u32[]{:S(2)}, u32[]{:S(2)}) collective-permute-start(bf16[120,3584]{1,0:T(8,128)(2,1)S(1)} %far.1), channel_id=1, source_target_pairs={{0,4},{1,17},{2,6},{3,19},{4,0},{5,21},{6,2},{7,23},{8,12},{9,25},... | collective-permute-start | bytes 2580488 | tf_op jit(solution)/shard_map/ppermute | solution.py:35
  49.9 1.7 %experts.4 = (bf16[120,3584]{1,0:T(8,128)(2,1)S(1)}, bf16[120,3584]{1,0:T(8,128)(2,1)S(1)}, s32[8,128]{1,0:T(8,128)S(1)}) custom-call(bf16[120,3584]{1,0:T(8,128)(2,1)S(1)} %collective-permute-done.5.refs_0_, bf16[120,3584]{1,0:T(8,128)(2,1)S(1)} %collective-permute-done.6.refs_1_, bf16[3584,128]{1,0:T(8,128)(2,1)S(1)} %bitcast.28, ...), custom_call_target="tpu_custom_call" | custom-call | tf_op jit(solution)/shard_map/experts/pallas_call | solution.py:389
  51.6 2.9 %collective-permute-start.9 = (bf16[120,3584]{1,0:T(8,128)(2,1)S(1)}, bf16[120,3584]{1,0:T(8,128)(2,1)S(1)}, u32[]{:S(2)}, u32[]{:S(2)}) collective-permute-start(bf16[120,3584]{1,0:T(8,128)(2,1)S(1)} %get-tuple-element.30), channel_id=1, source_target_pairs={{0,6},{1,25},{2,0},{3,27},{4,2},{5,29},{6,4},{7,31},{8,14},{9,1},{... | collective-permute-start | bytes 2580488 | tf_op jit(solution)/shard_map/ppermute | solution.py:35
  54.4 3.0 %collective-permute-start.10 = (bf16[120,3584]{1,0:T(8,128)(2,1)S(1)}, bf16[120,3584]{1,0:T(8,128)(2,1)S(1)}, u32[]{:S(2)}, u32[]{:S(2)}) collective-permute-start(bf16[120,3584]{1,0:T(8,128)(2,1)S(1)} %get-tuple-element.31), channel_id=1, source_target_pairs={{0,2},{1,9},{2,4},{3,11},{4,6},{5,13},{6,0},{7,15},{8,10},{9,17},{... | collective-permute-start | bytes 2580488 | tf_op jit(solution)/shard_map/ppermute | solution.py:35
  57.4 4.5 %collective-permute-done.7.refs_0_ = bf16[120,3584]{1,0:T(8,128)(2,1)S(1)} collective-permute-done((bf16[120,3584]{1,0:T(8,128)(2,1)S(1)}, bf16[120,3584]{1,0:T(8,128)(2,1)S(1)}, u32[]{:S(2)}, u32[]{:S(2)}) %collective-permute-start.7) | collective-permute-done | bytes 860192 | tf_op jit(solution)/shard_map/ppermute | solution.py:35
  61.9 1.5 %experts.5 = (bf16[120,3584]{1,0:T(8,128)(2,1)S(1)}, s32[8,128]{1,0:T(8,128)}) custom-call(bf16[120,3584]{1,0:T(8,128)(2,1)S(1)} %collective-permute-done.7.refs_0_, bf16[3584,128]{1,0:T(8,128)(2,1)S(1)} %bitcast.29, bf16[3584,128]{1,0:T(8,128)(2,1)S(1)} %bitcast.33, bf16[128,3584]{1,0:T(8,128)(2,1)S(1)} %bitcast.37, ...), custom_call_target="tpu_custom_call" | custom-call | tf_op jit(solution)/shard_map/experts/pallas_call | solution.py:389
  63.4 4.2 %collective-permute-start.8 = (bf16[120,3584]{1,0:T(8,128)(2,1)S(1)}, bf16[120,3584]{1,0:T(8,128)(2,1)S(1)}, u32[]{:S(2)}, u32[]{:S(2)}) collective-permute-start(bf16[120,3584]{1,0:T(8,128)(2,1)S(1)} %get-tuple-element.28), channel_id=1, source_target_pairs={{0,4},{1,17},{2,6},{3,19},{4,0},{5,21},{6,2},{7,23},{8,12},{9,25},... | collective-permute-start | bytes 2580488 | tf_op jit(solution)/shard_map/ppermute | solution.py:35
  69.1 1.9 %collective-permute-done.9.refs_2_ = bf16[120,3584]{1,0:T(8,128)(2,1)S(1)} collective-permute-done((bf16[120,3584]{1,0:T(8,128)(2,1)S(1)}, bf16[120,3584]{1,0:T(8,128)(2,1)S(1)}, u32[]{:S(2)}, u32[]{:S(2)}) %collective-permute-start.9) | collective-permute-done | bytes 860192 | tf_op jit(solution)/shard_map/ppermute | solution.py:35
  71.0 2.3 %gather.2.refs_2_ = f32[192,3584]{1,0:T(8,128)S(1)} custom-call(bf16[192,1024]{1,0:T(8,128)(2,1)S(1)} %get-tuple-element.22.refs_0_, bf16[120,3584]{1,0:T(8,128)(2,1)S(1)} %get-tuple-element.29.refs_1_, bf16[120,3584]{1,0:T(8,128)(2,1)S(1)} %collective-permute-done.9.refs_2_, bf16[120,3584]{1,0:T(8,128)(2,1)S(1)} %collective-permute-done.10.refs_3_), custom_call_target="tpu_custom_call" | custom-call | tf_op jit(solution)/shard_map/gather/pallas_call | solution.py:407
  73.3 6.9 %collective-permute-done.8.refs_1_ = bf16[120,3584]{1,0:T(8,128)(2,1)S(1)} collective-permute-done((bf16[120,3584]{1,0:T(8,128)(2,1)S(1)}, bf16[120,3584]{1,0:T(8,128)(2,1)S(1)}, u32[]{:S(2)}, u32[]{:S(2)}) %collective-permute-start.8) | collective-permute-done | bytes 860192 | tf_op jit(solution)/shard_map/ppermute | solution.py:35
  80.3 2.0 %gather.3 = bf16[192,3584]{1,0:T(8,128)(2,1)} custom-call(bf16[192,1024]{1,0:T(8,128)(2,1)S(1)} %get-tuple-element.22.refs_0_, bf16[120,3584]{1,0:T(8,128)(2,1)S(1)} %collective-permute-done.8.refs_1_, f32[192,3584]{1,0:T(8,128)S(1)} %gather.2.refs_2_, bf16[4,48,224]{2,1,0:T(8,128)(2,1)S(1)} %collective-permute-done.3.refs_3_), custom_call_target="tpu_custom_call" | custom-call | tf_op jit(solution)/shard_map/gather/pallas_call | solution.py:407
  82.3 3.7 %all-to-all-start.1 = ((bf16[4,48,3584]{2,1,0:T(8,128)(2,1)}), bf16[4,48,3584]{2,1,0:T(8,128)(2,1)S(1)}, u32[]{:S(2)}, u32[]{:S(2)}) async-start(bf16[4,48,3584]{2,1,0:T(8,128)(2,1)} %bitcast.15), calls=%async_computation.1 | async-start | bytes 2752512 | tf_op jit(solution)/shard_map/all_to_all | solution.py:49
  86.7 11.8 %all-to-all-done.1 = bf16[4,48,3584]{2,1,0:T(8,128)(2,1)S(1)} async-done(((bf16[4,48,3584]{2,1,0:T(8,128)(2,1)}), bf16[4,48,3584]{2,1,0:T(8,128)(2,1)S(1)}, u32[]{:S(2)}, u32[]{:S(2)}) %all-to-all-start.1) | async-done | bytes 1376288 | tf_op jit(solution)/shard_map/all_to_all | solution.py:49
  98.6 1.3 finish.1
  99.9 10.3 %collective-permute-start.14 = (bf16[24,3584]{1,0:T(8,128)(2,1)S(1)}, bf16[24,3584]{1,0:T(8,128)(2,1)S(1)}, u32[]{:S(2)}, u32[]{:S(2)}) collective-permute-start(bf16[24,3584]{1,0:T(8,128)(2,1)S(1)} %get-tuple-element.33.own_ref), channel_id=1, source_target_pairs={{32,0},{64,32},{96,64},{128,96},{160,128},{192,160},{224,192},{448... | collective-permute-start | bytes 516104 | tf_op jit(solution)/shard_map/ppermute | solution.py:440
  110.2 1.9 %collective-permute-start.11 = (bf16[24,3584]{1,0:T(8,128)(2,1)S(1)}, bf16[24,3584]{1,0:T(8,128)(2,1)S(1)}, u32[]{:S(2)}, u32[]{:S(2)}) collective-permute-start(bf16[24,3584]{1,0:T(8,128)(2,1)S(1)} %get-tuple-element.32), channel_id=1, source_target_pairs={{0,32},{32,64},{64,96},{96,128},{128,160},{160,192},{192,224},{1,3... | collective-permute-start | bytes 516104 | tf_op jit(solution)/shard_map/ppermute | solution.py:527
  112.8 1.1 blocks.4.refs_2_
  113.9 3.6 %collective-permute-done.11.refs_1_ = bf16[24,3584]{1,0:T(8,128)(2,1)S(1)} collective-permute-done((bf16[24,3584]{1,0:T(8,128)(2,1)S(1)}, bf16[24,3584]{1,0:T(8,128)(2,1)S(1)}, u32[]{:S(2)}, u32[]{:S(2)}) %collective-permute-start.11) | collective-permute-done | bytes 172064 | tf_op jit(solution)/shard_map/ppermute | solution.py:527
  117.5 1.0 blocks.5
  122.0 1.3 collective-permute-start.19
  124.1 8.3 %collective-permute-done.19 = bf16[1,48,224]{2,1,0:T(8,128)(2,1)S(1)} collective-permute-done((bf16[1,48,224]{2,1,0:T(8,128)(2,1)S(1)}, bf16[1,48,224]{2,1,0:T(8,128)(2,1)S(1)}, u32[]{:S(2)}, u32[]{:S(2)}) %collective-permute-start.19) | collective-permute-done | bytes 21536 | tf_op jit(solution)/shard_map/ppermute | solution.py:465
  (60 shorter events, 12.8 us)
Async XLA Ops:
  0.7 0.9 copy-start.3
  1.7 0.9 copy-start.5
  2.6 0.7 copy-start.7
  3.3 0.7 copy-start.10
  6.0 18.8 %copy-start.1 = (bf16[1,3584,128]{2,1,0:T(8,128)(2,1)S(1)}, bf16[1,3584,128]{2,1,0:T(8,128)(2,1)}, u32[]{:S(2)}) copy-start(bf16[1,3584,128]{2,1,0:T(8,128)(2,1)} %param.16) | copy-start | bytes 2752516
  6.1 18.8 %copy-start.2 = (bf16[1,128,3584]{2,1,0:T(8,128)(2,1)S(1)}, bf16[1,128,3584]{2,1,0:T(8,128)(2,1)}, u32[]{:S(2)}) copy-start(bf16[1,128,3584]{2,1,0:T(8,128)(2,1)} %param.17) | copy-start | bytes 2752516
  23.4 1.5 %copy-start = (bf16[1,3584,128]{2,1,0:T(8,128)(2,1)S(1)}, bf16[1,3584,128]{2,1,0:T(8,128)(2,1)}, u32[]{:S(2)}) copy-start(bf16[1,3584,128]{2,1,0:T(8,128)(2,1)} %param.15) | copy-start | bytes 2752516
  24.9 8.1 %copy-start.8 = (bf16[1,24,224]{2,1,0:T(8,128)(2,1)S(1)}, bf16[1,24,224]{2,1,0:T(8,128)(2,1)}, u32[]{:S(2)}) copy-start(bf16[1,24,224]{2,1,0:T(8,128)(2,1)} %fwd_ref.1) | copy-start | bytes 32260
  24.9 8.1 %copy-start.9 = (bf16[1,24,224]{2,1,0:T(8,128)(2,1)S(1)}, bf16[1,24,224]{2,1,0:T(8,128)(2,1)}, u32[]{:S(2)}) copy-start(bf16[1,24,224]{2,1,0:T(8,128)(2,1)} %bwd_ref.1) | copy-start | bytes 32260
  25.2 7.8 %collective-permute-start = (bf16[10752,128]{1,0:T(8,128)(2,1)S(1)}, bf16[10752,128]{1,0:T(8,128)(2,1)S(1)}, u32[]{:S(2)}, u32[]{:S(2)}) collective-permute-start(bf16[10752,128]{1,0:T(8,128)(2,1)S(1)} %pack.1), channel_id=1, source_target_pairs={{0,1},{1,0},{2,3},{3,2},{4,5},{5,4},{6,7},{7,6},{8,9},{9,8},{10,11... | collective-permute-start | bytes 8257544 | tf_op jit(solution)/shard_map/ppermute | solution.py:452
  27.1 14.7 %collective-permute-start.5 = (bf16[120,3584]{1,0:T(8,128)(2,1)S(1)}, bf16[120,3584]{1,0:T(8,128)(2,1)S(1)}, u32[]{:S(2)}, u32[]{:S(2)}) collective-permute-start(bf16[120,3584]{1,0:T(8,128)(2,1)S(1)} %get-tuple-element.23), channel_id=1, source_target_pairs={{0,2},{1,9},{2,4},{3,11},{4,6},{5,13},{6,0},{7,15},{8,10},{9,17},{... | collective-permute-start | bytes 2580488 | tf_op jit(solution)/shard_map/ppermute | solution.py:35
  30.5 14.7 %collective-permute-start.6 = (bf16[120,3584]{1,0:T(8,128)(2,1)S(1)}, bf16[120,3584]{1,0:T(8,128)(2,1)S(1)}, u32[]{:S(2)}, u32[]{:S(2)}) collective-permute-start(bf16[120,3584]{1,0:T(8,128)(2,1)S(1)} %get-tuple-element.24), channel_id=1, source_target_pairs={{0,6},{1,25},{2,0},{3,27},{4,2},{5,29},{6,4},{7,31},{8,14},{9,1},{... | collective-permute-start | bytes 2580488 | tf_op jit(solution)/shard_map/ppermute | solution.py:35
  33.6 11.6 %collective-permute-start.1 = (bf16[1,48,224]{2,1,0:T(8,128)(2,1)S(1)}, bf16[1,48,224]{2,1,0:T(8,128)(2,1)S(1)}, u32[]{:S(2)}, u32[]{:S(2)}) collective-permute-start(bf16[1,48,224]{2,1,0:T(8,128)(2,1)S(1)} %blocks.3), channel_id=1, source_target_pairs={{32,0},{96,64},{160,128},{224,192},{448,480},{384,416},{320,352},{... | collective-permute-start | bytes 64520 | tf_op jit(solution)/shard_map/ppermute | solution.py:459
  45.6 16.3 %collective-permute-start.7 = (bf16[120,3584]{1,0:T(8,128)(2,1)S(1)}, bf16[120,3584]{1,0:T(8,128)(2,1)S(1)}, u32[]{:S(2)}, u32[]{:S(2)}) collective-permute-start(bf16[120,3584]{1,0:T(8,128)(2,1)S(1)} %far.1), channel_id=1, source_target_pairs={{0,4},{1,17},{2,6},{3,19},{4,0},{5,21},{6,2},{7,23},{8,12},{9,25},... | collective-permute-start | bytes 2580488 | tf_op jit(solution)/shard_map/ppermute | solution.py:35
  51.6 19.5 %collective-permute-start.9 = (bf16[120,3584]{1,0:T(8,128)(2,1)S(1)}, bf16[120,3584]{1,0:T(8,128)(2,1)S(1)}, u32[]{:S(2)}, u32[]{:S(2)}) collective-permute-start(bf16[120,3584]{1,0:T(8,128)(2,1)S(1)} %get-tuple-element.30), channel_id=1, source_target_pairs={{0,6},{1,25},{2,0},{3,27},{4,2},{5,29},{6,4},{7,31},{8,14},{9,1},{... | collective-permute-start | bytes 2580488 | tf_op jit(solution)/shard_map/ppermute | solution.py:35
  54.4 16.6 %collective-permute-start.10 = (bf16[120,3584]{1,0:T(8,128)(2,1)S(1)}, bf16[120,3584]{1,0:T(8,128)(2,1)S(1)}, u32[]{:S(2)}, u32[]{:S(2)}) collective-permute-start(bf16[120,3584]{1,0:T(8,128)(2,1)S(1)} %get-tuple-element.31), channel_id=1, source_target_pairs={{0,2},{1,9},{2,4},{3,11},{4,6},{5,13},{6,0},{7,15},{8,10},{9,17},{... | collective-permute-start | bytes 2580488 | tf_op jit(solution)/shard_map/ppermute | solution.py:35
  63.4 16.8 %collective-permute-start.8 = (bf16[120,3584]{1,0:T(8,128)(2,1)S(1)}, bf16[120,3584]{1,0:T(8,128)(2,1)S(1)}, u32[]{:S(2)}, u32[]{:S(2)}) collective-permute-start(bf16[120,3584]{1,0:T(8,128)(2,1)S(1)} %get-tuple-element.28), channel_id=1, source_target_pairs={{0,4},{1,17},{2,6},{3,19},{4,0},{5,21},{6,2},{7,23},{8,12},{9,25},... | collective-permute-start | bytes 2580488 | tf_op jit(solution)/shard_map/ppermute | solution.py:35
  67.7 0.7 collective-permute-start.2
  68.4 4.9 %collective-permute-start.3 = (bf16[4,48,224]{2,1,0:T(8,128)(2,1)S(1)}, bf16[4,48,224]{2,1,0:T(8,128)(2,1)S(1)}, u32[]{:S(2)}, u32[]{:S(2)}) collective-permute-start(bf16[4,48,224]{2,1,0:T(8,128)(2,1)S(1)} %pad_maximum_fusion.1), channel_id=1, source_target_pairs={{128,0},{352,480},{129,1},{353,481},{130,2},{354,482},{131,3},{355... | collective-permute-start | bytes 258056 | tf_op jit(solution)/shard_map/ppermute | solution.py:459
  82.3 16.3 %copy-start.4 = (bf16[1,24,3584]{2,1,0:T(8,128)(2,1)S(1)}, bf16[1,24,3584]{2,1,0:T(8,128)(2,1)}, u32[]{:S(2)}) copy-start(bf16[1,24,3584]{2,1,0:T(8,128)(2,1)} %param.10) | copy-start | bytes 516100
  82.3 16.3 %copy-start.6 = (bf16[1,24,3584]{2,1,0:T(8,128)(2,1)S(1)}, bf16[1,24,3584]{2,1,0:T(8,128)(2,1)}, u32[]{:S(2)}) copy-start(bf16[1,24,3584]{2,1,0:T(8,128)(2,1)} %param.11) | copy-start | bytes 516100
  82.3 16.3 %all-to-all-start.1 = ((bf16[4,48,3584]{2,1,0:T(8,128)(2,1)}), bf16[4,48,3584]{2,1,0:T(8,128)(2,1)S(1)}, u32[]{:S(2)}, u32[]{:S(2)}) async-start(bf16[4,48,3584]{2,1,0:T(8,128)(2,1)} %bitcast.15), calls=%async_computation.1 | async-start | bytes 2752512 | tf_op jit(solution)/shard_map/all_to_all | solution.py:49
  86.1 0.7 collective-permute-start.4
  99.9 14.1 %collective-permute-start.14 = (bf16[24,3584]{1,0:T(8,128)(2,1)S(1)}, bf16[24,3584]{1,0:T(8,128)(2,1)S(1)}, u32[]{:S(2)}, u32[]{:S(2)}) collective-permute-start(bf16[24,3584]{1,0:T(8,128)(2,1)S(1)} %get-tuple-element.33.own_ref), channel_id=1, source_target_pairs={{32,0},{64,32},{96,64},{128,96},{160,128},{192,160},{224,192},{448... | collective-permute-start | bytes 516104 | tf_op jit(solution)/shard_map/ppermute | solution.py:440
  110.2 7.3 %collective-permute-start.11 = (bf16[24,3584]{1,0:T(8,128)(2,1)S(1)}, bf16[24,3584]{1,0:T(8,128)(2,1)S(1)}, u32[]{:S(2)}, u32[]{:S(2)}) collective-permute-start(bf16[24,3584]{1,0:T(8,128)(2,1)S(1)} %get-tuple-element.32), channel_id=1, source_target_pairs={{0,32},{32,64},{64,96},{96,128},{128,160},{160,192},{192,224},{1,3... | collective-permute-start | bytes 516104 | tf_op jit(solution)/shard_map/ppermute | solution.py:527
  112.1 5.4 %collective-permute-start.15 = (bf16[24,3584]{1,0:T(8,128)(2,1)S(1)}, bf16[24,3584]{1,0:T(8,128)(2,1)S(1)}, u32[]{:S(2)}, u32[]{:S(2)}) collective-permute-start(bf16[24,3584]{1,0:T(8,128)(2,1)S(1)} %get-tuple-element.33.own_ref), channel_id=1, source_target_pairs={{0,480},{480,0},{1,481},{481,1},{2,482},{482,2},{3,483},{483,3},{4... | collective-permute-start | bytes 516104 | tf_op jit(solution)/shard_map/ppermute | solution.py:444
  118.6 3.4 %collective-permute-start.16 = (bf16[2,48,224]{2,1,0:T(8,128)(2,1)S(1)}, bf16[2,48,224]{2,1,0:T(8,128)(2,1)S(1)}, u32[]{:S(2)}, u32[]{:S(2)}) collective-permute-start(bf16[2,48,224]{2,1,0:T(8,128)(2,1)S(1)} %get-tuple-element.38), channel_id=1, source_target_pairs={{0,192},{480,288},{1,193},{481,289},{2,194},{482,290},{3,195},{483... | collective-permute-start | bytes 129032 | tf_op jit(solution)/shard_map/ppermute | solution.py:465
  119.2 2.7 %collective-permute-start.17 = (bf16[2,48,224]{2,1,0:T(8,128)(2,1)S(1)}, bf16[2,48,224]{2,1,0:T(8,128)(2,1)S(1)}, u32[]{:S(2)}, u32[]{:S(2)}) collective-permute-start(bf16[2,48,224]{2,1,0:T(8,128)(2,1)S(1)} %get-tuple-element.37), channel_id=1, source_target_pairs={{0,128},{480,352},{1,129},{481,353},{2,130},{482,354},{3,131},{483... | collective-permute-start | bytes 129032 | tf_op jit(solution)/shard_map/ppermute | solution.py:465
  119.9 2.1 %collective-permute-start.18 = (bf16[2,48,224]{2,1,0:T(8,128)(2,1)S(1)}, bf16[2,48,224]{2,1,0:T(8,128)(2,1)S(1)}, u32[]{:S(2)}, u32[]{:S(2)}) collective-permute-start(bf16[2,48,224]{2,1,0:T(8,128)(2,1)S(1)} %get-tuple-element.36), channel_id=1, source_target_pairs={{0,64},{480,416},{1,65},{481,417},{2,66},{482,418},{3,67},{483,419... | collective-permute-start | bytes 129032 | tf_op jit(solution)/shard_map/ppermute | solution.py:465
  120.6 2.7 %collective-permute-start.13 = (bf16[24,3584]{1,0:T(8,128)(2,1)S(1)}, bf16[24,3584]{1,0:T(8,128)(2,1)S(1)}, u32[]{:S(2)}, u32[]{:S(2)}) collective-permute-start(bf16[24,3584]{1,0:T(8,128)(2,1)S(1)} %get-tuple-element.32), channel_id=1, source_target_pairs={{224,256},{256,224},{225,257},{257,225},{226,258},{258,226},{227,2... | collective-permute-start | bytes 516104 | tf_op jit(solution)/shard_map/ppermute | solution.py:440
  121.3 2.1 %collective-permute-start.12 = (bf16[24,3584]{1,0:T(8,128)(2,1)S(1)}, bf16[24,3584]{1,0:T(8,128)(2,1)S(1)}, u32[]{:S(2)}, u32[]{:S(2)}) collective-permute-start(bf16[24,3584]{1,0:T(8,128)(2,1)S(1)} %get-tuple-element.32), channel_id=1, source_target_pairs={{288,256},{320,288},{352,320},{384,352},{416,384},{448,416},{480,4... | collective-permute-start | bytes 516104 | tf_op jit(solution)/shard_map/ppermute | solution.py:532
  122.0 10.4 %collective-permute-start.19 = (bf16[1,48,224]{2,1,0:T(8,128)(2,1)S(1)}, bf16[1,48,224]{2,1,0:T(8,128)(2,1)S(1)}, u32[]{:S(2)}, u32[]{:S(2)}) collective-permute-start(bf16[1,48,224]{2,1,0:T(8,128)(2,1)S(1)} %slice.48), channel_id=1, source_target_pairs={{0,32},{64,96},{128,160},{192,224},{480,448},{416,384},{352,320},{... | collective-permute-start | bytes 64520 | tf_op jit(solution)/shard_map/ppermute | solution.py:465
  (1 other events, 0.7 us)

commit v13 on v11

--- a/solution.py
+++ b/solution.py
@@ -17,6 +17,7 @@
 EXTRA = 128
 WIDE = 1792
 CHUNK = 512
+PIECE = 896
 LANES = 128
 
 
@@ -223,7 +224,7 @@
         out_ref[:, cut] = total.astype(out_ref.dtype)
 
 
-def finish_kernel(place_ref, meta_ref, rows_ref, fwd_ref, bwd_ref, _, toward_ref, away_ref):
+def finish_kernel(place_ref, meta_ref, rows_ref, fwd_ref, bwd_ref, _, toward_ref, away_ref, leave_ref):
     meta = meta_ref[...]
     total = EXPERTS * BOTH
     column = iota((BOTH, total), 1)
@@ -243,14 +244,20 @@
     low = jnp.where(on_first, low, 0.0).astype(BF)
     lower = place_ref[3] == 1
     width = fwd_ref.shape[1]
-    for start in range(0, width, CHUNK):
-        cut = slice(start, min(start + CHUNK, width))
+    half = leave_ref.shape[1]
+    for start in range(0, width, PIECE):
+        cut = slice(start, start + PIECE)
         rows = rows_ref[:, cut]
         mixture = dot(high, rows) + dot(low, rows)
-        forward = fwd_ref[:, cut].astype(F32) + mixture[:ROWS]
-        backward = bwd_ref[:, cut].astype(F32) + mixture[ROWS:]
-        toward_ref[:, cut] = jnp.where(lower, backward, forward).astype(BF)
-        away_ref[:, cut] = jnp.where(lower, forward, backward).astype(BF)
+        forward = (fwd_ref[:, cut].astype(F32) + mixture[:ROWS]).astype(BF)
+        backward = (bwd_ref[:, cut].astype(F32) + mixture[ROWS:]).astype(BF)
+        toward_ref[:, cut] = jnp.where(lower, backward, forward)
+        away_ref[:, cut] = jnp.where(lower, forward, backward)
+
+        @pl.when(lower if start >= half else jnp.logical_not(lower))
+        def _():
+            at = start % half
+            leave_ref[:, at : at + PIECE] = backward if start >= half else forward
 
 
 def enter_kernel(place_ref, fwd_ref, bwd_ref, _, out_ref):
@@ -258,10 +265,12 @@
     out_ref[:, ROWS:, :] = bwd_ref[...]
 
 
-def ends_kernel(place_ref, own_ref, other_ref, _, out_ref):
+def ends_kernel(place_ref, own_ref, other_ref, *refs):
+    out_ref = refs[-1]
     count, _, part = out_ref.shape
     for r in range(count):
         near, far = [slice(j * part, (j + 1) * part) for j in (r, 2 * count - 1 - r)]
+        back = slice((count - 1 - r) * part, (count - r) * part)
 
         @pl.when(place_ref[2] == 0)
         def _():
@@ -271,7 +280,7 @@
         @pl.when(place_ref[2] != 0)
         def _():
             out_ref[r, :ROWS, :] = own_ref[:, far]
-            out_ref[r, ROWS:, :] = other_ref[:, far]
+            out_ref[r, ROWS:, :] = other_ref[:, back]
 
 
 def entered_kernel(place_ref, held_ref, got_ref, out_ref):
@@ -416,9 +425,9 @@
 def make_finish(place, meta, rows, fwd, bwd, before):
     return pl.pallas_call(
         finish_kernel,
-        out_shape=(shape(*fwd.shape),) * 2,
+        out_shape=(shape(*fwd.shape),) * 2 + (shape(fwd.shape[0], fwd.shape[1] // 2),),
         in_specs=[SMEM] + [VMEM] * 4 + [ANY],
-        out_specs=(VMEM,) * 2,
+        out_specs=(VMEM,) * 3,
         compiler_params=params(),
         name="finish",
     )(place, meta, rows, fwd, bwd, before)
@@ -520,11 +529,11 @@
     passed_on = jnp.where(at_start, held[:, ROWS:], held[:, :ROWS])
     got = swapped(passed_on, sections)
     rows = exchange(gathered)
-    toward, away = make_finish(place, meta, rows, fwd, bwd, got)
+    toward, away, leaving = make_finish(place, meta, rows, fwd, bwd, got)
     entered = make_simple(entered_kernel, (ROWS, features), place, held, got)
     inner = move_pp(toward, [(i, i - 1) for i in range(1, half)], sections)
-    other = swapped(toward, sections)
-    ends = make_simple(ends_kernel, (half, BOTH, part), place, toward, other, before=(inner,))
+    other = swapped(leaving, sections)
+    ends = make_simple(ends_kernel, (half, BOTH, part), place, toward, other, before=(inner, entered))
     mine = outward(ends, jnp.minimum(section, sections - 1 - section), sections)
     outer = move_pp(away, [(i, i + 1) for i in range(half - 1)], sections)
     middle = move_pp(away, [(half - 1, half)], sections)

time: 134 us -> 133 us (level)
  waiting for transfers between devices: 43.3 us -> 41.2 us
    ppermute x3, waiting for transfers between devices: 13.8 us -> 11.8 us  [move_pp(): return lax.ppermute(block, 'pp', mirrored(pairs, sections))]
where the time goes in v13:
time: 133 us; the launch traced here: 132 us
  starting transfers between devices  48.9 us (37%)
  waiting for transfers between devices  41.2 us (31%)
  Pallas kernels  17.6 us (13%)
  blocking collectives  17.3 us (13%)
  local copies, waits for them, and re-layouts  4.57 us (3%)
    ppermute x6, starting transfers between devices, hop(): return lax.ppermute(block, 'ep', route)  22.3 us
    ppermute x6, waiting for transfers between devices, hop(): return lax.ppermute(block, 'ep', route)  17.6 us
    all_to_all x1, blocking collectives, exchange(): lax.all_to_all(rows, 'ep', split_axis=0, concat_axis=0, axis_index_groups...  17.3 us
    all_to_all x1, waiting for transfers between devices, exchange(): lax.all_to_all(rows, 'ep', split_axis=0, concat_axis=0, axis_index_groups...  11.8 us
    ppermute x3, waiting for transfers between devices, move_pp(): return lax.ppermute(block, 'pp', mirrored(pairs, sections))  11.8 us
    ppermute x3, starting transfers between devices, move_pp(): return lax.ppermute(block, 'pp', mirrored(pairs, sections))  9.52 us
    ppermute x3, starting transfers between devices, inward(): got.append(lax.ppermute(held, 'pp', mirrored(pairs, sections)))  6.89 us
    pallas_call x2, Pallas kernels, make_gather(): pl.pallas_call(body, out_shape=shape(total, features, BF if last else F32...  4.33 us
  transfers between devices with their start and end apart: 20, of which 8 were waited for; matrix products, arithmetic and copies ran while one was open for 1% of the time, Pallas kernels for 7%

profile of v13, /device:TPU:32, one launch (start us, length us, event | category | flops | bytes accessed | tf_op | source)
XLA Modules:
  0.0 131.8 jit_solution(6858414918967277213)
XLA Ops:
  0.7 0.9 copy-done.3
  4.6 1.4 %normed.1 = (bf16[192,3712]{1,0:T(8,128)(2,1)S(1)}, f32[48,128]{1,0:T(8,128)S(1)}) custom-call(s32[4]{0:T(128)S(1)} %pad_add_fusion.place_ref, bf16[24,3584]{1,0:T(8,128)(2,1)S(1)} %bitcast.40, bf16[24,3584]{1,0:T(8,128)(2,1)S(1)} %bitcast.42, f32[1,3584]{1,0:T(1,128)S(1)} %copy-done.7, s32[2,2,24]{2,1,0:T(2,128)S(1)} %bitcast.44, f32[2,2,24]{2,1,0:T(2,128)S(1)} %bitcast.45), custom_call_target="tpu_custom_call" | custom-call | tf_op jit(solution)/shard_map/normed/pallas_call | solution.py:320
  6.1 17.3 %all_to_all.22 = bf16[4,48,3712]{2,1,0:T(8,128)(2,1)S(1)} all-to-all(bf16[4,48,3712]{2,1,0:T(8,128)(2,1)S(1)} %bitcast.39), channel_id=1, replica_groups={{0,8,16,24},{2,10,18,26},{4,12,20,28},{6,14,22,30},{1,3,5,7},{9,11,13,1..., dimensions={0} | all-to-all | bytes 2850816 | tf_op jit(solution)/shard_map/all_to_all | solution.py:50
  23.4 1.5 %near.1 = (bf16[120,3584]{1,0:T(8,128)(2,1)S(1)}, bf16[120,3584]{1,0:T(8,128)(2,1)S(1)}, bf16[512,192]{1,0:T(8,128)(2,1)S(1)}, s32[8,128]{1,0:T(8,128)}) custom-call(s32[4]{0:T(128)S(1)} %pad_add_fusion.place_ref, bf16[192,3712]{1,0:T(8,128)(2,1)S(1)} %bitcast.23), custom_call_target="tpu_custom_call" | custom-call | tf_op jit(solution)/shard_map/near/pallas_call | solution.py:333
  25.2 1.9 %collective-permute-start = (bf16[10752,128]{1,0:T(8,128)(2,1)S(1)}, bf16[10752,128]{1,0:T(8,128)(2,1)S(1)}, u32[]{:S(2)}, u32[]{:S(2)}) collective-permute-start(bf16[10752,128]{1,0:T(8,128)(2,1)S(1)} %pack.1), channel_id=1, source_target_pairs={{0,1},{1,0},{2,3},{3,2},{4,5},{5,4},{6,7},{7,6},{8,9},{9,8},{10,11... | collective-permute-start | bytes 8257544 | tf_op jit(solution)/shard_map/ppermute | solution.py:460
  27.1 3.4 %collective-permute-start.5 = (bf16[120,3584]{1,0:T(8,128)(2,1)S(1)}, bf16[120,3584]{1,0:T(8,128)(2,1)S(1)}, u32[]{:S(2)}, u32[]{:S(2)}) collective-permute-start(bf16[120,3584]{1,0:T(8,128)(2,1)S(1)} %get-tuple-element.24), channel_id=1, source_target_pairs={{0,2},{1,9},{2,4},{3,11},{4,6},{5,13},{6,0},{7,15},{8,10},{9,17},{... | collective-permute-start | bytes 2580488 | tf_op jit(solution)/shard_map/ppermute | solution.py:36
  30.5 3.7 %collective-permute-start.6 = (bf16[120,3584]{1,0:T(8,128)(2,1)S(1)}, bf16[120,3584]{1,0:T(8,128)(2,1)S(1)}, u32[]{:S(2)}, u32[]{:S(2)}) collective-permute-start(bf16[120,3584]{1,0:T(8,128)(2,1)S(1)} %get-tuple-element.25), channel_id=1, source_target_pairs={{0,6},{1,25},{2,0},{3,27},{4,2},{5,29},{6,4},{7,31},{8,14},{9,1},{... | collective-permute-start | bytes 2580488 | tf_op jit(solution)/shard_map/ppermute | solution.py:36
  34.8 5.6 %collective-permute-start.1 = (bf16[1,48,224]{2,1,0:T(8,128)(2,1)S(1)}, bf16[1,48,224]{2,1,0:T(8,128)(2,1)S(1)}, u32[]{:S(2)}, u32[]{:S(2)}) collective-permute-start(bf16[1,48,224]{2,1,0:T(8,128)(2,1)S(1)} %blocks.3), channel_id=1, source_target_pairs={{32,0},{96,64},{160,128},{224,192},{448,480},{384,416},{320,352},{... | collective-permute-start | bytes 64520 | tf_op jit(solution)/shard_map/ppermute | solution.py:467
  40.3 1.1 rest.1
  41.5 1.0 experts.3
  43.0 2.2 %collective-permute-done.6.refs_1_ = bf16[120,3584]{1,0:T(8,128)(2,1)S(1)} collective-permute-done((bf16[120,3584]{1,0:T(8,128)(2,1)S(1)}, bf16[120,3584]{1,0:T(8,128)(2,1)S(1)}, u32[]{:S(2)}, u32[]{:S(2)}) %collective-permute-start.6) | collective-permute-done | bytes 860192 | tf_op jit(solution)/shard_map/ppermute | solution.py:36
  45.6 4.7 %collective-permute-start.7 = (bf16[120,3584]{1,0:T(8,128)(2,1)S(1)}, bf16[120,3584]{1,0:T(8,128)(2,1)S(1)}, u32[]{:S(2)}, u32[]{:S(2)}) collective-permute-start(bf16[120,3584]{1,0:T(8,128)(2,1)S(1)} %far.1), channel_id=1, source_target_pairs={{0,4},{1,17},{2,6},{3,19},{4,0},{5,21},{6,2},{7,23},{8,12},{9,25},... | collective-permute-start | bytes 2580488 | tf_op jit(solution)/shard_map/ppermute | solution.py:36
  50.3 1.7 %experts.4 = (bf16[120,3584]{1,0:T(8,128)(2,1)S(1)}, bf16[120,3584]{1,0:T(8,128)(2,1)S(1)}, s32[8,128]{1,0:T(8,128)S(1)}) custom-call(bf16[120,3584]{1,0:T(8,128)(2,1)S(1)} %collective-permute-done.5.refs_0_, bf16[120,3584]{1,0:T(8,128)(2,1)S(1)} %collective-permute-done.6.refs_1_, bf16[3584,128]{1,0:T(8,128)(2,1)S(1)} %bitcast.28, ...), custom_call_target="tpu_custom_call" | custom-call | tf_op jit(solution)/shard_map/experts/pallas_call | solution.py:397
  52.0 3.3 %collective-permute-start.9 = (bf16[120,3584]{1,0:T(8,128)(2,1)S(1)}, bf16[120,3584]{1,0:T(8,128)(2,1)S(1)}, u32[]{:S(2)}, u32[]{:S(2)}) collective-permute-start(bf16[120,3584]{1,0:T(8,128)(2,1)S(1)} %get-tuple-element.31), channel_id=1, source_target_pairs={{0,6},{1,25},{2,0},{3,27},{4,2},{5,29},{6,4},{7,31},{8,14},{9,1},{... | collective-permute-start | bytes 2580488 | tf_op jit(solution)/shard_map/ppermute | solution.py:36
  55.3 2.5 %collective-permute-start.10 = (bf16[120,3584]{1,0:T(8,128)(2,1)S(1)}, bf16[120,3584]{1,0:T(8,128)(2,1)S(1)}, u32[]{:S(2)}, u32[]{:S(2)}) collective-permute-start(bf16[120,3584]{1,0:T(8,128)(2,1)S(1)} %get-tuple-element.32), channel_id=1, source_target_pairs={{0,2},{1,9},{2,4},{3,11},{4,6},{5,13},{6,0},{7,15},{8,10},{9,17},{... | collective-permute-start | bytes 2580488 | tf_op jit(solution)/shard_map/ppermute | solution.py:36
  57.8 4.0 %collective-permute-done.7.refs_0_ = bf16[120,3584]{1,0:T(8,128)(2,1)S(1)} collective-permute-done((bf16[120,3584]{1,0:T(8,128)(2,1)S(1)}, bf16[120,3584]{1,0:T(8,128)(2,1)S(1)}, u32[]{:S(2)}, u32[]{:S(2)}) %collective-permute-start.7) | collective-permute-done | bytes 860192 | tf_op jit(solution)/shard_map/ppermute | solution.py:36
  61.8 1.5 %experts.5 = (bf16[120,3584]{1,0:T(8,128)(2,1)S(1)}, s32[8,128]{1,0:T(8,128)}) custom-call(bf16[120,3584]{1,0:T(8,128)(2,1)S(1)} %collective-permute-done.7.refs_0_, bf16[3584,128]{1,0:T(8,128)(2,1)S(1)} %bitcast.29, bf16[3584,128]{1,0:T(8,128)(2,1)S(1)} %bitcast.33, bf16[128,3584]{1,0:T(8,128)(2,1)S(1)} %bitcast.37, ...), custom_call_target="tpu_custom_call" | custom-call | tf_op jit(solution)/shard_map/experts/pallas_call | solution.py:397
  63.3 4.7 %collective-permute-start.8 = (bf16[120,3584]{1,0:T(8,128)(2,1)S(1)}, bf16[120,3584]{1,0:T(8,128)(2,1)S(1)}, u32[]{:S(2)}, u32[]{:S(2)}) collective-permute-start(bf16[120,3584]{1,0:T(8,128)(2,1)S(1)} %get-tuple-element.29), channel_id=1, source_target_pairs={{0,4},{1,17},{2,6},{3,19},{4,0},{5,21},{6,2},{7,23},{8,12},{9,25},... | collective-permute-start | bytes 2580488 | tf_op jit(solution)/shard_map/ppermute | solution.py:36
  69.5 1.8 %collective-permute-done.9.refs_2_ = bf16[120,3584]{1,0:T(8,128)(2,1)S(1)} collective-permute-done((bf16[120,3584]{1,0:T(8,128)(2,1)S(1)}, bf16[120,3584]{1,0:T(8,128)(2,1)S(1)}, u32[]{:S(2)}, u32[]{:S(2)}) %collective-permute-start.9) | collective-permute-done | bytes 860192 | tf_op jit(solution)/shard_map/ppermute | solution.py:36
  71.3 9.1 %collective-permute-done.10.refs_3_ = bf16[120,3584]{1,0:T(8,128)(2,1)S(1)} collective-permute-done((bf16[120,3584]{1,0:T(8,128)(2,1)S(1)}, bf16[120,3584]{1,0:T(8,128)(2,1)S(1)}, u32[]{:S(2)}, u32[]{:S(2)}) %collective-permute-start.10) | collective-permute-done | bytes 860192 | tf_op jit(solution)/shard_map/ppermute | solution.py:36
  80.4 2.3 %gather.2.refs_2_ = f32[192,3584]{1,0:T(8,128)S(1)} custom-call(bf16[192,1024]{1,0:T(8,128)(2,1)S(1)} %get-tuple-element.23.refs_0_, bf16[120,3584]{1,0:T(8,128)(2,1)S(1)} %get-tuple-element.30.refs_1_, bf16[120,3584]{1,0:T(8,128)(2,1)S(1)} %collective-permute-done.9.refs_2_, bf16[120,3584]{1,0:T(8,128)(2,1)S(1)} %collective-permute-done.10.refs_3_), custom_call_target="tpu_custom_call" | custom-call | tf_op jit(solution)/shard_map/gather/pallas_call | solution.py:415
  82.7 2.0 %gather.3 = bf16[192,3584]{1,0:T(8,128)(2,1)} custom-call(bf16[192,1024]{1,0:T(8,128)(2,1)S(1)} %get-tuple-element.23.refs_0_, bf16[120,3584]{1,0:T(8,128)(2,1)S(1)} %collective-permute-done.8.refs_1_, f32[192,3584]{1,0:T(8,128)S(1)} %gather.2.refs_2_, bf16[4,48,224]{2,1,0:T(8,128)(2,1)S(1)} %collective-permute-done.3.refs_3_), custom_call_target="tpu_custom_call" | custom-call | tf_op jit(solution)/shard_map/gather/pallas_call | solution.py:415
  84.8 3.7 %all-to-all-start.1 = ((bf16[4,48,3584]{2,1,0:T(8,128)(2,1)}), bf16[4,48,3584]{2,1,0:T(8,128)(2,1)S(1)}, u32[]{:S(2)}, u32[]{:S(2)}) async-start(bf16[4,48,3584]{2,1,0:T(8,128)(2,1)} %bitcast.15), calls=%async_computation.1 | async-start | bytes 2752512 | tf_op jit(solution)/shard_map/all_to_all | solution.py:50
  89.2 11.8 %all-to-all-done.1 = bf16[4,48,3584]{2,1,0:T(8,128)(2,1)S(1)} async-done(((bf16[4,48,3584]{2,1,0:T(8,128)(2,1)}), bf16[4,48,3584]{2,1,0:T(8,128)(2,1)S(1)}, u32[]{:S(2)}, u32[]{:S(2)}) %all-to-all-start.1) | async-done | bytes 1376288 | tf_op jit(solution)/shard_map/all_to_all | solution.py:50
  101.1 1.7 %finish.1 = (bf16[24,3584]{1,0:T(8,128)(2,1)S(1)}, bf16[24,3584]{1,0:T(8,128)(2,1)S(1)}, bf16[24,1792]{1,0:T(8,128)(2,1)S(1)}) custom-call(s32[4]{0:T(128)S(1)} %pad_add_fusion.place_ref, f32[48,128]{1,0:T(8,128)S(1)} %get-tuple-element.22.meta_ref, bf16[192,3584]{1,0:T(8,128)(2,1)S(1)} %bitcast.38, bf16[24,3584]{1,0:T(8,128)(2,1)S(1)} %bitcast.41, ...), custom_call_target="tpu_custom_call" | custom-call | tf_op jit(solution)/shard_map/finish/pallas_call | solution.py:426
  102.8 6.6 %collective-permute-start.13 = (bf16[24,3584]{1,0:T(8,128)(2,1)S(1)}, bf16[24,3584]{1,0:T(8,128)(2,1)S(1)}, u32[]{:S(2)}, u32[]{:S(2)}) collective-permute-start(bf16[24,3584]{1,0:T(8,128)(2,1)S(1)} %get-tuple-element.34.own_ref), channel_id=1, source_target_pairs={{32,0},{64,32},{96,64},{128,96},{160,128},{192,160},{224,192},{448... | collective-permute-start | bytes 516104 | tf_op jit(solution)/shard_map/ppermute | solution.py:448
  110.1 1.1 blocks.4.refs_1_
  111.2 1.1 collective-permute-done.13.refs_0_
  112.3 1.0 blocks.5
  115.4 2.2 %collective-permute-start.11 = (bf16[24,3584]{1,0:T(8,128)(2,1)S(1)}, bf16[24,3584]{1,0:T(8,128)(2,1)S(1)}, u32[]{:S(2)}, u32[]{:S(2)}) collective-permute-start(bf16[24,3584]{1,0:T(8,128)(2,1)S(1)} %get-tuple-element.33), channel_id=1, source_target_pairs={{0,32},{32,64},{64,96},{96,128},{128,160},{160,192},{192,224},{480... | collective-permute-start | bytes 516104 | tf_op jit(solution)/shard_map/ppermute | solution.py:448
  118.4 1.3 collective-permute-start.18
  119.7 10.7 %collective-permute-done.11 = bf16[24,3584]{1,0:T(8,128)(2,1)S(1)} collective-permute-done((bf16[24,3584]{1,0:T(8,128)(2,1)S(1)}, bf16[24,3584]{1,0:T(8,128)(2,1)S(1)}, u32[]{:S(2)}, u32[]{:S(2)}) %collective-permute-start.11) | collective-permute-done | bytes 172064 | tf_op jit(solution)/shard_map/ppermute | solution.py:448
  (58 shorter events, 11.7 us)
Async XLA Ops:
  0.7 0.9 copy-start.3
  1.7 0.9 copy-start.5
  2.6 0.7 copy-start.7
  3.3 0.7 copy-start.10
  4.0 0.7 copy-start.11
  6.0 18.8 %copy-start.1 = (bf16[1,3584,128]{2,1,0:T(8,128)(2,1)S(1)}, bf16[1,3584,128]{2,1,0:T(8,128)(2,1)}, u32[]{:S(2)}) copy-start(bf16[1,3584,128]{2,1,0:T(8,128)(2,1)} %param.16) | copy-start | bytes 2752516
  6.1 18.8 %copy-start.2 = (bf16[1,128,3584]{2,1,0:T(8,128)(2,1)S(1)}, bf16[1,128,3584]{2,1,0:T(8,128)(2,1)}, u32[]{:S(2)}) copy-start(bf16[1,128,3584]{2,1,0:T(8,128)(2,1)} %param.17) | copy-start | bytes 2752516
  23.4 1.5 %copy-start = (bf16[1,3584,128]{2,1,0:T(8,128)(2,1)S(1)}, bf16[1,3584,128]{2,1,0:T(8,128)(2,1)}, u32[]{:S(2)}) copy-start(bf16[1,3584,128]{2,1,0:T(8,128)(2,1)} %param.15) | copy-start | bytes 2752516
  24.9 9.3 %copy-start.8 = (bf16[1,24,224]{2,1,0:T(8,128)(2,1)S(1)}, bf16[1,24,224]{2,1,0:T(8,128)(2,1)}, u32[]{:S(2)}) copy-start(bf16[1,24,224]{2,1,0:T(8,128)(2,1)} %fwd_ref.1) | copy-start | bytes 32260
  24.9 9.3 %copy-start.9 = (bf16[1,24,224]{2,1,0:T(8,128)(2,1)S(1)}, bf16[1,24,224]{2,1,0:T(8,128)(2,1)}, u32[]{:S(2)}) copy-start(bf16[1,24,224]{2,1,0:T(8,128)(2,1)} %bwd_ref.1) | copy-start | bytes 32260
  25.2 9.0 %collective-permute-start = (bf16[10752,128]{1,0:T(8,128)(2,1)S(1)}, bf16[10752,128]{1,0:T(8,128)(2,1)S(1)}, u32[]{:S(2)}, u32[]{:S(2)}) collective-permute-start(bf16[10752,128]{1,0:T(8,128)(2,1)S(1)} %pack.1), channel_id=1, source_target_pairs={{0,1},{1,0},{2,3},{3,2},{4,5},{5,4},{6,7},{7,6},{8,9},{9,8},{10,11... | collective-permute-start | bytes 8257544 | tf_op jit(solution)/shard_map/ppermute | solution.py:460
  27.1 15.9 %collective-permute-start.5 = (bf16[120,3584]{1,0:T(8,128)(2,1)S(1)}, bf16[120,3584]{1,0:T(8,128)(2,1)S(1)}, u32[]{:S(2)}, u32[]{:S(2)}) collective-permute-start(bf16[120,3584]{1,0:T(8,128)(2,1)S(1)} %get-tuple-element.24), channel_id=1, source_target_pairs={{0,2},{1,9},{2,4},{3,11},{4,6},{5,13},{6,0},{7,15},{8,10},{9,17},{... | collective-permute-start | bytes 2580488 | tf_op jit(solution)/shard_map/ppermute | solution.py:36
  30.5 14.7 %collective-permute-start.6 = (bf16[120,3584]{1,0:T(8,128)(2,1)S(1)}, bf16[120,3584]{1,0:T(8,128)(2,1)S(1)}, u32[]{:S(2)}, u32[]{:S(2)}) collective-permute-start(bf16[120,3584]{1,0:T(8,128)(2,1)S(1)} %get-tuple-element.25), channel_id=1, source_target_pairs={{0,6},{1,25},{2,0},{3,27},{4,2},{5,29},{6,4},{7,31},{8,14},{9,1},{... | collective-permute-start | bytes 2580488 | tf_op jit(solution)/shard_map/ppermute | solution.py:36
  34.8 10.4 %collective-permute-start.1 = (bf16[1,48,224]{2,1,0:T(8,128)(2,1)S(1)}, bf16[1,48,224]{2,1,0:T(8,128)(2,1)S(1)}, u32[]{:S(2)}, u32[]{:S(2)}) collective-permute-start(bf16[1,48,224]{2,1,0:T(8,128)(2,1)S(1)} %blocks.3), channel_id=1, source_target_pairs={{32,0},{96,64},{160,128},{224,192},{448,480},{384,416},{320,352},{... | collective-permute-start | bytes 64520 | tf_op jit(solution)/shard_map/ppermute | solution.py:467
  45.6 16.2 %collective-permute-start.7 = (bf16[120,3584]{1,0:T(8,128)(2,1)S(1)}, bf16[120,3584]{1,0:T(8,128)(2,1)S(1)}, u32[]{:S(2)}, u32[]{:S(2)}) collective-permute-start(bf16[120,3584]{1,0:T(8,128)(2,1)S(1)} %far.1), channel_id=1, source_target_pairs={{0,4},{1,17},{2,6},{3,19},{4,0},{5,21},{6,2},{7,23},{8,12},{9,25},... | collective-permute-start | bytes 2580488 | tf_op jit(solution)/shard_map/ppermute | solution.py:36
  52.0 19.4 %collective-permute-start.9 = (bf16[120,3584]{1,0:T(8,128)(2,1)S(1)}, bf16[120,3584]{1,0:T(8,128)(2,1)S(1)}, u32[]{:S(2)}, u32[]{:S(2)}) collective-permute-start(bf16[120,3584]{1,0:T(8,128)(2,1)S(1)} %get-tuple-element.31), channel_id=1, source_target_pairs={{0,6},{1,25},{2,0},{3,27},{4,2},{5,29},{6,4},{7,31},{8,14},{9,1},{... | collective-permute-start | bytes 2580488 | tf_op jit(solution)/shard_map/ppermute | solution.py:36
  55.3 25.1 %collective-permute-start.10 = (bf16[120,3584]{1,0:T(8,128)(2,1)S(1)}, bf16[120,3584]{1,0:T(8,128)(2,1)S(1)}, u32[]{:S(2)}, u32[]{:S(2)}) collective-permute-start(bf16[120,3584]{1,0:T(8,128)(2,1)S(1)} %get-tuple-element.32), channel_id=1, source_target_pairs={{0,2},{1,9},{2,4},{3,11},{4,6},{5,13},{6,0},{7,15},{8,10},{9,17},{... | collective-permute-start | bytes 2580488 | tf_op jit(solution)/shard_map/ppermute | solution.py:36
  63.3 19.4 %collective-permute-start.8 = (bf16[120,3584]{1,0:T(8,128)(2,1)S(1)}, bf16[120,3584]{1,0:T(8,128)(2,1)S(1)}, u32[]{:S(2)}, u32[]{:S(2)}) collective-permute-start(bf16[120,3584]{1,0:T(8,128)(2,1)S(1)} %get-tuple-element.29), channel_id=1, source_target_pairs={{0,4},{1,17},{2,6},{3,19},{4,0},{5,21},{6,2},{7,23},{8,12},{9,25},... | collective-permute-start | bytes 2580488 | tf_op jit(solution)/shard_map/ppermute | solution.py:36
  68.1 0.7 collective-permute-start.2
  68.8 13.9 %collective-permute-start.3 = (bf16[4,48,224]{2,1,0:T(8,128)(2,1)S(1)}, bf16[4,48,224]{2,1,0:T(8,128)(2,1)S(1)}, u32[]{:S(2)}, u32[]{:S(2)}) collective-permute-start(bf16[4,48,224]{2,1,0:T(8,128)(2,1)S(1)} %pad_maximum_fusion.1), channel_id=1, source_target_pairs={{128,0},{352,480},{129,1},{353,481},{130,2},{354,482},{131,3},{355... | collective-permute-start | bytes 258056 | tf_op jit(solution)/shard_map/ppermute | solution.py:467
  84.8 16.3 %copy-start.4 = (bf16[1,24,3584]{2,1,0:T(8,128)(2,1)S(1)}, bf16[1,24,3584]{2,1,0:T(8,128)(2,1)}, u32[]{:S(2)}) copy-start(bf16[1,24,3584]{2,1,0:T(8,128)(2,1)} %param.10) | copy-start | bytes 516100
  84.8 16.3 %copy-start.6 = (bf16[1,24,3584]{2,1,0:T(8,128)(2,1)S(1)}, bf16[1,24,3584]{2,1,0:T(8,128)(2,1)}, u32[]{:S(2)}) copy-start(bf16[1,24,3584]{2,1,0:T(8,128)(2,1)} %param.11) | copy-start | bytes 516100
  84.8 16.3 %all-to-all-start.1 = ((bf16[4,48,3584]{2,1,0:T(8,128)(2,1)}), bf16[4,48,3584]{2,1,0:T(8,128)(2,1)S(1)}, u32[]{:S(2)}, u32[]{:S(2)}) async-start(bf16[4,48,3584]{2,1,0:T(8,128)(2,1)} %bitcast.15), calls=%async_computation.1 | async-start | bytes 2752512 | tf_op jit(solution)/shard_map/all_to_all | solution.py:50
  88.5 0.7 collective-permute-start.4
  102.8 9.6 %collective-permute-start.13 = (bf16[24,3584]{1,0:T(8,128)(2,1)S(1)}, bf16[24,3584]{1,0:T(8,128)(2,1)S(1)}, u32[]{:S(2)}, u32[]{:S(2)}) collective-permute-start(bf16[24,3584]{1,0:T(8,128)(2,1)S(1)} %get-tuple-element.34.own_ref), channel_id=1, source_target_pairs={{32,0},{64,32},{96,64},{128,96},{160,128},{192,160},{224,192},{448... | collective-permute-start | bytes 516104 | tf_op jit(solution)/shard_map/ppermute | solution.py:448
  109.4 1.8 %collective-permute-start.14 = (bf16[24,1792]{1,0:T(8,128)(2,1)S(1)}, bf16[24,1792]{1,0:T(8,128)(2,1)S(1)}, u32[]{:S(2)}, u32[]{:S(2)}) collective-permute-start(bf16[24,1792]{1,0:T(8,128)(2,1)S(1)} %get-tuple-element.35), channel_id=1, source_target_pairs={{0,480},{480,0},{1,481},{481,1},{2,482},{482,2},{3,483},{483,3},{4... | collective-permute-start | bytes 258056 | tf_op jit(solution)/shard_map/ppermute | solution.py:452
  113.4 4.9 %collective-permute-start.15 = (bf16[2,48,224]{2,1,0:T(8,128)(2,1)S(1)}, bf16[2,48,224]{2,1,0:T(8,128)(2,1)S(1)}, u32[]{:S(2)}, u32[]{:S(2)}) collective-permute-start(bf16[2,48,224]{2,1,0:T(8,128)(2,1)S(1)} %get-tuple-element.40), channel_id=1, source_target_pairs={{0,192},{480,288},{1,193},{481,289},{2,194},{482,290},{3,195},{483... | collective-permute-start | bytes 129032 | tf_op jit(solution)/shard_map/ppermute | solution.py:473
  114.1 4.3 %collective-permute-start.16 = (bf16[2,48,224]{2,1,0:T(8,128)(2,1)S(1)}, bf16[2,48,224]{2,1,0:T(8,128)(2,1)S(1)}, u32[]{:S(2)}, u32[]{:S(2)}) collective-permute-start(bf16[2,48,224]{2,1,0:T(8,128)(2,1)S(1)} %get-tuple-element.39), channel_id=1, source_target_pairs={{0,128},{480,352},{1,129},{481,353},{2,130},{482,354},{3,131},{483... | collective-permute-start | bytes 129032 | tf_op jit(solution)/shard_map/ppermute | solution.py:473
  114.7 3.6 %collective-permute-start.17 = (bf16[2,48,224]{2,1,0:T(8,128)(2,1)S(1)}, bf16[2,48,224]{2,1,0:T(8,128)(2,1)S(1)}, u32[]{:S(2)}, u32[]{:S(2)}) collective-permute-start(bf16[2,48,224]{2,1,0:T(8,128)(2,1)S(1)} %get-tuple-element.38), channel_id=1, source_target_pairs={{0,64},{480,416},{1,65},{481,417},{2,66},{482,418},{3,67},{483,419... | collective-permute-start | bytes 129032 | tf_op jit(solution)/shard_map/ppermute | solution.py:473
  115.4 14.9 %collective-permute-start.11 = (bf16[24,3584]{1,0:T(8,128)(2,1)S(1)}, bf16[24,3584]{1,0:T(8,128)(2,1)S(1)}, u32[]{:S(2)}, u32[]{:S(2)}) collective-permute-start(bf16[24,3584]{1,0:T(8,128)(2,1)S(1)} %get-tuple-element.33), channel_id=1, source_target_pairs={{0,32},{32,64},{64,96},{96,128},{128,160},{160,192},{192,224},{480... | collective-permute-start | bytes 516104 | tf_op jit(solution)/shard_map/ppermute | solution.py:448
  117.7 12.7 %collective-permute-start.12 = (bf16[24,3584]{1,0:T(8,128)(2,1)S(1)}, bf16[24,3584]{1,0:T(8,128)(2,1)S(1)}, u32[]{:S(2)}, u32[]{:S(2)}) collective-permute-start(bf16[24,3584]{1,0:T(8,128)(2,1)S(1)} %get-tuple-element.33), channel_id=1, source_target_pairs={{224,256},{256,224},{225,257},{257,225},{226,258},{258,226},{227,2... | collective-permute-start | bytes 516104 | tf_op jit(solution)/shard_map/ppermute | solution.py:448
  118.4 12.8 %collective-permute-start.18 = (bf16[1,48,224]{2,1,0:T(8,128)(2,1)S(1)}, bf16[1,48,224]{2,1,0:T(8,128)(2,1)S(1)}, u32[]{:S(2)}, u32[]{:S(2)}) collective-permute-start(bf16[1,48,224]{2,1,0:T(8,128)(2,1)S(1)} %slice.48), channel_id=1, source_target_pairs={{0,32},{64,96},{128,160},{192,224},{480,448},{416,384},{352,320},{... | collective-permute-start | bytes 64520 | tf_op jit(solution)/shard_map/ppermute | solution.py:473

commit v14 on v13

--- a/solution.py
+++ b/solution.py
@@ -516,7 +516,7 @@
         enter_kernel, (1, BOTH, part), place, enter_fwd, enter_bwd, before=(weights[1],)
     )
     held, got = inward(entering, 1, 2, sections)
-    last = hop(make_far(rows, pick, near, far, got, token), 2)
+    last = hop(make_far(rows, pick, near, got, token), 2)
     done1, done3, token = run_experts([near, far], *weights)
     back1, back3 = hop(done1, -1), hop(done3, -3)
     done2, token = run_experts([last], *weights, token)

time: 133 us -> 143 us (1.075)
  waiting for transfers between devices: 41.2 us -> 49 us
  starting transfers between devices: 48.9 us -> 51.9 us
    ppermute x3, starting transfers between devices: 9.52 us -> 17 us  [move_pp(): return lax.ppermute(block, 'pp', mirrored(pairs, sections))]
    ppermute x6, waiting for transfers between devices: 17.6 us -> 23.1 us  [hop(): return lax.ppermute(block, 'ep', route)]
    ppermute x6, starting transfers between devices: 22.3 us -> 17.7 us  [hop(): return lax.ppermute(block, 'ep', route)]
    ppermute x1, waiting for transfers between devices: 0.01 us -> 1.66 us  [from_other_core(): lax.ppermute(block, 'ep', [(i, i ^ 1) for i in range(lax.axis_size('ep'))])]
where the time goes in v14:
time: 143 us; the launch traced here: 142 us
  starting transfers between devices  51.9 us (36%)
  waiting for transfers between devices  49 us (34%)
  Pallas kernels  17.6 us (12%)
  blocking collectives  17.3 us (12%)
  local copies, waits for them, and re-layouts  4.57 us (3%)
    ppermute x6, waiting for transfers between devices, hop(): return lax.ppermute(block, 'ep', route)  23.1 us
    ppermute x6, starting transfers between devices, hop(): return lax.ppermute(block, 'ep', route)  17.7 us
    all_to_all x1, blocking collectives, exchange(): lax.all_to_all(rows, 'ep', split_axis=0, concat_axis=0, axis_index_groups...  17.3 us
    ppermute x3, starting transfers between devices, move_pp(): return lax.ppermute(block, 'pp', mirrored(pairs, sections))  17 us
    ppermute x3, waiting for transfers between devices, move_pp(): return lax.ppermute(block, 'pp', mirrored(pairs, sections))  12.4 us
    all_to_all x1, waiting for transfers between devices, exchange(): lax.all_to_all(rows, 'ep', split_axis=0, concat_axis=0, axis_index_groups...  11.8 us
    ppermute x3, starting transfers between devices, inward(): got.append(lax.ppermute(held, 'pp', mirrored(pairs, sections)))  6.89 us
    pallas_call x2, Pallas kernels, make_gather(): pl.pallas_call(body, out_shape=shape(total, features, BF if last else F32...  4.33 us
  transfers between devices with their start and end apart: 20, of which 8 were waited for; matrix products, arithmetic and copies ran while one was open for 1% of the time, Pallas kernels for 7%

profile of v14, /device:TPU:32, one launch (start us, length us, event | category | flops | bytes accessed | tf_op | source)
XLA Modules:
  0.0 142.5 jit_solution(13031292204729720473)
XLA Ops:
  0.7 0.9 copy-done.3
  4.6 1.4 normed.1
  6.1 17.3 %all_to_all.22 = bf16[4,48,3712]{2,1,0:T(8,128)(2,1)S(1)} all-to-all(bf16[4,48,3712]{2,1,0:T(8,128)(2,1)S(1)} %bitcast.39), channel_id=1, replica_groups={{0,8,16,24},{2,10,18,26},{4,12,20,28},{6,14,22,30},{1,3,5,7},{9,11,13,1..., dimensions={0} | all-to-all | bytes 2850816 | tf_op jit(solution)/shard_map/all_to_all | solution.py:50
  23.4 1.5 %near.1 = (bf16[120,3584]{1,0:T(8,128)(2,1)S(1)}, bf16[120,3584]{1,0:T(8,128)(2,1)S(1)}, bf16[512,192]{1,0:T(8,128)(2,1)S(1)}, s32[8,128]{1,0:T(8,128)}) custom-call(s32[4]{0:T(128)S(1)} %pad_add_fusion.place_ref, bf16[192,3712]{1,0:T(8,128)(2,1)S(1)} %bitcast.23), custom_call_target="tpu_custom_call" | custom-call | tf_op jit(solution)/shard_map/near/pallas_call | solution.py:333
  25.2 1.9 %collective-permute-start = (bf16[10752,128]{1,0:T(8,128)(2,1)S(1)}, bf16[10752,128]{1,0:T(8,128)(2,1)S(1)}, u32[]{:S(2)}, u32[]{:S(2)}) collective-permute-start(bf16[10752,128]{1,0:T(8,128)(2,1)S(1)} %pack.1), channel_id=1, source_target_pairs={{0,1},{1,0},{2,3},{3,2},{4,5},{5,4},{6,7},{7,6},{8,9},{9,8},{10,11... | collective-permute-start | bytes 8257544 | tf_op jit(solution)/shard_map/ppermute | solution.py:460
  27.1 3.4 %collective-permute-start.5 = (bf16[120,3584]{1,0:T(8,128)(2,1)S(1)}, bf16[120,3584]{1,0:T(8,128)(2,1)S(1)}, u32[]{:S(2)}, u32[]{:S(2)}) collective-permute-start(bf16[120,3584]{1,0:T(8,128)(2,1)S(1)} %get-tuple-element.24), channel_id=1, source_target_pairs={{0,2},{1,9},{2,4},{3,11},{4,6},{5,13},{6,0},{7,15},{8,10},{9,17},{... | collective-permute-start | bytes 2580488 | tf_op jit(solution)/shard_map/ppermute | solution.py:36
  30.5 1.7 %collective-permute-done._.refs_4_.refs_5_ = bf16[10752,128]{1,0:T(8,128)(2,1)S(1)} collective-permute-done((bf16[10752,128]{1,0:T(8,128)(2,1)S(1)}, bf16[10752,128]{1,0:T(8,128)(2,1)S(1)}, u32[]{:S(2)}, u32[]{:S(2)}) %collective-permute-start) | collective-permute-done | bytes 2752544 | tf_op jit(solution)/shard_map/ppermute | solution.py:460
  32.8 5.6 %collective-permute-start.1 = (bf16[1,48,224]{2,1,0:T(8,128)(2,1)S(1)}, bf16[1,48,224]{2,1,0:T(8,128)(2,1)S(1)}, u32[]{:S(2)}, u32[]{:S(2)}) collective-permute-start(bf16[1,48,224]{2,1,0:T(8,128)(2,1)S(1)} %blocks.3), channel_id=1, source_target_pairs={{32,0},{96,64},{160,128},{224,192},{448,480},{384,416},{320,352},{... | collective-permute-start | bytes 64520 | tf_op jit(solution)/shard_map/ppermute | solution.py:467
  38.3 2.0 %collective-permute-start.7 = (bf16[120,3584]{1,0:T(8,128)(2,1)S(1)}, bf16[120,3584]{1,0:T(8,128)(2,1)S(1)}, u32[]{:S(2)}, u32[]{:S(2)}) collective-permute-start(bf16[120,3584]{1,0:T(8,128)(2,1)S(1)} %get-tuple-element.27), channel_id=1, source_target_pairs={{0,6},{1,25},{2,0},{3,27},{4,2},{5,29},{6,4},{7,31},{8,14},{9,1},{... | collective-permute-start | bytes 2580488 | tf_op jit(solution)/shard_map/ppermute | solution.py:36
  40.3 1.1 rest.1
  41.5 1.0 experts.3
  43.4 3.7 %collective-permute-start.6 = (bf16[120,3584]{1,0:T(8,128)(2,1)S(1)}, bf16[120,3584]{1,0:T(8,128)(2,1)S(1)}, u32[]{:S(2)}, u32[]{:S(2)}) collective-permute-start(bf16[120,3584]{1,0:T(8,128)(2,1)S(1)} %far.1), channel_id=1, source_target_pairs={{0,4},{1,17},{2,6},{3,19},{4,0},{5,21},{6,2},{7,23},{8,12},{9,25},... | collective-permute-start | bytes 2580488 | tf_op jit(solution)/shard_map/ppermute | solution.py:36
  47.1 5.8 %collective-permute-done.7.refs_1_ = bf16[120,3584]{1,0:T(8,128)(2,1)S(1)} collective-permute-done((bf16[120,3584]{1,0:T(8,128)(2,1)S(1)}, bf16[120,3584]{1,0:T(8,128)(2,1)S(1)}, u32[]{:S(2)}, u32[]{:S(2)}) %collective-permute-start.7) | collective-permute-done | bytes 860192 | tf_op jit(solution)/shard_map/ppermute | solution.py:36
  53.0 1.7 %experts.4 = (bf16[120,3584]{1,0:T(8,128)(2,1)S(1)}, bf16[120,3584]{1,0:T(8,128)(2,1)S(1)}, s32[8,128]{1,0:T(8,128)S(1)}) custom-call(bf16[120,3584]{1,0:T(8,128)(2,1)S(1)} %collective-permute-done.5.refs_0_, bf16[120,3584]{1,0:T(8,128)(2,1)S(1)} %collective-permute-done.7.refs_1_, bf16[3584,128]{1,0:T(8,128)(2,1)S(1)} %bitcast.28, ...), custom_call_target="tpu_custom_call" | custom-call | tf_op jit(solution)/shard_map/experts/pallas_call | solution.py:397
  54.7 3.2 %collective-permute-start.9 = (bf16[120,3584]{1,0:T(8,128)(2,1)S(1)}, bf16[120,3584]{1,0:T(8,128)(2,1)S(1)}, u32[]{:S(2)}, u32[]{:S(2)}) collective-permute-start(bf16[120,3584]{1,0:T(8,128)(2,1)S(1)} %get-tuple-element.31), channel_id=1, source_target_pairs={{0,6},{1,25},{2,0},{3,27},{4,2},{5,29},{6,4},{7,31},{8,14},{9,1},{... | collective-permute-start | bytes 2580488 | tf_op jit(solution)/shard_map/ppermute | solution.py:36
  57.9 2.6 %collective-permute-start.10 = (bf16[120,3584]{1,0:T(8,128)(2,1)S(1)}, bf16[120,3584]{1,0:T(8,128)(2,1)S(1)}, u32[]{:S(2)}, u32[]{:S(2)}) collective-permute-start(bf16[120,3584]{1,0:T(8,128)(2,1)S(1)} %get-tuple-element.32), channel_id=1, source_target_pairs={{0,2},{1,9},{2,4},{3,11},{4,6},{5,13},{6,0},{7,15},{8,10},{9,17},{... | collective-permute-start | bytes 2580488 | tf_op jit(solution)/shard_map/ppermute | solution.py:36
  60.6 1.5 %experts.5 = (bf16[120,3584]{1,0:T(8,128)(2,1)S(1)}, s32[8,128]{1,0:T(8,128)}) custom-call(bf16[120,3584]{1,0:T(8,128)(2,1)S(1)} %collective-permute-done.6.refs_0_, bf16[3584,128]{1,0:T(8,128)(2,1)S(1)} %bitcast.29, bf16[3584,128]{1,0:T(8,128)(2,1)S(1)} %bitcast.33, bf16[128,3584]{1,0:T(8,128)(2,1)S(1)} %bitcast.37, ...), custom_call_target="tpu_custom_call" | custom-call | tf_op jit(solution)/shard_map/experts/pallas_call | solution.py:397
  62.1 2.7 %collective-permute-start.8 = (bf16[120,3584]{1,0:T(8,128)(2,1)S(1)}, bf16[120,3584]{1,0:T(8,128)(2,1)S(1)}, u32[]{:S(2)}, u32[]{:S(2)}) collective-permute-start(bf16[120,3584]{1,0:T(8,128)(2,1)S(1)} %get-tuple-element.29), channel_id=1, source_target_pairs={{0,4},{1,17},{2,6},{3,19},{4,0},{5,21},{6,2},{7,23},{8,12},{9,25},... | collective-permute-start | bytes 2580488 | tf_op jit(solution)/shard_map/ppermute | solution.py:36
  66.3 5.2 %collective-permute-done.9.refs_2_ = bf16[120,3584]{1,0:T(8,128)(2,1)S(1)} collective-permute-done((bf16[120,3584]{1,0:T(8,128)(2,1)S(1)}, bf16[120,3584]{1,0:T(8,128)(2,1)S(1)}, u32[]{:S(2)}, u32[]{:S(2)}) %collective-permute-start.9) | collective-permute-done | bytes 860192 | tf_op jit(solution)/shard_map/ppermute | solution.py:36
  71.5 11.6 %collective-permute-done.10.refs_3_ = bf16[120,3584]{1,0:T(8,128)(2,1)S(1)} collective-permute-done((bf16[120,3584]{1,0:T(8,128)(2,1)S(1)}, bf16[120,3584]{1,0:T(8,128)(2,1)S(1)}, u32[]{:S(2)}, u32[]{:S(2)}) %collective-permute-start.10) | collective-permute-done | bytes 860192 | tf_op jit(solution)/shard_map/ppermute | solution.py:36
  83.0 2.3 %gather.2.refs_2_ = f32[192,3584]{1,0:T(8,128)S(1)} custom-call(bf16[192,1024]{1,0:T(8,128)(2,1)S(1)} %get-tuple-element.23.refs_0_, bf16[120,3584]{1,0:T(8,128)(2,1)S(1)} %get-tuple-element.30.refs_1_, bf16[120,3584]{1,0:T(8,128)(2,1)S(1)} %collective-permute-done.9.refs_2_, bf16[120,3584]{1,0:T(8,128)(2,1)S(1)} %collective-permute-done.10.refs_3_), custom_call_target="tpu_custom_call" | custom-call | tf_op jit(solution)/shard_map/gather/pallas_call | solution.py:415
  85.4 2.0 %gather.3 = bf16[192,3584]{1,0:T(8,128)(2,1)} custom-call(bf16[192,1024]{1,0:T(8,128)(2,1)S(1)} %get-tuple-element.23.refs_0_, bf16[120,3584]{1,0:T(8,128)(2,1)S(1)} %collective-permute-done.8.refs_1_, f32[192,3584]{1,0:T(8,128)S(1)} %gather.2.refs_2_, bf16[4,48,224]{2,1,0:T(8,128)(2,1)S(1)} %collective-permute-done.3.refs_3_), custom_call_target="tpu_custom_call" | custom-call | tf_op jit(solution)/shard_map/gather/pallas_call | solution.py:415
  87.4 3.7 %all-to-all-start.1 = ((bf16[4,48,3584]{2,1,0:T(8,128)(2,1)}), bf16[4,48,3584]{2,1,0:T(8,128)(2,1)S(1)}, u32[]{:S(2)}, u32[]{:S(2)}) async-start(bf16[4,48,3584]{2,1,0:T(8,128)(2,1)} %bitcast.15), calls=%async_computation.1 | async-start | bytes 2752512 | tf_op jit(solution)/shard_map/all_to_all | solution.py:50
  91.9 11.8 %all-to-all-done.1 = bf16[4,48,3584]{2,1,0:T(8,128)(2,1)S(1)} async-done(((bf16[4,48,3584]{2,1,0:T(8,128)(2,1)}), bf16[4,48,3584]{2,1,0:T(8,128)(2,1)S(1)}, u32[]{:S(2)}, u32[]{:S(2)}) %all-to-all-start.1) | async-done | bytes 1376288 | tf_op jit(solution)/shard_map/all_to_all | solution.py:50
  103.7 1.7 %finish.1 = (bf16[24,3584]{1,0:T(8,128)(2,1)S(1)}, bf16[24,3584]{1,0:T(8,128)(2,1)S(1)}, bf16[24,1792]{1,0:T(8,128)(2,1)S(1)}) custom-call(s32[4]{0:T(128)S(1)} %pad_add_fusion.place_ref, f32[48,128]{1,0:T(8,128)S(1)} %get-tuple-element.22.meta_ref, bf16[192,3584]{1,0:T(8,128)(2,1)S(1)} %bitcast.38, bf16[24,3584]{1,0:T(8,128)(2,1)S(1)} %bitcast.41, ...), custom_call_target="tpu_custom_call" | custom-call | tf_op jit(solution)/shard_map/finish/pallas_call | solution.py:426
  105.4 11.7 %collective-permute-start.13 = (bf16[24,3584]{1,0:T(8,128)(2,1)S(1)}, bf16[24,3584]{1,0:T(8,128)(2,1)S(1)}, u32[]{:S(2)}, u32[]{:S(2)}) collective-permute-start(bf16[24,3584]{1,0:T(8,128)(2,1)S(1)} %get-tuple-element.34.own_ref), channel_id=1, source_target_pairs={{32,0},{64,32},{96,64},{128,96},{160,128},{192,160},{224,192},{448... | collective-permute-start | bytes 516104 | tf_op jit(solution)/shard_map/ppermute | solution.py:448
  117.8 1.1 blocks.4.refs_1_
  118.9 1.8 %collective-permute-done.13.refs_0_ = bf16[24,3584]{1,0:T(8,128)(2,1)S(1)} collective-permute-done((bf16[24,3584]{1,0:T(8,128)(2,1)S(1)}, bf16[24,3584]{1,0:T(8,128)(2,1)S(1)}, u32[]{:S(2)}, u32[]{:S(2)}) %collective-permute-start.13) | collective-permute-done | bytes 172064 | tf_op jit(solution)/shard_map/ppermute | solution.py:448
  120.7 1.0 blocks.5
  123.8 4.7 %collective-permute-start.11 = (bf16[24,3584]{1,0:T(8,128)(2,1)S(1)}, bf16[24,3584]{1,0:T(8,128)(2,1)S(1)}, u32[]{:S(2)}, u32[]{:S(2)}) collective-permute-start(bf16[24,3584]{1,0:T(8,128)(2,1)S(1)} %get-tuple-element.33), channel_id=1, source_target_pairs={{0,32},{32,64},{64,96},{96,128},{128,160},{160,192},{192,224},{480... | collective-permute-start | bytes 516104 | tf_op jit(solution)/shard_map/ppermute | solution.py:448
  129.2 1.3 collective-permute-start.18
  130.5 10.6 %collective-permute-done.11 = bf16[24,3584]{1,0:T(8,128)(2,1)S(1)} collective-permute-done((bf16[24,3584]{1,0:T(8,128)(2,1)S(1)}, bf16[24,3584]{1,0:T(8,128)(2,1)S(1)}, u32[]{:S(2)}, u32[]{:S(2)}) %collective-permute-start.11) | collective-permute-done | bytes 172064 | tf_op jit(solution)/shard_map/ppermute | solution.py:448
  (58 shorter events, 11.7 us)
Async XLA Ops:
  0.7 0.9 copy-start.3
  1.7 0.9 copy-start.5
  2.6 0.7 copy-start.7
  3.3 0.7 copy-start.10
  4.0 0.7 copy-start.11
  6.0 18.8 %copy-start.1 = (bf16[1,3584,128]{2,1,0:T(8,128)(2,1)S(1)}, bf16[1,3584,128]{2,1,0:T(8,128)(2,1)}, u32[]{:S(2)}) copy-start(bf16[1,3584,128]{2,1,0:T(8,128)(2,1)} %param.16) | copy-start | bytes 2752516
  6.1 18.8 %copy-start.2 = (bf16[1,128,3584]{2,1,0:T(8,128)(2,1)S(1)}, bf16[1,128,3584]{2,1,0:T(8,128)(2,1)}, u32[]{:S(2)}) copy-start(bf16[1,128,3584]{2,1,0:T(8,128)(2,1)} %param.17) | copy-start | bytes 2752516
  23.4 1.5 %copy-start = (bf16[1,3584,128]{2,1,0:T(8,128)(2,1)S(1)}, bf16[1,3584,128]{2,1,0:T(8,128)(2,1)}, u32[]{:S(2)}) copy-start(bf16[1,3584,128]{2,1,0:T(8,128)(2,1)} %param.15) | copy-start | bytes 2752516
  24.9 7.3 %copy-start.8 = (bf16[1,24,224]{2,1,0:T(8,128)(2,1)S(1)}, bf16[1,24,224]{2,1,0:T(8,128)(2,1)}, u32[]{:S(2)}) copy-start(bf16[1,24,224]{2,1,0:T(8,128)(2,1)} %fwd_ref.1) | copy-start | bytes 32260
  24.9 7.3 %copy-start.9 = (bf16[1,24,224]{2,1,0:T(8,128)(2,1)S(1)}, bf16[1,24,224]{2,1,0:T(8,128)(2,1)}, u32[]{:S(2)}) copy-start(bf16[1,24,224]{2,1,0:T(8,128)(2,1)} %bwd_ref.1) | copy-start | bytes 32260
  25.2 7.0 %collective-permute-start = (bf16[10752,128]{1,0:T(8,128)(2,1)S(1)}, bf16[10752,128]{1,0:T(8,128)(2,1)S(1)}, u32[]{:S(2)}, u32[]{:S(2)}) collective-permute-start(bf16[10752,128]{1,0:T(8,128)(2,1)S(1)} %pack.1), channel_id=1, source_target_pairs={{0,1},{1,0},{2,3},{3,2},{4,5},{5,4},{6,7},{7,6},{8,9},{9,8},{10,11... | collective-permute-start | bytes 8257544 | tf_op jit(solution)/shard_map/ppermute | solution.py:460
  27.1 15.9 %collective-permute-start.5 = (bf16[120,3584]{1,0:T(8,128)(2,1)S(1)}, bf16[120,3584]{1,0:T(8,128)(2,1)S(1)}, u32[]{:S(2)}, u32[]{:S(2)}) collective-permute-start(bf16[120,3584]{1,0:T(8,128)(2,1)S(1)} %get-tuple-element.24), channel_id=1, source_target_pairs={{0,2},{1,9},{2,4},{3,11},{4,6},{5,13},{6,0},{7,15},{8,10},{9,17},{... | collective-permute-start | bytes 2580488 | tf_op jit(solution)/shard_map/ppermute | solution.py:36
  32.8 10.3 %collective-permute-start.1 = (bf16[1,48,224]{2,1,0:T(8,128)(2,1)S(1)}, bf16[1,48,224]{2,1,0:T(8,128)(2,1)S(1)}, u32[]{:S(2)}, u32[]{:S(2)}) collective-permute-start(bf16[1,48,224]{2,1,0:T(8,128)(2,1)S(1)} %blocks.3), channel_id=1, source_target_pairs={{32,0},{96,64},{160,128},{224,192},{448,480},{384,416},{320,352},{... | collective-permute-start | bytes 64520 | tf_op jit(solution)/shard_map/ppermute | solution.py:467
  38.3 14.7 %collective-permute-start.7 = (bf16[120,3584]{1,0:T(8,128)(2,1)S(1)}, bf16[120,3584]{1,0:T(8,128)(2,1)S(1)}, u32[]{:S(2)}, u32[]{:S(2)}) collective-permute-start(bf16[120,3584]{1,0:T(8,128)(2,1)S(1)} %get-tuple-element.27), channel_id=1, source_target_pairs={{0,6},{1,25},{2,0},{3,27},{4,2},{5,29},{6,4},{7,31},{8,14},{9,1},{... | collective-permute-start | bytes 2580488 | tf_op jit(solution)/shard_map/ppermute | solution.py:36
  43.4 17.1 %collective-permute-start.6 = (bf16[120,3584]{1,0:T(8,128)(2,1)S(1)}, bf16[120,3584]{1,0:T(8,128)(2,1)S(1)}, u32[]{:S(2)}, u32[]{:S(2)}) collective-permute-start(bf16[120,3584]{1,0:T(8,128)(2,1)S(1)} %far.1), channel_id=1, source_target_pairs={{0,4},{1,17},{2,6},{3,19},{4,0},{5,21},{6,2},{7,23},{8,12},{9,25},... | collective-permute-start | bytes 2580488 | tf_op jit(solution)/shard_map/ppermute | solution.py:36
  54.7 16.8 %collective-permute-start.9 = (bf16[120,3584]{1,0:T(8,128)(2,1)S(1)}, bf16[120,3584]{1,0:T(8,128)(2,1)S(1)}, u32[]{:S(2)}, u32[]{:S(2)}) collective-permute-start(bf16[120,3584]{1,0:T(8,128)(2,1)S(1)} %get-tuple-element.31), channel_id=1, source_target_pairs={{0,6},{1,25},{2,0},{3,27},{4,2},{5,29},{6,4},{7,31},{8,14},{9,1},{... | collective-permute-start | bytes 2580488 | tf_op jit(solution)/shard_map/ppermute | solution.py:36
  57.9 25.1 %collective-permute-start.10 = (bf16[120,3584]{1,0:T(8,128)(2,1)S(1)}, bf16[120,3584]{1,0:T(8,128)(2,1)S(1)}, u32[]{:S(2)}, u32[]{:S(2)}) collective-permute-start(bf16[120,3584]{1,0:T(8,128)(2,1)S(1)} %get-tuple-element.32), channel_id=1, source_target_pairs={{0,2},{1,9},{2,4},{3,11},{4,6},{5,13},{6,0},{7,15},{8,10},{9,17},{... | collective-permute-start | bytes 2580488 | tf_op jit(solution)/shard_map/ppermute | solution.py:36
  62.1 23.2 %collective-permute-start.8 = (bf16[120,3584]{1,0:T(8,128)(2,1)S(1)}, bf16[120,3584]{1,0:T(8,128)(2,1)S(1)}, u32[]{:S(2)}, u32[]{:S(2)}) collective-permute-start(bf16[120,3584]{1,0:T(8,128)(2,1)S(1)} %get-tuple-element.29), channel_id=1, source_target_pairs={{0,4},{1,17},{2,6},{3,19},{4,0},{5,21},{6,2},{7,23},{8,12},{9,25},... | collective-permute-start | bytes 2580488 | tf_op jit(solution)/shard_map/ppermute | solution.py:36
  64.9 0.7 collective-permute-start.2
  65.6 19.8 %collective-permute-start.3 = (bf16[4,48,224]{2,1,0:T(8,128)(2,1)S(1)}, bf16[4,48,224]{2,1,0:T(8,128)(2,1)S(1)}, u32[]{:S(2)}, u32[]{:S(2)}) collective-permute-start(bf16[4,48,224]{2,1,0:T(8,128)(2,1)S(1)} %pad_maximum_fusion.1), channel_id=1, source_target_pairs={{128,0},{352,480},{129,1},{353,481},{130,2},{354,482},{131,3},{355... | collective-permute-start | bytes 258056 | tf_op jit(solution)/shard_map/ppermute | solution.py:467
  87.4 16.3 %copy-start.4 = (bf16[1,24,3584]{2,1,0:T(8,128)(2,1)S(1)}, bf16[1,24,3584]{2,1,0:T(8,128)(2,1)}, u32[]{:S(2)}) copy-start(bf16[1,24,3584]{2,1,0:T(8,128)(2,1)} %param.10) | copy-start | bytes 516100
  87.4 16.3 %copy-start.6 = (bf16[1,24,3584]{2,1,0:T(8,128)(2,1)S(1)}, bf16[1,24,3584]{2,1,0:T(8,128)(2,1)}, u32[]{:S(2)}) copy-start(bf16[1,24,3584]{2,1,0:T(8,128)(2,1)} %param.11) | copy-start | bytes 516100
  87.4 16.3 %all-to-all-start.1 = ((bf16[4,48,3584]{2,1,0:T(8,128)(2,1)}), bf16[4,48,3584]{2,1,0:T(8,128)(2,1)S(1)}, u32[]{:S(2)}, u32[]{:S(2)}) async-start(bf16[4,48,3584]{2,1,0:T(8,128)(2,1)} %bitcast.15), calls=%async_computation.1 | async-start | bytes 2752512 | tf_op jit(solution)/shard_map/all_to_all | solution.py:50
  91.2 0.7 collective-permute-start.4
  105.4 15.3 %collective-permute-start.13 = (bf16[24,3584]{1,0:T(8,128)(2,1)S(1)}, bf16[24,3584]{1,0:T(8,128)(2,1)S(1)}, u32[]{:S(2)}, u32[]{:S(2)}) collective-permute-start(bf16[24,3584]{1,0:T(8,128)(2,1)S(1)} %get-tuple-element.34.own_ref), channel_id=1, source_target_pairs={{32,0},{64,32},{96,64},{128,96},{160,128},{192,160},{224,192},{448... | collective-permute-start | bytes 516104 | tf_op jit(solution)/shard_map/ppermute | solution.py:448
  117.1 1.8 %collective-permute-start.14 = (bf16[24,1792]{1,0:T(8,128)(2,1)S(1)}, bf16[24,1792]{1,0:T(8,128)(2,1)S(1)}, u32[]{:S(2)}, u32[]{:S(2)}) collective-permute-start(bf16[24,1792]{1,0:T(8,128)(2,1)S(1)} %get-tuple-element.35), channel_id=1, source_target_pairs={{0,480},{480,0},{1,481},{481,1},{2,482},{482,2},{3,483},{483,3},{4... | collective-permute-start | bytes 258056 | tf_op jit(solution)/shard_map/ppermute | solution.py:452
  121.8 7.4 %collective-permute-start.15 = (bf16[2,48,224]{2,1,0:T(8,128)(2,1)S(1)}, bf16[2,48,224]{2,1,0:T(8,128)(2,1)S(1)}, u32[]{:S(2)}, u32[]{:S(2)}) collective-permute-start(bf16[2,48,224]{2,1,0:T(8,128)(2,1)S(1)} %get-tuple-element.40), channel_id=1, source_target_pairs={{0,192},{480,288},{1,193},{481,289},{2,194},{482,290},{3,195},{483... | collective-permute-start | bytes 129032 | tf_op jit(solution)/shard_map/ppermute | solution.py:473
  122.5 6.7 %collective-permute-start.16 = (bf16[2,48,224]{2,1,0:T(8,128)(2,1)S(1)}, bf16[2,48,224]{2,1,0:T(8,128)(2,1)S(1)}, u32[]{:S(2)}, u32[]{:S(2)}) collective-permute-start(bf16[2,48,224]{2,1,0:T(8,128)(2,1)S(1)} %get-tuple-element.39), channel_id=1, source_target_pairs={{0,128},{480,352},{1,129},{481,353},{2,130},{482,354},{3,131},{483... | collective-permute-start | bytes 129032 | tf_op jit(solution)/shard_map/ppermute | solution.py:473
  123.1 6.1 %collective-permute-start.17 = (bf16[2,48,224]{2,1,0:T(8,128)(2,1)S(1)}, bf16[2,48,224]{2,1,0:T(8,128)(2,1)S(1)}, u32[]{:S(2)}, u32[]{:S(2)}) collective-permute-start(bf16[2,48,224]{2,1,0:T(8,128)(2,1)S(1)} %get-tuple-element.38), channel_id=1, source_target_pairs={{0,64},{480,416},{1,65},{481,417},{2,66},{482,418},{3,67},{483,419... | collective-permute-start | bytes 129032 | tf_op jit(solution)/shard_map/ppermute | solution.py:473
  123.8 17.3 %collective-permute-start.11 = (bf16[24,3584]{1,0:T(8,128)(2,1)S(1)}, bf16[24,3584]{1,0:T(8,128)(2,1)S(1)}, u32[]{:S(2)}, u32[]{:S(2)}) collective-permute-start(bf16[24,3584]{1,0:T(8,128)(2,1)S(1)} %get-tuple-element.33), channel_id=1, source_target_pairs={{0,32},{32,64},{64,96},{96,128},{128,160},{160,192},{192,224},{480... | collective-permute-start | bytes 516104 | tf_op jit(solution)/shard_map/ppermute | solution.py:448
  128.5 12.6 %collective-permute-start.12 = (bf16[24,3584]{1,0:T(8,128)(2,1)S(1)}, bf16[24,3584]{1,0:T(8,128)(2,1)S(1)}, u32[]{:S(2)}, u32[]{:S(2)}) collective-permute-start(bf16[24,3584]{1,0:T(8,128)(2,1)S(1)} %get-tuple-element.33), channel_id=1, source_target_pairs={{224,256},{256,224},{225,257},{257,225},{226,258},{258,226},{227,2... | collective-permute-start | bytes 516104 | tf_op jit(solution)/shard_map/ppermute | solution.py:448
  129.2 12.6 %collective-permute-start.18 = (bf16[1,48,224]{2,1,0:T(8,128)(2,1)S(1)}, bf16[1,48,224]{2,1,0:T(8,128)(2,1)S(1)}, u32[]{:S(2)}, u32[]{:S(2)}) collective-permute-start(bf16[1,48,224]{2,1,0:T(8,128)(2,1)S(1)} %slice.48), channel_id=1, source_target_pairs={{0,32},{64,96},{128,160},{192,224},{480,448},{416,384},{352,320},{... | collective-permute-start | bytes 64520 | tf_op jit(solution)/shard_map/ppermute | solution.py:473
